TPU v7x, 32 devices: a whole 2x2x4 slice. The times are simulated.
32 devices in a mesh: dp: 8 (over y, x, core), mp: 4 (over z).
Axes of the slice: x: 2, y: 2, z: 4, core: 2. Of those that a mesh axis runs over, the one named last changes fastest.
Arguments:
- embedded: bfloat16 [8192, 1040], P('dp', 'mp'), may hold values from -6 to 6, as said below
- feature_ids: int32 [8192, 26], P('dp'), may hold values from 0 to 127
- day_ids: int32 [8192], P('dp'), may hold values from 0 to 23, as said below
- labels: int32 [8192], P('dp'), may hold values 0 or 1
- cross_weight: bfloat16 [3, 1040, 1040], P(None, 'mp'), may hold values from -0.1875 to 0.1875
- cross_bias: bfloat16 [3, 1040], P(None, 'mp'), may hold values from -3 to 3
- tower1: bfloat16 [1040, 1024], P(None, 'mp'), may hold values from -0.1875 to 0.1875
- tower1_bias: bfloat16 [1024], P('mp'), may hold values from -3 to 3
- tower2: bfloat16 [1024, 1024], P('mp'), may hold values from -0.1875 to 0.1875
- tower2_bias: bfloat16 [1024], P('mp'), may hold values from -3 to 3
- head_weight: bfloat16 [1024], P('mp'), may hold values from -0.1875 to 0.1875
Outputs:
- mean_loss: float32 [], replicated
- logits: float32 [8192], P('dp')
- embedded_grad: float32 [8192, 1040], P('dp', 'mp')
- cross_weight_grad: float32 [3, 1040, 1040], P(None, 'mp')
- cross_bias_grad: float32 [3, 1040], P(None, 'mp')
- tower1_grad: float32 [1040, 1024], P(None, 'mp')
- tower1_bias_grad: float32 [1024], P('mp')
- tower2_grad: float32 [1024, 1024], P('mp')
- tower2_bias_grad: float32 [1024], P('mp')
- head_grad: float32 [1024], P('mp')
- day_counts: int32 [24], replicated
- field_counts: int32 [26, 128], replicated
Inputs may be any that keep to these rules, and one draw needn't show every extreme that they name: `day_ids`: every day occurs in at least one example. `embedded`: columns 1027 to 1039 are zero.
All inputs are finite; a program needn't handle non-finite values. No bound on the sum of `labels` on one device may be relied on, other than what follows from the above.
Results may differ from a plain program's by a relative error of at most 0.0096.
Values may be sent and summed in bfloat16 or wider, within the bound.
No kernel may reach another device: no remote copies, remote signals or barrier semaphores. Data moves between devices by JAX's collectives and lax.ppermute only.
A program may use at most 64 MiB of HBM per device.

v0:
```python
import jax
import jax.numpy as jnp
from jax import lax
from jax.sharding import PartitionSpec as P

DAYS = 24
BUCKETS = 128


def gelu_parts(values):
    cdf_part = 0.5 * (1.0 + jax.scipy.special.erf(values * 0.7071067811865476))
    slope = cdf_part + values * jnp.exp(-0.5 * values * values) * 0.3989422804014327
    return (values * cdf_part, slope)


def spread_features(values):
    return lax.all_gather(values, "mp", axis=1, tiled=True)


def tally_field(column):
    return jnp.sum(
        (column[:, None] == jnp.arange(BUCKETS, dtype=jnp.int32)[None, :]).astype(jnp.int32), axis=0
    )


def per_device(
    embedded,
    feature_ids,
    day_ids,
    labels,
    cross_weight,
    cross_bias,
    tower1,
    tower1_bias,
    tower2,
    tower2_bias,
    head_weight,
):
    tok_rows = embedded.shape[0]
    layer_count = cross_weight.shape[0]
    examples = tok_rows * lax.axis_size("dp")
    day_table = day_ids[:, None] == jnp.arange(DAYS, dtype=jnp.int32)[None, :]
    local_days = jnp.sum(day_table.astype(jnp.int32), axis=0)
    local_fields = lax.map(tally_field, feature_ids.T)
    day_counts, field_counts = lax.psum((local_days, local_fields), "dp")
    x_start = embedded.astype(jnp.float32)
    state = x_start
    gathered = []
    zvalues = []
    for layer_index in range(layer_count):
        whole = spread_features(state.astype(jnp.bfloat16))
        gathered.append(whole)
        z_value = lax.dot_general(
            whole,
            cross_weight[layer_index],
            (((1,), (1,)), ((), ())),
            preferred_element_type=jnp.float32,
        )
        z_value = z_value + cross_bias[layer_index].astype(jnp.float32)[None, :]
        zvalues.append(z_value)
        state = x_start * z_value + state
    top_whole = spread_features(state.astype(jnp.bfloat16))
    pre_one = (
        jnp.dot(top_whole, tower1, preferred_element_type=jnp.float32)
        + tower1_bias.astype(jnp.float32)[None, :]
    )
    act_one, slope_one = gelu_parts(pre_one)
    act_low = act_one.astype(jnp.bfloat16)
    partial_two = jnp.dot(act_low, tower2, preferred_element_type=jnp.float32)
    pre_two = (
        lax.psum_scatter(partial_two, "mp", scatter_dimension=1, tiled=True)
        + tower2_bias.astype(jnp.float32)[None, :]
    )
    act_two, slope_two = gelu_parts(pre_two)
    head_full = head_weight.astype(jnp.float32)
    logits = lax.psum(jnp.sum(act_two * head_full[None, :], axis=1), "mp")
    day_float = day_table.astype(jnp.float32)
    label_float = labels.astype(jnp.float32)
    losses = jax.nn.softplus(logits) - label_float * logits
    local_loss = jnp.sum(day_float * losses[:, None], axis=0)
    loss_sums = lax.psum(local_loss, "dp")
    day_totals = day_counts.astype(jnp.float32)
    share_day = examples / (DAYS * day_totals)
    row_weight = jnp.sum(day_float * share_day[None, :], axis=1)
    total_loss = jnp.sum(loss_sums / day_totals) / DAYS
    grad_logit = row_weight * (jax.nn.sigmoid(logits) - label_float)
    head_grad = jnp.sum(grad_logit[:, None] * act_two, axis=0)
    grad_two = (grad_logit[:, None] * head_full[None, :] * slope_two).astype(jnp.bfloat16)
    tower2_bias_grad = jnp.sum(grad_two.astype(jnp.float32), axis=0)
    grad_two_whole = lax.all_gather(grad_two, "mp", axis=1, tiled=True)
    tower2_grad = lax.dot_general(
        act_low, grad_two_whole, (((0,), (0,)), ((), ())), preferred_element_type=jnp.float32
    )
    back_one = lax.dot_general(
        grad_two_whole, tower2, (((1,), (1,)), ((), ())), preferred_element_type=jnp.float32
    )
    grad_one = (back_one * slope_one).astype(jnp.bfloat16)
    tower1_bias_grad = jnp.sum(grad_one.astype(jnp.float32), axis=0)
    tower1_grad = lax.dot_general(
        top_whole, grad_one, (((0,), (0,)), ((), ())), preferred_element_type=jnp.float32
    )
    tower_terms = lax.dot_general(
        grad_one, tower1, (((1,), (1,)), ((), ())), preferred_element_type=jnp.float32
    )
    flow_grad = lax.psum_scatter(tower_terms, "mp", scatter_dimension=1, tiled=True)
    input_grad = jnp.zeros_like(x_start)
    weight_grads = [None] * layer_count
    bias_grads = [None] * layer_count
    for layer_index in reversed(range(layer_count)):
        grad_z = (flow_grad * x_start).astype(jnp.bfloat16)
        input_grad = input_grad + flow_grad * zvalues[layer_index]
        bias_grads[layer_index] = jnp.sum(grad_z.astype(jnp.float32), axis=0)
        weight_grads[layer_index] = lax.dot_general(
            grad_z,
            gathered[layer_index],
            (((0,), (0,)), ((), ())),
            preferred_element_type=jnp.float32,
        )
        back_term = lax.psum_scatter(
            jnp.dot(grad_z, cross_weight[layer_index], preferred_element_type=jnp.float32),
            "mp",
            scatter_dimension=1,
            tiled=True,
        )
        flow_grad = flow_grad + back_term
    input_grad = input_grad + flow_grad
    totals = lax.psum(
        (
            jnp.stack(weight_grads),
            jnp.stack(bias_grads),
            tower1_grad,
            tower1_bias_grad,
            tower2_grad,
            tower2_bias_grad,
            head_grad,
        ),
        "dp",
    )
    return (
        total_loss,
        logits,
        input_grad,
        totals[0],
        totals[1],
        totals[2],
        totals[3],
        totals[4],
        totals[5],
        totals[6],
        day_counts,
        field_counts,
    )


def solution(mesh):
    in_specs = (
        P("dp", "mp"),
        P("dp", None),
        P("dp"),
        P("dp"),
        P(None, "mp", None),
        P(None, "mp"),
        P(None, "mp"),
        P("mp"),
        P("mp", None),
        P("mp"),
        P("mp"),
    )
    out_specs = (
        P(),
        P("dp"),
        P("dp", "mp"),
        P(None, "mp", None),
        P(None, "mp"),
        P(None, "mp"),
        P("mp"),
        P("mp", None),
        P("mp"),
        P("mp"),
        P(),
        P(),
    )
    return jax.shard_map(
        per_device, mesh=mesh, in_specs=in_specs, out_specs=out_specs, check_vma=False
    )
```

profile of v0, /device:TPU:9, one launch (start us, length us, event | category | flops | bytes accessed | tf_op | source)
XLA Modules:
  0.0 767.7 jit_solution(13243699713034614396)
XLA Ops:
  8.8 47.1 %all-gather.12.cloned.1.call-done = bf16[4,260,1024]{2,1,0:T(8,128)(2,1)} async-done(((bf16[1,260,1024]{2,1,0:T(8,128)(2,1)}), bf16[4,260,1024]{2,1,0:T(8,128)(2,1)}) %all-gather.12.cloned.1.call-update) | async-done | bytes 2129936 | tf_op jit(solution)/shard_map/all_gather | solution.py:17
  55.9 2.8 reshape.37
  58.7 2.6 convolution_add_fusion.2
  62.4 46.1 %all-gather.14.cloned.1.call-done = bf16[4,260,1024]{2,1,0:T(8,128)(2,1)} async-done(((bf16[1,260,1024]{2,1,0:T(8,128)(2,1)}), bf16[4,260,1024]{2,1,0:T(8,128)(2,1)}) %all-gather.14.cloned.1.call-update) | async-done | bytes 2129936 | tf_op jit(solution)/shard_map/all_gather | solution.py:17
  108.5 2.8 reshape.39
  111.2 2.6 convolution_add_fusion.1
  115.1 46.1 %all-gather.16.cloned.1.call-done = bf16[4,260,1024]{2,1,0:T(8,128)(2,1)} async-done(((bf16[1,260,1024]{2,1,0:T(8,128)(2,1)}), bf16[4,260,1024]{2,1,0:T(8,128)(2,1)}) %all-gather.16.cloned.1.call-update) | async-done | bytes 2129936 | tf_op jit(solution)/shard_map/all_gather | solution.py:17
  161.1 2.8 reshape.41
  163.9 2.6 convolution_add_fusion
  167.5 1.2 fusion.33
  168.9 46.1 %all-gather.18.cloned.1.call-done = bf16[4,260,1024]{2,1,0:T(8,128)(2,1)} async-done(((bf16[1,260,1024]{2,1,0:T(8,128)(2,1)}), bf16[4,260,1024]{2,1,0:T(8,128)(2,1)}) %all-gather.18.cloned.1.call-update) | async-done | bytes 2129936 | tf_op jit(solution)/shard_map/all_gather | solution.py:17
  214.9 2.9 reshape.43
  217.8 3.5 multiply_convert_fusion
  221.3 2.7 fusion.46
  224.9 26.9 %while.10 = (s32[]{:T(128)}, s32[26,128]{1,0:T(8,128)S(1)}, s32[26,1024]{1,0:T(8,128)}, s32[]{:T(128)}, s32[]{:T(128)}) while((s32[]{:T(128)}, s32[26,128]{1,0:T(8,128)S(1)}, s32[26,1024]{1,0:T(8,128)}, s32[]{:T(128)}, s32[]{:T(128)}) %tuple.52), condition=%wide.region_28.29_spmd, body=%wide.region_26.28_spmd.sunk | while | flops 393090 | bytes 13901 | solution.py:44
  251.8 21.5 %all-reduce.8 = (s32[24]{0:T(128)S(1)}, s32[26,128]{1,0:T(8,128)}) all-reduce(s32[24]{0:T(128)S(1)} %convert_reduce_fusion.6, s32[26,128]{1,0:T(8,128)S(1)} %get-tuple-element.29), channel_id=1, replica_groups=mesh['dp'=8,'mp'=4] {'dp'}, use_global_device_ids=true, to_apply=%region_6.7 | all-reduce | flops 3352 | bytes 26816 | tf_op jit(solution)/shard_map/psum | solution.py:45
  273.3 28.6 %reduce-scatter.10.cloned.1.call-done = f32[1024,256]{1,0:T(8,128)} async-done(((f32[1024,1024]{1,0:T(8,128)}), f32[1024,256]{1,0:T(8,128)}) %reduce-scatter.10.cloned.1.call-update) | async-done | bytes 1048592 | tf_op jit(solution)/shard_map/reduce_scatter | solution.py:71
  301.9 2.6 multiply_reduce_fusion.1
  304.4 7.4 psum.77
  312.0 2.5 convert_reduce_fusion.4
  315.9 45.5 %all-gather.10.cloned.1.call-done = bf16[1024,1024]{1,0:T(8,128)(2,1)} async-done(((bf16[1024,256]{1,0:T(8,128)(2,1)}), bf16[1024,1024]{1,0:T(8,128)(2,1)}) %all-gather.10.cloned.1.call-update) | async-done | bytes 2097168 | tf_op jit(solution)/shard_map/all_gather | solution.py:90
  361.4 3.1 convert_reduce_fusion.5
  364.5 1.7 fusion.48
  366.2 2.8 fusion.47
  369.0 75.9 %fusion = f32[1024,264]{0,1:T(8,128)S(1)} fusion(f32[1024,1040]{0,1:T(8,128)} %fusion.47), kind=kCustom, calls=%all-reduce-scatter | all-reduce-scatter fusion | flops 1081345 | bytes 5341696
  444.9 2.7 collective-permute-start
  447.6 3.3 fusion.49
  450.9 3.1 concatenate
  455.1 4.4 fusion.23
  459.5 74.8 %fusion.1 = f32[1024,264]{0,1:T(8,128)} fusion(f32[1024,1040]{0,1:T(8,128)} %fusion.23), kind=kCustom, calls=%all-reduce-scatter.1 | all-reduce-scatter fusion | flops 1081345 | bytes 5341696
  535.2 2.5 collective-permute-start.1
  537.7 3.7 convolution_bitcast_fusion
  541.5 4.5 concatenate.1
  546.0 1.6 convert_reduce_fusion.2
  548.5 4.5 fusion.26
  553.0 73.4 %fusion.2 = f32[1024,264]{0,1:T(8,128)} fusion(f32[1024,1040]{0,1:T(8,128)} %fusion.26), kind=kCustom, calls=%all-reduce-scatter.2 | all-reduce-scatter fusion | flops 1081345 | bytes 5341696
  627.3 2.3 collective-permute-start.2
  629.6 3.8 convolution_bitcast_fusion.1
  633.4 4.6 concatenate.2
  638.0 2.3 convert_reduce_fusion.3
  641.2 4.6 fusion.29
  645.8 2.1 pad_maximum_fusion
  647.9 72.2 %fusion.3 = f32[1024,264]{0,1:T(8,128)} fusion(f32[1024,1040]{0,1:T(8,128)} %fusion.29), kind=kCustom, calls=%all-reduce-scatter.3 | all-reduce-scatter fusion | flops 1081345 | bytes 5341696
  720.9 3.5 collective-permute-start.3
  724.4 18.1 %all-reduce.9 = (f32[24]{0:T(128)S(1)}, f32[3,260]{1,0:T(4,128)}, f32[256]{0:T(256)}, f32[256]{0:T(256)}, f32[256]{0:T(256)}) all-reduce(f32[24]{0:T(128)S(1)} %get-tuple-element.31, f32[3,260]{1,0:T(4,128)S(1)} %pad_maximum_fusion.1, f32[256]{0:T(256)S(1)} %get-tuple-element.64, ...), channel_id=1, replica_groups=mesh['dp'=8,'mp'=4] {'dp'}, use_global_device_ids=true, to_apply=%region_4.5 | all-reduce | flops 1572 | bytes 12576 | tf_op jit(solution)/shard_map/psum | solution.py:81
  743.8 4.6 concatenate.3
  748.4 4.6 fusion.11
  753.0 4.2 copy.33
  (175 shorter events, 41.7 us)
Async XLA Ops:
  7.2 210.6 %copy-start = (bf16[1040,256]{1,0:T(8,128)(2,1)S(1)}, bf16[1040,256]{1,0:T(8,128)(2,1)}, u32[]{:S(2)}) copy-start(bf16[1040,256]{1,0:T(8,128)(2,1)} %param.19) | copy-start | bytes 1597444
  7.2 48.7 %all-gather.12.cloned.1.call-start = ((), (), s32[]{:S(2)}) async-start(), calls=%async_computation.3 | async-start | bytes 2703360 | tf_op jit(solution)/shard_map/all_gather | solution.py:17
  7.9 100.6 %all-gather.14.cloned.1.call-start = ((), (), s32[]{:S(2)}) async-start(), calls=%async_computation.4 | async-start | bytes 2703360 | tf_op jit(solution)/shard_map/all_gather | solution.py:17
  58.7 2.7 copy-start.2
  62.4 98.8 %all-gather.16.cloned.1.call-start = ((), (), s32[]{:S(2)}) async-start(), calls=%async_computation.5 | async-start | bytes 2703360 | tf_op jit(solution)/shard_map/all_gather | solution.py:17
  113.8 52.7 %copy-start.3 = (f32[1024,260]{0,1:T(8,128)}, f32[1024,260]{0,1:T(8,128)S(1)}, u32[]{:S(2)}) copy-start(f32[1024,260]{0,1:T(8,128)S(1)} %convolution_add_fusion.1) | copy-start | bytes 3194884
  115.0 99.9 %all-gather.18.cloned.1.call-start = ((), (), s32[]{:S(2)}) async-start(), calls=%async_computation.6 | async-start | bytes 2703360 | tf_op jit(solution)/shard_map/all_gather | solution.py:17
  166.5 1.0 copy-start.5
  167.5 1.3 copy-start.22
  168.8 133.1 %reduce-scatter.10.cloned.1.call-start = ((), (), s32[]{:S(2)}) async-start(), calls=%async_computation.1 | async-start | bytes 5242880 | tf_op jit(solution)/shard_map/reduce_scatter | solution.py:71
  217.8 3.5 copy-start.17
  221.3 2.7 copy-start.9
  224.1 0.7 copy-start.19
  224.1 49.2 %copy-start.23 = (bf16[256]{0:T(256)(128)(2,1)S(1)}, bf16[256]{0:T(256)(128)(2,1)}, u32[]{:S(2)}) copy-start(bf16[256]{0:T(256)(128)(2,1)} %param.22) | copy-start | bytes 1540
  224.1 49.2 %copy-start.24 = (bf16[256]{0:T(256)(128)(2,1)S(1)}, bf16[256]{0:T(256)(128)(2,1)}, u32[]{:S(2)}) copy-start(bf16[256]{0:T(256)(128)(2,1)} %param.23) | copy-start | bytes 1540
  224.1 137.3 %all-gather.10.cloned.1.call-start = ((), (), s32[]{:S(2)}) async-start(), calls=%async_computation.2 | async-start | bytes 2621440 | tf_op jit(solution)/shard_map/all_gather | solution.py:90
  224.9 87.0 %copy-start.20 = (s32[1024]{0:T(1024)S(1)}, s32[1024]{0:T(1024)}, u32[]{:S(2)}) copy-start(s32[1024]{0:T(1024)} %param.16) | copy-start | bytes 12292
  273.3 469.3 %copy-start.25 = (s32[24]{0:T(128)}, s32[24]{0:T(128)S(1)}, u32[]{:S(2)}) copy-start(s32[24]{0:T(128)S(1)} %get-tuple-element.110) | copy-start | bytes 292
  301.9 10.1 %copy-start.6 = (f32[1024,256]{1,0:T(8,128)S(1)}, f32[1024,256]{1,0:T(8,128)}, u32[]{:S(2)}) copy-start(f32[1024,256]{1,0:T(8,128)} %reduce-scatter.10.cloned.1.call-done) | copy-start | bytes 3145732
  311.8 2.7 copy-start.18
  312.0 2.6 copy-start.21
  314.6 438.4 %all-reduce.13.cloned.1.call-start = ((), (), s32[]{:S(2)}) async-start(), calls=%async_computation.7 | async-start | bytes 11526144 | tf_op jit(solution)/shard_map/psum | solution.py:127
  361.4 3.1 copy-start.12
  369.0 78.6 %copy-start.10 = (bf16[1024,256]{1,0:T(8,128)(2,1)S(1)}, bf16[1024,256]{1,0:T(8,128)(2,1)}, u32[]{:S(2)}) copy-start(bf16[1024,256]{1,0:T(8,128)(2,1)} %copy-done.9) | copy-start | bytes 1572868
  444.9 6.0 copy-start.4
  444.9 6.0 collective-permute-start
  454.3 0.8 copy-start.7
  535.2 6.3 collective-permute-start.1
  547.7 0.8 copy-start.8
  627.3 6.2 collective-permute-start.2
  638.0 2.3 copy-start.11
  641.2 4.6 copy-start.13
  641.2 4.6 copy-start.14
  720.9 22.9 %collective-permute-start.3 = (f32[1024,12]{0,1:T(8,128)S(1)}, f32[1024,12]{0,1:T(8,128)S(1)}, u32[]{:S(2)}, u32[]{:S(2)}) collective-permute-start(f32[1024,12]{0,1:T(8,128)S(1)} %slice.30), channel_id=1, source_target_pairs={{0,1},{1,2},{2,3},{4,5},{5,6},{6,7},{8,9},{9,10},{10,11},{12,13},{... | collective-permute-start | bytes 147464
  753.0 4.2 copy-start.15
  757.2 1.6 copy-start.16
  757.2 2.6 copy-start.1
Sparse Core Ops, SparseCore 0:
  9.6 46.2 all-gather.11
  62.5 45.9 all-gather.13
  115.1 45.9 all-gather.15
  168.9 45.9 all-gather.17
  224.2 77.6 reduce-scatter.9
  314.7 46.6 all-gather.9
  648.0 103.3 all-reduce.12
where the time goes:
time: 774 us; the launch traced here: 768 us
  blocking collectives  343 us (44%)
  waiting for transfers between devices  260 us (34%)
  local copies, waits for them, and re-layouts  62.1 us (8%)
  matrix products  47 us (6%)
  other arithmetic  26.6 us (3%)
  between operations  16.9 us (2%)
  starting transfers between devices  11.3 us (1%)
    unnamed x4, blocking collectives  296 us
    all_gather x4, waiting for transfers between devices, spread_features(): return lax.all_gather(values, 'mp', axis=1, tiled=True)  185 us
    all_gather x1, waiting for transfers between devices, per_device(): grad_two_whole = lax.all_gather(grad_two, 'mp', axis=1, tiled=True)  45.5 us
    unnamed x68, local copies, waits for them, and re-layouts  41.2 us
    reduce_scatter x1, waiting for transfers between devices, per_device(): lax.psum_scatter(partial_two, 'mp', scatter_dimension=1, tiled=True)  28.6 us
    psum x1, blocking collectives, per_device(): day_counts, field_counts = lax.psum((local_days, local_fields), 'dp')  21.5 us
    dynamic_slice x26, local copies, waits for them, and re-layouts, per_device(): local_fields = lax.map(tally_field, feature_ids.T)  20 us
    psum x1, blocking collectives, per_device(): loss_sums = lax.psum(local_loss, 'dp')  18.1 us
  transfers between devices with their start and end apart: 11, of which 6 were waited for; matrix products, arithmetic and copies ran while one was open for 16% of the time, Pallas kernels for 0%

commit v1 on v0

v1 whole, which is shorter than its diff:
```python
import functools

import jax
import jax.numpy as jnp
from jax import lax
from jax.experimental import pallas as pl
from jax.experimental.pallas import tpu as pltpu
from jax.sharding import PartitionSpec as P

DAYS = 24
BUCKETS = 128
BF16 = jnp.bfloat16
F32 = jnp.float32
MAIN = 256
SHARE = 32
VMEM = pl.BlockSpec(memory_space=pltpu.VMEM)
SMEM = pl.BlockSpec(memory_space=pltpu.SMEM)
NT = (((1,), (1,)), ((), ()))
TN = (((0,), (0,)), ((), ()))
NN = (((1,), (0,)), ((), ()))


def gelu_parts(values):
    cdf_part = 0.5 * (1.0 + lax.erf(values * 0.7071067811865476))
    slope = cdf_part + values * jnp.exp(-0.5 * values * values) * 0.3989422804014327
    return (values * cdf_part, slope)


def dot(lhs, rhs, dims, precision=None):
    return lax.dot_general(lhs, rhs, dims, preferred_element_type=F32, precision=precision)


def call(kernel, outs, scratch, *args, flops=0, nbytes=0):
    return pl.pallas_call(
        kernel,
        out_shape=outs,
        in_specs=[SMEM] + [VMEM] * (len(args) - 1),
        out_specs=jax.tree.map(lambda _: VMEM, outs),
        scratch_shapes=scratch,
        compiler_params=pltpu.CompilerParams(vmem_limit_bytes=60 * 1024 * 1024),
        cost_estimate=pl.CostEstimate(flops=flops, bytes_accessed=nbytes, transcendentals=0),
    )(*args)


def places(idx):
    core, plane = idx[1], idx[2]
    first, second = core + 1, 2 - core
    mine = [plane, plane ^ first, plane ^ second, plane ^ 3]
    theirs = [plane, plane ^ second, plane ^ first, plane ^ 3]
    return [core * 128 + SHARE * q for q in mine] + [(1 - core) * 128 + SHARE * q for q in theirs]


def block_of(idx, turn, blocks):
    return lax.rem(idx[0] - turn + blocks, blocks)


def rows_at(offset, size, unit=16):
    return pl.ds(pl.multiple_of(offset, unit), size)


def cross_forward(idx, *refs, blocks, layers, width, pad, depth):
    pieces, refs = refs[:blocks], refs[blocks:]
    own, refs = refs[0], refs[1:]
    turned, refs = refs[: blocks - 1], refs[blocks - 1 :]
    slices, refs = refs[:8], refs[8:]
    w_out, z_out, x_out, x0_out, start, state, nat, tail, tails = refs
    left = width - MAIN
    offsets = places(idx)
    tail[...] = jnp.zeros_like(tail)
    start[...] = jnp.zeros_like(start)
    for turn in range(blocks):
        start[block_of(idx, turn, blocks), 0:width, :] = pieces[turn][...].astype(F32)
    state[...] = start[...]
    for block in range(blocks):
        x0_out[pad * block : pad * (block + 1), :] = start[block].astype(BF16)
    for layer in range(layers):
        base = idx[0] * pad
        w_out[layer, rows_at(base, MAIN), :] = own[layer, 0:MAIN, :]
        tail[0:left, :] = own[layer, MAIN:width, :].astype(F32)
        w_out[layer, rows_at(base + MAIN, 16), :] = tail[...].astype(BF16)
    for turn in range(1, blocks):
        base = block_of(idx, turn, blocks) * pad
        tails[...] = turned[turn - 1][layers * SHARE : layers * SHARE + 16, :].astype(F32)
        for layer in range(layers):
            tail[0:left, :] = tails[left * layer : left * (layer + 1), :]
            w_out[layer, rows_at(base + MAIN, 16), :] = tail[...].astype(BF16)
            for offset, piece in zip(offsets, slices):
                w_out[layer, rows_at(base + offset, SHARE), :] = piece[
                    turn - 1, SHARE * layer : SHARE * (layer + 1), :
                ]
    full = nat.shape[0]
    ones = lax.broadcasted_iota(jnp.int32, (full - depth, nat.shape[1]), 0) == 0
    nat[depth:full, :] = ones.astype(F32)
    for layer in range(layers + 1):
        for block in range(blocks):
            nat[width * block : width * (block + 1), :] = state[block, 0:width, :]
        x_out[layer] = nat[...].astype(BF16)
        if layer == layers:
            break

        def step(block, carry, layer=layer):
            rows = rows_at(block * pad, pad)
            z_value = dot(w_out[layer, rows, :], x_out[layer], NN)
            z_out[layer, rows, :] = z_value
            state[block] = start[block] * z_value + state[block]
            return carry

        lax.fori_loop(0, blocks, step, 0)


def tower_both(idx, *refs, blocks, depth, days):
    x3, own1, own2 = refs[:3]
    slices, refs = refs[3:11], refs[11:]
    labels, day_ids, share = refs[:3]
    g1, da2, da1, dx3, logits_out, row1, row2, row_head, row_loss = refs[3:12]
    t1, t2, slope1, act2, headed, total = refs[12:]
    hidden = t1.shape[0]
    size = hidden // blocks
    offsets = places(idx)
    base = idx[0] * size
    t1[rows_at(base, size), :] = own1[...]
    t2[rows_at(base, size), :] = own2[...]
    for turn in range(1, blocks):
        base = block_of(idx, turn, blocks) * size
        for offset, piece in zip(offsets, slices):
            t1[rows_at(base + offset, SHARE), :] = piece[turn - 1, 0:SHARE, :]
            t2[rows_at(base + offset, SHARE), :] = piece[turn - 1, SHARE : 2 * SHARE, 0:hidden]
    low = depth // 128 * 128

    def first(block, carry):
        rows = rows_at(block * size, size)
        act, slope = gelu_parts(dot(t1[rows, :], x3[...], NN))
        g1[rows, :] = act.astype(BF16)
        slope1[rows, :] = slope
        return carry

    lax.fori_loop(0, blocks, first, 0)
    total[...] = jnp.zeros_like(total)

    def second(block, carry):
        rows = rows_at(block * size, size, 128)
        columns = t1[rows, low:].astype(F32)
        head = columns[:, depth - low + 1 : depth - low + 2]
        bias = columns[:, depth - low + 2 : depth - low + 3]
        act, slope = gelu_parts(dot(t2[:, rows], g1[...], TN) + bias)
        act2[rows, :] = act
        headed[rows, :] = head * slope
        total[...] += jnp.sum(act * head, axis=0, keepdims=True)
        return carry

    lax.fori_loop(0, blocks, second, 0)
    logits = total[...]
    logits_out[...] = logits
    lab = labels[...].astype(F32)
    table = (
        lax.broadcasted_iota(jnp.int32, share.shape, 0) == day_ids[...]
    ).astype(F32)
    weight = jnp.sum(table * share[...], axis=0, keepdims=True)
    decay = jnp.exp(-jnp.abs(logits))
    loss = jnp.maximum(logits, 0.0) + jnp.log1p(decay) - lab * logits
    sigmoid = jnp.where(logits >= 0.0, 1.0, decay) / (1.0 + decay)
    dl = weight * (sigmoid - lab)
    exact = lax.Precision.HIGHEST
    spread = lambda row: jnp.broadcast_to(row, (8, row.shape[1]))
    row_loss[...] = dot(spread(loss), table, NT, exact)
    row_head[...] = dot(spread(dl), act2[...], NT, exact)
    da2[...] = (dl * headed[...]).astype(BF16)
    ones = jnp.ones((8, dl.shape[1]), BF16)
    row2[...] = dot(ones, da2[...], NT)

    def third(block, carry):
        rows = rows_at(block * size, size)
        da1[rows, :] = (dot(t2[rows, :], da2[...], NN) * slope1[rows, :]).astype(BF16)
        return carry

    lax.fori_loop(0, blocks, third, 0)
    row1[...] = dot(ones, da1[...], NT)

    def fourth(tile, carry):
        rows = rows_at(tile * 384, 384, 128)
        dx3[rows, :] = dot(t1[:, rows], da1[...], TN)
        return carry

    lax.fori_loop(0, t1.shape[1] // 384, fourth, 0)


def cross_backward(idx, dx3, x0, z_all, w_all, x_all, logits, dz_out, eg_out, rows_out, left_out, flow, padded, total, *, blocks, layers, width, pad, depth):
    flow[...] = dx3[...]
    total[...] = jnp.zeros_like(total)
    padded[...] = jnp.zeros_like(padded)
    ones = jnp.ones((8, x0.shape[1]), BF16)
    left = width - MAIN
    for layer in reversed(range(layers)):
        for block in range(blocks):
            padded[block, 0:width, :] = flow[width * block : width * (block + 1), :]
            rows = slice(pad * block, pad * (block + 1))
            dx = padded[block]
            dz_out[layer, rows, :] = (dx * x0[rows, :].astype(F32)).astype(BF16)
            total[block] += dx * z_all[layer, rows, :]
            left_out[layer, 16 * block : 16 * (block + 1), :] = dot(
                dz_out[layer, pad * block + MAIN : pad * (block + 1), :], x_all[layer], NT
            )
        rows_out[layer, :, :] = dot(ones, dz_out[layer], NT)

        def step(tile, carry, layer=layer):
            rows = rows_at(tile * 384, 384, 128)
            flow[rows, :] += dot(w_all[layer, :, rows], dz_out[layer], TN)
            return carry

        lax.fori_loop(0, flow.shape[0] // 384, step, 0)
    line = logits[...]
    high = line.astype(BF16).astype(F32)
    middle = (line - high).astype(BF16).astype(F32)
    low = line - high - middle
    for block in range(blocks):
        padded[block, 0:width, :] = flow[width * block : width * (block + 1), :]
        total[block] += padded[block]
        total[block, width : width + 1, :] = high
        total[block, width + 1 : width + 2, :] = middle
        total[block, width + 2 : width + 3, :] = low
        eg_out[pad * block : pad * (block + 1), :] = total[block].astype(BF16)


def relative(idx, part):
    turned = part ^ idx[2]
    one, two = turned & 1, (turned >> 1) & 1
    return jnp.where(idx[1] == 0, one * 2 + two, two * 2 + one)


def tower_grads(idx, x_own, x_far, g1_own, g1_far, da2_own, da2_far, da1_own, da1_far, out, *, blocks, depth):
    hidden = g1_own.shape[0]
    size = hidden // blocks

    def step(block, carry):
        rows = rows_at(block * size + idx[1] * 128, 128)
        slot = lax.rem(block - idx[0] + blocks, blocks)
        grad1 = dot(da1_own[rows, :], x_own[...], NT) + dot(da1_far[block], x_far[...], NT)
        grad2 = dot(g1_own[rows, :], da2_own[...], NT) + dot(g1_far[block], da2_far[...], NT)
        for part in range(4):
            at = relative(idx, part)
            lines = slice(SHARE * part, SHARE * (part + 1))
            out[at, slot, 0:SHARE, :] = grad1[lines, :].astype(BF16)
            out[at, slot, SHARE : 2 * SHARE, 0:hidden] = grad2[lines, :].astype(BF16)
            out[at, slot, SHARE : 2 * SHARE, hidden:] = jnp.zeros((SHARE, out.shape[3] - hidden), BF16)
        return carry

    lax.fori_loop(0, blocks, step, 0)


def cross_grads(idx, x_own, x_far, dz_own, dz_far, out, *, blocks, layers, pad):
    for layer in range(layers):

        def step(block, carry, layer=layer):
            rows = rows_at(block * pad + idx[1] * 128, 128)
            slot = lax.rem(block - idx[0] + blocks, blocks)
            grad = dot(dz_own[layer, rows, :], x_own[layer], NT) + dot(dz_far[layer, block], x_far[layer], NT)
            for part in range(4):
                out[relative(idx, part), slot, SHARE * layer : SHARE * (layer + 1), :] = grad[
                    SHARE * part : SHARE * (part + 1), :
                ].astype(BF16)
            return carry

        lax.fori_loop(0, blocks, step, 0)


def finish_tower(idx, *refs):
    slices, (out1, out2, lines) = refs[:8], refs[8:]
    hidden = out2.shape[1]
    for offset, piece in zip(places(idx), slices):
        lines[rows_at(offset, SHARE), :] = piece[0:SHARE, :].astype(F32)
        out2[rows_at(offset, SHARE), :] = piece[SHARE : 2 * SHARE, 0:hidden].astype(F32)
    out1[...] = lines[...].T[0 : out1.shape[0], :]


def finish_cross(idx, *refs):
    slices, (rest, out) = refs[:8], refs[8:]
    left = out.shape[1] - MAIN
    depth = out.shape[2]
    for layer in range(out.shape[0]):
        for offset, piece in zip(places(idx), slices):
            out[layer, rows_at(offset, SHARE), :] = piece[SHARE * layer : SHARE * (layer + 1), 0:depth].astype(F32)
        out[layer, MAIN:, :] = rest[left * layer : left * (layer + 1), 0:depth]


def finish_input(idx, *refs):
    pieces, (out, logits) = refs[:-2], refs[-2:]
    width = out.shape[0]
    size = pieces[0].shape[1]
    for turn, piece in enumerate(pieces):
        lanes = pl.ds(pl.multiple_of(block_of(idx, turn, len(pieces)) * size, 128), size)
        values = piece[...].astype(F32)
        out[:, lanes] = values[0:width, :]
        logits[:, lanes] = values[width : width + 1, :] + values[width + 1 : width + 2, :] + values[width + 2 : width + 3, :]


def per_device(
    embedded,
    feature_ids,
    day_ids,
    labels,
    cross_weight,
    cross_bias,
    tower1,
    tower1_bias,
    tower2,
    tower2_bias,
    head_weight,
):
    blocks = lax.axis_size("mp")
    groups = lax.axis_size("dp")
    tokens, width = embedded.shape
    layers, _, depth = cross_weight.shape
    size, hidden = tower2.shape
    pad = -(-width // 16) * 16
    full = -(-(depth + 3) // 128) * 128
    left = width - MAIN
    part = tokens // blocks
    examples = tokens * groups
    shape = jax.ShapeDtypeStruct

    me = lax.axis_index("mp")
    group = lax.axis_index("dp")
    core, plane = group & 1, (group >> 1) & 3
    idx = jnp.stack([me, core, plane]).astype(jnp.int32)
    own_row = core * 128 + plane * SHARE
    swap = lambda bits: [(i, i ^ bits(i)) for i in range(groups)]
    first = swap(lambda i: 4 if i & 1 else 2)
    second = swap(lambda i: 2 if i & 1 else 4)
    pair = swap(lambda i: 1)
    others = [swap(lambda i, b=b: 1 << b) for b in range(3, groups.bit_length() - 1)]
    turn_by = lambda r: [(i, (i + r) % blocks) for i in range(blocks)]
    hop = lambda value, perm: lax.ppermute(value, "dp", perm)
    turns = lambda values: [
        lax.ppermute(value, "mp", turn_by(r + 1)) for r, value in enumerate(values)
    ]
    ahead = [lax.rem(me + r, blocks) for r in range(blocks)]

    day_hits = day_ids[None, :] == jnp.arange(DAYS, dtype=jnp.int32)[:, None]
    field_hits = feature_ids.T[:, None, :] == jnp.arange(BUCKETS, dtype=jnp.int32)[None, :, None]
    day_line = jnp.pad(jnp.sum(day_hits.astype(jnp.int32), axis=1), (0, BUCKETS - DAYS))
    counts = jnp.concatenate([jnp.sum(field_hits.astype(jnp.int32), axis=2), day_line[None, :]])

    turned_inputs = embedded.T
    chunks = [lax.dynamic_slice(turned_inputs, (0, ahead[r] * part), (width, part)) for r in range(blocks)]
    pieces = [chunks[0]] + turns(chunks[1:])
    fill = lambda *s: jnp.zeros(s, BF16)
    cross_own = jnp.concatenate(
        [cross_weight, cross_bias[:, :, None], fill(layers, width, full - depth - 1)], axis=2
    )
    tower_own = jnp.concatenate(
        [tower1.T, tower1_bias[:, None], head_weight[:, None], tower2_bias[:, None], fill(size, full - depth - 3)],
        axis=1,
    )
    cross_send = jnp.concatenate(
        [
            lax.dynamic_slice(cross_own, (0, own_row, 0), (layers, SHARE, full)).reshape(layers * SHARE, full),
            cross_own[:, MAIN:, :].reshape(layers * left, full),
            fill(16 - layers * left, full),
        ]
    )
    tower_send = jnp.concatenate(
        [
            lax.dynamic_slice(tower_own, (own_row, 0), (SHARE, full)),
            jnp.pad(lax.dynamic_slice(tower2, (own_row, 0), (SHARE, hidden)), ((0, 0), (0, full - hidden))),
        ]
    )

    def hand_round(mine):
        one, two = hop(mine, first), hop(mine, second)
        held = [mine, one, two, hop(one, second)]
        return held + [hop(value, pair) for value in held]

    cross_turned = turns([cross_send] * (blocks - 1))
    cross_slices = hand_round(jnp.stack([value[: layers * SHARE] for value in cross_turned]))
    tower_turned = turns([tower_send] * (blocks - 1))
    tower_slices = hand_round(jnp.stack(tower_turned))

    for perm in [pair, first, second] + others:
        counts = counts + hop(counts, perm)
    field_counts, day_counts = counts[:-1], counts[-1, :DAYS]
    day_totals = day_counts.astype(F32)
    share_day = jnp.pad(examples / (DAYS * day_totals), (0, 32 - DAYS))
    share_day = jnp.broadcast_to(share_day[:, None], (32, part))

    cut = lambda values: lax.dynamic_slice(values, (me * part,), (part,))[None, :]
    flat = blocks * pad
    cross_w, z_all, x_all, x0 = call(
        functools.partial(cross_forward, blocks=blocks, layers=layers, width=width, pad=pad, depth=depth),
        (
            shape((layers, flat, full), BF16),
            shape((layers, flat, part), F32),
            shape((layers + 1, full, part), BF16),
            shape((flat, part), BF16),
        ),
        [
            pltpu.VMEM((blocks, pad, part), F32),
            pltpu.VMEM((blocks, pad, part), F32),
            pltpu.VMEM((full, part), F32),
            pltpu.VMEM((16, full), F32),
            pltpu.VMEM((16, full), F32),
        ],
        idx,
        *pieces,
        cross_own,
        *cross_turned,
        *cross_slices,
        flops=2 * layers * flat * full * part,
        nbytes=20 << 20,
    )
    x_far = hop(x_all, pair)
    g1, da2, da1, dx3, logits, row1, row2, row_head, row_loss = call(
        functools.partial(tower_both, blocks=blocks, depth=depth, days=DAYS),
        (
            shape((hidden, part), BF16),
            shape((hidden, part), BF16),
            shape((hidden, part), BF16),
            shape((full, part), F32),
            shape((1, part), F32),
            shape((8, hidden), F32),
            shape((8, hidden), F32),
            shape((8, hidden), F32),
            shape((8, 32), F32),
        ),
        [
            pltpu.VMEM((hidden, full), BF16),
            pltpu.VMEM((hidden, hidden), BF16),
            pltpu.VMEM((hidden, part), F32),
            pltpu.VMEM((hidden, part), F32),
            pltpu.VMEM((hidden, part), F32),
            pltpu.VMEM((1, part), F32),
        ],
        idx,
        x_all[layers],
        tower_own,
        tower2,
        *tower_slices,
        cut(labels),
        cut(day_ids),
        share_day,
        flops=4 * 2 * hidden * full * part,
        nbytes=10 << 20,
    )
    far_half = lambda values, rows: lax.dynamic_slice_in_dim(
        values.reshape(values.shape[:-2] + (blocks, rows, part)), (1 - core) * 128, 128, axis=values.ndim - 1
    )
    g1_far = hop(far_half(g1, size), pair)
    da2_far = hop(da2, pair)
    da1_far = hop(far_half(da1, size), pair)
    tower_parts = call(
        functools.partial(tower_grads, blocks=blocks, depth=depth),
        shape((4, blocks, 2 * SHARE, full), BF16),
        [],
        idx,
        x_all[layers],
        x_far[layers],
        g1,
        g1_far,
        da2,
        da2_far,
        da1,
        da1_far,
        flops=4 * hidden * full * part,
        nbytes=10 << 20,
    )
    dz, input_grad, row_cross, left_cross = call(
        functools.partial(cross_backward, blocks=blocks, layers=layers, width=width, pad=pad, depth=depth),
        (
            shape((layers, flat, part), BF16),
            shape((flat, part), BF16),
            shape((layers, 8, flat), F32),
            shape((layers, 16 * blocks, full), F32),
        ),
        [
            pltpu.VMEM((full, part), F32),
            pltpu.VMEM((blocks, pad, part), F32),
            pltpu.VMEM((blocks, pad, part), F32),
        ],
        idx,
        dx3,
        x0,
        z_all,
        cross_w,
        x_all,
        logits,
        flops=2 * layers * flat * full * part,
        nbytes=20 << 20,
    )
    dz_far = hop(far_half(dz, pad), pair)
    cross_parts = call(
        functools.partial(cross_grads, blocks=blocks, layers=layers, pad=pad),
        shape((4, blocks, layers * SHARE, full), BF16),
        [],
        idx,
        x_all,
        x_far,
        dz,
        dz_far,
        flops=2 * layers * flat * full * part,
        nbytes=20 << 20,
    )

    def gather_sum(parts):
        held = parts[:2].astype(F32) + hop(parts[2:], first).astype(F32)
        held = held[0] + hop(held[1].astype(BF16), second).astype(F32)
        arrived = turns([held[r].astype(BF16) for r in range(1, blocks)])
        held = held[0] + sum(value.astype(F32) for value in arrived)
        for perm in others:
            held = held + hop(held, perm)
        return hand_round(held.astype(BF16))

    tower_sums = gather_sum(tower_parts)
    cross_sums = gather_sum(cross_parts)

    blocks_of = [lax.dynamic_slice(input_grad, (ahead[r] * pad, 0), (pad, part)) for r in range(blocks)]
    grad_pieces = [blocks_of[0]] + turns(blocks_of[1:])
    input_out, logits_all = call(
        finish_input,
        (shape((width, tokens), F32), shape((1, tokens), F32)),
        [],
        idx,
        *grad_pieces,
        nbytes=2 << 20,
    )

    lines = lambda values: jnp.pad(values, ((0, 0), (0, full - values.shape[1])))
    common = jnp.concatenate(
        [lines(row_cross[:, 0, :]), lines(row1[:1]), lines(row2[:1]), lines(row_head[:1]), lines(row_loss[:1])]
    )
    rest = left_cross.reshape(layers, blocks, 16, full)[:, :, :left, :]
    rest = rest.transpose(1, 0, 2, 3).reshape(blocks, layers * left, full)
    small = jnp.concatenate([rest, jnp.broadcast_to(common[None], (blocks,) + common.shape)], axis=1)
    small_turned = [lax.dynamic_index_in_dim(small, ahead[r], 0, keepdims=False) for r in range(blocks)]
    small_turned = [small_turned[0]] + turns(small_turned[1:])
    in_order = jnp.stack(small_turned[::-1] * 2)
    in_order = lax.dynamic_slice_in_dim(in_order, blocks - 1 - me, blocks, axis=0)
    small = in_order[0]
    for value in range(1, blocks):
        small = small + in_order[value]
    for perm in [pair, first, second] + others:
        small = small + hop(small, perm)

    tower1_grad, tower2_grad = call(
        finish_tower,
        (shape((depth, size), F32), shape((size, hidden), F32)),
        [pltpu.VMEM((size, full), F32)],
        idx,
        *tower_sums,
        nbytes=4 << 20,
    )
    cross_grad = call(
        finish_cross,
        shape((layers, width, depth), F32),
        [],
        idx,
        *cross_sums,
        small,
        nbytes=4 << 20,
    )
    count = layers * left
    cross_bias_grad = lax.dynamic_slice(small, (count, me * pad), (layers, width))
    line = lambda at: lax.dynamic_slice(small, (at, me * size), (1, size))[0]
    loss_sums = small[count + layers + 3, :DAYS]
    total_loss = jnp.sum(loss_sums / day_totals) / DAYS
    return (
        total_loss,
        logits_all[0],
        input_out.T,
        cross_grad,
        cross_bias_grad,
        tower1_grad,
        line(count + layers),
        tower2_grad,
        line(count + layers + 1),
        line(count + layers + 2),
        day_counts,
        field_counts,
    )


def solution(mesh):
    in_specs = (
        P("dp", "mp"),
        P("dp", None),
        P("dp"),
        P("dp"),
        P(None, "mp", None),
        P(None, "mp"),
        P(None, "mp"),
        P("mp"),
        P("mp", None),
        P("mp"),
        P("mp"),
    )
    out_specs = (
        P(),
        P("dp"),
        P("dp", "mp"),
        P(None, "mp", None),
        P(None, "mp"),
        P(None, "mp"),
        P("mp"),
        P("mp", None),
        P("mp"),
        P("mp"),
        P(),
        P(),
    )
    return jax.shard_map(
        per_device, mesh=mesh, in_specs=in_specs, out_specs=out_specs, check_vma=False
    )
```

time: 774 us -> 291 us (0.38)
  blocking collectives: 343 us -> 0 us
  waiting for transfers between devices: 260 us -> 106 us
  Pallas kernels: 0 us -> 65.2 us
  starting transfers between devices: 11.3 us -> 73.9 us
  matrix products: 47 us -> 0 us
  local copies, waits for them, and re-layouts: 62.1 us -> 31.9 us
  other arithmetic: 26.6 us -> 7.74 us
  between operations: 16.9 us -> 3.35 us
    unnamed x4 -> x0, blocking collectives: 296 us -> none
    all_gather x5 -> x0, waiting for transfers between devices: 231 us -> none  [the longest x4 185 us: spread_features(): return lax.all_gather(values, 'mp', axis=1, tiled=True)]
    ppermute x0 -> x64, waiting for transfers between devices: none -> 106 us  [the longest x43 54.5 us: per_device(): hop = lambda value, perm: lax.ppermute(value, 'dp', perm)]
    ppermute x0 -> x64, starting transfers between devices: none -> 73.9 us  [the longest x43 43.4 us: per_device(): hop = lambda value, perm: lax.ppermute(value, 'dp', perm)]
    pallas_call x0 -> x8, Pallas kernels: none -> 65.2 us  [call(): pl.pallas_call(kernel, out_shape=outs, in_specs=[SMEM] + [VMEM] * (len(ar...]
    dot_general x15 -> x0, matrix products: 47 us -> none  [the longest x3 13.5 us: per_device(): jnp.dot(grad_z, cross_weight[layer_index], preferred_element_type=jnp.flo...]
    psum x3 -> x0, blocking collectives: 47 us -> none  [the longest x1 21.5 us: per_device(): day_counts, field_counts = lax.psum((local_days, local_fields), 'dp')]
    unnamed x68 -> x107, local copies, waits for them, and re-layouts: 41.2 us -> 3.72 us
  transfers between devices with their start and end apart: 11 -> 64, of which waited for: 6 -> 20; matrix products, arithmetic and copies ran while one was open for 16% -> 11% of each run, Pallas kernels for 0% -> 21%
where the time goes in v1:
time: 291 us; the launch traced here: 289 us
  waiting for transfers between devices  106 us (36%)
  starting transfers between devices  73.9 us (25%)
  Pallas kernels  65.2 us (22%)
  local copies, waits for them, and re-layouts  31.9 us (11%)
  other arithmetic  7.74 us (3%)
  between operations  3.35 us (1%)
    pallas_call x8, Pallas kernels, call(): pl.pallas_call(kernel, out_shape=outs, in_specs=[SMEM] + [VMEM] * (len(ar...  65.2 us
    ppermute x43, waiting for transfers between devices, per_device(): hop = lambda value, perm: lax.ppermute(value, 'dp', perm)  54.5 us
    ppermute x21, waiting for transfers between devices, per_device(): lax.ppermute(value, 'mp', turn_by(r + 1))  52 us
    ppermute x43, starting transfers between devices, per_device(): hop = lambda value, perm: lax.ppermute(value, 'dp', perm)  43.4 us
    ppermute x21, starting transfers between devices, per_device(): lax.ppermute(value, 'mp', turn_by(r + 1))  30.5 us
  transfers between devices with their start and end apart: 64, of which 20 were waited for; matrix products, arithmetic and copies ran while one was open for 11% of the time, Pallas kernels for 21%

profile of v1, /device:TPU:9, one launch (start us, length us, event | category | flops | bytes accessed | tf_op | source)
XLA Modules:
  0.0 288.6 jit_solution(2994890205892388667)
XLA Ops:
  1.6 2.9 %concatenate.21.refs_4_ = bf16[3,260,1152]{2,1,0:T(8,128)(2,1)S(1)} concatenate(bf16[3,260,1040]{2,1,0:T(8,128)(2,1)} %param.15, bf16[3,260,1]{2,1,0:T(8,128)(2,1)S(1)} %copy.32, bf16[3,260,111]{2,1,0:T(8,128)(2,1)S(1)} %broadcast_in_dim.47), dimensions={2} | concatenate | bytes 3594240 | tf_op jit(solution)/shard_map/concatenate | solution.py:347
  8.1 1.5 collective-permute-start.5
  16.0 22.0 %collective-permute-done.5.refs_7_ = bf16[112,1152]{1,0:T(8,128)(2,1)S(1)} collective-permute-done((bf16[112,1152]{1,0:T(8,128)(2,1)}, bf16[112,1152]{1,0:T(8,128)(2,1)S(1)}, u32[]{:S(2)}, u32[]{:S(2)}) %collective-permute-start.5) | collective-permute-done | bytes 258080 | tf_op jit(solution)/shard_map/ppermute | solution.py:334
  39.7 1.4 convert_reduce_fusion
  42.1 1.8 dynamic-slice_bitcast_fusion
  44.3 4.7 %collective-permute-done.6.refs_9_ = bf16[3,96,1152]{2,1,0:T(8,128)(2,1)S(1)} collective-permute-done((bf16[3,96,1152]{2,1,0:T(8,128)(2,1)S(1)}, bf16[3,96,1152]{2,1,0:T(8,128)(2,1)S(1)}, u32[]{:S(2)}, u32[]{:S(2)}) %collective-permute-start.6) | collective-permute-done | bytes 663584 | tf_op jit(solution)/shard_map/ppermute | solution.py:332
  49.1 1.6 collective-permute-start.8
  50.8 1.9 collective-permute-start.16
  52.8 11.1 %collective-permute-done.24 = s32[27,128]{1,0:T(8,128)S(1)} collective-permute-done((s32[27,128]{1,0:T(8,128)S(1)}, s32[27,128]{1,0:T(8,128)S(1)}, u32[]{:S(2)}, u32[]{:S(2)}) %collective-permute-start.24) | collective-permute-done | bytes 13856 | tf_op jit(solution)/shard_map/ppermute | solution.py:332
  63.9 4.3 %collective-permute-done.25 = s32[27,128]{1,0:T(8,128)S(1)} collective-permute-done((s32[27,128]{1,0:T(8,128)S(1)}, s32[27,128]{1,0:T(8,128)S(1)}, u32[]{:S(2)}, u32[]{:S(2)}) %collective-permute-start.25) | collective-permute-done | bytes 13856 | tf_op jit(solution)/shard_map/ppermute | solution.py:332
  68.2 2.3 collective-permute-start.1
  73.1 2.5 collective-permute-start.2
  75.6 4.2 %collective-permute-done.2.refs_3_ = bf16[260,256]{1,0:T(8,128)(2,1)S(1)} collective-permute-done((bf16[260,256]{1,0:T(8,128)(2,1)S(1)}, bf16[260,256]{1,0:T(8,128)(2,1)S(1)}, u32[]{:S(2)}, u32[]{:S(2)}) %collective-permute-start.2) | collective-permute-done | bytes 133152 | tf_op jit(solution)/shard_map/ppermute | solution.py:334
  79.8 4.4 %collective-permute-start.9 = (bf16[3,96,1152]{2,1,0:T(8,128)(2,1)S(1)}, bf16[3,96,1152]{2,1,0:T(8,128)(2,1)}, u32[]{:S(2)}, u32[]{:S(2)}) collective-permute-start(bf16[3,96,1152]{2,1,0:T(8,128)(2,1)S(1)} %pad_maximum_fusion.refs_8_), channel_id=1, source_target_pairs={{0,4},{4,0},{8,12},{12,8},{16,20},{20,16},{24,28},{28,24},{1,5},{5... | collective-permute-start | bytes 1990664 | tf_op jit(solution)/shard_map/ppermute | solution.py:332
  84.8 1.5 collective-permute-start.18
  89.4 3.2 %collective-permute-done.18.refs_6_ = bf16[3,64,1152]{2,1,0:T(8,128)(2,1)} collective-permute-done((bf16[3,64,1152]{2,1,0:T(8,128)(2,1)}, bf16[3,64,1152]{2,1,0:T(8,128)(2,1)}, u32[]{:S(2)}, u32[]{:S(2)}) %collective-permute-start.18) | collective-permute-done | bytes 442400 | tf_op jit(solution)/shard_map/ppermute | solution.py:332
  94.5 14.1 %shard_map.202 = (bf16[3,1088,1152]{2,1,0:T(8,128)(2,1)}, f32[3,1088,256]{2,1,0:T(8,128)}, bf16[4,1152,256]{2,1,0:T(8,128)(2,1)}, bf16[1088,256]{1,0:T(8,128)(2,1)}) custom-call(s32[3]{0:T(128)} %pad_add_fusion.1.idx, bf16[260,256]{1,0:T(8,128)(2,1)} %get-tuple-element.72.refs_0_, bf16[260,256]{1,0:T(8,128)(2,1)} %copy-done.37, bf16[260,256]{1,0:T(8,128)(2,1)} %copy-done.38, ...), custom_call_target="tpu_custom_call" | custom-call | flops 1925185536 | bytes 20971520 | tf_op jit(solution)/shard_map/pallas_call | solution.py:34
  108.8 1.9 slice_bitcast_fusion.3.refs_0_.x_own
  111.5 11.2 %shard_map.203 = (bf16[1024,256]{1,0:T(8,128)(2,1)}, bf16[1024,256]{1,0:T(8,128)(2,1)}, bf16[1024,256]{1,0:T(8,128)(2,1)}, f32[1152,256]{1,0:T(8,128)}, f32[1,25...) custom-call(s32[3]{0:T(128)} %pad_add_fusion.1.idx, ...), custom_call_target="tpu_custom_call" | custom-call | flops 2415919104 | bytes 10485760 | tf_op jit(solution)/shard_map/pallas_call | solution.py:34
  122.7 13.5 %shard_map.204 = (bf16[3,1088,256]{2,1,0:T(8,128)(2,1)}, bf16[1088,256]{1,0:T(8,128)(2,1)}, f32[3,8,1088]{2,1,0:T(8,128)}, f32[3,64,1152]{2,1,0:T(8,128)}) custom-call(s32[3]{0:T(128)} %pad_add_fusion.1.idx, f32[1152,256]{1,0:T(8,128)} %get-tuple-element.34.dx3, bf16[1088,256]{1,0:T(8,128)(2,1)} %get-tuple-element.35.x0, ...), custom_call_target="tpu_custom_call" | custom-call | flops 1925185536 | bytes 20971520 | tf_op jit(solution)/shard_map/pallas_call | solution.py:34
  141.5 2.2 collective-permute-start.26
  144.1 2.3 collective-permute-start.28
  146.4 2.1 constant_dynamic-slice_fusion.2
  150.1 2.9 %collective-permute-start.50 = (bf16[1024,256]{1,0:T(8,128)(2,1)S(1)}, bf16[1024,256]{1,0:T(8,128)(2,1)}, u32[]{:S(2)}, u32[]{:S(2)}) collective-permute-start(bf16[1024,256]{1,0:T(8,128)(2,1)S(1)} %copy-done.15), channel_id=1, source_target_pairs={{0,4},{4,0},{8,12},{12,8},{16,20},{20,16},{24,28},{28,24},{1,5},{5... | collective-permute-start | bytes 1572872 | tf_op jit(solution)/shard_map/ppermute | solution.py:332
  155.8 6.7 %shard_map.208 = bf16[4,4,64,1152]{3,2,1,0:T(8,128)(2,1)} custom-call(s32[3]{0:T(128)} %pad_add_fusion.1.idx, bf16[1152,256]{1,0:T(8,128)(2,1)} %slice_bitcast_fusion.3.refs_0_.x_own, bf16[1152,256]{1,0:T(8,128)(2,1)} %slice_bitcast_fusion.2.x_far, bf16[1024,256]{1,0:T(8,128)(2,1)} %get-tuple-element.49.g1_own, ...), custom_call_target="tpu_custom_call" | custom-call | flops 1207959552 | bytes 10485760 | tf_op jit(solution)/shard_map/pallas_call | solution.py:34
  162.5 2.5 slice.166
  165.9 10.7 %shard_map.206 = bf16[4,4,96,1152]{3,2,1,0:T(8,128)(2,1)} custom-call(s32[3]{0:T(128)} %pad_add_fusion.1.idx, bf16[4,1152,256]{2,1,0:T(8,128)(2,1)} %get-tuple-element.33.x_all.x_own, bf16[4,1152,256]{2,1,0:T(8,128)(2,1)} %copy-done.3, bf16[3,1088,256]{2,1,0:T(8,128)(2,1)} %get-tuple-element.48.dz_own, bf16[3,4,128,256]{3,2,1,0:T(8,128)(2,1)} %collective-permute-done.36.dz_far), custom_call_target="tpu_custom_call" | custom-call | flops 1925185536 | bytes 20971520 | tf_op jit(solution)/shard_map/pallas_call | solution.py:34
  176.6 1.8 slice.157
  180.7 1.5 convert_add_fusion.1
  182.2 1.5 collective-permute-start.53
  183.8 22.6 %collective-permute-done.37 = bf16[2,4,96,1152]{3,2,1,0:T(8,128)(2,1)S(1)} collective-permute-done((bf16[2,4,96,1152]{3,2,1,0:T(8,128)(2,1)S(1)}, bf16[2,4,96,1152]{3,2,1,0:T(8,128)(2,1)S(1)}, u32[]{:S(2)}, u32[]{:S(2)}) %collective-permute-start.37) | collective-permute-done | bytes 1769504 | tf_op jit(solution)/shard_map/ppermute | solution.py:332
  209.8 2.2 collective-permute-start.32
  212.0 2.3 collective-permute-start.33
  214.5 5.8 %collective-permute-done.38 = bf16[4,96,1152]{2,1,0:T(8,128)(2,1)S(1)} collective-permute-done((bf16[4,96,1152]{2,1,0:T(8,128)(2,1)S(1)}, bf16[4,96,1152]{2,1,0:T(8,128)(2,1)S(1)}, u32[]{:S(2)}, u32[]{:S(2)}) %collective-permute-start.38) | collective-permute-done | bytes 884768 | tf_op jit(solution)/shard_map/ppermute | solution.py:332
  220.6 2.4 collective-permute-start.41
  225.4 1.4 collective-permute-done.41
  227.8 12.2 %collective-permute-done.40 = bf16[96,1152]{1,0:T(8,128)(2,1)S(1)} collective-permute-done((bf16[96,1152]{1,0:T(8,128)(2,1)S(1)}, bf16[96,1152]{1,0:T(8,128)(2,1)S(1)}, u32[]{:S(2)}, u32[]{:S(2)}) %collective-permute-start.40) | collective-permute-done | bytes 221216 | tf_op jit(solution)/shard_map/ppermute | solution.py:334
  240.0 3.2 %collective-permute-start.55 = (bf16[64,1152]{1,0:T(8,128)(2,1)S(1)}, bf16[64,1152]{1,0:T(8,128)(2,1)S(1)}, u32[]{:S(2)}, u32[]{:S(2)}) collective-permute-start(bf16[64,1152]{1,0:T(8,128)(2,1)S(1)} %get-tuple-element.65), channel_id=1, source_target_pairs={{0,2},{1,3},{2,0},{3,1},{4,6},{5,7},{6,4},{7,5},{8,10},{9,11},{10,... | collective-permute-start | bytes 442376 | tf_op jit(solution)/shard_map/ppermute | solution.py:334
  243.2 4.8 %collective-permute-done.39 = bf16[96,1152]{1,0:T(8,128)(2,1)S(1)} collective-permute-done((bf16[96,1152]{1,0:T(8,128)(2,1)S(1)}, bf16[96,1152]{1,0:T(8,128)(2,1)S(1)}, u32[]{:S(2)}, u32[]{:S(2)}) %collective-permute-start.39) | collective-permute-done | bytes 221216 | tf_op jit(solution)/shard_map/ppermute | solution.py:334
  248.0 2.2 collective-permute-start.54
  251.2 2.7 collective-permute-start.31
  253.9 4.9 %collective-permute-done.54 = bf16[64,1152]{1,0:T(8,128)(2,1)S(1)} collective-permute-done((bf16[64,1152]{1,0:T(8,128)(2,1)S(1)}, bf16[64,1152]{1,0:T(8,128)(2,1)S(1)}, u32[]{:S(2)}, u32[]{:S(2)}) %collective-permute-start.54) | collective-permute-done | bytes 147488 | tf_op jit(solution)/shard_map/ppermute | solution.py:334
  262.5 1.5 collective-permute-start.43
  264.7 1.5 collective-permute-done.57.refs_1_
  266.6 4.6 %collective-permute-start.61 = (bf16[64,1152]{1,0:T(8,128)(2,1)S(1)}, bf16[64,1152]{1,0:T(8,128)(2,1)S(1)}, u32[]{:S(2)}, u32[]{:S(2)}) collective-permute-start(bf16[64,1152]{1,0:T(8,128)(2,1)S(1)} %collective-permute-done.57.refs_1_), channel_id=1, source_target_pairs={{0,4},{4,0},{8,12},{12,8},{16,20},{20,16},{24,28},{28,24},{1,5},{5... | collective-permute-start | bytes 442376 | tf_op jit(solution)/shard_map/ppermute | solution.py:332
  271.3 2.2 shard_map.205
  279.2 3.1 %shard_map.209 = (f32[1040,256]{1,0:T(8,128)}, f32[256,1024]{1,0:T(8,128)}) custom-call(s32[3]{0:T(128)} %pad_add_fusion.1.idx, bf16[64,1152]{1,0:T(8,128)(2,1)} %copy-done.13, bf16[64,1152]{1,0:T(8,128)(2,1)} %copy-done.27, bf16[64,1152]{1,0:T(8,128)(2,1)} %copy-done.28, bf16[64,1152]{1,0:T(8,128)(2,1)} %copy-done.30, bf16[64,1152]{1,0:T(8,128)(2,1)} %copy-done.29, ...), custom_call_target="tpu_custom_call" | custom-call | bytes 4194304 | tf_op jit(solution)/shard_map/pallas_call | solution.py:34
  283.8 3.6 %shard_map.207 = f32[3,260,1040]{2,1,0:T(8,128)} custom-call(s32[3]{0:T(128)} %pad_add_fusion.1.idx, bf16[96,1152]{1,0:T(8,128)(2,1)} %copy-done.10, bf16[96,1152]{1,0:T(8,128)(2,1)} %copy-done.20, bf16[96,1152]{1,0:T(8,128)(2,1)} %copy-done.21, bf16[96,1152]{1,0:T(8,128)(2,1)} %copy-done.22, bf16[96,1152]{1,0:T(8,128)(2,1)} %copy-done.23, ...), custom_call_target="tpu_custom_call" | custom-call | bytes 4194304 | tf_op jit(solution)/shard_map/pallas_call | solution.py:34
  (273 shorter events, 55.6 us)
Async XLA Ops:
  5.8 32.3 %collective-permute-start.3 = (bf16[112,1152]{1,0:T(8,128)(2,1)}, bf16[112,1152]{1,0:T(8,128)(2,1)S(1)}, u32[]{:S(2)}, u32[]{:S(2)}) collective-permute-start(bf16[112,1152]{1,0:T(8,128)(2,1)} %maximum_maximum_fusion), channel_id=1, source_target_pairs={{0,1},{1,2},{2,3},{3,0},{4,5},{5,6},{6,7},{7,4},{8,9},{9,10},{10,1... | collective-permute-start | bytes 774152 | tf_op jit(solution)/shard_map/ppermute | solution.py:334
  7.1 30.9 %collective-permute-start.4 = (bf16[112,1152]{1,0:T(8,128)(2,1)}, bf16[112,1152]{1,0:T(8,128)(2,1)S(1)}, u32[]{:S(2)}, u32[]{:S(2)}) collective-permute-start(bf16[112,1152]{1,0:T(8,128)(2,1)} %maximum_maximum_fusion), channel_id=1, source_target_pairs={{0,2},{1,3},{2,0},{3,1},{4,6},{5,7},{6,4},{7,5},{8,10},{9,11},{10,... | collective-permute-start | bytes 774152 | tf_op jit(solution)/shard_map/ppermute | solution.py:334
  8.1 29.9 %collective-permute-start.5 = (bf16[112,1152]{1,0:T(8,128)(2,1)}, bf16[112,1152]{1,0:T(8,128)(2,1)S(1)}, u32[]{:S(2)}, u32[]{:S(2)}) collective-permute-start(bf16[112,1152]{1,0:T(8,128)(2,1)} %maximum_maximum_fusion), channel_id=1, source_target_pairs={{0,3},{1,0},{2,1},{3,2},{4,7},{5,4},{6,5},{7,6},{8,11},{9,8},{10,9... | collective-permute-start | bytes 774152 | tf_op jit(solution)/shard_map/ppermute | solution.py:334
  14.8 29.0 %collective-permute-start.15 = (bf16[64,1152]{1,0:T(8,128)(2,1)}, bf16[64,1152]{1,0:T(8,128)(2,1)S(1)}, u32[]{:S(2)}, u32[]{:S(2)}) collective-permute-start(bf16[64,1152]{1,0:T(8,128)(2,1)} %fusion.9), channel_id=1, source_target_pairs={{0,3},{1,0},{2,1},{3,2},{4,7},{5,4},{6,5},{7,6},{8,11},{9,8},{10,9... | collective-permute-start | bytes 442376 | tf_op jit(solution)/shard_map/ppermute | solution.py:334
  15.9 28.0 %collective-permute-start.14 = (bf16[64,1152]{1,0:T(8,128)(2,1)}, bf16[64,1152]{1,0:T(8,128)(2,1)S(1)}, u32[]{:S(2)}, u32[]{:S(2)}) collective-permute-start(bf16[64,1152]{1,0:T(8,128)(2,1)} %fusion.9), channel_id=1, source_target_pairs={{0,2},{1,3},{2,0},{3,1},{4,6},{5,7},{6,4},{7,5},{8,10},{9,11},{10,... | collective-permute-start | bytes 442376 | tf_op jit(solution)/shard_map/ppermute | solution.py:334
  38.0 12.7 %collective-permute-start.13 = (bf16[64,1152]{1,0:T(8,128)(2,1)}, bf16[64,1152]{1,0:T(8,128)(2,1)S(1)}, u32[]{:S(2)}, u32[]{:S(2)}) collective-permute-start(bf16[64,1152]{1,0:T(8,128)(2,1)} %fusion.9), channel_id=1, source_target_pairs={{0,1},{1,2},{2,3},{3,0},{4,5},{5,6},{6,7},{7,4},{8,9},{9,10},{10,1... | collective-permute-start | bytes 442376 | tf_op jit(solution)/shard_map/ppermute | solution.py:334
  38.3 10.8 %collective-permute-start.6 = (bf16[3,96,1152]{2,1,0:T(8,128)(2,1)S(1)}, bf16[3,96,1152]{2,1,0:T(8,128)(2,1)S(1)}, u32[]{:S(2)}, u32[]{:S(2)}) collective-permute-start(bf16[3,96,1152]{2,1,0:T(8,128)(2,1)S(1)} %pad_maximum_fusion.refs_8_), channel_id=1, source_target_pairs={{0,8},{4,20},{8,0},{12,28},{16,24},{20,4},{24,16},{28,12},{1,9},{5... | collective-permute-start | bytes 1990664 | tf_op jit(solution)/shard_map/ppermute | solution.py:332
  41.2 11.5 %collective-permute-start.23 = (s32[27,128]{1,0:T(8,128)S(1)}, s32[27,128]{1,0:T(8,128)S(1)}, u32[]{:S(2)}, u32[]{:S(2)}) collective-permute-start(s32[27,128]{1,0:T(8,128)S(1)} %pad_add_fusion), channel_id=1, source_target_pairs={{0,4},{4,0},{8,12},{12,8},{16,20},{20,16},{24,28},{28,24},{1,5},{5... | collective-permute-start | bytes 41480 | tf_op jit(solution)/shard_map/ppermute | solution.py:332
  43.8 26.7 %collective-permute-start = (bf16[260,256]{1,0:T(8,128)(2,1)S(1)}, bf16[260,256]{1,0:T(8,128)(2,1)S(1)}, u32[]{:S(2)}, u32[]{:S(2)}) collective-permute-start(bf16[260,256]{1,0:T(8,128)(2,1)S(1)} %get-tuple-element.71), channel_id=1, source_target_pairs={{0,1},{1,2},{2,3},{3,0},{4,5},{5,6},{6,7},{7,4},{8,9},{9,10},{10,1... | collective-permute-start | bytes 399368 | tf_op jit(solution)/shard_map/ppermute | solution.py:334
  43.9 40.4 %collective-permute-start.7 = (bf16[3,96,1152]{2,1,0:T(8,128)(2,1)S(1)}, bf16[3,96,1152]{2,1,0:T(8,128)(2,1)S(1)}, u32[]{:S(2)}, u32[]{:S(2)}) collective-permute-start(bf16[3,96,1152]{2,1,0:T(8,128)(2,1)S(1)} %pad_maximum_fusion.refs_8_), channel_id=1, source_target_pairs={{0,16},{4,12},{8,24},{12,4},{16,0},{20,28},{24,8},{28,20},{1,17},{... | collective-permute-start | bytes 1990664 | tf_op jit(solution)/shard_map/ppermute | solution.py:332
  49.1 35.6 %collective-permute-start.8 = (bf16[3,96,1152]{2,1,0:T(8,128)(2,1)S(1)}, bf16[3,96,1152]{2,1,0:T(8,128)(2,1)}, u32[]{:S(2)}, u32[]{:S(2)}) collective-permute-start(bf16[3,96,1152]{2,1,0:T(8,128)(2,1)S(1)} %collective-permute-done.6.refs_9_), channel_id=1, source_target_pairs={{0,16},{4,12},{8,24},{12,4},{16,0},{20,28},{24,8},{28,20},{1,17},{... | collective-permute-start | bytes 1990664 | tf_op jit(solution)/shard_map/ppermute | solution.py:332
  50.8 33.4 %collective-permute-start.16 = (bf16[3,64,1152]{2,1,0:T(8,128)(2,1)S(1)}, bf16[3,64,1152]{2,1,0:T(8,128)(2,1)}, u32[]{:S(2)}, u32[]{:S(2)}) collective-permute-start(bf16[3,64,1152]{2,1,0:T(8,128)(2,1)S(1)} %pad_maximum_fusion.1.refs_3_), channel_id=1, source_target_pairs={{0,8},{4,20},{8,0},{12,28},{16,24},{20,4},{24,16},{28,12},{1,9},{5... | collective-permute-start | bytes 1327112 | tf_op jit(solution)/shard_map/ppermute | solution.py:332
  52.7 11.2 %collective-permute-start.24 = (s32[27,128]{1,0:T(8,128)S(1)}, s32[27,128]{1,0:T(8,128)S(1)}, u32[]{:S(2)}, u32[]{:S(2)}) collective-permute-start(s32[27,128]{1,0:T(8,128)S(1)} %fusion.27), channel_id=1, source_target_pairs={{0,8},{4,20},{8,0},{12,28},{16,24},{20,4},{24,16},{28,12},{1,9},{5... | collective-permute-start | bytes 41480 | tf_op jit(solution)/shard_map/ppermute | solution.py:332
  70.5 14.3 %collective-permute-start.17 = (bf16[3,64,1152]{2,1,0:T(8,128)(2,1)S(1)}, bf16[3,64,1152]{2,1,0:T(8,128)(2,1)S(1)}, u32[]{:S(2)}, u32[]{:S(2)}) collective-permute-start(bf16[3,64,1152]{2,1,0:T(8,128)(2,1)S(1)} %pad_maximum_fusion.1.refs_3_), channel_id=1, source_target_pairs={{0,16},{4,12},{8,24},{12,4},{16,0},{20,28},{24,8},{28,20},{1,17},{... | collective-permute-start | bytes 1327112 | tf_op jit(solution)/shard_map/ppermute | solution.py:332
  79.8 9.6 %collective-permute-start.9 = (bf16[3,96,1152]{2,1,0:T(8,128)(2,1)S(1)}, bf16[3,96,1152]{2,1,0:T(8,128)(2,1)}, u32[]{:S(2)}, u32[]{:S(2)}) collective-permute-start(bf16[3,96,1152]{2,1,0:T(8,128)(2,1)S(1)} %pad_maximum_fusion.refs_8_), channel_id=1, source_target_pairs={{0,4},{4,0},{8,12},{12,8},{16,20},{20,16},{24,28},{28,24},{1,5},{5... | collective-permute-start | bytes 1990664 | tf_op jit(solution)/shard_map/ppermute | solution.py:332
  84.2 9.7 %collective-permute-start.10 = (bf16[3,96,1152]{2,1,0:T(8,128)(2,1)S(1)}, bf16[3,96,1152]{2,1,0:T(8,128)(2,1)}, u32[]{:S(2)}, u32[]{:S(2)}) collective-permute-start(bf16[3,96,1152]{2,1,0:T(8,128)(2,1)S(1)} %collective-permute-done.6.refs_9_), channel_id=1, source_target_pairs={{0,4},{4,0},{8,12},{12,8},{16,20},{20,16},{24,28},{28,24},{1,5},{5... | collective-permute-start | bytes 1990664 | tf_op jit(solution)/shard_map/ppermute | solution.py:332
  84.3 9.7 %collective-permute-start.11 = (bf16[3,96,1152]{2,1,0:T(8,128)(2,1)S(1)}, bf16[3,96,1152]{2,1,0:T(8,128)(2,1)}, u32[]{:S(2)}, u32[]{:S(2)}) collective-permute-start(bf16[3,96,1152]{2,1,0:T(8,128)(2,1)S(1)} %collective-permute-done.7.refs_10_), channel_id=1, source_target_pairs={{0,4},{4,0},{8,12},{12,8},{16,20},{20,16},{24,28},{28,24},{1,5},{5... | collective-permute-start | bytes 1990664 | tf_op jit(solution)/shard_map/ppermute | solution.py:332
  84.7 9.7 %collective-permute-start.12 = (bf16[3,96,1152]{2,1,0:T(8,128)(2,1)}, bf16[3,96,1152]{2,1,0:T(8,128)(2,1)}, u32[]{:S(2)}, u32[]{:S(2)}) collective-permute-start(bf16[3,96,1152]{2,1,0:T(8,128)(2,1)} %collective-permute-done.8.refs_11_), channel_id=1, source_target_pairs={{0,4},{4,0},{8,12},{12,8},{16,20},{20,16},{24,28},{28,24},{1,5},{5... | collective-permute-start | bytes 1990664 | tf_op jit(solution)/shard_map/ppermute | solution.py:332
  84.8 7.8 %collective-permute-start.18 = (bf16[3,64,1152]{2,1,0:T(8,128)(2,1)}, bf16[3,64,1152]{2,1,0:T(8,128)(2,1)}, u32[]{:S(2)}, u32[]{:S(2)}) collective-permute-start(bf16[3,64,1152]{2,1,0:T(8,128)(2,1)} %collective-permute-done.16.refs_4_), channel_id=1, source_target_pairs={{0,16},{4,12},{8,24},{12,4},{16,0},{20,28},{24,8},{28,20},{1,17},{... | collective-permute-start | bytes 1327112 | tf_op jit(solution)/shard_map/ppermute | solution.py:332
  89.4 21.3 %collective-permute-start.19 = (bf16[3,64,1152]{2,1,0:T(8,128)(2,1)}, bf16[3,64,1152]{2,1,0:T(8,128)(2,1)S(1)}, u32[]{:S(2)}, u32[]{:S(2)}) collective-permute-start(bf16[3,64,1152]{2,1,0:T(8,128)(2,1)} %copy-done.17), channel_id=1, source_target_pairs={{0,4},{4,0},{8,12},{12,8},{16,20},{20,16},{24,28},{28,24},{1,5},{5... | collective-permute-start | bytes 1327112 | tf_op jit(solution)/shard_map/ppermute | solution.py:332
  92.7 18.0 %collective-permute-start.20 = (bf16[3,64,1152]{2,1,0:T(8,128)(2,1)}, bf16[3,64,1152]{2,1,0:T(8,128)(2,1)}, u32[]{:S(2)}, u32[]{:S(2)}) collective-permute-start(bf16[3,64,1152]{2,1,0:T(8,128)(2,1)} %collective-permute-done.16.refs_4_), channel_id=1, source_target_pairs={{0,4},{4,0},{8,12},{12,8},{16,20},{20,16},{24,28},{28,24},{1,5},{5... | collective-permute-start | bytes 1327112 | tf_op jit(solution)/shard_map/ppermute | solution.py:332
  93.9 16.8 %collective-permute-start.21 = (bf16[3,64,1152]{2,1,0:T(8,128)(2,1)S(1)}, bf16[3,64,1152]{2,1,0:T(8,128)(2,1)}, u32[]{:S(2)}, u32[]{:S(2)}) collective-permute-start(bf16[3,64,1152]{2,1,0:T(8,128)(2,1)S(1)} %collective-permute-done.17.refs_5_), channel_id=1, source_target_pairs={{0,4},{4,0},{8,12},{12,8},{16,20},{20,16},{24,28},{28,24},{1,5},{5... | collective-permute-start | bytes 1327112 | tf_op jit(solution)/shard_map/ppermute | solution.py:332
  94.0 16.8 %collective-permute-start.22 = (bf16[3,64,1152]{2,1,0:T(8,128)(2,1)}, bf16[3,64,1152]{2,1,0:T(8,128)(2,1)}, u32[]{:S(2)}, u32[]{:S(2)}) collective-permute-start(bf16[3,64,1152]{2,1,0:T(8,128)(2,1)} %collective-permute-done.18.refs_6_), channel_id=1, source_target_pairs={{0,4},{4,0},{8,12},{12,8},{16,20},{20,16},{24,28},{28,24},{1,5},{5... | collective-permute-start | bytes 1327112 | tf_op jit(solution)/shard_map/ppermute | solution.py:332
  108.6 45.9 %collective-permute-start.35 = (bf16[4,1152,256]{2,1,0:T(8,128)(2,1)}, bf16[4,1152,256]{2,1,0:T(8,128)(2,1)S(1)}, u32[]{:S(2)}, u32[]{:S(2)}) collective-permute-start(bf16[4,1152,256]{2,1,0:T(8,128)(2,1)} %get-tuple-element.33.x_all.x_own), channel_id=1, source_target_pairs={{0,4},{4,0},{8,12},{12,8},{16,20},{20,16},{24,28},{28,24},{1,5},{5... | collective-permute-start | bytes 7077896 | tf_op jit(solution)/shard_map/ppermute | solution.py:332
  141.5 8.3 %collective-permute-start.26 = (f32[19,1152]{1,0:T(8,128)S(1)}, f32[19,1152]{1,0:T(8,128)S(1)}, u32[]{:S(2)}, u32[]{:S(2)}) collective-permute-start(f32[19,1152]{1,0:T(8,128)S(1)} %get-tuple-element.75), channel_id=1, source_target_pairs={{0,3},{1,0},{2,1},{3,2},{4,7},{5,4},{6,5},{7,6},{8,11},{9,8},{10,9... | collective-permute-start | bytes 262664 | tf_op jit(solution)/shard_map/ppermute | solution.py:334
  144.1 9.1 %collective-permute-start.28 = (f32[19,1152]{1,0:T(8,128)S(1)}, f32[19,1152]{1,0:T(8,128)S(1)}, u32[]{:S(2)}, u32[]{:S(2)}) collective-permute-start(f32[19,1152]{1,0:T(8,128)S(1)} %get-tuple-element.74), channel_id=1, source_target_pairs={{0,1},{1,2},{2,3},{3,0},{4,5},{5,6},{6,7},{7,4},{8,9},{9,10},{10,1... | collective-permute-start | bytes 262664 | tf_op jit(solution)/shard_map/ppermute | solution.py:334
  148.5 17.4 %collective-permute-start.36 = (bf16[3,4,128,256]{3,2,1,0:T(8,128)(2,1)}, bf16[3,4,128,256]{3,2,1,0:T(8,128)(2,1)}, u32[]{:S(2)}, u32[]{:S(2)}) collective-permute-start(bf16[3,4,128,256]{3,2,1,0:T(8,128)(2,1)} %constant_dynamic-slice_fusion.2), channel_id=1, source_target_pairs={{0,4},{4,0},{8,12},{12,8},{16,20},{20,16},{24,28},{28,24},{1,5},{5... | collective-permute-start | bytes 2359304 | tf_op jit(solution)/shard_map/ppermute | solution.py:332
  165.0 15.7 %collective-permute-start.52 = (bf16[2,4,64,1152]{3,2,1,0:T(8,128)(2,1)}, bf16[2,4,64,1152]{3,2,1,0:T(8,128)(2,1)}, u32[]{:S(2)}, u32[]{:S(2)}) collective-permute-start(bf16[2,4,64,1152]{3,2,1,0:T(8,128)(2,1)} %slice.166), channel_id=1, source_target_pairs={{0,8},{4,20},{8,0},{12,28},{16,24},{20,4},{24,16},{28,12},{1,9},{5... | collective-permute-start | bytes 3538952 | tf_op jit(solution)/shard_map/ppermute | solution.py:332
  178.3 28.1 %collective-permute-start.37 = (bf16[2,4,96,1152]{3,2,1,0:T(8,128)(2,1)S(1)}, bf16[2,4,96,1152]{3,2,1,0:T(8,128)(2,1)S(1)}, u32[]{:S(2)}, u32[]{:S(2)}) collective-permute-start(bf16[2,4,96,1152]{3,2,1,0:T(8,128)(2,1)S(1)} %slice.157), channel_id=1, source_target_pairs={{0,8},{4,20},{8,0},{12,28},{16,24},{20,4},{24,16},{28,12},{1,9},{5... | collective-permute-start | bytes 5308424 | tf_op jit(solution)/shard_map/ppermute | solution.py:332
  179.1 29.0 %collective-permute-start.29 = (f32[19,1152]{1,0:T(8,128)S(1)}, f32[19,1152]{1,0:T(8,128)S(1)}, u32[]{:S(2)}, u32[]{:S(2)}) collective-permute-start(f32[19,1152]{1,0:T(8,128)S(1)} %fusion.17), channel_id=1, source_target_pairs={{0,4},{4,0},{8,12},{12,8},{16,20},{20,16},{24,28},{28,24},{1,5},{5... | collective-permute-start | bytes 262664 | tf_op jit(solution)/shard_map/ppermute | solution.py:332
  182.2 32.1 %collective-permute-start.53 = (bf16[4,64,1152]{2,1,0:T(8,128)(2,1)S(1)}, bf16[4,64,1152]{2,1,0:T(8,128)(2,1)S(1)}, u32[]{:S(2)}, u32[]{:S(2)}) collective-permute-start(bf16[4,64,1152]{2,1,0:T(8,128)(2,1)S(1)} %fusion.3), channel_id=1, source_target_pairs={{0,16},{4,12},{8,24},{12,4},{16,0},{20,28},{24,8},{28,20},{1,17},{... | collective-permute-start | bytes 1769480 | tf_op jit(solution)/shard_map/ppermute | solution.py:332
  206.9 13.4 %collective-permute-start.38 = (bf16[4,96,1152]{2,1,0:T(8,128)(2,1)S(1)}, bf16[4,96,1152]{2,1,0:T(8,128)(2,1)S(1)}, u32[]{:S(2)}, u32[]{:S(2)}) collective-permute-start(bf16[4,96,1152]{2,1,0:T(8,128)(2,1)S(1)} %fusion.2), channel_id=1, source_target_pairs={{0,16},{4,12},{8,24},{12,4},{16,0},{20,28},{24,8},{28,20},{1,17},{... | collective-permute-start | bytes 2654216 | tf_op jit(solution)/shard_map/ppermute | solution.py:332
  209.8 49.8 %collective-permute-start.32 = (bf16[272,256]{1,0:T(8,128)(2,1)S(1)}, bf16[272,256]{1,0:T(8,128)(2,1)S(1)}, u32[]{:S(2)}, u32[]{:S(2)}) collective-permute-start(bf16[272,256]{1,0:T(8,128)(2,1)S(1)} %get-tuple-element.68), channel_id=1, source_target_pairs={{0,1},{1,2},{2,3},{3,0},{4,5},{5,6},{6,7},{7,4},{8,9},{9,10},{10,1... | collective-permute-start | bytes 417800 | tf_op jit(solution)/shard_map/ppermute | solution.py:334
  212.0 48.5 %collective-permute-start.33 = (bf16[272,256]{1,0:T(8,128)(2,1)S(1)}, bf16[272,256]{1,0:T(8,128)(2,1)S(1)}, u32[]{:S(2)}, u32[]{:S(2)}) collective-permute-start(bf16[272,256]{1,0:T(8,128)(2,1)S(1)} %get-tuple-element.67), channel_id=1, source_target_pairs={{0,2},{1,3},{2,0},{3,1},{4,6},{5,7},{6,4},{7,5},{8,10},{9,11},{10,... | collective-permute-start | bytes 417800 | tf_op jit(solution)/shard_map/ppermute | solution.py:334
  222.9 17.0 %collective-permute-start.40 = (bf16[96,1152]{1,0:T(8,128)(2,1)S(1)}, bf16[96,1152]{1,0:T(8,128)(2,1)S(1)}, u32[]{:S(2)}, u32[]{:S(2)}) collective-permute-start(bf16[96,1152]{1,0:T(8,128)(2,1)S(1)} %get-tuple-element.62), channel_id=1, source_target_pairs={{0,2},{1,3},{2,0},{3,1},{4,6},{5,7},{6,4},{7,5},{8,10},{9,11},{10,... | collective-permute-start | bytes 663560 | tf_op jit(solution)/shard_map/ppermute | solution.py:334
  224.0 24.0 %collective-permute-start.39 = (bf16[96,1152]{1,0:T(8,128)(2,1)S(1)}, bf16[96,1152]{1,0:T(8,128)(2,1)S(1)}, u32[]{:S(2)}, u32[]{:S(2)}) collective-permute-start(bf16[96,1152]{1,0:T(8,128)(2,1)S(1)} %get-tuple-element.60), channel_id=1, source_target_pairs={{0,1},{1,2},{2,3},{3,0},{4,5},{5,6},{6,7},{7,4},{8,9},{9,10},{10,1... | collective-permute-start | bytes 663560 | tf_op jit(solution)/shard_map/ppermute | solution.py:334
  226.8 23.6 %collective-permute-start.56 = (bf16[64,1152]{1,0:T(8,128)(2,1)S(1)}, bf16[64,1152]{1,0:T(8,128)(2,1)S(1)}, u32[]{:S(2)}, u32[]{:S(2)}) collective-permute-start(bf16[64,1152]{1,0:T(8,128)(2,1)S(1)} %get-tuple-element.64), channel_id=1, source_target_pairs={{0,3},{1,0},{2,1},{3,2},{4,7},{5,4},{6,5},{7,6},{8,11},{9,8},{10,9... | collective-permute-start | bytes 442376 | tf_op jit(solution)/shard_map/ppermute | solution.py:334
  240.0 11.2 %collective-permute-start.55 = (bf16[64,1152]{1,0:T(8,128)(2,1)S(1)}, bf16[64,1152]{1,0:T(8,128)(2,1)S(1)}, u32[]{:S(2)}, u32[]{:S(2)}) collective-permute-start(bf16[64,1152]{1,0:T(8,128)(2,1)S(1)} %get-tuple-element.65), channel_id=1, source_target_pairs={{0,2},{1,3},{2,0},{3,1},{4,6},{5,7},{6,4},{7,5},{8,10},{9,11},{10,... | collective-permute-start | bytes 442376 | tf_op jit(solution)/shard_map/ppermute | solution.py:334
  248.0 10.8 %collective-permute-start.54 = (bf16[64,1152]{1,0:T(8,128)(2,1)S(1)}, bf16[64,1152]{1,0:T(8,128)(2,1)S(1)}, u32[]{:S(2)}, u32[]{:S(2)}) collective-permute-start(bf16[64,1152]{1,0:T(8,128)(2,1)S(1)} %get-tuple-element.63), channel_id=1, source_target_pairs={{0,1},{1,2},{2,3},{3,0},{4,5},{5,6},{6,7},{7,4},{8,9},{9,10},{10,1... | collective-permute-start | bytes 442376 | tf_op jit(solution)/shard_map/ppermute | solution.py:334
  250.3 10.9 %collective-permute-start.34 = (bf16[272,256]{1,0:T(8,128)(2,1)S(1)}, bf16[272,256]{1,0:T(8,128)(2,1)S(1)}, u32[]{:S(2)}, u32[]{:S(2)}) collective-permute-start(bf16[272,256]{1,0:T(8,128)(2,1)S(1)} %get-tuple-element.66), channel_id=1, source_target_pairs={{0,3},{1,0},{2,1},{3,2},{4,7},{5,4},{6,5},{7,6},{8,11},{9,8},{10,9... | collective-permute-start | bytes 417800 | tf_op jit(solution)/shard_map/ppermute | solution.py:334
  251.2 11.3 %collective-permute-start.31 = (f32[19,1152]{1,0:T(8,128)S(1)}, f32[19,1152]{1,0:T(8,128)S(1)}, u32[]{:S(2)}, u32[]{:S(2)}) collective-permute-start(f32[19,1152]{1,0:T(8,128)S(1)} %add.181), channel_id=1, source_target_pairs={{0,16},{4,12},{8,24},{12,4},{16,0},{20,28},{24,8},{28,20},{1,17},{... | collective-permute-start | bytes 262664 | tf_op jit(solution)/shard_map/ppermute | solution.py:332
  261.3 9.9 %collective-permute-start.60 = (bf16[64,1152]{1,0:T(8,128)(2,1)S(1)}, bf16[64,1152]{1,0:T(8,128)(2,1)S(1)}, u32[]{:S(2)}, u32[]{:S(2)}) collective-permute-start(bf16[64,1152]{1,0:T(8,128)(2,1)S(1)} %fusion.7.refs_0_), channel_id=1, source_target_pairs={{0,4},{4,0},{8,12},{12,8},{16,20},{20,16},{24,28},{28,24},{1,5},{5... | collective-permute-start | bytes 442376 | tf_op jit(solution)/shard_map/ppermute | solution.py:332
  262.5 13.5 %collective-permute-start.43 = (bf16[96,1152]{1,0:T(8,128)(2,1)S(1)}, bf16[96,1152]{1,0:T(8,128)(2,1)S(1)}, u32[]{:S(2)}, u32[]{:S(2)}) collective-permute-start(bf16[96,1152]{1,0:T(8,128)(2,1)S(1)} %fusion.5.refs_0_), channel_id=1, source_target_pairs={{0,16},{4,12},{8,24},{12,4},{16,0},{20,28},{24,8},{28,20},{1,17},{... | collective-permute-start | bytes 663560 | tf_op jit(solution)/shard_map/ppermute | solution.py:332
  264.0 12.1 %collective-permute-start.44 = (bf16[96,1152]{1,0:T(8,128)(2,1)S(1)}, bf16[96,1152]{1,0:T(8,128)(2,1)S(1)}, u32[]{:S(2)}, u32[]{:S(2)}) collective-permute-start(bf16[96,1152]{1,0:T(8,128)(2,1)S(1)} %collective-permute-done.42.refs_1_), channel_id=1, source_target_pairs={{0,16},{4,12},{8,24},{12,4},{16,0},{20,28},{24,8},{28,20},{1,17},{... | collective-permute-start | bytes 663560 | tf_op jit(solution)/shard_map/ppermute | solution.py:332
  266.2 8.3 %collective-permute-start.59 = (bf16[64,1152]{1,0:T(8,128)(2,1)S(1)}, bf16[64,1152]{1,0:T(8,128)(2,1)S(1)}, u32[]{:S(2)}, u32[]{:S(2)}) collective-permute-start(bf16[64,1152]{1,0:T(8,128)(2,1)S(1)} %collective-permute-done.57.refs_1_), channel_id=1, source_target_pairs={{0,16},{4,12},{8,24},{12,4},{16,0},{20,28},{24,8},{28,20},{1,17},{... | collective-permute-start | bytes 442376 | tf_op jit(solution)/shard_map/ppermute | solution.py:332
  266.6 8.9 %collective-permute-start.61 = (bf16[64,1152]{1,0:T(8,128)(2,1)S(1)}, bf16[64,1152]{1,0:T(8,128)(2,1)S(1)}, u32[]{:S(2)}, u32[]{:S(2)}) collective-permute-start(bf16[64,1152]{1,0:T(8,128)(2,1)S(1)} %collective-permute-done.57.refs_1_), channel_id=1, source_target_pairs={{0,4},{4,0},{8,12},{12,8},{16,20},{20,16},{24,28},{28,24},{1,5},{5... | collective-permute-start | bytes 442376 | tf_op jit(solution)/shard_map/ppermute | solution.py:332
  275.5 6.8 %collective-permute-start.45 = (bf16[96,1152]{1,0:T(8,128)(2,1)S(1)}, bf16[96,1152]{1,0:T(8,128)(2,1)S(1)}, u32[]{:S(2)}, u32[]{:S(2)}) collective-permute-start(bf16[96,1152]{1,0:T(8,128)(2,1)S(1)} %fusion.5.refs_0_), channel_id=1, source_target_pairs={{0,4},{4,0},{8,12},{12,8},{16,20},{20,16},{24,28},{28,24},{1,5},{5... | collective-permute-start | bytes 663560 | tf_op jit(solution)/shard_map/ppermute | solution.py:332
  275.5 6.8 %collective-permute-start.46 = (bf16[96,1152]{1,0:T(8,128)(2,1)S(1)}, bf16[96,1152]{1,0:T(8,128)(2,1)S(1)}, u32[]{:S(2)}, u32[]{:S(2)}) collective-permute-start(bf16[96,1152]{1,0:T(8,128)(2,1)S(1)} %collective-permute-done.42.refs_1_), channel_id=1, source_target_pairs={{0,4},{4,0},{8,12},{12,8},{16,20},{20,16},{24,28},{28,24},{1,5},{5... | collective-permute-start | bytes 663560 | tf_op jit(solution)/shard_map/ppermute | solution.py:332
  (65 other events, 871.1 us)

commit v2 on v0

v2 whole, which is shorter than its diff:
```python
import functools

import jax
import jax.numpy as jnp
from jax import lax
from jax.experimental import pallas as pl
from jax.experimental.pallas import tpu as pltpu
from jax.sharding import PartitionSpec as P

DAYS = 24
BUCKETS = 128
BF16 = jnp.bfloat16
F32 = jnp.float32
MAIN = 256
SHARE = 32
HALF = MAIN // 2
LANES = 128
REST = 32
COUNT = 32
VMEM = pl.BlockSpec(memory_space=pltpu.VMEM)
SMEM = pl.BlockSpec(memory_space=pltpu.SMEM)
HBM = pl.BlockSpec(memory_space=pl.ANY)
NT = (((1,), (1,)), ((), ()))
TN = (((0,), (0,)), ((), ()))
NN = (((1,), (0,)), ((), ()))


def gelu_parts(values):
    cdf_part = 0.5 * (1.0 + lax.erf(values * 0.7071067811865476))
    slope = cdf_part + values * jnp.exp(-0.5 * values * values) * 0.3989422804014327
    return (values * cdf_part, slope)


def dot(lhs, rhs, dims, precision=None):
    return lax.dot_general(lhs, rhs, dims, preferred_element_type=F32, precision=precision)


def call(kernel, outs, scratch, args, mib, spec=VMEM, copies=0, out_spec=None, aliases={}, flops=0, nbytes=0):
    arrays = [a[0] if isinstance(a, tuple) else a for a in args[1:]]
    specs = [a[1] if isinstance(a, tuple) else spec for a in args[1:]]
    if copies:
        scratch = scratch + [pltpu.SemaphoreType.DMA((copies,))]
    return pl.pallas_call(
        kernel,
        out_shape=outs,
        in_specs=[SMEM] + specs,
        out_specs=out_spec or jax.tree.map(lambda _: spec, outs),
        scratch_shapes=scratch,
        input_output_aliases=aliases,
        compiler_params=pltpu.CompilerParams(vmem_limit_bytes=mib << 20),
        cost_estimate=pl.CostEstimate(flops=flops, bytes_accessed=nbytes, transcendentals=0),
    )(args[0], *arrays)


class Copies:
    def __init__(self, sems):
        self.sems, self.count = sems, 0

    def start(self, source, target):
        copy = pltpu.make_async_copy(source, target, self.sems.at[self.count])
        self.count += 1
        copy.start()
        return copy


def wait(*copies):
    for copy in copies:
        copy.wait()


def after(value, *others):
    return lax.optimization_barrier((value,) + others)[0]


def places(idx):
    core, plane = idx[1], idx[2]
    first, second = core + 1, 2 - core
    mine = [plane, plane ^ first, plane ^ second, plane ^ 3]
    theirs = [plane, plane ^ second, plane ^ first, plane ^ 3]
    return [core * HALF + SHARE * q for q in mine] + [(1 - core) * HALF + SHARE * q for q in theirs]


def relative(idx):
    core, plane = idx[1], idx[2]
    first, second = core + 1, 2 - core
    return [plane, plane ^ second, plane ^ first, plane ^ 3]


def block_of(idx, turn, blocks):
    return lax.rem(idx[0] - turn + blocks, blocks)


def block_ahead(idx, turn, blocks):
    return lax.rem(idx[0] + turn, blocks)


def rows_at(offset, size, unit=16):
    return pl.ds(pl.multiple_of(offset, unit), size)


def split3(line):
    high = line.astype(BF16).astype(F32)
    middle = (line - high).astype(BF16).astype(F32)
    return high, middle, line - high - middle


def lane_of(shape):
    return lax.broadcasted_iota(jnp.int32, shape, 1)


def pack_first(idx, weight, out, sems):
    copies = Copies(sems)
    wait(copies.start(weight.at[0, rows_at(idx[1] * HALF + idx[2] * SHARE, SHARE), :], out))


def pack_cross(idx, weight, bias, out, lines):
    layers, width, depth = weight.shape
    left = width - MAIN
    own_row = idx[1] * HALF + idx[2] * SHARE
    lines[...] = jnp.zeros_like(lines)
    for layer in range(layers):
        if layer:
            out[SHARE * (layer - 1) : SHARE * layer, :] = weight[layer, rows_at(own_row, SHARE), :]
        lines[left * layer : left * (layer + 1), :] = weight[layer, MAIN:width, :].astype(F32)
        at = left * layers + layer
        lines[at : at + 1, 0:width] = bias[layer : layer + 1, :].astype(F32)
    out[(layers - 1) * SHARE :, :] = lines[...].astype(BF16)


def pack_rest(idx, inputs, vectors, weight1, weight2, ids, days, *refs, blocks):
    out, own1, tally, chunks = refs[0], refs[1], refs[2], refs[3:]
    depth, size = weight1.shape
    width = inputs.shape[0]
    hidden = weight2.shape[1]
    part = chunks[0].shape[1]
    own_row = idx[1] * HALF + idx[2] * SHARE
    own1[:, 0:depth] = weight1[...].T
    own1[:, depth:] = jnp.zeros((size, own1.shape[1] - depth), BF16)
    out[0:SHARE, :] = own1[rows_at(own_row, SHARE), 0:depth]
    out[SHARE : 2 * SHARE, 0:hidden] = weight2[rows_at(own_row, SHARE), :]
    out[SHARE : 2 * SHARE, hidden:] = jnp.zeros((SHARE, depth - hidden), BF16)
    for turn in range(blocks):
        lanes = pl.ds(pl.multiple_of(block_ahead(idx, turn, blocks) * part, LANES), part)
        chunks[turn][0:width, :] = inputs[:, lanes]
        chunks[turn][width : width + 3, :] = vectors[...]
    fields, tokens = ids.shape
    bucket = lax.broadcasted_iota(jnp.int32, (BUCKETS, tokens), 0)
    lane = lane_of((BUCKETS, LANES))
    tile = jnp.zeros((BUCKETS, LANES), F32)
    for field in range(fields + 1):
        line = ids[field : field + 1, :] if field < fields else days[...]
        hits = jnp.sum((bucket == line).astype(F32), axis=1, keepdims=True)
        high = jnp.floor(hits * (1.0 / 256.0))
        tile = jnp.where(lane == field, high, tile)
        tile = jnp.where(lane == COUNT + field, hits - 256.0 * high, tile)
    tally[0:BUCKETS, :] = tile.astype(BF16)
    tally[BUCKETS:, :] = jnp.zeros((tally.shape[0] - BUCKETS, LANES), BF16)


def place_cross(idx, weight, own, slices, blocks, layer, pad):
    weight[layer, rows_at(idx[0] * pad, MAIN), :] = own[layer, 0:MAIN, :]
    pieces = slices[8:] if layer else slices[:8]
    at = SHARE * (layer - 1) if layer else 0
    for turn in range(1, blocks):
        base = block_of(idx, turn, blocks) * pad
        for offset, piece in zip(places(idx), pieces):
            weight[layer, rows_at(base + offset, SHARE), :] = piece[turn - 1, at : at + SHARE, :]


def place_rest(idx, weight, turned, lines, tail, blocks, layers, left, pad):
    tail[...] = jnp.zeros_like(tail)
    for turn, piece in enumerate(turned):
        lines[block_of(idx, turn, blocks)] = piece[(layers - 1) * SHARE :, :].astype(F32)
    for block in range(blocks):
        for layer in range(layers):
            tail[0:left, :] = lines[block, left * layer : left * (layer + 1), :]
            at = pad * block + MAIN
            weight[layer, at : at + 16, :] = tail[...].astype(BF16)


def cross_forward(idx, *refs, blocks, layers, width, pad, depth):
    pieces, refs = refs[:blocks], refs[blocks:]
    own, refs = refs[0], refs[1:]
    turned, refs = refs[:blocks], refs[blocks:]
    slices, refs = refs[:16], refs[16:]
    z_out, x_out, weight, lines, tail, start, state, nat = refs
    left = width - MAIN
    place_rest(idx, weight, turned, lines, tail, blocks, layers, left, pad)
    bias = [lines[block, :, 0:384].T for block in range(blocks)]
    for turn, piece in enumerate(pieces):
        block = block_of(idx, turn, blocks)
        start[block, 0:width, :] = piece[0:width, :].astype(F32)
        start[block, width:, :] = jnp.zeros((pad - width, piece.shape[1]), F32)
    full = nat.shape[0]
    ones = lax.broadcasted_iota(jnp.int32, (full - depth, nat.shape[1]), 0) == 0
    nat[depth:full, :] = ones.astype(F32)
    for block in range(blocks):
        nat[width * block : width * (block + 1), :] = start[block, 0:width, :]
    for layer in range(layers):
        x_out[layer] = nat[...].astype(BF16)
        place_cross(idx, weight, own, slices, blocks, layer, pad)
        at = left * layers + layer
        for block in range(blocks):
            rows = slice(pad * block, pad * (block + 1))
            value = dot(weight[layer, rows, :], x_out[layer, 0:depth, :], NN) + bias[block][0:pad, at : at + 1]
            z_out[layer, rows, :] = value
            before = start[block] if layer == 0 else state[block]
            value = start[block] * value + before
            state[block] = value
            nat[width * block : width * (block + 1), :] = value[0:width, :]
    x_out[layers] = nat[...].astype(BF16)


def tower_both(idx, *refs, blocks, layers, width, depth, fields, examples):
    (labels, day_ids), refs = refs[:2], refs[2:]
    pieces, refs = refs[:blocks], refs[blocks:]
    (own1, own2), refs = refs[:2], refs[2:]
    slices, refs = refs[:8], refs[8:]
    x_all, acts, far, heads, flow, lines_out, day_out, field_out = refs[:8]
    inputs, t1, t2, slope1, act2, headed, vectors = refs[8:]
    hidden = t1.shape[0]
    size = hidden // blocks
    part = x_all.shape[2]
    low = depth // LANES * LANES
    offsets = places(idx)
    base = idx[0] * size
    t1[rows_at(base, size), :] = own1[...]
    t2[rows_at(base, size), :] = own2[...]
    for turn, piece in enumerate(pieces):
        inputs[block_of(idx, turn, blocks)] = piece[width : width + 3, :].astype(F32)
    for turn in range(1, blocks):
        base = block_of(idx, turn, blocks) * size
        for offset, piece in zip(offsets, slices):
            rows = rows_at(base + offset, SHARE)
            t1[rows, :] = piece[turn - 1, 0:SHARE, :]
            t2[rows, :] = piece[turn - 1, SHARE : 2 * SHARE, 0:hidden]
    parts = [slice(size * block, size * (block + 1)) for block in range(blocks)]
    columns = []
    for block in range(blocks):
        vectors[0:3, :] = inputs[block]
        columns.append(vectors[...].T)
    for rows, column in zip(parts, columns):
        act, slope = gelu_parts(dot(t1[rows, 0:depth], x_all[layers, 0:depth, :], NN) + column[:, 0:1])
        acts[0, rows, :] = act.astype(BF16)
        slope1[rows, :] = slope
    logits = jnp.zeros((1, part), F32)
    for rows, column in zip(parts, columns):
        act, slope = gelu_parts(dot(t2[:, rows], acts[0], TN) + column[:, 2:3])
        act2[rows, :] = act
        headed[rows, :] = column[:, 1:2] * slope
        logits += jnp.sum(act * column[:, 1:2], axis=0, keepdims=True)

    tally = jnp.zeros(slices[0].shape[:2] + (LANES,), F32)
    for piece in slices:
        tally += piece[:, :, low:].astype(F32)
    tally = tally.reshape(-1, LANES)[0:BUCKETS, :]
    shift = depth - low
    high = tally[:, shift : shift + fields + 1]
    count = 256.0 * high + tally[:, shift + COUNT : shift + COUNT + fields + 1]
    days = count[0:32, fields : fields + 1]
    padded = jnp.concatenate([count, jnp.zeros((BUCKETS, LANES - fields - 1), F32)], axis=1).T
    field_out[...] = padded[0:fields, :].astype(jnp.int32)
    day_out[...] = padded[fields : fields + 1, :].astype(jnp.int32)

    mine = pl.ds(pl.multiple_of(idx[0] * part, LANES), part)
    lab = labels[:, mine].astype(F32)
    table = (lax.broadcasted_iota(jnp.int32, (32, part), 0) == day_ids[:, mine]).astype(F32)
    share = examples / (DAYS * jnp.maximum(days, 1.0))
    weights = jnp.sum(table * share, axis=0, keepdims=True)
    decay = jnp.exp(-jnp.abs(logits))
    loss = jnp.maximum(logits, 0.0) + jnp.log1p(decay) - lab * logits
    sigmoid = jnp.where(logits >= 0.0, 1.0, decay) / (1.0 + decay)
    dl = weights * (sigmoid - lab)
    losses = dot(jnp.broadcast_to(loss, (8, part)), table, NT, lax.Precision.HIGHEST)[0:1, :]
    lines_out[0:1, :] = logits
    lines_out[1:2, :] = jnp.zeros_like(logits)
    lines_out[1:2, 0 : losses.shape[1]] = losses

    acts[1] = (dl * headed[...]).astype(BF16)
    far[0:hidden, :] = acts[1]
    for rows in parts:
        acts[2, rows, :] = (dot(t2[rows, :], acts[1], NN) * slope1[rows, :]).astype(BF16)
    for block in range(blocks):
        rows = rows_at(block * size + (1 - idx[1]) * HALF, HALF)
        at = hidden + HALF * block
        far[at : at + HALF, :] = acts[0, rows, :]
        at = hidden + HALF * (block + blocks)
        far[at : at + HALF, :] = acts[2, rows, :]
    for rows in parts:
        heads[rows, :] = jnp.broadcast_to(jnp.sum(act2[rows, :] * dl, axis=1, keepdims=True), (size, LANES))
    flow[...] = dot(t1[:, 0:depth], acts[2], TN)


def cross_backward(idx, *refs, blocks, layers, width, pad, depth):
    extra_lines, refs = refs[0], refs[1:]
    pieces, refs = refs[:blocks], refs[blocks:]
    own, refs = refs[0], refs[1:]
    turned, refs = refs[:blocks], refs[blocks:]
    slices, refs = refs[:16], refs[16:]
    (dx3, z_all), refs = refs[:2], refs[2:]
    eg_out, refs = refs[:blocks], refs[blocks:]
    dz_out, rest_out, dz_far_last, dz_far_out = refs[:4]
    weight, inputs, lines, tail, flow, padded, total, rest = refs[4:]
    left = width - MAIN
    place_rest(idx, weight, turned, lines, tail, blocks, layers, left, pad)
    for turn, piece in enumerate(pieces):
        inputs[block_of(idx, turn, blocks)] = piece[0:width, :].astype(F32)
    padded[...] = jnp.zeros_like(padded)
    rest[...] = jnp.zeros_like(rest)
    for layer in reversed(range(layers)):
        source = dx3 if layer == layers - 1 else flow
        for block in range(blocks):
            rows = slice(pad * block, pad * (block + 1))
            dx = source[width * block : width * (block + 1), :]
            padded[block, 0:width, :] = dx
            dx = padded[block, 0:width, :]
            dz = dx * inputs[block]
            term = dx * z_all[layer, pad * block : pad * block + width, :]
            total[block, 0:width, :] = term if layer == layers - 1 else total[block, 0:width, :] + term
            rest[left * block : left * (block + 1), :] = dz[MAIN:width, :]
            padded[block, 0:width, :] = dz
            dz_out[layer, rows, :] = padded[block].astype(BF16)
        rest_out[layer] = rest[...].astype(BF16)
        far = dz_far_last.at[0] if layer == layers - 1 else dz_far_out.at[layer]
        far[HALF * blocks :, :] = rest[...].astype(BF16)
        for block in range(blocks):
            rows = rows_at(pad * block + (1 - idx[1]) * HALF, HALF)
            far[HALF * block : HALF * (block + 1), :] = dz_out[layer, rows, :]
        place_cross(idx, weight, own, slices, blocks, layer, pad)
        flow[...] = source[...] + dot(weight[layer], dz_out[layer], TN)
    extras = split3(extra_lines[0:1, :]) + split3(extra_lines[1:2, :])
    for block in range(blocks):
        total[block, 0:width, :] += flow[width * block : width * (block + 1), :]
        total[block, width:, :] = jnp.zeros((pad - width, flow.shape[1]), F32)
        for at, extra in enumerate(extras):
            total[block, width + at : width + at + 1, :] = extra
    for turn in range(blocks):
        eg_out[turn][...] = total[block_ahead(idx, turn, blocks)].astype(BF16)


def tower_grads(idx, x_all, x_far, acts, far, head, near_out, far_out, send_out, *refs, blocks, depth, layers):
    x_cat, acts_in, far_in, heads, lhs, d_cat, near, away, send, sems = refs
    hidden = acts.shape[1]
    size = hidden // blocks
    part = acts.shape[2]
    low = depth // LANES * LANES
    bias = depth - low
    copies = Copies(sems)
    first = [
        copies.start(acts, acts_in),
        copies.start(far, far_in),
        copies.start(x_all.at[layers], x_cat.at[:, 0:part]),
        copies.start(x_far.at[layers], x_cat.at[:, part : 2 * part]),
        copies.start(head, heads),
    ]
    wait(*first)
    lane = lane_of((SHARE, LANES))
    pick = (lax.broadcasted_iota(jnp.int32, (LANES, 2 * part), 0) == bias + 1).astype(BF16)
    order = [(where, slot) for where in range(4) for slot in range(blocks)]
    shares = relative(idx)
    d_cat[:, 0:part] = acts_in[1]
    d_cat[:, part:] = far_in[0:hidden, :]
    scale = []
    for at, (where, slot) in enumerate(order):
        block = block_ahead(idx, slot, blocks)
        rows = rows_at(block * size + idx[1] * HALF + SHARE * shares[where], SHARE)
        other = rows_at(block * size + (1 - idx[1]) * HALF + SHARE * shares[where], SHARE)
        lines = rows_at(hidden + HALF * block + SHARE * shares[where], SHARE)
        after_it = rows_at(hidden + HALF * (block + blocks) + SHARE * shares[where], SHARE)
        here = slice(SHARE * at, SHARE * (at + 1))
        lhs[0, here, 0:part] = acts_in[2, rows, :]
        lhs[0, here, part:] = far_in[after_it, :]
        lhs[1, here, 0:part] = acts_in[0, rows, :]
        lhs[1, here, part:] = far_in[lines, :]
        lhs[2, here, 0:part] = acts_in[1, rows, :]
        lhs[2, here, part:] = far_in[rows, :]
        scale.append(
            jnp.where(lane == bias + 2, heads[rows, :], 0.0) + jnp.where(lane == bias + 3, heads[other, :], 0.0)
        )
    extra = dot(lhs[2], pick, NT)
    wide = dot(lhs[0], x_cat[...], NT)
    deep = dot(lhs[1], d_cat[...], NT)
    for at, (where, slot) in enumerate(order):
        target = (near, away, send.at[0], send.at[1])[where].at[slot]
        here = slice(SHARE * at, SHARE * (at + 1))
        target[0:SHARE, 0:low] = wide[here, 0:low].astype(BF16)
        target[0:SHARE, low:] = (wide[here, low:] + extra[here, :] + scale[at]).astype(BF16)
        target[SHARE : 2 * SHARE, 0:hidden] = deep[here, :].astype(BF16)
        target[SHARE : 2 * SHARE, hidden:] = jnp.zeros((SHARE, target.shape[1] - hidden), BF16)
    wait(copies.start(send, send_out), copies.start(near, near_out), copies.start(away, far_out))


def cross_grads(idx, x_all, x_far, dz, rest, dz_far, near_out, far_out, send_out, *refs, blocks, base, pad, depth):
    x_cat, dz_in, far_in, rest_in, lhs, few, near, away, send, sems = refs
    part = dz.shape[2]
    low = depth // LANES * LANES
    groups = -(-depth // MAIN)
    count = dz_far.shape[0]
    copies = Copies(sems)
    first = []
    for layer in reversed(range(count)):
        first.append(
            [
                copies.start(dz.at[base + layer], dz_in.at[layer]),
                copies.start(dz_far.at[layer], far_in.at[layer]),
                copies.start(rest.at[base + layer], rest_in.at[layer]),
                copies.start(x_all.at[base + layer], x_cat.at[layer, :, 0:part]),
                copies.start(x_far.at[base + layer], x_cat.at[layer, :, part : 2 * part]),
            ]
        )
    few[...] = jnp.zeros_like(few)
    order = [(where, slot) for where in range(4) for slot in range(blocks)]
    shares = relative(idx)
    for layer, started in zip(reversed(range(count)), first):
        wait(*started)
        extra = jnp.zeros((HALF, LANES), F32)
        for group in range(groups):
            lines = slice(REST + 16 * group, REST + 16 * (group + 1))
            few[group, lines, 0:part] = rest_in[layer]
            few[group, lines, part:] = far_in[layer, HALF * blocks :, :]
            if MAIN * (group + 1) <= depth:
                rows = rows_at(MAIN * group + idx[1] * HALF, HALF)
            else:
                rows = slice(MAIN * group, MAIN * group + HALF)
            extra += dot(x_cat[layer, rows, :], few[group], NT)
        for at, (where, slot) in enumerate(order):
            block = block_ahead(idx, slot, blocks)
            rows = rows_at(pad * block + idx[1] * HALF + SHARE * shares[where], SHARE)
            lines = rows_at(HALF * block + SHARE * shares[where], SHARE)
            here = slice(SHARE * at, SHARE * (at + 1))
            lhs[here, 0:part] = dz_in[layer, rows, :]
            lhs[here, part:] = far_in[layer, lines, :]
        grad = dot(lhs[...], x_cat[layer], NT)
        lines = slice(SHARE * layer, SHARE * (layer + 1))
        wide = [extra[SHARE * q : SHARE * (q + 1), :] for q in range(4)]
        for at, (where, slot) in enumerate(order):
            target = (near, away, send.at[0], send.at[1])[where].at[slot]
            here = slice(SHARE * at, SHARE * (at + 1))
            target[lines, 0:low] = grad[here, 0:low].astype(BF16)
            more = wide[0]
            for q in range(1, 4):
                more = jnp.where(shares[where] == q, wide[q], more)
            target[lines, low:] = (grad[here, low:] + more).astype(BF16)
    wait(copies.start(send, send_out), copies.start(near, near_out), copies.start(away, far_out))


def eight(mine, one, two, far):
    return [mine, one, two.at[0], two.at[1]] + [far.at[at] for at in range(4)]


def finish_input(idx, *refs, blocks, lane):
    pieces, (out, logits, losses, day_held) = refs[:blocks], refs[blocks:]
    width = out.shape[0]
    size = pieces[0].shape[1]
    for turn, piece in enumerate(pieces):
        block = block_of(idx, turn, blocks)
        lanes = pl.ds(pl.multiple_of(block * size, LANES), size)
        values = piece[...].astype(F32)
        line = lambda at: values[width + at : width + at + 1, :]
        out[:, lanes] = values[0:width, :]
        logits[:, lanes] = line(0) + line(1) + line(2)
        day_held[block] = jnp.broadcast_to(line(3) + line(4) + line(5), day_held.shape[1:])
    days = day_held[0]
    for block in range(1, blocks):
        days += day_held[block]
    row = lax.broadcasted_iota(jnp.int32, losses.shape, 0)
    tile = jnp.zeros(losses.shape, F32)
    for at, value in enumerate(split3(days[0:1, 0:LANES])):
        tile = jnp.where(row == SHARE + at, value, tile)
    losses[...] = pltpu.roll(tile, lane, 1)


def finish_tower(idx, *refs, depth):
    slices, (counts, out1, out2, rows_out, mean_out, lines, day_held) = eight(*refs[:4]), refs[4:]
    low = depth // LANES * LANES
    size, hidden = out2.shape
    for offset, piece in zip(places(idx), slices):
        lines[rows_at(offset, SHARE), :] = piece[0:SHARE, :].astype(F32)
        out2[rows_at(offset, SHARE), :] = piece[SHARE : 2 * SHARE, 0:hidden].astype(F32)
        tile = piece[SHARE : SHARE + 16, low:].astype(F32)
        day_held[lax.div(offset, SHARE)] = tile[0:1, :] + tile[1:2, :] + tile[2:3, :]
    turned = lines[...].T
    out1[...] = turned[0:depth, :]
    head = turned[depth + 3 : depth + 4, :]
    rows_out[0:1, :] = turned[depth : depth + 1, :]
    rows_out[1:2, :] = turned[depth + 1 : depth + 2, :]
    rows_out[2:3, 0:HALF] = turned[depth + 2 : depth + 3, 0:HALF] + head[:, HALF:]
    rows_out[2:3, HALF:] = turned[depth + 2 : depth + 3, HALF:] + head[:, 0:HALF]
    days = day_held[0]
    for at in range(1, day_held.shape[0]):
        days += day_held[at]
    at = depth - low
    days = days[:, at : at + DAYS]
    mean = days / jnp.maximum(counts[:, 0:DAYS].astype(F32), 1.0)
    mean_out[...] = jnp.sum(mean, axis=1, keepdims=True) / DAYS


def finish_cross(idx, *refs, blocks, base, more):
    slices, refs = eight(*refs[:4]), refs[4:]
    before, (out, bias_out, held, lines, sems) = refs[:more], refs[more:]
    count, width, depth = held.shape
    left = width - MAIN
    low = depth // LANES * LANES
    copies = Copies(sems)
    last = []
    if more:
        bias_out[count:, :] = before[1][...]
    for layer in range(count):
        rows = slice(SHARE * layer, SHARE * (layer + 1))
        for offset, piece in zip(places(idx), slices):
            held[layer, rows_at(offset, SHARE), :] = piece[rows, 0:depth].astype(F32)
            lines[rows_at(offset, SHARE), :] = piece[rows, low:].astype(F32)
        turned = lines[...].T
        bias_out[layer : layer + 1, 0:MAIN] = turned[depth - low : depth - low + 1, :]
        for group in range(-(-depth // MAIN)):
            rest = jnp.zeros((left, MAIN), F32)
            for block in range(blocks):
                at = REST + 16 * group + left * block
                rest = jnp.where(idx[0] == block, turned[at : at + left, :], rest)
            stop = min(depth, MAIN * (group + 1)) - MAIN * group
            held[layer, MAIN:width, MAIN * group : MAIN * group + stop] = rest[:, 0:stop]
        last.append(copies.start(held.at[layer], out.at[base + layer]))
        corner = jnp.broadcast_to(rest[:, stop : stop + 1], (left, LANES))
        ahead = lax.broadcasted_iota(jnp.int32, (left, LANES), 0) == lane_of((left, LANES))
        line = jnp.sum(jnp.where(ahead, corner, 0.0), axis=0, keepdims=True)
        bias_out[layer : layer + 1, MAIN:width] = line[:, 0:left]
    wait(*last)


def per_device(
    embedded,
    feature_ids,
    day_ids,
    labels,
    cross_weight,
    cross_bias,
    tower1,
    tower1_bias,
    tower2,
    tower2_bias,
    head_weight,
):
    blocks = lax.axis_size("mp")
    groups = lax.axis_size("dp")
    tokens, width = embedded.shape
    layers, _, depth = cross_weight.shape
    size, hidden = tower2.shape
    pad = -(-width // 16) * 16
    full = -(-(depth + 3) // LANES) * LANES
    part = tokens // blocks
    examples = tokens * groups
    flat = blocks * pad
    shape = jax.ShapeDtypeStruct
    vmem = pltpu.VMEM

    me = lax.axis_index("mp")
    group = lax.axis_index("dp")
    core, plane = group & 1, (group >> 1) & 3
    idx = jnp.stack([me, core, plane]).astype(jnp.int32)
    swap = lambda bits: [(i, i ^ bits(i)) for i in range(groups)]
    first = swap(lambda i: 4 if i & 1 else 2)
    second = swap(lambda i: 2 if i & 1 else 4)
    pair = swap(lambda i: 1)
    others = [swap(lambda i, b=b: 1 << b) for b in range(3, groups.bit_length() - 1)]
    turn_by = lambda r: [(i, (i + r) % blocks) for i in range(blocks)]
    hop = lambda value, perm: lax.ppermute(value, "dp", perm)
    turns = lambda values: [
        lax.ppermute(value, "mp", turn_by(r + 1)) for r, value in enumerate(values)
    ]

    first_send = call(
        pack_first,
        shape((SHARE, depth), BF16),
        [],
        [idx, cross_weight],
        mib=4,
        spec=HBM,
        out_spec=VMEM,
        copies=1,
    )
    first_turned = turns([first_send] * (blocks - 1))
    cross_send = call(
        pack_cross,
        shape(((layers - 1) * SHARE + 16, depth), BF16),
        [vmem((16, depth), F32)],
        [after(idx, first_send), cross_weight, cross_bias],
        mib=8,
        nbytes=2 << 20,
    )
    vectors = jnp.stack([tower1_bias, head_weight, tower2_bias])
    tower_send, tower_own, tally, *chunks = call(
        functools.partial(pack_rest, blocks=blocks),
        tuple(
            [shape((2 * SHARE, depth), BF16), shape((size, full), BF16), shape(((blocks - 1) * 2 * SHARE, LANES), BF16)]
            + [shape((width + 3, part), BF16)] * blocks
        ),
        [],
        [after(idx, first_send), embedded.T, vectors, tower1, tower2, feature_ids.T, day_ids[None, :]],
        mib=24,
        nbytes=2 << 20,
    )
    for perm in others:
        tally = tally + hop(tally, perm)

    join = lambda *values: lax.optimization_barrier(values)
    with_pair = lambda held: held + [hop(value, pair) for value in held]
    first_mine = jnp.stack(first_turned)
    first_mine, cross_send = join(first_mine, cross_send)
    first_one, first_two = hop(first_mine, first), hop(first_mine, second)
    cross_turned = turns([cross_send] * (blocks - 1))
    first_one, first_two, tower_send, *cross_turned = join(first_one, first_two, tower_send, *cross_turned)

    first_three = hop(first_one, second)
    cross_mine = jnp.stack([value[: (layers - 1) * SHARE] for value in cross_turned])
    cross_one, cross_two = hop(cross_mine, first), hop(cross_mine, second)
    tower_turned = turns([tower_send] * (blocks - 1))
    first_three, cross_one, cross_two, *tower_turned = join(first_three, cross_one, cross_two, *tower_turned)

    first_slices = with_pair([first_mine, first_one, first_two, first_three])
    cross_three = hop(cross_one, second)
    tower_mine = jnp.concatenate(
        [jnp.stack(tower_turned), tally.reshape(blocks - 1, 2 * SHARE, LANES)[:, :, : full - depth]], axis=2
    )
    tower_one, tower_two = hop(tower_mine, first), hop(tower_mine, second)
    pieces = [chunks[0]] + turns([after(chunk, tower_turned[0]) for chunk in chunks[1:]])
    cross_three, tower_one, tower_two, *pieces = join(cross_three, tower_one, tower_two, *pieces)

    tower_three = hop(tower_one, second)
    cross_slices = first_slices + with_pair([cross_mine, cross_one, cross_two, cross_three])
    tower_slices = with_pair([tower_mine, tower_one, tower_two, tower_three])

    z_all, x_all = call(
        functools.partial(cross_forward, blocks=blocks, layers=layers, width=width, pad=pad, depth=depth),
        (shape((layers, flat, part), F32), shape((layers + 1, full, part), BF16)),
        [
            vmem((layers, flat, depth), BF16),
            vmem((blocks, 16, depth), F32),
            vmem((16, depth), F32),
            vmem((blocks, pad, part), F32),
            vmem((blocks, pad, part), F32),
            vmem((full, part), F32),
        ],
        [idx, *pieces, cross_weight, cross_send, *cross_turned, *cross_slices],
        mib=28,
        flops=2 * layers * flat * full * part,
        nbytes=20 << 20,
    )
    x_far = hop(x_all, pair)
    fields = feature_ids.shape[1]
    acts, far, head_col, dx3, lines, day_line, field_counts = call(
        functools.partial(
            tower_both, blocks=blocks, layers=layers, width=width, depth=depth, fields=fields, examples=examples
        ),
        (
            shape((3, hidden, part), BF16),
            shape((2 * hidden, part), BF16),
            shape((hidden, LANES), F32),
            shape((depth, part), F32),
            shape((2, part), F32),
            shape((1, BUCKETS), jnp.int32),
            shape((fields, BUCKETS), jnp.int32),
        ),
        [
            vmem((blocks, 3, part), F32),
            vmem((hidden, full), BF16),
            vmem((hidden, hidden), BF16),
            vmem((hidden, part), F32),
            vmem((hidden, part), F32),
            vmem((hidden, part), F32),
            vmem((8, part), F32),
        ],
        [
            idx,
            labels[None, :],
            day_ids[None, :],
            *pieces,
            tower_own,
            tower2,
            *tower_slices,
            x_all,
        ],
        mib=28,
        flops=8 * hidden * full * part,
        nbytes=10 << 20,
    )
    far = hop(far, pair)

    def halves(rows):
        keep = (blocks, rows, full)
        return keep, keep, (2,) + keep

    def grads(kernel, rows, scratch, args, copies, flops):
        return call(
            kernel,
            tuple(shape(s, BF16) for s in halves(rows)),
            scratch + [vmem(s, BF16) for s in halves(rows)],
            args,
            mib=20,
            spec=HBM,
            copies=copies,
            flops=flops,
            nbytes=10 << 20,
        )

    tower_parts = grads(
        functools.partial(tower_grads, blocks=blocks, depth=depth, layers=layers),
        2 * SHARE,
        [
            vmem((full, 2 * part), BF16),
            vmem((3, hidden, part), BF16),
            vmem((2 * hidden, part), BF16),
            vmem((hidden, LANES), F32),
            vmem((3, HALF * blocks, 2 * part), BF16),
            vmem((hidden, 2 * part), BF16),
        ],
        [idx, x_all, x_far, acts, far, head_col],
        8,
        4 * hidden * full * part,
    )
    tower_arrived = hop(tower_parts[2], first)
    *input_grads, dz, dz_rest, last_far, dz_far = call(
        functools.partial(cross_backward, blocks=blocks, layers=layers, width=width, pad=pad, depth=depth),
        tuple([shape((pad, part), BF16)] * blocks)
        + (
            shape((layers, flat, part), BF16),
            shape((layers, 16, part), BF16),
            shape((1, HALF * blocks + 16, part), BF16),
            shape((layers - 1, HALF * blocks + 16, part), BF16),
        ),
        [
            vmem((layers, flat, depth), BF16),
            vmem((blocks, width, part), F32),
            vmem((blocks, 16, depth), F32),
            vmem((16, depth), F32),
            vmem((depth, part), F32),
            vmem((blocks, pad, part), F32),
            vmem((blocks, pad, part), F32),
            vmem((16, part), F32),
        ],
        [
            after(idx, tower_parts[2]),
            lines,
            *pieces,
            cross_weight,
            cross_send,
            *cross_turned,
            *cross_slices,
            dx3,
            z_all,
        ],
        mib=34,
        flops=2 * layers * flat * full * part,
        nbytes=20 << 20,
    )
    last_far = hop(last_far, pair)
    dz_far = hop(dz_far, pair)

    def cross_parts_of(base, count, far, start):
        return grads(
            functools.partial(cross_grads, blocks=blocks, base=base, pad=pad, depth=depth),
            count * SHARE,
            [
                vmem((count, full, 2 * part), BF16),
                vmem((count, flat, part), BF16),
                vmem((count, HALF * blocks + 16, part), BF16),
                vmem((count, 16, part), BF16),
                vmem((HALF * blocks, 2 * part), BF16),
                vmem((-(-depth // MAIN), LANES, 2 * part), BF16),
            ],
            [start, x_all, x_far, dz, dz_rest, far],
            5 * count + 3,
            2 * count * flat * full * part,
        )

    last_parts = cross_parts_of(layers - 1, 1, last_far, idx)
    cross_parts = cross_parts_of(0, layers - 1, dz_far, after(idx, last_parts[2]))

    down = lambda value: value.astype(BF16)
    up = lambda value: value.astype(F32)

    def near_sum(parts, arrived, last):
        return up(parts[0]) + up(arrived[0]) + up(last)

    def far_send(parts, arrived):
        return hop(down(up(parts[1]) + up(arrived[1])), second)

    def send_blocks(held):
        return turns([down(held[r]) for r in range(1, blocks)])

    def total_of(held, turned):
        held = held[0] + sum(up(value) for value in turned)
        for perm in others:
            held = held + hop(held, perm)
        return held

    def two_of(mine, one):
        return hop(jnp.stack([mine, one]), second)

    def far_of(mine, one, two):
        return hop(jnp.concatenate([jnp.stack([mine, one]), two]), pair)

    tower_arrived, last_send = join(tower_arrived, last_parts[2])
    tower_second = far_send(tower_parts, tower_arrived)
    last_arrived = hop(last_send, first)
    grad_pieces = [input_grads[0]] + turns([after(value, last_send) for value in input_grads[1:]])
    tower_second, last_arrived, cross_send, *grad_pieces = join(
        tower_second, last_arrived, cross_parts[2], *grad_pieces
    )

    tower_held = near_sum(tower_parts, tower_arrived, tower_second)
    tower_turned = send_blocks(tower_held)
    last_second = far_send(last_parts, last_arrived)
    cross_arrived = hop(cross_send, first)
    input_out, logits_all, losses = call(
        functools.partial(finish_input, blocks=blocks, lane=depth % LANES),
        (shape((width, tokens), F32), shape((1, tokens), F32), shape((2 * SHARE, LANES), F32)),
        [vmem((blocks, 8, part), F32)],
        [idx, *grad_pieces],
        mib=16,
        nbytes=2 << 20,
    )
    last_second, cross_arrived, losses, *tower_turned = join(last_second, cross_arrived, losses, *tower_turned)

    last_held = near_sum(last_parts, last_arrived, last_second)
    last_turned = send_blocks(last_held)
    cross_second = far_send(cross_parts, cross_arrived)
    tower_mine = down(total_of(tower_held, tower_turned) + jnp.pad(losses, ((0, 0), (full - LANES, 0))))
    tower_one = hop(tower_mine, first)
    cross_second, tower_one, *last_turned = join(cross_second, tower_one, *last_turned)

    cross_held = near_sum(cross_parts, cross_arrived, cross_second)
    cross_turned = send_blocks(cross_held)
    tower_two = two_of(tower_mine, tower_one)
    last_mine = down(total_of(last_held, last_turned))
    last_one = hop(last_mine, first)
    tower_two, last_one, *cross_turned = join(tower_two, last_one, *cross_turned)

    cross_mine = down(total_of(cross_held, cross_turned))
    cross_one = hop(cross_mine, first)
    last_two = two_of(last_mine, last_one)
    tower_far = far_of(tower_mine, tower_one, tower_two)
    cross_one, last_two, tower_far = join(cross_one, last_two, tower_far)

    cross_two = two_of(cross_mine, cross_one)
    last_far = far_of(last_mine, last_one, last_two)
    tower_sums = [tower_mine, tower_one, tower_two, tower_far]
    last_sums = [last_mine, last_one, last_two, last_far]
    tower1_grad, tower2_grad, rows, mean = call(
        functools.partial(finish_tower, depth=depth),
        (shape((depth, size), F32), shape((size, hidden), F32), shape((3, size), F32), shape((1, 1), F32)),
        [vmem((size, full), F32), vmem((8, 1, LANES), F32)],
        [idx, *tower_sums, day_line],
        mib=16,
        nbytes=4 << 20,
    )
    def finish(sums, base, count, before):
        alias = {5: 0} if before else {}
        return call(
            functools.partial(finish_cross, blocks=blocks, base=base, more=len(before)),
            (shape((layers, width, depth), F32), shape((count + len(before) // 2, width), F32)),
            [vmem((count, width, depth), F32), vmem((MAIN, LANES), F32)],
            [idx, *sums] + [(value, spec) for value, spec in zip(before, (HBM, VMEM))],
            mib=16,
            out_spec=(HBM, VMEM),
            aliases=alias,
            copies=count,
            nbytes=4 << 20,
        )

    before = finish(last_sums, layers - 1, 1, ())
    cross_far = far_of(cross_mine, cross_one, cross_two)
    cross_grad, cross_bias_grad = finish([cross_mine, cross_one, cross_two, cross_far], 0, layers - 1, before)
    day_counts = day_line[0, :DAYS]
    return (
        mean[0, 0],
        logits_all[0],
        input_out.T,
        cross_grad,
        cross_bias_grad,
        tower1_grad,
        rows[0],
        tower2_grad,
        rows[1],
        rows[2],
        day_counts,
        field_counts,
    )


def solution(mesh):
    in_specs = (
        P("dp", "mp"),
        P("dp", None),
        P("dp"),
        P("dp"),
        P(None, "mp", None),
        P(None, "mp"),
        P(None, "mp"),
        P("mp"),
        P("mp", None),
        P("mp"),
        P("mp"),
    )
    out_specs = (
        P(),
        P("dp"),
        P("dp", "mp"),
        P(None, "mp", None),
        P(None, "mp"),
        P(None, "mp"),
        P("mp"),
        P("mp", None),
        P("mp"),
        P("mp"),
        P(),
        P(),
    )
    return jax.shard_map(
        per_device, mesh=mesh, in_specs=in_specs, out_specs=out_specs, check_vma=False
    )
```

time: 774 us -> 197 us (0.25)
  blocking collectives: 343 us -> 0 us
  waiting for transfers between devices: 260 us -> 104 us
  local copies, waits for them, and re-layouts: 62.1 us -> 2.79 us
  matrix products: 47 us -> 0 us
  starting transfers between devices: 11.3 us -> 52 us
  Pallas kernels: 0 us -> 35.2 us
  other arithmetic: 26.6 us -> 1.71 us
  between operations: 16.9 us -> 1.28 us
    unnamed x4 -> x0, blocking collectives: 296 us -> none
    all_gather x5 -> x0, waiting for transfers between devices: 231 us -> none  [the longest x4 185 us: spread_features(): return lax.all_gather(values, 'mp', axis=1, tiled=True)]
    ppermute x0 -> x64, waiting for transfers between devices: none -> 104 us  [the longest x24 70.2 us: per_device(): lax.ppermute(value, 'mp', turn_by(r + 1))]
    ppermute x0 -> x64, starting transfers between devices: none -> 52 us  [the longest x40 30.4 us: per_device(): hop = lambda value, perm: lax.ppermute(value, 'dp', perm)]
    dot_general x15 -> x0, matrix products: 47 us -> none  [the longest x3 13.5 us: per_device(): jnp.dot(grad_z, cross_weight[layer_index], preferred_element_type=jnp.flo...]
    psum x3 -> x0, blocking collectives: 47 us -> none  [the longest x1 21.5 us: per_device(): day_counts, field_counts = lax.psum((local_days, local_fields), 'dp')]
    unnamed x68 -> x24, local copies, waits for them, and re-layouts: 41.2 us -> 1.56 us
    pallas_call x0 -> x13, Pallas kernels: none -> 35.2 us  [call(): pl.pallas_call(kernel, out_shape=outs, in_specs=[SMEM] + specs, out_specs...]
  transfers between devices with their start and end apart: 11 -> 64, of which waited for: 6 -> 32; matrix products, arithmetic and copies ran while one was open for 16% -> 1% of each run, Pallas kernels for 0% -> 13%
where the time goes in v2:
time: 197 us
  waiting for transfers between devices  104 us (53%)
  starting transfers between devices  52 us (26%)
  Pallas kernels  35.2 us (18%)
  local copies, waits for them, and re-layouts  2.79 us (1%)
    ppermute x24, waiting for transfers between devices, per_device(): lax.ppermute(value, 'mp', turn_by(r + 1))  70.2 us
    pallas_call x13, Pallas kernels, call(): pl.pallas_call(kernel, out_shape=outs, in_specs=[SMEM] + specs, out_specs...  35.2 us
    ppermute x40, waiting for transfers between devices, per_device(): hop = lambda value, perm: lax.ppermute(value, 'dp', perm)  33.8 us
    ppermute x40, starting transfers between devices, per_device(): hop = lambda value, perm: lax.ppermute(value, 'dp', perm)  30.4 us
    ppermute x24, starting transfers between devices, per_device(): lax.ppermute(value, 'mp', turn_by(r + 1))  21.5 us
  transfers between devices with their start and end apart: 64, of which 32 were waited for; matrix products, arithmetic and copies ran while one was open for 1% of the time, Pallas kernels for 13%

profile of v2, /device:TPU:9, one launch (start us, length us, event | category | flops | bytes accessed | tf_op | source)
XLA Modules:
  0.0 196.9 jit_solution(10483345415561125227)
XLA Ops:
  0.7 1.5 copy-done
  3.0 1.3 collective-permute-start
  5.4 1.4 collective-permute-start.2
  7.4 1.4 collective-permute-done.1
  8.8 4.0 %collective-permute-done.2 = bf16[32,1040]{1,0:T(8,128)(2,1)S(1)} collective-permute-done((bf16[32,1040]{1,0:T(8,128)(2,1)S(1)}, bf16[32,1040]{1,0:T(8,128)(2,1)S(1)}, u32[]{:S(2)}, u32[]{:S(2)}) %collective-permute-start.2) | collective-permute-done | bytes 66592 | tf_op jit(solution)/shard_map/ppermute | solution.py:568
  15.2 1.7 collective-permute-start.6
  17.8 2.6 %shard_map.204 = (bf16[64,1040]{1,0:T(8,128)(2,1)S(1)}, bf16[256,1152]{1,0:T(8,128)(2,1)S(1)}, bf16[192,128]{1,0:T(8,128)(2,1)S(1)}, bf16[263,256]{1,0:T(8,128)(...) custom-call(s32[3]{0:T(128)S(1)} %pad_add_fusion.idx, ...), custom_call_target="tpu_custom_call" | custom-call | bytes 2097152 | tf_op jit(solution)/shard_map/pallas_call | solution.py:43
  20.5 9.3 %collective-permute-done.6.refs_7_.refs_8_ = bf16[80,1040]{1,0:T(8,128)(2,1)S(1)} collective-permute-done((bf16[80,1040]{1,0:T(8,128)(2,1)S(1)}, bf16[80,1040]{1,0:T(8,128)(2,1)S(1)}, u32[]{:S(2)}, u32[]{:S(2)}) %collective-permute-start.6) | collective-permute-done | bytes 166432 | tf_op jit(solution)/shard_map/ppermute | solution.py:568
  29.8 4.1 %collective-permute-done.7.refs_8_.refs_9_ = bf16[80,1040]{1,0:T(8,128)(2,1)S(1)} collective-permute-done((bf16[80,1040]{1,0:T(8,128)(2,1)S(1)}, bf16[80,1040]{1,0:T(8,128)(2,1)S(1)}, u32[]{:S(2)}, u32[]{:S(2)}) %collective-permute-start.7) | collective-permute-done | bytes 166432 | tf_op jit(solution)/shard_map/ppermute | solution.py:568
  35.7 3.3 %collective-permute-done.11 = bf16[64,1040]{1,0:T(8,128)(2,1)S(1)} collective-permute-done((bf16[64,1040]{1,0:T(8,128)(2,1)S(1)}, bf16[64,1040]{1,0:T(8,128)(2,1)S(1)}, u32[]{:S(2)}, u32[]{:S(2)}) %collective-permute-start.11) | collective-permute-done | bytes 133152 | tf_op jit(solution)/shard_map/ppermute | solution.py:568
  39.0 7.4 %collective-permute-done.12 = bf16[64,1040]{1,0:T(8,128)(2,1)S(1)} collective-permute-done((bf16[64,1040]{1,0:T(8,128)(2,1)S(1)}, bf16[64,1040]{1,0:T(8,128)(2,1)S(1)}, u32[]{:S(2)}, u32[]{:S(2)}) %collective-permute-start.12) | collective-permute-done | bytes 133152 | tf_op jit(solution)/shard_map/ppermute | solution.py:568
  46.4 2.4 %collective-permute-done.13 = bf16[64,1040]{1,0:T(8,128)(2,1)S(1)} collective-permute-done((bf16[64,1040]{1,0:T(8,128)(2,1)S(1)}, bf16[64,1040]{1,0:T(8,128)(2,1)S(1)}, u32[]{:S(2)}, u32[]{:S(2)}) %collective-permute-start.13) | collective-permute-done | bytes 133152 | tf_op jit(solution)/shard_map/ppermute | solution.py:568
  53.9 2.6 %collective-permute-done.18.refs_2_.refs_4_.refs_3_ = bf16[263,256]{1,0:T(8,128)(2,1)S(1)} collective-permute-done((bf16[263,256]{1,0:T(8,128)(2,1)S(1)}, bf16[263,256]{1,0:T(8,128)(2,1)S(1)}, u32[]{:S(2)}, u32[]{:S(2)}) %collective-permute-start.18) | collective-permute-done | bytes 134688 | tf_op jit(solution)/shard_map/ppermute | solution.py:568
  56.5 5.5 %collective-permute-start.20 = (bf16[3,32,1040]{2,1,0:T(8,128)(2,1)S(1)}, bf16[3,32,1040]{2,1,0:T(8,128)(2,1)S(1)}, u32[]{:S(2)}, u32[]{:S(2)}) collective-permute-start(bf16[3,32,1040]{2,1,0:T(8,128)(2,1)S(1)} %pad_maximum_fusion.7.refs_9_.refs_10_), channel_id=1, source_target_pairs={{0,4},{4,0},{8,12},{12,8},{16,20},{20,16},{24,28},{28,24},{1,5},{5... | collective-permute-start | bytes 599048 | tf_op jit(solution)/shard_map/ppermute | solution.py:566
  62.0 1.3 collective-permute-done.19.refs_3_.refs_5_.refs_4_
  64.3 2.3 %collective-permute-done.14.refs_20_.refs_21_ = bf16[3,64,1040]{2,1,0:T(8,128)(2,1)S(1)} collective-permute-done((bf16[3,64,1040]{2,1,0:T(8,128)(2,1)S(1)}, bf16[3,64,1040]{2,1,0:T(8,128)(2,1)S(1)}, u32[]{:S(2)}, u32[]{:S(2)}) %collective-permute-start.14) | collective-permute-done | bytes 399392 | tf_op jit(solution)/shard_map/ppermute | solution.py:566
  68.9 2.1 %collective-permute-done.23.refs_16_.refs_17_ = bf16[3,32,1040]{2,1,0:T(8,128)(2,1)S(1)} collective-permute-done((bf16[3,32,1040]{2,1,0:T(8,128)(2,1)S(1)}, bf16[3,32,1040]{2,1,0:T(8,128)(2,1)S(1)}, u32[]{:S(2)}, u32[]{:S(2)}) %collective-permute-start.23) | collective-permute-done | bytes 199712 | tf_op jit(solution)/shard_map/ppermute | solution.py:566
  71.0 3.9 %shard_map.205 = (f32[3,1088,256]{2,1,0:T(8,128)S(1)}, bf16[4,1152,256]{2,1,0:T(8,128)(2,1)S(1)}) custom-call(s32[3]{0:T(128)S(1)} %pad_add_fusion.idx, bf16[263,256]{1,0:T(8,128)(2,1)S(1)} %get-tuple-element.135.refs_0_.refs_2_.refs_1_, bf16[263,256]{1,0:T(8,128)(2,1)S(1)} %collective-permute-done.17.refs_1_.refs_3_.refs_2_, ...), custom_call_target="tpu_custom_call" | custom-call | flops 1925185536 | bytes 20971520 | tf_op jit(solution)/shard_map/pallas_call | solution.py:43
  76.8 5.8 %collective-permute-done.29.refs_11_ = bf16[3,64,1152]{2,1,0:T(8,128)(2,1)S(1)} collective-permute-done((bf16[3,64,1152]{2,1,0:T(8,128)(2,1)S(1)}, bf16[3,64,1152]{2,1,0:T(8,128)(2,1)S(1)}, u32[]{:S(2)}, u32[]{:S(2)}) %collective-permute-start.29) | collective-permute-done | bytes 442400 | tf_op jit(solution)/shard_map/ppermute | solution.py:566
  82.5 1.2 collective-permute-start.33
  83.8 1.4 collective-permute-done.33.refs_15_
  85.2 4.4 %shard_map.206 = (bf16[3,1024,256]{2,1,0:T(8,128)(2,1)S(1)}, bf16[2048,256]{1,0:T(8,128)(2,1)S(1)}, f32[1024,128]{1,0:T(8,128)S(1)}, f32[1040,256]{1,0:T(8,128)S...) custom-call(s32[3]{0:T(128)S(1)} %pad_add_fusion.idx, s32[1,1024]{1,0:T(1,128)S(1)} %bitcast.111, ...), custom_call_target="tpu_custom_call" | custom-call | flops 2415919104 | bytes 10485760 | tf_op jit(solution)/shard_map/pallas_call | solution.py:43
  90.0 2.3 %collective-permute-done.34.far = bf16[2048,256]{1,0:T(8,128)(2,1)S(1)} collective-permute-done((bf16[2048,256]{1,0:T(8,128)(2,1)S(1)}, bf16[2048,256]{1,0:T(8,128)(2,1)S(1)}, u32[]{:S(2)}, u32[]{:S(2)}) %collective-permute-start.34) | collective-permute-done | bytes 1048608 | tf_op jit(solution)/shard_map/ppermute | solution.py:566
  92.3 3.2 %shard_map.207 = (bf16[4,64,1152]{2,1,0:T(8,128)(2,1)S(1)}, bf16[4,64,1152]{2,1,0:T(8,128)(2,1)S(1)}, bf16[2,4,64,1152]{3,2,1,0:T(8,128)(2,1)S(1)}) custom-call(s32[3]{0:T(128)S(1)} %pad_add_fusion.idx, bf16[4,1152,256]{2,1,0:T(8,128)(2,1)S(1)} %get-tuple-element.143.refs_16_.x_all, bf16[4,1152,256]{2,1,0:T(8,128)(2,1)S(1)} %collective-permute-done.28.x_far, ...), custom_call_target="tpu_custom_call" | custom-call | flops 1207959552 | bytes 10485760 | tf_op jit(solution)/shard_map/pallas_call | solution.py:43
  96.1 5.2 %shard_map.208 = (bf16[272,256]{1,0:T(8,128)(2,1)S(1)}, bf16[272,256]{1,0:T(8,128)(2,1)S(1)}, bf16[272,256]{1,0:T(8,128)(2,1)S(1)}, bf16[272,256]{1,0:T(8,128)(2...) custom-call(s32[3]{0:T(128)S(1)} %pad_add_fusion.idx, ...), custom_call_target="tpu_custom_call" | custom-call | flops 1925185536 | bytes 20971520 | tf_op jit(solution)/shard_map/pallas_call | solution.py:43
  101.3 1.2 collective-permute-start.36
  103.7 2.2 %shard_map.209 = (bf16[4,32,1152]{2,1,0:T(8,128)(2,1)S(1)}, bf16[4,32,1152]{2,1,0:T(8,128)(2,1)S(1)}, bf16[2,4,32,1152]{3,2,1,0:T(8,128)(2,1)S(1)}) custom-call(s32[3]{0:T(128)S(1)} %pad_add_fusion.idx, bf16[4,1152,256]{2,1,0:T(8,128)(2,1)S(1)} %get-tuple-element.143.refs_16_.x_all, bf16[4,1152,256]{2,1,0:T(8,128)(2,1)S(1)} %collective-permute-done.28.x_far, ...), custom_call_target="tpu_custom_call" | custom-call | flops 641728512 | bytes 10485760 | tf_op jit(solution)/shard_map/pallas_call | solution.py:43
  105.9 5.0 %collective-permute-done.35 = bf16[2,4,64,1152]{3,2,1,0:T(8,128)(2,1)S(1)} collective-permute-done((bf16[2,4,64,1152]{3,2,1,0:T(8,128)(2,1)S(1)}, bf16[2,4,64,1152]{3,2,1,0:T(8,128)(2,1)S(1)}, u32[]{:S(2)}, u32[]{:S(2)}) %collective-permute-start.35) | collective-permute-done | bytes 1179680 | tf_op jit(solution)/shard_map/ppermute | solution.py:566
  112.8 1.5 collective-permute-start.42
  116.0 3.8 %shard_map.210 = (bf16[4,64,1152]{2,1,0:T(8,128)(2,1)S(1)}, bf16[4,64,1152]{2,1,0:T(8,128)(2,1)S(1)}, bf16[2,4,64,1152]{3,2,1,0:T(8,128)(2,1)S(1)}) custom-call(s32[3]{0:T(128)S(1)} %pad_add_fusion.idx, bf16[4,1152,256]{2,1,0:T(8,128)(2,1)S(1)} %get-tuple-element.143.refs_16_.x_all, bf16[4,1152,256]{2,1,0:T(8,128)(2,1)S(1)} %collective-permute-done.28.x_far, ...), custom_call_target="tpu_custom_call" | custom-call | flops 1283457024 | bytes 10485760 | tf_op jit(solution)/shard_map/pallas_call | solution.py:43
  119.8 4.1 %collective-permute-done.41.refs_2_ = bf16[272,256]{1,0:T(8,128)(2,1)S(1)} collective-permute-done((bf16[272,256]{1,0:T(8,128)(2,1)S(1)}, bf16[272,256]{1,0:T(8,128)(2,1)S(1)}, u32[]{:S(2)}, u32[]{:S(2)}) %collective-permute-start.41) | collective-permute-done | bytes 139296 | tf_op jit(solution)/shard_map/ppermute | solution.py:568
  123.9 3.0 %collective-permute-done.40.refs_1_ = bf16[272,256]{1,0:T(8,128)(2,1)S(1)} collective-permute-done((bf16[272,256]{1,0:T(8,128)(2,1)S(1)}, bf16[272,256]{1,0:T(8,128)(2,1)S(1)}, u32[]{:S(2)}, u32[]{:S(2)}) %collective-permute-start.40) | collective-permute-done | bytes 139296 | tf_op jit(solution)/shard_map/ppermute | solution.py:568
  128.7 2.3 %collective-permute-start.45 = (bf16[64,1152]{1,0:T(8,128)(2,1)S(1)}, bf16[64,1152]{1,0:T(8,128)(2,1)S(1)}, u32[]{:S(2)}, u32[]{:S(2)}) collective-permute-start(bf16[64,1152]{1,0:T(8,128)(2,1)S(1)} %get-tuple-element.227), channel_id=1, source_target_pairs={{0,1},{1,2},{2,3},{3,0},{4,5},{5,6},{6,7},{7,4},{8,9},{9,10},{10,1... | collective-permute-start | bytes 442376 | tf_op jit(solution)/shard_map/ppermute | solution.py:568
  132.2 1.6 shard_map.211
  133.9 9.0 %collective-permute-done.46 = bf16[64,1152]{1,0:T(8,128)(2,1)S(1)} collective-permute-done((bf16[64,1152]{1,0:T(8,128)(2,1)S(1)}, bf16[64,1152]{1,0:T(8,128)(2,1)S(1)}, u32[]{:S(2)}, u32[]{:S(2)}) %collective-permute-start.46) | collective-permute-done | bytes 147488 | tf_op jit(solution)/shard_map/ppermute | solution.py:568
  142.8 2.1 %collective-permute-done.47 = bf16[64,1152]{1,0:T(8,128)(2,1)S(1)} collective-permute-done((bf16[64,1152]{1,0:T(8,128)(2,1)S(1)}, bf16[64,1152]{1,0:T(8,128)(2,1)S(1)}, u32[]{:S(2)}, u32[]{:S(2)}) %collective-permute-start.47) | collective-permute-done | bytes 147488 | tf_op jit(solution)/shard_map/ppermute | solution.py:568
  148.2 2.2 %collective-permute-start.50 = (bf16[32,1152]{1,0:T(8,128)(2,1)S(1)}, bf16[32,1152]{1,0:T(8,128)(2,1)S(1)}, u32[]{:S(2)}, u32[]{:S(2)}) collective-permute-start(bf16[32,1152]{1,0:T(8,128)(2,1)S(1)} %get-tuple-element.230), channel_id=1, source_target_pairs={{0,1},{1,2},{2,3},{3,0},{4,5},{5,6},{6,7},{7,4},{8,9},{9,10},{10,1... | collective-permute-start | bytes 221192 | tf_op jit(solution)/shard_map/ppermute | solution.py:568
  151.8 4.8 %collective-permute-done.51 = bf16[32,1152]{1,0:T(8,128)(2,1)S(1)} collective-permute-done((bf16[32,1152]{1,0:T(8,128)(2,1)S(1)}, bf16[32,1152]{1,0:T(8,128)(2,1)S(1)}, u32[]{:S(2)}, u32[]{:S(2)}) %collective-permute-start.51) | collective-permute-done | bytes 73760 | tf_op jit(solution)/shard_map/ppermute | solution.py:568
  159.0 1.7 collective-permute-start.56
  162.5 2.6 %collective-permute-done.54.refs_1_ = bf16[32,1152]{1,0:T(8,128)(2,1)S(1)} collective-permute-done((bf16[32,1152]{1,0:T(8,128)(2,1)S(1)}, bf16[32,1152]{1,0:T(8,128)(2,1)S(1)}, u32[]{:S(2)}, u32[]{:S(2)}) %collective-permute-start.54) | collective-permute-done | bytes 73760 | tf_op jit(solution)/shard_map/ppermute | solution.py:566
  165.1 5.6 %collective-permute-done.56 = bf16[64,1152]{1,0:T(8,128)(2,1)S(1)} collective-permute-done((bf16[64,1152]{1,0:T(8,128)(2,1)S(1)}, bf16[64,1152]{1,0:T(8,128)(2,1)S(1)}, u32[]{:S(2)}, u32[]{:S(2)}) %collective-permute-start.56) | collective-permute-done | bytes 147488 | tf_op jit(solution)/shard_map/ppermute | solution.py:568
  170.7 3.7 %collective-permute-done.57 = bf16[64,1152]{1,0:T(8,128)(2,1)S(1)} collective-permute-done((bf16[64,1152]{1,0:T(8,128)(2,1)S(1)}, bf16[64,1152]{1,0:T(8,128)(2,1)S(1)}, u32[]{:S(2)}, u32[]{:S(2)}) %collective-permute-start.57) | collective-permute-done | bytes 147488 | tf_op jit(solution)/shard_map/ppermute | solution.py:568
  176.8 2.9 %collective-permute-done.59.refs_2_ = bf16[2,32,1152]{2,1,0:T(8,128)(2,1)S(1)} collective-permute-done((bf16[2,32,1152]{2,1,0:T(8,128)(2,1)S(1)}, bf16[2,32,1152]{2,1,0:T(8,128)(2,1)S(1)}, u32[]{:S(2)}, u32[]{:S(2)}) %collective-permute-start.59) | collective-permute-done | bytes 147488 | tf_op jit(solution)/shard_map/ppermute | solution.py:566
  179.7 1.5 collective-permute-done.58.refs_1_
  182.3 4.9 %collective-permute-done.61.refs_2_ = bf16[2,64,1152]{2,1,0:T(8,128)(2,1)S(1)} collective-permute-done((bf16[2,64,1152]{2,1,0:T(8,128)(2,1)S(1)}, bf16[2,64,1152]{2,1,0:T(8,128)(2,1)S(1)}, u32[]{:S(2)}, u32[]{:S(2)}) %collective-permute-start.61) | collective-permute-done | bytes 294944 | tf_op jit(solution)/shard_map/ppermute | solution.py:566
  189.1 2.5 %shard_map.212 = (f32[1040,256]{1,0:T(8,128)}, f32[256,1024]{1,0:T(8,128)}, f32[3,256]{1,0:T(4,128)S(1)}, f32[1,1]{1,0:T(1,128)}) custom-call(s32[3]{0:T(128)S(1)} %pad_add_fusion.idx, bf16[64,1152]{1,0:T(8,128)(2,1)S(1)} %fusion.10.refs_0_, bf16[64,1152]{1,0:T(8,128)(2,1)S(1)} %collective-permute-done.49.refs_1_, ...), custom_call_target="tpu_custom_call" | custom-call | bytes 4194304 | tf_op jit(solution)/shard_map/pallas_call | solution.py:43
  192.1 1.8 shard_map.213
  194.0 2.7 %shard_map.214 = (f32[3,260,1040]{2,1,0:T(8,128)}, f32[3,260]{1,0:T(4,128)}) custom-call(s32[3]{0:T(128)S(1)} %pad_add_fusion.idx, bf16[64,1152]{1,0:T(8,128)(2,1)S(1)} %fusion.7.refs_0_, bf16[64,1152]{1,0:T(8,128)(2,1)S(1)} %collective-permute-done.58.refs_1_, ...), custom_call_target="tpu_custom_call", output_to_operand_aliasing={{0}: (5, {})} | custom-call | bytes 4194304 | tf_op jit(solution)/shard_map/pallas_call | solution.py:43
  (147 shorter events, 41.3 us)
Async XLA Ops:
  5.4 7.4 %collective-permute-start.2 = (bf16[32,1040]{1,0:T(8,128)(2,1)S(1)}, bf16[32,1040]{1,0:T(8,128)(2,1)S(1)}, u32[]{:S(2)}, u32[]{:S(2)}) collective-permute-start(bf16[32,1040]{1,0:T(8,128)(2,1)S(1)} %shard_map.202), channel_id=1, source_target_pairs={{0,3},{1,0},{2,1},{3,2},{4,7},{5,4},{6,5},{7,6},{8,11},{9,8},{10,9... | collective-permute-start | bytes 199688 | tf_op jit(solution)/shard_map/ppermute | solution.py:568
  12.9 21.0 %collective-permute-start.3 = (bf16[3,32,1040]{2,1,0:T(8,128)(2,1)S(1)}, bf16[3,32,1040]{2,1,0:T(8,128)(2,1)S(1)}, u32[]{:S(2)}, u32[]{:S(2)}) collective-permute-start(bf16[3,32,1040]{2,1,0:T(8,128)(2,1)S(1)} %pad_maximum_fusion.7.refs_9_.refs_10_), channel_id=1, source_target_pairs={{0,8},{4,20},{8,0},{12,28},{16,24},{20,4},{24,16},{28,12},{1,9},{5... | collective-permute-start | bytes 599048 | tf_op jit(solution)/shard_map/ppermute | solution.py:566
  14.0 19.8 %collective-permute-start.4 = (bf16[3,32,1040]{2,1,0:T(8,128)(2,1)S(1)}, bf16[3,32,1040]{2,1,0:T(8,128)(2,1)S(1)}, u32[]{:S(2)}, u32[]{:S(2)}) collective-permute-start(bf16[3,32,1040]{2,1,0:T(8,128)(2,1)S(1)} %pad_maximum_fusion.7.refs_9_.refs_10_), channel_id=1, source_target_pairs={{0,16},{4,12},{8,24},{12,4},{16,0},{20,28},{24,8},{28,20},{1,17},{... | collective-permute-start | bytes 599048 | tf_op jit(solution)/shard_map/ppermute | solution.py:566
  15.2 5.3 %collective-permute-start.5 = (bf16[80,1040]{1,0:T(8,128)(2,1)S(1)}, bf16[80,1040]{1,0:T(8,128)(2,1)S(1)}, u32[]{:S(2)}, u32[]{:S(2)}) collective-permute-start(bf16[80,1040]{1,0:T(8,128)(2,1)S(1)} %shard_map.203.refs_5_.refs_6_), channel_id=1, source_target_pairs={{0,1},{1,2},{2,3},{3,0},{4,5},{5,6},{6,7},{7,4},{8,9},{9,10},{10,1... | collective-permute-start | bytes 499208 | tf_op jit(solution)/shard_map/ppermute | solution.py:568
  15.2 14.6 %collective-permute-start.6 = (bf16[80,1040]{1,0:T(8,128)(2,1)S(1)}, bf16[80,1040]{1,0:T(8,128)(2,1)S(1)}, u32[]{:S(2)}, u32[]{:S(2)}) collective-permute-start(bf16[80,1040]{1,0:T(8,128)(2,1)S(1)} %shard_map.203.refs_5_.refs_6_), channel_id=1, source_target_pairs={{0,2},{1,3},{2,0},{3,1},{4,6},{5,7},{6,4},{7,5},{8,10},{9,11},{10,... | collective-permute-start | bytes 499208 | tf_op jit(solution)/shard_map/ppermute | solution.py:568
  16.9 16.9 %collective-permute-start.7 = (bf16[80,1040]{1,0:T(8,128)(2,1)S(1)}, bf16[80,1040]{1,0:T(8,128)(2,1)S(1)}, u32[]{:S(2)}, u32[]{:S(2)}) collective-permute-start(bf16[80,1040]{1,0:T(8,128)(2,1)S(1)} %shard_map.203.refs_5_.refs_6_), channel_id=1, source_target_pairs={{0,3},{1,0},{2,1},{3,2},{4,7},{5,4},{6,5},{7,6},{8,11},{9,8},{10,9... | collective-permute-start | bytes 499208 | tf_op jit(solution)/shard_map/ppermute | solution.py:568
  34.0 14.8 %collective-permute-start.10 = (bf16[3,64,1040]{2,1,0:T(8,128)(2,1)S(1)}, bf16[3,64,1040]{2,1,0:T(8,128)(2,1)S(1)}, u32[]{:S(2)}, u32[]{:S(2)}) collective-permute-start(bf16[3,64,1040]{2,1,0:T(8,128)(2,1)S(1)} %pad_maximum_fusion.2.refs_17_.refs_18_), channel_id=1, source_target_pairs={{0,16},{4,12},{8,24},{12,4},{16,0},{20,28},{24,8},{28,20},{1,17},{... | collective-permute-start | bytes 1198088 | tf_op jit(solution)/shard_map/ppermute | solution.py:566
  34.3 14.5 %collective-permute-start.9 = (bf16[3,64,1040]{2,1,0:T(8,128)(2,1)S(1)}, bf16[3,64,1040]{2,1,0:T(8,128)(2,1)S(1)}, u32[]{:S(2)}, u32[]{:S(2)}) collective-permute-start(bf16[3,64,1040]{2,1,0:T(8,128)(2,1)S(1)} %pad_maximum_fusion.2.refs_17_.refs_18_), channel_id=1, source_target_pairs={{0,8},{4,20},{8,0},{12,28},{16,24},{20,4},{24,16},{28,12},{1,9},{5... | collective-permute-start | bytes 1198088 | tf_op jit(solution)/shard_map/ppermute | solution.py:566
  34.7 14.1 %collective-permute-start.8 = (bf16[3,32,1040]{2,1,0:T(8,128)(2,1)S(1)}, bf16[3,32,1040]{2,1,0:T(8,128)(2,1)S(1)}, u32[]{:S(2)}, u32[]{:S(2)}) collective-permute-start(bf16[3,32,1040]{2,1,0:T(8,128)(2,1)S(1)} %collective-permute-done.3.refs_10_.refs_11_), channel_id=1, source_target_pairs={{0,16},{4,12},{8,24},{12,4},{16,0},{20,28},{24,8},{28,20},{1,17},{... | collective-permute-start | bytes 599048 | tf_op jit(solution)/shard_map/ppermute | solution.py:566
  35.7 10.7 %collective-permute-start.12 = (bf16[64,1040]{1,0:T(8,128)(2,1)S(1)}, bf16[64,1040]{1,0:T(8,128)(2,1)S(1)}, u32[]{:S(2)}, u32[]{:S(2)}) collective-permute-start(bf16[64,1040]{1,0:T(8,128)(2,1)S(1)} %get-tuple-element.122), channel_id=1, source_target_pairs={{0,2},{1,3},{2,0},{3,1},{4,6},{5,7},{6,4},{7,5},{8,10},{9,11},{10,... | collective-permute-start | bytes 399368 | tf_op jit(solution)/shard_map/ppermute | solution.py:568
  39.0 9.8 %collective-permute-start.13 = (bf16[64,1040]{1,0:T(8,128)(2,1)S(1)}, bf16[64,1040]{1,0:T(8,128)(2,1)S(1)}, u32[]{:S(2)}, u32[]{:S(2)}) collective-permute-start(bf16[64,1040]{1,0:T(8,128)(2,1)S(1)} %get-tuple-element.122), channel_id=1, source_target_pairs={{0,3},{1,0},{2,1},{3,2},{4,7},{5,4},{6,5},{7,6},{8,11},{9,8},{10,9... | collective-permute-start | bytes 399368 | tf_op jit(solution)/shard_map/ppermute | solution.py:568
  48.8 4.7 %collective-permute-start.17 = (bf16[263,256]{1,0:T(8,128)(2,1)S(1)}, bf16[263,256]{1,0:T(8,128)(2,1)S(1)}, u32[]{:S(2)}, u32[]{:S(2)}) collective-permute-start(bf16[263,256]{1,0:T(8,128)(2,1)S(1)} %get-tuple-element.130), channel_id=1, source_target_pairs={{0,1},{1,2},{2,3},{3,0},{4,5},{5,6},{6,7},{7,4},{8,9},{9,10},{10,1... | collective-permute-start | bytes 403976 | tf_op jit(solution)/shard_map/ppermute | solution.py:568
  49.0 17.7 %collective-permute-start.15 = (bf16[3,64,1152]{2,1,0:T(8,128)(2,1)S(1)}, bf16[3,64,1152]{2,1,0:T(8,128)(2,1)S(1)}, u32[]{:S(2)}, u32[]{:S(2)}) collective-permute-start(bf16[3,64,1152]{2,1,0:T(8,128)(2,1)S(1)} %pad_maximum_fusion.3.refs_8_), channel_id=1, source_target_pairs={{0,8},{4,20},{8,0},{12,28},{16,24},{20,4},{24,16},{28,12},{1,9},{5... | collective-permute-start | bytes 1327112 | tf_op jit(solution)/shard_map/ppermute | solution.py:566
  50.2 17.0 %collective-permute-start.16 = (bf16[3,64,1152]{2,1,0:T(8,128)(2,1)S(1)}, bf16[3,64,1152]{2,1,0:T(8,128)(2,1)S(1)}, u32[]{:S(2)}, u32[]{:S(2)}) collective-permute-start(bf16[3,64,1152]{2,1,0:T(8,128)(2,1)S(1)} %pad_maximum_fusion.3.refs_8_), channel_id=1, source_target_pairs={{0,16},{4,12},{8,24},{12,4},{16,0},{20,28},{24,8},{28,20},{1,17},{... | collective-permute-start | bytes 1327112 | tf_op jit(solution)/shard_map/ppermute | solution.py:566
  51.3 15.3 %collective-permute-start.14 = (bf16[3,64,1040]{2,1,0:T(8,128)(2,1)S(1)}, bf16[3,64,1040]{2,1,0:T(8,128)(2,1)S(1)}, u32[]{:S(2)}, u32[]{:S(2)}) collective-permute-start(bf16[3,64,1040]{2,1,0:T(8,128)(2,1)S(1)} %collective-permute-done.9.refs_18_.refs_19_), channel_id=1, source_target_pairs={{0,16},{4,12},{8,24},{12,4},{16,0},{20,28},{24,8},{28,20},{1,17},{... | collective-permute-start | bytes 1198088 | tf_op jit(solution)/shard_map/ppermute | solution.py:566
  51.7 4.9 %collective-permute-start.18 = (bf16[263,256]{1,0:T(8,128)(2,1)S(1)}, bf16[263,256]{1,0:T(8,128)(2,1)S(1)}, u32[]{:S(2)}, u32[]{:S(2)}) collective-permute-start(bf16[263,256]{1,0:T(8,128)(2,1)S(1)} %get-tuple-element.132), channel_id=1, source_target_pairs={{0,2},{1,3},{2,0},{3,1},{4,6},{5,7},{6,4},{7,5},{8,10},{9,11},{10,... | collective-permute-start | bytes 403976 | tf_op jit(solution)/shard_map/ppermute | solution.py:568
  53.5 9.9 %collective-permute-start.19 = (bf16[263,256]{1,0:T(8,128)(2,1)S(1)}, bf16[263,256]{1,0:T(8,128)(2,1)S(1)}, u32[]{:S(2)}, u32[]{:S(2)}) collective-permute-start(bf16[263,256]{1,0:T(8,128)(2,1)S(1)} %get-tuple-element.134), channel_id=1, source_target_pairs={{0,3},{1,0},{2,1},{3,2},{4,7},{5,4},{6,5},{7,6},{8,11},{9,8},{10,9... | collective-permute-start | bytes 403976 | tf_op jit(solution)/shard_map/ppermute | solution.py:568
  56.5 10.7 %collective-permute-start.20 = (bf16[3,32,1040]{2,1,0:T(8,128)(2,1)S(1)}, bf16[3,32,1040]{2,1,0:T(8,128)(2,1)S(1)}, u32[]{:S(2)}, u32[]{:S(2)}) collective-permute-start(bf16[3,32,1040]{2,1,0:T(8,128)(2,1)S(1)} %pad_maximum_fusion.7.refs_9_.refs_10_), channel_id=1, source_target_pairs={{0,4},{4,0},{8,12},{12,8},{16,20},{20,16},{24,28},{28,24},{1,5},{5... | collective-permute-start | bytes 599048 | tf_op jit(solution)/shard_map/ppermute | solution.py:566
  74.9 17.4 %collective-permute-start.28 = (bf16[4,1152,256]{2,1,0:T(8,128)(2,1)S(1)}, bf16[4,1152,256]{2,1,0:T(8,128)(2,1)S(1)}, u32[]{:S(2)}, u32[]{:S(2)}) collective-permute-start(bf16[4,1152,256]{2,1,0:T(8,128)(2,1)S(1)} %get-tuple-element.143.refs_16_.x_all), channel_id=1, source_target_pairs={{0,4},{4,0},{8,12},{12,8},{16,20},{20,16},{24,28},{28,24},{1,5},{5... | collective-permute-start | bytes 7077896 | tf_op jit(solution)/shard_map/ppermute | solution.py:566
  75.1 7.4 %collective-permute-start.29 = (bf16[3,64,1152]{2,1,0:T(8,128)(2,1)S(1)}, bf16[3,64,1152]{2,1,0:T(8,128)(2,1)S(1)}, u32[]{:S(2)}, u32[]{:S(2)}) collective-permute-start(bf16[3,64,1152]{2,1,0:T(8,128)(2,1)S(1)} %collective-permute-done.15.refs_9_), channel_id=1, source_target_pairs={{0,16},{4,12},{8,24},{12,4},{16,0},{20,28},{24,8},{28,20},{1,17},{... | collective-permute-start | bytes 1327112 | tf_op jit(solution)/shard_map/ppermute | solution.py:566
  76.1 7.6 %collective-permute-start.30 = (bf16[3,64,1152]{2,1,0:T(8,128)(2,1)S(1)}, bf16[3,64,1152]{2,1,0:T(8,128)(2,1)S(1)}, u32[]{:S(2)}, u32[]{:S(2)}) collective-permute-start(bf16[3,64,1152]{2,1,0:T(8,128)(2,1)S(1)} %pad_maximum_fusion.3.refs_8_), channel_id=1, source_target_pairs={{0,4},{4,0},{8,12},{12,8},{16,20},{20,16},{24,28},{28,24},{1,5},{5... | collective-permute-start | bytes 1327112 | tf_op jit(solution)/shard_map/ppermute | solution.py:566
  76.2 7.5 %collective-permute-start.31 = (bf16[3,64,1152]{2,1,0:T(8,128)(2,1)S(1)}, bf16[3,64,1152]{2,1,0:T(8,128)(2,1)S(1)}, u32[]{:S(2)}, u32[]{:S(2)}) collective-permute-start(bf16[3,64,1152]{2,1,0:T(8,128)(2,1)S(1)} %collective-permute-done.15.refs_9_), channel_id=1, source_target_pairs={{0,4},{4,0},{8,12},{12,8},{16,20},{20,16},{24,28},{28,24},{1,5},{5... | collective-permute-start | bytes 1327112 | tf_op jit(solution)/shard_map/ppermute | solution.py:566
  76.6 7.1 %collective-permute-start.32 = (bf16[3,64,1152]{2,1,0:T(8,128)(2,1)S(1)}, bf16[3,64,1152]{2,1,0:T(8,128)(2,1)S(1)}, u32[]{:S(2)}, u32[]{:S(2)}) collective-permute-start(bf16[3,64,1152]{2,1,0:T(8,128)(2,1)S(1)} %collective-permute-done.16.refs_10_), channel_id=1, source_target_pairs={{0,4},{4,0},{8,12},{12,8},{16,20},{20,16},{24,28},{28,24},{1,5},{5... | collective-permute-start | bytes 1327112 | tf_op jit(solution)/shard_map/ppermute | solution.py:566
  95.5 15.4 %collective-permute-start.35 = (bf16[2,4,64,1152]{3,2,1,0:T(8,128)(2,1)S(1)}, bf16[2,4,64,1152]{3,2,1,0:T(8,128)(2,1)S(1)}, u32[]{:S(2)}, u32[]{:S(2)}) collective-permute-start(bf16[2,4,64,1152]{3,2,1,0:T(8,128)(2,1)S(1)} %get-tuple-element.151), channel_id=1, source_target_pairs={{0,8},{4,20},{8,0},{12,28},{16,24},{20,4},{24,16},{28,12},{1,9},{5... | collective-permute-start | bytes 3538952 | tf_op jit(solution)/shard_map/ppermute | solution.py:566
  102.5 12.6 %collective-permute-start.39 = (bf16[2,528,256]{2,1,0:T(8,128)(2,1)S(1)}, bf16[2,528,256]{2,1,0:T(8,128)(2,1)S(1)}, u32[]{:S(2)}, u32[]{:S(2)}) collective-permute-start(bf16[2,528,256]{2,1,0:T(8,128)(2,1)S(1)} %get-tuple-element.164), channel_id=1, source_target_pairs={{0,4},{4,0},{8,12},{12,8},{16,20},{20,16},{24,28},{28,24},{1,5},{5... | collective-permute-start | bytes 1622024 | tf_op jit(solution)/shard_map/ppermute | solution.py:566
  111.1 15.8 %collective-permute-start.37 = (bf16[4,64,1152]{2,1,0:T(8,128)(2,1)S(1)}, bf16[4,64,1152]{2,1,0:T(8,128)(2,1)S(1)}, u32[]{:S(2)}, u32[]{:S(2)}) collective-permute-start(bf16[4,64,1152]{2,1,0:T(8,128)(2,1)S(1)} %fusion.2), channel_id=1, source_target_pairs={{0,16},{4,12},{8,24},{12,4},{16,0},{20,28},{24,8},{28,20},{1,17},{... | collective-permute-start | bytes 1769480 | tf_op jit(solution)/shard_map/ppermute | solution.py:566
  112.2 14.7 %collective-permute-start.38 = (bf16[2,4,32,1152]{3,2,1,0:T(8,128)(2,1)S(1)}, bf16[2,4,32,1152]{3,2,1,0:T(8,128)(2,1)S(1)}, u32[]{:S(2)}, u32[]{:S(2)}) collective-permute-start(bf16[2,4,32,1152]{3,2,1,0:T(8,128)(2,1)S(1)} %get-tuple-element.162), channel_id=1, source_target_pairs={{0,8},{4,20},{8,0},{12,28},{16,24},{20,4},{24,16},{28,12},{1,9},{5... | collective-permute-start | bytes 1769480 | tf_op jit(solution)/shard_map/ppermute | solution.py:566
  112.8 7.0 %collective-permute-start.42 = (bf16[272,256]{1,0:T(8,128)(2,1)S(1)}, bf16[272,256]{1,0:T(8,128)(2,1)S(1)}, u32[]{:S(2)}, u32[]{:S(2)}) collective-permute-start(bf16[272,256]{1,0:T(8,128)(2,1)S(1)} %get-tuple-element.172), channel_id=1, source_target_pairs={{0,3},{1,0},{2,1},{3,2},{4,7},{5,4},{6,5},{7,6},{8,11},{9,8},{10,9... | collective-permute-start | bytes 417800 | tf_op jit(solution)/shard_map/ppermute | solution.py:568
  114.2 9.7 %collective-permute-start.41 = (bf16[272,256]{1,0:T(8,128)(2,1)S(1)}, bf16[272,256]{1,0:T(8,128)(2,1)S(1)}, u32[]{:S(2)}, u32[]{:S(2)}) collective-permute-start(bf16[272,256]{1,0:T(8,128)(2,1)S(1)} %get-tuple-element.170), channel_id=1, source_target_pairs={{0,2},{1,3},{2,0},{3,1},{4,6},{5,7},{6,4},{7,5},{8,10},{9,11},{10,... | collective-permute-start | bytes 417800 | tf_op jit(solution)/shard_map/ppermute | solution.py:568
  115.1 11.8 %collective-permute-start.40 = (bf16[272,256]{1,0:T(8,128)(2,1)S(1)}, bf16[272,256]{1,0:T(8,128)(2,1)S(1)}, u32[]{:S(2)}, u32[]{:S(2)}) collective-permute-start(bf16[272,256]{1,0:T(8,128)(2,1)S(1)} %get-tuple-element.168), channel_id=1, source_target_pairs={{0,1},{1,2},{2,3},{3,0},{4,5},{5,6},{6,7},{7,4},{8,9},{9,10},{10,1... | collective-permute-start | bytes 417800 | tf_op jit(solution)/shard_map/ppermute | solution.py:568
  127.0 17.9 %collective-permute-start.43 = (bf16[4,32,1152]{2,1,0:T(8,128)(2,1)S(1)}, bf16[4,32,1152]{2,1,0:T(8,128)(2,1)S(1)}, u32[]{:S(2)}, u32[]{:S(2)}) collective-permute-start(bf16[4,32,1152]{2,1,0:T(8,128)(2,1)S(1)} %fusion.5), channel_id=1, source_target_pairs={{0,16},{4,12},{8,24},{12,4},{16,0},{20,28},{24,8},{28,20},{1,17},{... | collective-permute-start | bytes 884744 | tf_op jit(solution)/shard_map/ppermute | solution.py:566
  127.4 18.2 %collective-permute-start.44 = (bf16[2,4,64,1152]{3,2,1,0:T(8,128)(2,1)S(1)}, bf16[2,4,64,1152]{3,2,1,0:T(8,128)(2,1)S(1)}, u32[]{:S(2)}, u32[]{:S(2)}) collective-permute-start(bf16[2,4,64,1152]{3,2,1,0:T(8,128)(2,1)S(1)} %get-tuple-element.176), channel_id=1, source_target_pairs={{0,8},{4,20},{8,0},{12,28},{16,24},{20,4},{24,16},{28,12},{1,9},{5... | collective-permute-start | bytes 3538952 | tf_op jit(solution)/shard_map/ppermute | solution.py:566
  128.7 5.1 %collective-permute-start.45 = (bf16[64,1152]{1,0:T(8,128)(2,1)S(1)}, bf16[64,1152]{1,0:T(8,128)(2,1)S(1)}, u32[]{:S(2)}, u32[]{:S(2)}) collective-permute-start(bf16[64,1152]{1,0:T(8,128)(2,1)S(1)} %get-tuple-element.227), channel_id=1, source_target_pairs={{0,1},{1,2},{2,3},{3,0},{4,5},{5,6},{6,7},{7,4},{8,9},{9,10},{10,1... | collective-permute-start | bytes 442376 | tf_op jit(solution)/shard_map/ppermute | solution.py:568
  131.0 11.8 %collective-permute-start.46 = (bf16[64,1152]{1,0:T(8,128)(2,1)S(1)}, bf16[64,1152]{1,0:T(8,128)(2,1)S(1)}, u32[]{:S(2)}, u32[]{:S(2)}) collective-permute-start(bf16[64,1152]{1,0:T(8,128)(2,1)S(1)} %get-tuple-element.226), channel_id=1, source_target_pairs={{0,2},{1,3},{2,0},{3,1},{4,6},{5,7},{6,4},{7,5},{8,10},{9,11},{10,... | collective-permute-start | bytes 442376 | tf_op jit(solution)/shard_map/ppermute | solution.py:568
  131.7 13.1 %collective-permute-start.47 = (bf16[64,1152]{1,0:T(8,128)(2,1)S(1)}, bf16[64,1152]{1,0:T(8,128)(2,1)S(1)}, u32[]{:S(2)}, u32[]{:S(2)}) collective-permute-start(bf16[64,1152]{1,0:T(8,128)(2,1)S(1)} %get-tuple-element.225), channel_id=1, source_target_pairs={{0,3},{1,0},{2,1},{3,2},{4,7},{5,4},{6,5},{7,6},{8,11},{9,8},{10,9... | collective-permute-start | bytes 442376 | tf_op jit(solution)/shard_map/ppermute | solution.py:568
  145.8 11.9 %collective-permute-start.48 = (bf16[4,64,1152]{2,1,0:T(8,128)(2,1)S(1)}, bf16[4,64,1152]{2,1,0:T(8,128)(2,1)S(1)}, u32[]{:S(2)}, u32[]{:S(2)}) collective-permute-start(bf16[4,64,1152]{2,1,0:T(8,128)(2,1)S(1)} %fusion.1), channel_id=1, source_target_pairs={{0,16},{4,12},{8,24},{12,4},{16,0},{20,28},{24,8},{28,20},{1,17},{... | collective-permute-start | bytes 1769480 | tf_op jit(solution)/shard_map/ppermute | solution.py:566
  147.1 10.6 %collective-permute-start.49 = (bf16[64,1152]{1,0:T(8,128)(2,1)S(1)}, bf16[64,1152]{1,0:T(8,128)(2,1)S(1)}, u32[]{:S(2)}, u32[]{:S(2)}) collective-permute-start(bf16[64,1152]{1,0:T(8,128)(2,1)S(1)} %fusion.10.refs_0_), channel_id=1, source_target_pairs={{0,8},{4,20},{8,0},{12,28},{16,24},{20,4},{24,16},{28,12},{1,9},{5... | collective-permute-start | bytes 442376 | tf_op jit(solution)/shard_map/ppermute | solution.py:566
  150.4 6.2 %collective-permute-start.51 = (bf16[32,1152]{1,0:T(8,128)(2,1)S(1)}, bf16[32,1152]{1,0:T(8,128)(2,1)S(1)}, u32[]{:S(2)}, u32[]{:S(2)}) collective-permute-start(bf16[32,1152]{1,0:T(8,128)(2,1)S(1)} %get-tuple-element.229), channel_id=1, source_target_pairs={{0,2},{1,3},{2,0},{3,1},{4,6},{5,7},{6,4},{7,5},{8,10},{9,11},{10,... | collective-permute-start | bytes 221192 | tf_op jit(solution)/shard_map/ppermute | solution.py:568
  151.6 6.1 %collective-permute-start.52 = (bf16[32,1152]{1,0:T(8,128)(2,1)S(1)}, bf16[32,1152]{1,0:T(8,128)(2,1)S(1)}, u32[]{:S(2)}, u32[]{:S(2)}) collective-permute-start(bf16[32,1152]{1,0:T(8,128)(2,1)S(1)} %get-tuple-element.228), channel_id=1, source_target_pairs={{0,3},{1,0},{2,1},{3,2},{4,7},{5,4},{6,5},{7,6},{8,11},{9,8},{10,9... | collective-permute-start | bytes 221192 | tf_op jit(solution)/shard_map/ppermute | solution.py:568
  158.0 7.1 %collective-permute-start.55 = (bf16[64,1152]{1,0:T(8,128)(2,1)S(1)}, bf16[64,1152]{1,0:T(8,128)(2,1)S(1)}, u32[]{:S(2)}, u32[]{:S(2)}) collective-permute-start(bf16[64,1152]{1,0:T(8,128)(2,1)S(1)} %get-tuple-element.224), channel_id=1, source_target_pairs={{0,1},{1,2},{2,3},{3,0},{4,5},{5,6},{6,7},{7,4},{8,9},{9,10},{10,1... | collective-permute-start | bytes 442376 | tf_op jit(solution)/shard_map/ppermute | solution.py:568
  159.0 11.7 %collective-permute-start.56 = (bf16[64,1152]{1,0:T(8,128)(2,1)S(1)}, bf16[64,1152]{1,0:T(8,128)(2,1)S(1)}, u32[]{:S(2)}, u32[]{:S(2)}) collective-permute-start(bf16[64,1152]{1,0:T(8,128)(2,1)S(1)} %get-tuple-element.223), channel_id=1, source_target_pairs={{0,2},{1,3},{2,0},{3,1},{4,6},{5,7},{6,4},{7,5},{8,10},{9,11},{10,... | collective-permute-start | bytes 442376 | tf_op jit(solution)/shard_map/ppermute | solution.py:568
  160.7 13.7 %collective-permute-start.57 = (bf16[64,1152]{1,0:T(8,128)(2,1)S(1)}, bf16[64,1152]{1,0:T(8,128)(2,1)S(1)}, u32[]{:S(2)}, u32[]{:S(2)}) collective-permute-start(bf16[64,1152]{1,0:T(8,128)(2,1)S(1)} %get-tuple-element.222), channel_id=1, source_target_pairs={{0,3},{1,0},{2,1},{3,2},{4,7},{5,4},{6,5},{7,6},{8,11},{9,8},{10,9... | collective-permute-start | bytes 442376 | tf_op jit(solution)/shard_map/ppermute | solution.py:568
  161.7 12.7 %collective-permute-start.53 = (bf16[2,64,1152]{2,1,0:T(8,128)(2,1)S(1)}, bf16[2,64,1152]{2,1,0:T(8,128)(2,1)S(1)}, u32[]{:S(2)}, u32[]{:S(2)}) collective-permute-start(bf16[2,64,1152]{2,1,0:T(8,128)(2,1)S(1)} %pad_maximum_fusion.4), channel_id=1, source_target_pairs={{0,16},{4,12},{8,24},{12,4},{16,0},{20,28},{24,8},{28,20},{1,17},{... | collective-permute-start | bytes 884744 | tf_op jit(solution)/shard_map/ppermute | solution.py:566
  174.5 6.8 %collective-permute-start.60 = (bf16[4,64,1152]{2,1,0:T(8,128)(2,1)S(1)}, bf16[4,64,1152]{2,1,0:T(8,128)(2,1)S(1)}, u32[]{:S(2)}, u32[]{:S(2)}) collective-permute-start(bf16[4,64,1152]{2,1,0:T(8,128)(2,1)S(1)} %pad_maximum_fusion), channel_id=1, source_target_pairs={{0,4},{4,0},{8,12},{12,8},{16,20},{20,16},{24,28},{28,24},{1,5},{5... | collective-permute-start | bytes 1769480 | tf_op jit(solution)/shard_map/ppermute | solution.py:566
  175.1 4.6 %collective-permute-start.59 = (bf16[2,32,1152]{2,1,0:T(8,128)(2,1)S(1)}, bf16[2,32,1152]{2,1,0:T(8,128)(2,1)S(1)}, u32[]{:S(2)}, u32[]{:S(2)}) collective-permute-start(bf16[2,32,1152]{2,1,0:T(8,128)(2,1)S(1)} %pad_maximum_fusion.8), channel_id=1, source_target_pairs={{0,16},{4,12},{8,24},{12,4},{16,0},{20,28},{24,8},{28,20},{1,17},{... | collective-permute-start | bytes 442376 | tf_op jit(solution)/shard_map/ppermute | solution.py:566
  176.2 5.1 %collective-permute-start.58 = (bf16[64,1152]{1,0:T(8,128)(2,1)S(1)}, bf16[64,1152]{1,0:T(8,128)(2,1)S(1)}, u32[]{:S(2)}, u32[]{:S(2)}) collective-permute-start(bf16[64,1152]{1,0:T(8,128)(2,1)S(1)} %fusion.7.refs_0_), channel_id=1, source_target_pairs={{0,8},{4,20},{8,0},{12,28},{16,24},{20,4},{24,16},{28,12},{1,9},{5... | collective-permute-start | bytes 442376 | tf_op jit(solution)/shard_map/ppermute | solution.py:566
  181.3 5.9 %collective-permute-start.61 = (bf16[2,64,1152]{2,1,0:T(8,128)(2,1)S(1)}, bf16[2,64,1152]{2,1,0:T(8,128)(2,1)S(1)}, u32[]{:S(2)}, u32[]{:S(2)}) collective-permute-start(bf16[2,64,1152]{2,1,0:T(8,128)(2,1)S(1)} %pad_maximum_fusion.5), channel_id=1, source_target_pairs={{0,16},{4,12},{8,24},{12,4},{16,0},{20,28},{24,8},{28,20},{1,17},{... | collective-permute-start | bytes 884744 | tf_op jit(solution)/shard_map/ppermute | solution.py:566
  187.3 6.7 %collective-permute-start.62 = (bf16[4,64,1152]{2,1,0:T(8,128)(2,1)S(1)}, bf16[4,64,1152]{2,1,0:T(8,128)(2,1)S(1)}, u32[]{:S(2)}, u32[]{:S(2)}) collective-permute-start(bf16[4,64,1152]{2,1,0:T(8,128)(2,1)S(1)} %pad_maximum_fusion.1), channel_id=1, source_target_pairs={{0,4},{4,0},{8,12},{12,8},{16,20},{20,16},{24,28},{28,24},{1,5},{5... | collective-permute-start | bytes 1769480 | tf_op jit(solution)/shard_map/ppermute | solution.py:566
  (28 other events, 202.2 us)

commit v3 on v2

--- a/solution.py
+++ b/solution.py
@@ -16,10 +16,12 @@
 HALF = MAIN // 2
 LANES = 128
 REST = 32
-COUNT = 32
+LOSS = 24
+COUNT = 16
 VMEM = pl.BlockSpec(memory_space=pltpu.VMEM)
 SMEM = pl.BlockSpec(memory_space=pltpu.SMEM)
 HBM = pl.BlockSpec(memory_space=pl.ANY)
+FAR = pl.BlockSpec(memory_space=pltpu.HBM)
 NT = (((1,), (1,)), ((), ()))
 TN = (((0,), (0,)), ((), ()))
 NN = (((1,), (0,)), ((), ()))
@@ -108,41 +110,37 @@
     return lax.broadcasted_iota(jnp.int32, shape, 1)
 
 
-def pack_first(idx, weight, out, sems):
-    copies = Copies(sems)
-    wait(copies.start(weight.at[0, rows_at(idx[1] * HALF + idx[2] * SHARE, SHARE), :], out))
-
-
-def pack_cross(idx, weight, bias, out, lines):
+def pack_rest(idx, weight, bias, inputs, vectors, weight1, weight2, ids, days, *refs, blocks):
+    out, own1, tally = refs[:3]
+    chunks, (lines,) = refs[3 : 3 + blocks], refs[3 + blocks :]
     layers, width, depth = weight.shape
+    size = weight2.shape[0]
     left = width - MAIN
+    part = chunks[0].shape[1]
+    full = own1.shape[1]
     own_row = idx[1] * HALF + idx[2] * SHARE
+
     lines[...] = jnp.zeros_like(lines)
     for layer in range(layers):
-        if layer:
-            out[SHARE * (layer - 1) : SHARE * layer, :] = weight[layer, rows_at(own_row, SHARE), :]
-        lines[left * layer : left * (layer + 1), :] = weight[layer, MAIN:width, :].astype(F32)
+        lines[left * layer : left * (layer + 1), 0:depth] = weight[layer, MAIN:width, :].astype(F32)
         at = left * layers + layer
         lines[at : at + 1, 0:width] = bias[layer : layer + 1, :].astype(F32)
-    out[(layers - 1) * SHARE :, :] = lines[...].astype(BF16)
-
-
-def pack_rest(idx, inputs, vectors, weight1, weight2, ids, days, *refs, blocks):
-    out, own1, tally, chunks = refs[0], refs[1], refs[2], refs[3:]
-    depth, size = weight1.shape
-    width = inputs.shape[0]
-    hidden = weight2.shape[1]
-    part = chunks[0].shape[1]
-    own_row = idx[1] * HALF + idx[2] * SHARE
+    rest = [lines[:, at : at + part].astype(BF16) for at in range(0, lines.shape[1], part)]
+
     own1[:, 0:depth] = weight1[...].T
-    own1[:, depth:] = jnp.zeros((size, own1.shape[1] - depth), BF16)
-    out[0:SHARE, :] = own1[rows_at(own_row, SHARE), 0:depth]
-    out[SHARE : 2 * SHARE, 0:hidden] = weight2[rows_at(own_row, SHARE), :]
-    out[SHARE : 2 * SHARE, hidden:] = jnp.zeros((SHARE, depth - hidden), BF16)
+    own1[:, depth:] = jnp.zeros((size, full - depth), BF16)
+    out[0:SHARE, :] = own1[rows_at(own_row, SHARE), :]
+    out[SHARE:, 0 : weight2.shape[1]] = weight2[rows_at(own_row, SHARE), :]
+    out[SHARE:, weight2.shape[1] :] = jnp.zeros((SHARE, full - weight2.shape[1]), BF16)
+
+    first = 16 * len(rest)
     for turn in range(blocks):
         lanes = pl.ds(pl.multiple_of(block_ahead(idx, turn, blocks) * part, LANES), part)
-        chunks[turn][0:width, :] = inputs[:, lanes]
-        chunks[turn][width : width + 3, :] = vectors[...]
+        for at, value in enumerate(rest):
+            chunks[turn][16 * at : 16 * (at + 1), :] = value
+        chunks[turn][first : first + width, :] = inputs[:, lanes]
+        chunks[turn][first + width : first + width + 3, :] = vectors[...]
+
     fields, tokens = ids.shape
     bucket = lax.broadcasted_iota(jnp.int32, (BUCKETS, tokens), 0)
     lane = lane_of((BUCKETS, LANES))
@@ -151,26 +149,39 @@
         line = ids[field : field + 1, :] if field < fields else days[...]
         hits = jnp.sum((bucket == line).astype(F32), axis=1, keepdims=True)
         high = jnp.floor(hits * (1.0 / 256.0))
-        tile = jnp.where(lane == field, high, tile)
-        tile = jnp.where(lane == COUNT + field, hits - 256.0 * high, tile)
-    tally[0:BUCKETS, :] = tile.astype(BF16)
-    tally[BUCKETS:, :] = jnp.zeros((tally.shape[0] - BUCKETS, LANES), BF16)
+        tile = jnp.where(lane == COUNT + field, high, tile)
+        tile = jnp.where(lane == COUNT + fields + 1 + field, hits - 256.0 * high, tile)
+    half = BUCKETS // 2
+    tile = tile[0:half, :] + pltpu.roll(tile[half:, :], 2 * (fields + 1), 1)
+    tally[0:half, :] = tile.astype(BF16)
+    tally[half:, :] = jnp.zeros((tally.shape[0] - half, LANES), BF16)
+
+
+def cross_eight(refs):
+    near, last, near_far, last_far = refs
+    return [near.at[at] for at in range(3)] + [last] + [near_far.at[at] for at in range(3)] + [last_far]
 
 
 def place_cross(idx, weight, own, slices, blocks, layer, pad):
     weight[layer, rows_at(idx[0] * pad, MAIN), :] = own[layer, 0:MAIN, :]
-    pieces = slices[8:] if layer else slices[:8]
-    at = SHARE * (layer - 1) if layer else 0
+    at = SHARE * layer
     for turn in range(1, blocks):
         base = block_of(idx, turn, blocks) * pad
-        for offset, piece in zip(places(idx), pieces):
-            weight[layer, rows_at(base + offset, SHARE), :] = piece[turn - 1, at : at + SHARE, :]
-
-
-def place_rest(idx, weight, turned, lines, tail, blocks, layers, left, pad):
+        for offset, piece in zip(places(idx), slices):
+            weight[layer, rows_at(base + offset, SHARE), :] = piece[turn - 1, at : at + SHARE, 0 : weight.shape[2]]
+
+
+def place_rest(idx, weight, pieces, lines, tail, layers, left, pad):
+    blocks = len(pieces)
+    depth = weight.shape[2]
+    part = pieces[0].shape[1]
     tail[...] = jnp.zeros_like(tail)
-    for turn, piece in enumerate(turned):
-        lines[block_of(idx, turn, blocks)] = piece[(layers - 1) * SHARE :, :].astype(F32)
+    for turn, piece in enumerate(pieces):
+        for group in range(-(-depth // part)):
+            stop = min(depth, part * (group + 1))
+            lines[block_of(idx, turn, blocks), :, part * group : stop] = piece[
+                16 * group : 16 * (group + 1), 0 : stop - part * group
+            ].astype(F32)
     for block in range(blocks):
         for layer in range(layers):
             tail[0:left, :] = lines[block, left * layer : left * (layer + 1), :]
@@ -181,15 +192,15 @@
 def cross_forward(idx, *refs, blocks, layers, width, pad, depth):
     pieces, refs = refs[:blocks], refs[blocks:]
     own, refs = refs[0], refs[1:]
-    turned, refs = refs[:blocks], refs[blocks:]
-    slices, refs = refs[:16], refs[16:]
+    slices, refs = cross_eight(refs[:4]), refs[4:]
     z_out, x_out, weight, lines, tail, start, state, nat = refs
     left = width - MAIN
-    place_rest(idx, weight, turned, lines, tail, blocks, layers, left, pad)
+    place_rest(idx, weight, pieces, lines, tail, layers, left, pad)
+    at = 16 * -(-depth // pieces[0].shape[1])
     bias = [lines[block, :, 0:384].T for block in range(blocks)]
     for turn, piece in enumerate(pieces):
         block = block_of(idx, turn, blocks)
-        start[block, 0:width, :] = piece[0:width, :].astype(F32)
+        start[block, 0:width, :] = piece[at : at + width, :].astype(F32)
         start[block, width:, :] = jnp.zeros((pad - width, piece.shape[1]), F32)
     full = nat.shape[0]
     ones = lax.broadcasted_iota(jnp.int32, (full - depth, nat.shape[1]), 0) == 0
@@ -217,46 +228,49 @@
     (own1, own2), refs = refs[:2], refs[2:]
     slices, refs = refs[:8], refs[8:]
     x_all, acts, far, heads, flow, lines_out, day_out, field_out = refs[:8]
-    inputs, t1, t2, slope1, act2, headed, vectors = refs[8:]
-    hidden = t1.shape[0]
+    inputs, tower, slope1, act2, headed, vectors = refs[8:]
+    hidden = tower.shape[0]
+    full = x_all.shape[1]
     size = hidden // blocks
     part = x_all.shape[2]
     low = depth // LANES * LANES
-    offsets = places(idx)
+    at = 16 * -(-depth // part) + width
+    for turn, piece in enumerate(pieces):
+        inputs[block_of(idx, turn, blocks)] = piece[at : at + 3, :].astype(F32)
     base = idx[0] * size
-    t1[rows_at(base, size), :] = own1[...]
-    t2[rows_at(base, size), :] = own2[...]
-    for turn, piece in enumerate(pieces):
-        inputs[block_of(idx, turn, blocks)] = piece[width : width + 3, :].astype(F32)
+    tower[rows_at(base, size), 0:full] = own1[...]
+    tower[rows_at(base, size), full:] = own2[...]
     for turn in range(1, blocks):
         base = block_of(idx, turn, blocks) * size
-        for offset, piece in zip(offsets, slices):
+        for offset, piece in zip(places(idx), slices):
             rows = rows_at(base + offset, SHARE)
-            t1[rows, :] = piece[turn - 1, 0:SHARE, :]
-            t2[rows, :] = piece[turn - 1, SHARE : 2 * SHARE, 0:hidden]
+            start = piece.shape[1] - 2 * SHARE
+            tower[rows, 0:full] = piece[turn - 1, start : start + SHARE, :]
+            tower[rows, full:] = piece[turn - 1, start + SHARE :, 0:hidden]
     parts = [slice(size * block, size * (block + 1)) for block in range(blocks)]
     columns = []
     for block in range(blocks):
         vectors[0:3, :] = inputs[block]
         columns.append(vectors[...].T)
     for rows, column in zip(parts, columns):
-        act, slope = gelu_parts(dot(t1[rows, 0:depth], x_all[layers, 0:depth, :], NN) + column[:, 0:1])
+        act, slope = gelu_parts(dot(tower[rows, 0:depth], x_all[layers, 0:depth, :], NN) + column[:, 0:1])
         acts[0, rows, :] = act.astype(BF16)
         slope1[rows, :] = slope
     logits = jnp.zeros((1, part), F32)
     for rows, column in zip(parts, columns):
-        act, slope = gelu_parts(dot(t2[:, rows], acts[0], TN) + column[:, 2:3])
+        act, slope = gelu_parts(dot(tower[:, full + rows.start : full + rows.stop], acts[0], TN) + column[:, 2:3])
         act2[rows, :] = act
         headed[rows, :] = column[:, 1:2] * slope
         logits += jnp.sum(act * column[:, 1:2], axis=0, keepdims=True)
 
-    tally = jnp.zeros(slices[0].shape[:2] + (LANES,), F32)
+    half = BUCKETS // 2
+    tally = jnp.zeros((half, LANES), F32)
     for piece in slices:
-        tally += piece[:, :, low:].astype(F32)
-    tally = tally.reshape(-1, LANES)[0:BUCKETS, :]
-    shift = depth - low
-    high = tally[:, shift : shift + fields + 1]
-    count = 256.0 * high + tally[:, shift + COUNT : shift + COUNT + fields + 1]
+        start = piece.shape[1] - 2 * SHARE
+        tally += piece[0 : half // SHARE, start : start + SHARE, low:].astype(F32).reshape(half, LANES)
+    count = jnp.concatenate([tally, pltpu.roll(tally, LANES - 2 * (fields + 1), 1)], axis=0)
+    high = count[:, COUNT : COUNT + fields + 1]
+    count = 256.0 * high + count[:, COUNT + fields + 1 : COUNT + 2 * (fields + 1)]
     days = count[0:32, fields : fields + 1]
     padded = jnp.concatenate([count, jnp.zeros((BUCKETS, LANES - fields - 1), F32)], axis=1).T
     field_out[...] = padded[0:fields, :].astype(jnp.int32)
@@ -279,7 +293,7 @@
     acts[1] = (dl * headed[...]).astype(BF16)
     far[0:hidden, :] = acts[1]
     for rows in parts:
-        acts[2, rows, :] = (dot(t2[rows, :], acts[1], NN) * slope1[rows, :]).astype(BF16)
+        acts[2, rows, :] = (dot(tower[rows, full:], acts[1], NN) * slope1[rows, :]).astype(BF16)
     for block in range(blocks):
         rows = rows_at(block * size + (1 - idx[1]) * HALF, HALF)
         at = hidden + HALF * block
@@ -288,23 +302,23 @@
         far[at : at + HALF, :] = acts[2, rows, :]
     for rows in parts:
         heads[rows, :] = jnp.broadcast_to(jnp.sum(act2[rows, :] * dl, axis=1, keepdims=True), (size, LANES))
-    flow[...] = dot(t1[:, 0:depth], acts[2], TN)
+    flow[...] = dot(tower[:, 0:depth], acts[2], TN)
 
 
 def cross_backward(idx, *refs, blocks, layers, width, pad, depth):
     extra_lines, refs = refs[0], refs[1:]
     pieces, refs = refs[:blocks], refs[blocks:]
     own, refs = refs[0], refs[1:]
-    turned, refs = refs[:blocks], refs[blocks:]
-    slices, refs = refs[:16], refs[16:]
+    slices, refs = cross_eight(refs[:4]), refs[4:]
     (dx3, z_all), refs = refs[:2], refs[2:]
     eg_out, refs = refs[:blocks], refs[blocks:]
     dz_out, rest_out, dz_far_last, dz_far_out = refs[:4]
     weight, inputs, lines, tail, flow, padded, total, rest = refs[4:]
     left = width - MAIN
-    place_rest(idx, weight, turned, lines, tail, blocks, layers, left, pad)
+    place_rest(idx, weight, pieces, lines, tail, layers, left, pad)
+    at = 16 * -(-depth // pieces[0].shape[1])
     for turn, piece in enumerate(pieces):
-        inputs[block_of(idx, turn, blocks)] = piece[0:width, :].astype(F32)
+        inputs[block_of(idx, turn, blocks)] = piece[at : at + width, :].astype(F32)
     padded[...] = jnp.zeros_like(padded)
     rest[...] = jnp.zeros_like(rest)
     for layer in reversed(range(layers)):
@@ -383,10 +397,9 @@
     for at, (where, slot) in enumerate(order):
         target = (near, away, send.at[0], send.at[1])[where].at[slot]
         here = slice(SHARE * at, SHARE * (at + 1))
-        target[0:SHARE, 0:low] = wide[here, 0:low].astype(BF16)
-        target[0:SHARE, low:] = (wide[here, low:] + extra[here, :] + scale[at]).astype(BF16)
-        target[SHARE : 2 * SHARE, 0:hidden] = deep[here, :].astype(BF16)
-        target[SHARE : 2 * SHARE, hidden:] = jnp.zeros((SHARE, target.shape[1] - hidden), BF16)
+        target[:, 0:low] = wide[here, 0:low].astype(BF16)
+        target[:, low : low + LANES] = (wide[here, low:] + extra[here, :] + scale[at]).astype(BF16)
+        target[:, low + LANES :] = deep[here, :].astype(BF16)
     wait(copies.start(send, send_out), copies.start(near, near_out), copies.start(away, far_out))
 
 
@@ -448,7 +461,7 @@
     return [mine, one, two.at[0], two.at[1]] + [far.at[at] for at in range(4)]
 
 
-def finish_input(idx, *refs, blocks, lane):
+def finish_input(idx, *refs, blocks):
     pieces, (out, logits, losses, day_held) = refs[:blocks], refs[blocks:]
     width = out.shape[0]
     size = pieces[0].shape[1]
@@ -466,18 +479,18 @@
     row = lax.broadcasted_iota(jnp.int32, losses.shape, 0)
     tile = jnp.zeros(losses.shape, F32)
     for at, value in enumerate(split3(days[0:1, 0:LANES])):
-        tile = jnp.where(row == SHARE + at, value, tile)
-    losses[...] = pltpu.roll(tile, lane, 1)
+        tile = jnp.where(row == at, value, tile)
+    losses[...] = jnp.where(lane_of(tile.shape) < LOSS, 0.0, pltpu.roll(tile, LOSS, 1))
 
 
 def finish_tower(idx, *refs, depth):
     slices, (counts, out1, out2, rows_out, mean_out, lines, day_held) = eight(*refs[:4]), refs[4:]
     low = depth // LANES * LANES
-    size, hidden = out2.shape
+    size = out2.shape[0]
     for offset, piece in zip(places(idx), slices):
-        lines[rows_at(offset, SHARE), :] = piece[0:SHARE, :].astype(F32)
-        out2[rows_at(offset, SHARE), :] = piece[SHARE : 2 * SHARE, 0:hidden].astype(F32)
-        tile = piece[SHARE : SHARE + 16, low:].astype(F32)
+        lines[rows_at(offset, SHARE), :] = piece[:, 0 : low + LANES].astype(F32)
+        out2[rows_at(offset, SHARE), :] = piece[:, low + LANES :].astype(F32)
+        tile = piece[0:16, low : low + LANES].astype(F32)
         day_held[lax.div(offset, SHARE)] = tile[0:1, :] + tile[1:2, :] + tile[2:3, :]
     turned = lines[...].T
     out1[...] = turned[0:depth, :]
@@ -489,8 +502,7 @@
     days = day_held[0]
     for at in range(1, day_held.shape[0]):
         days += day_held[at]
-    at = depth - low
-    days = days[:, at : at + DAYS]
+    days = days[:, LOSS : LOSS + DAYS]
     mean = days / jnp.maximum(counts[:, 0:DAYS].astype(F32), 1.0)
     mean_out[...] = jnp.sum(mean, axis=1, keepdims=True) / DAYS
 
@@ -556,7 +568,7 @@
     me = lax.axis_index("mp")
     group = lax.axis_index("dp")
     core, plane = group & 1, (group >> 1) & 3
-    idx = jnp.stack([me, core, plane]).astype(jnp.int32)
+    idx = jnp.stack([me, core, plane, group & 7]).astype(jnp.int32)
     swap = lambda bits: [(i, i ^ bits(i)) for i in range(groups)]
     first = swap(lambda i: 4 if i & 1 else 2)
     second = swap(lambda i: 2 if i & 1 else 4)
@@ -568,66 +580,61 @@
         lax.ppermute(value, "mp", turn_by(r + 1)) for r, value in enumerate(values)
     ]
 
-    first_send = call(
-        pack_first,
-        shape((SHARE, depth), BF16),
-        [],
-        [idx, cross_weight],
-        mib=4,
-        spec=HBM,
-        out_spec=VMEM,
-        copies=1,
-    )
-    first_turned = turns([first_send] * (blocks - 1))
-    cross_send = call(
-        pack_cross,
-        shape(((layers - 1) * SHARE + 16, depth), BF16),
-        [vmem((16, depth), F32)],
-        [after(idx, first_send), cross_weight, cross_bias],
-        mib=8,
-        nbytes=2 << 20,
-    )
+    own_row = core * HALF + plane * SHARE
+    cross_send = lax.dynamic_slice(cross_weight, (0, own_row, 0), (layers, SHARE, depth))
+    cross_send = cross_send.reshape(layers * SHARE, depth)
+    cross_turned = turns([cross_send] * (blocks - 1))
     vectors = jnp.stack([tower1_bias, head_weight, tower2_bias])
+    wide = full + hidden
+    groups_of = -(-depth // part)
     tower_send, tower_own, tally, *chunks = call(
         functools.partial(pack_rest, blocks=blocks),
         tuple(
-            [shape((2 * SHARE, depth), BF16), shape((size, full), BF16), shape(((blocks - 1) * 2 * SHARE, LANES), BF16)]
-            + [shape((width + 3, part), BF16)] * blocks
+            [
+                shape((2 * SHARE, full), BF16),
+                shape((size, full), BF16),
+                shape(((blocks - 1) * SHARE, LANES), BF16),
+            ]
+            + [shape((16 * groups_of + width + 3, part), BF16)] * blocks
         ),
-        [],
-        [after(idx, first_send), embedded.T, vectors, tower1, tower2, feature_ids.T, day_ids[None, :]],
+        [vmem((16, groups_of * part), F32)],
+        [
+            after(idx, cross_send),
+            cross_weight,
+            cross_bias,
+            embedded.T,
+            vectors,
+            tower1,
+            tower2,
+            feature_ids.T,
+            day_ids[None, :],
+        ],
         mib=24,
         nbytes=2 << 20,
     )
     for perm in others:
         tally = tally + hop(tally, perm)
+    tally = jnp.pad(tally.reshape(blocks - 1, SHARE, LANES), ((0, 0), (0, SHARE), (full - LANES, 0)))
 
     join = lambda *values: lax.optimization_barrier(values)
-    with_pair = lambda held: held + [hop(value, pair) for value in held]
-    first_mine = jnp.stack(first_turned)
-    first_mine, cross_send = join(first_mine, cross_send)
-    first_one, first_two = hop(first_mine, first), hop(first_mine, second)
-    cross_turned = turns([cross_send] * (blocks - 1))
-    first_one, first_two, tower_send, *cross_turned = join(first_one, first_two, tower_send, *cross_turned)
-
-    first_three = hop(first_one, second)
-    cross_mine = jnp.stack([value[: (layers - 1) * SHARE] for value in cross_turned])
+    cross_mine = jnp.stack(cross_turned)
+    cross_mine, tower_send, *chunks = join(cross_mine, tower_send, *chunks)
     cross_one, cross_two = hop(cross_mine, first), hop(cross_mine, second)
     tower_turned = turns([tower_send] * (blocks - 1))
-    first_three, cross_one, cross_two, *tower_turned = join(first_three, cross_one, cross_two, *tower_turned)
-
-    first_slices = with_pair([first_mine, first_one, first_two, first_three])
-    cross_three = hop(cross_one, second)
-    tower_mine = jnp.concatenate(
-        [jnp.stack(tower_turned), tally.reshape(blocks - 1, 2 * SHARE, LANES)[:, :, : full - depth]], axis=2
-    )
-    tower_one, tower_two = hop(tower_mine, first), hop(tower_mine, second)
+    cross_one, cross_two, *tower_turned = join(cross_one, cross_two, *tower_turned)
+
     pieces = [chunks[0]] + turns([after(chunk, tower_turned[0]) for chunk in chunks[1:]])
-    cross_three, tower_one, tower_two, *pieces = join(cross_three, tower_one, tower_two, *pieces)
+    tower_mine = jnp.stack(tower_turned) + tally
+    both = jnp.concatenate([jnp.pad(cross_one, ((0, 0), (0, 0), (0, full - depth))), tower_mine], axis=1)
+    tower_one, both = hop(tower_mine, first), hop(both, second)
+    cross_near = jnp.stack([cross_mine, cross_one, cross_two])
+    both, tower_one, cross_near, *pieces = join(both, tower_one, cross_near, *pieces)
 
     tower_three = hop(tower_one, second)
-    cross_slices = first_slices + with_pair([cross_mine, cross_one, cross_two, cross_three])
-    tower_slices = with_pair([tower_mine, tower_one, tower_two, tower_three])
+    both_far, tower_far, tower_next = hop(both, pair), hop(tower_mine, pair), hop(tower_one, pair)
+    cross_far = hop(cross_near, pair)
+    both_far, tower_far, tower_next, cross_far = join(both_far, tower_far, tower_next, cross_far)
+    cross_slices = [cross_near, both, cross_far, both_far]
 
     z_all, x_all = call(
         functools.partial(cross_forward, blocks=blocks, layers=layers, width=width, pad=pad, depth=depth),
@@ -640,12 +647,14 @@
             vmem((blocks, pad, part), F32),
             vmem((full, part), F32),
         ],
-        [idx, *pieces, cross_weight, cross_send, *cross_turned, *cross_slices],
+        [idx, *pieces, cross_weight, *cross_slices],
         mib=28,
         flops=2 * layers * flat * full * part,
         nbytes=20 << 20,
     )
-    x_far = hop(x_all, pair)
+    tower_last = hop(after(tower_three, z_all), pair)
+    tower_slices = [tower_mine, tower_one, both, tower_three, tower_far, tower_next, both_far, tower_last]
+    x_far = hop(after(x_all, tower_last), pair)
     fields = feature_ids.shape[1]
     acts, far, head_col, dx3, lines, day_line, field_counts = call(
         functools.partial(
@@ -662,8 +671,7 @@
         ),
         [
             vmem((blocks, 3, part), F32),
-            vmem((hidden, full), BF16),
-            vmem((hidden, hidden), BF16),
+            vmem((hidden, wide), BF16),
             vmem((hidden, part), F32),
             vmem((hidden, part), F32),
             vmem((hidden, part), F32),
@@ -685,15 +693,12 @@
     )
     far = hop(far, pair)
 
-    def halves(rows):
-        keep = (blocks, rows, full)
-        return keep, keep, (2,) + keep
-
-    def grads(kernel, rows, scratch, args, copies, flops):
+    def grads(kernel, keep, scratch, args, copies, flops):
+        outs = keep, keep, (2,) + keep
         return call(
             kernel,
-            tuple(shape(s, BF16) for s in halves(rows)),
-            scratch + [vmem(s, BF16) for s in halves(rows)],
+            tuple(shape(s, BF16) for s in outs),
+            scratch + [vmem(s, BF16) for s in outs],
             args,
             mib=20,
             spec=HBM,
@@ -704,7 +709,7 @@
 
     tower_parts = grads(
         functools.partial(tower_grads, blocks=blocks, depth=depth, layers=layers),
-        2 * SHARE,
+        (blocks, SHARE, wide),
         [
             vmem((full, 2 * part), BF16),
             vmem((3, hidden, part), BF16),
@@ -742,8 +747,6 @@
             lines,
             *pieces,
             cross_weight,
-            cross_send,
-            *cross_turned,
             *cross_slices,
             dx3,
             z_all,
@@ -758,7 +761,7 @@
     def cross_parts_of(base, count, far, start):
         return grads(
             functools.partial(cross_grads, blocks=blocks, base=base, pad=pad, depth=depth),
-            count * SHARE,
+            (blocks, count * SHARE, full),
             [
                 vmem((count, full, 2 * part), BF16),
                 vmem((count, flat, part), BF16),
@@ -799,10 +802,10 @@
     def far_of(mine, one, two):
         return hop(jnp.concatenate([jnp.stack([mine, one]), two]), pair)
 
-    tower_arrived, last_send = join(tower_arrived, last_parts[2])
+    grad_pieces = [input_grads[0]] + turns(input_grads[1:])
+    tower_arrived, last_send, grad_pieces[1] = join(tower_arrived, last_parts[2], grad_pieces[1])
     tower_second = far_send(tower_parts, tower_arrived)
     last_arrived = hop(last_send, first)
-    grad_pieces = [input_grads[0]] + turns([after(value, last_send) for value in input_grads[1:]])
     tower_second, last_arrived, cross_send, *grad_pieces = join(
         tower_second, last_arrived, cross_parts[2], *grad_pieces
     )
@@ -812,8 +815,8 @@
     last_second = far_send(last_parts, last_arrived)
     cross_arrived = hop(cross_send, first)
     input_out, logits_all, losses = call(
-        functools.partial(finish_input, blocks=blocks, lane=depth % LANES),
-        (shape((width, tokens), F32), shape((1, tokens), F32), shape((2 * SHARE, LANES), F32)),
+        functools.partial(finish_input, blocks=blocks),
+        (shape((width, tokens), F32), shape((1, tokens), F32), shape((SHARE, LANES), F32)),
         [vmem((blocks, 8, part), F32)],
         [idx, *grad_pieces],
         mib=16,
@@ -824,7 +827,7 @@
     last_held = near_sum(last_parts, last_arrived, last_second)
     last_turned = send_blocks(last_held)
     cross_second = far_send(cross_parts, cross_arrived)
-    tower_mine = down(total_of(tower_held, tower_turned) + jnp.pad(losses, ((0, 0), (full - LANES, 0))))
+    tower_mine = down(total_of(tower_held, tower_turned) + jnp.pad(losses, ((0, 0), (full - LANES, hidden))))
     tower_one = hop(tower_mine, first)
     cross_second, tower_one, *last_turned = join(cross_second, tower_one, *last_turned)
 
@@ -868,6 +871,7 @@
         )
 
     before = finish(last_sums, layers - 1, 1, ())
+    cross_two, tower1_grad, before = join(cross_two, tower1_grad, before)
     cross_far = far_of(cross_mine, cross_one, cross_two)
     cross_grad, cross_bias_grad = finish([cross_mine, cross_one, cross_two, cross_far], 0, layers - 1, before)
     day_counts = day_line[0, :DAYS]

time: 197 us -> 180 us (0.914)
  starting transfers between devices: 52 us -> 33.9 us
  local copies, waits for them, and re-layouts: 2.79 us -> 11.1 us
  waiting for transfers between devices: 104 us -> 97.2 us
    ppermute x40 -> x29, starting transfers between devices: 30.4 us -> 20.7 us  [per_device(): hop = lambda value, perm: lax.ppermute(value, 'dp', perm)]
    ppermute x24 -> x21, starting transfers between devices: 21.5 us -> 13.2 us  [per_device(): lax.ppermute(value, 'mp', turn_by(r + 1))]
    unnamed x24 -> x22, local copies, waits for them, and re-layouts: 1.56 us -> 6.92 us
    ppermute x24 -> x21, waiting for transfers between devices: 70.2 us -> 65.9 us  [per_device(): lax.ppermute(value, 'mp', turn_by(r + 1))]
    ppermute x40 -> x29, waiting for transfers between devices: 33.8 us -> 31.3 us  [per_device(): hop = lambda value, perm: lax.ppermute(value, 'dp', perm)]
    pallas_call x13 -> x11, Pallas kernels: 35.2 us -> 33.9 us  [call(): pl.pallas_call(kernel, out_shape=outs, in_specs=[SMEM] + specs, out_specs...]
  transfers between devices with their start and end apart: 64 -> 50, of which waited for: 32 -> 35; matrix products, arithmetic and copies ran while one was open for 1% -> 2% of each run, Pallas kernels for 13% -> 16%
where the time goes in v3:
time: 180 us; the launch traced here: 179 us
  waiting for transfers between devices  97.2 us (54%)
  starting transfers between devices  33.9 us (19%)
  Pallas kernels  33.9 us (19%)
  local copies, waits for them, and re-layouts  11.1 us (6%)
  other arithmetic  2.02 us (1%)
    ppermute x21, waiting for transfers between devices, per_device(): lax.ppermute(value, 'mp', turn_by(r + 1))  65.9 us
    pallas_call x11, Pallas kernels, call(): pl.pallas_call(kernel, out_shape=outs, in_specs=[SMEM] + specs, out_specs...  33.9 us
    ppermute x29, waiting for transfers between devices, per_device(): hop = lambda value, perm: lax.ppermute(value, 'dp', perm)  31.3 us
    ppermute x29, starting transfers between devices, per_device(): hop = lambda value, perm: lax.ppermute(value, 'dp', perm)  20.7 us
    ppermute x21, starting transfers between devices, per_device(): lax.ppermute(value, 'mp', turn_by(r + 1))  13.2 us
    unnamed x22, local copies, waits for them, and re-layouts  6.92 us
  transfers between devices with their start and end apart: 50, of which 35 were waited for; matrix products, arithmetic and copies ran while one was open for 2% of the time, Pallas kernels for 16%

profile of v3, /device:TPU:9, one launch (start us, length us, event | category | flops | bytes accessed | tf_op | source)
XLA Modules:
  0.0 179.4 jit_solution(163866083247223705)
XLA Ops:
  1.7 1.3 collective-permute-start
  4.1 1.4 collective-permute-start.2
  7.6 1.5 copy-done
  14.5 2.9 %shard_map.202 = (bf16[64,1152]{1,0:T(8,128)(2,1)S(1)}, bf16[256,1152]{1,0:T(8,128)(2,1)S(1)}, bf16[96,128]{1,0:T(8,128)(2,1)S(1)}, bf16[343,256]{1,0:T(8,128)(2...) custom-call(s32[4]{0:T(128)S(1)} %pad_add_fusion.idx, ...), custom_call_target="tpu_custom_call" | custom-call | bytes 2097152 | tf_op jit(solution)/shard_map/pallas_call | solution.py:45
  17.4 4.0 %collective-permute-done.1 = bf16[96,1040]{1,0:T(8,128)(2,1)S(1)} collective-permute-done((bf16[96,1040]{1,0:T(8,128)(2,1)S(1)}, bf16[96,1040]{1,0:T(8,128)(2,1)S(1)}, u32[]{:S(2)}, u32[]{:S(2)}) %collective-permute-start.1) | collective-permute-done | bytes 199712 | tf_op jit(solution)/shard_map/ppermute | solution.py:580
  21.3 2.8 %collective-permute-done.2 = bf16[96,1040]{1,0:T(8,128)(2,1)S(1)} collective-permute-done((bf16[96,1040]{1,0:T(8,128)(2,1)S(1)}, bf16[96,1040]{1,0:T(8,128)(2,1)S(1)}, u32[]{:S(2)}, u32[]{:S(2)}) %collective-permute-start.2) | collective-permute-done | bytes 199712 | tf_op jit(solution)/shard_map/ppermute | solution.py:580
  27.1 1.5 collective-permute-start.7
  28.5 2.6 %collective-permute-done.5 = bf16[64,1152]{1,0:T(8,128)(2,1)S(1)} collective-permute-done((bf16[64,1152]{1,0:T(8,128)(2,1)S(1)}, bf16[64,1152]{1,0:T(8,128)(2,1)S(1)}, u32[]{:S(2)}, u32[]{:S(2)}) %collective-permute-start.5) | collective-permute-done | bytes 147488 | tf_op jit(solution)/shard_map/ppermute | solution.py:580
  31.1 7.5 %collective-permute-done.6 = bf16[64,1152]{1,0:T(8,128)(2,1)S(1)} collective-permute-done((bf16[64,1152]{1,0:T(8,128)(2,1)S(1)}, bf16[64,1152]{1,0:T(8,128)(2,1)S(1)}, u32[]{:S(2)}, u32[]{:S(2)}) %collective-permute-start.6) | collective-permute-done | bytes 147488 | tf_op jit(solution)/shard_map/ppermute | solution.py:580
  38.6 2.8 %collective-permute-done.7 = bf16[64,1152]{1,0:T(8,128)(2,1)S(1)} collective-permute-done((bf16[64,1152]{1,0:T(8,128)(2,1)S(1)}, bf16[64,1152]{1,0:T(8,128)(2,1)S(1)}, u32[]{:S(2)}, u32[]{:S(2)}) %collective-permute-start.7) | collective-permute-done | bytes 147488 | tf_op jit(solution)/shard_map/ppermute | solution.py:580
  43.5 1.5 collective-permute-start.12
  45.3 2.8 %collective-permute-done.10.refs_1_.refs_3_.refs_2_ = bf16[343,256]{1,0:T(8,128)(2,1)S(1)} collective-permute-done((bf16[343,256]{1,0:T(8,128)(2,1)S(1)}, bf16[343,256]{1,0:T(8,128)(2,1)S(1)}, u32[]{:S(2)}, u32[]{:S(2)}) %collective-permute-start.10) | collective-permute-done | bytes 175648 | tf_op jit(solution)/shard_map/ppermute | solution.py:580
  48.1 9.0 %collective-permute-done.11.refs_2_.refs_4_.refs_3_ = bf16[343,256]{1,0:T(8,128)(2,1)S(1)} collective-permute-done((bf16[343,256]{1,0:T(8,128)(2,1)S(1)}, bf16[343,256]{1,0:T(8,128)(2,1)S(1)}, u32[]{:S(2)}, u32[]{:S(2)}) %collective-permute-start.11) | collective-permute-done | bytes 175648 | tf_op jit(solution)/shard_map/ppermute | solution.py:580
  57.1 2.9 %collective-permute-done.12.refs_3_.refs_5_.refs_4_ = bf16[343,256]{1,0:T(8,128)(2,1)S(1)} collective-permute-done((bf16[343,256]{1,0:T(8,128)(2,1)S(1)}, bf16[343,256]{1,0:T(8,128)(2,1)S(1)}, u32[]{:S(2)}, u32[]{:S(2)}) %collective-permute-start.12) | collective-permute-done | bytes 175648 | tf_op jit(solution)/shard_map/ppermute | solution.py:580
  59.9 1.5 collective-permute-done.8.refs_6_.refs_10_.refs_7_
  63.8 4.7 %collective-permute-done.14.refs_12_ = bf16[3,64,1152]{2,1,0:T(8,128)(2,1)S(1)} collective-permute-done((bf16[3,64,1152]{2,1,0:T(8,128)(2,1)S(1)}, bf16[3,64,1152]{2,1,0:T(8,128)(2,1)S(1)}, u32[]{:S(2)}, u32[]{:S(2)}) %collective-permute-start.14) | collective-permute-done | bytes 442400 | tf_op jit(solution)/shard_map/ppermute | solution.py:578
  69.2 3.9 %shard_map.203 = (f32[3,1088,256]{2,1,0:T(8,128)S(1)}, bf16[4,1152,256]{2,1,0:T(8,128)(2,1)S(1)}) custom-call(s32[4]{0:T(128)S(1)} %pad_add_fusion.idx, bf16[343,256]{1,0:T(8,128)(2,1)S(1)} %get-tuple-element.140.refs_0_.refs_2_.refs_1_, bf16[343,256]{1,0:T(8,128)(2,1)S(1)} %collective-permute-done.10.refs_1_.refs_3_.refs_2_, ...), custom_call_target="tpu_custom_call" | custom-call | flops 1925185536 | bytes 20971520 | tf_op jit(solution)/shard_map/pallas_call | solution.py:45
  73.5 1.4 collective-permute-done.18.refs_15_
  75.3 4.4 %shard_map.204 = (bf16[3,1024,256]{2,1,0:T(8,128)(2,1)S(1)}, bf16[2048,256]{1,0:T(8,128)(2,1)S(1)}, f32[1024,128]{1,0:T(8,128)S(1)}, f32[1040,256]{1,0:T(8,128)S...) custom-call(s32[4]{0:T(128)S(1)} %pad_add_fusion.idx, s32[1,1024]{1,0:T(1,128)S(1)} %bitcast.109, ...), custom_call_target="tpu_custom_call" | custom-call | flops 2415919104 | bytes 10485760 | tf_op jit(solution)/shard_map/pallas_call | solution.py:45
  79.9 2.5 %collective-permute-done.20.far = bf16[2048,256]{1,0:T(8,128)(2,1)S(1)} collective-permute-done((bf16[2048,256]{1,0:T(8,128)(2,1)S(1)}, bf16[2048,256]{1,0:T(8,128)(2,1)S(1)}, u32[]{:S(2)}, u32[]{:S(2)}) %collective-permute-start.20) | collective-permute-done | bytes 1048608 | tf_op jit(solution)/shard_map/ppermute | solution.py:578
  82.5 3.0 %shard_map.205 = (bf16[4,32,2176]{2,1,0:T(8,128)(2,1)S(1)}, bf16[4,32,2176]{2,1,0:T(8,128)(2,1)S(1)}, bf16[2,4,32,2176]{3,2,1,0:T(8,128)(2,1)S(1)}) custom-call(s32[4]{0:T(128)S(1)} %pad_add_fusion.idx, bf16[4,1152,256]{2,1,0:T(8,128)(2,1)S(1)} %get-tuple-element.152.refs_16_.x_all, bf16[4,1152,256]{2,1,0:T(8,128)(2,1)S(1)} %collective-permute-done.19.x_far, ...), custom_call_target="tpu_custom_call" | custom-call | flops 1207959552 | bytes 10485760 | tf_op jit(solution)/shard_map/pallas_call | solution.py:45
  86.0 5.2 %shard_map.206 = (bf16[272,256]{1,0:T(8,128)(2,1)S(1)}, bf16[272,256]{1,0:T(8,128)(2,1)S(1)}, bf16[272,256]{1,0:T(8,128)(2,1)S(1)}, bf16[272,256]{1,0:T(8,128)(2...) custom-call(s32[4]{0:T(128)S(1)} %pad_add_fusion.idx, ...), custom_call_target="tpu_custom_call" | custom-call | flops 1925185536 | bytes 20971520 | tf_op jit(solution)/shard_map/pallas_call | solution.py:45
  93.0 2.2 %shard_map.207 = (bf16[4,32,1152]{2,1,0:T(8,128)(2,1)S(1)}, bf16[4,32,1152]{2,1,0:T(8,128)(2,1)S(1)}, bf16[2,4,32,1152]{3,2,1,0:T(8,128)(2,1)S(1)}) custom-call(s32[4]{0:T(128)S(1)} %pad_add_fusion.idx, bf16[4,1152,256]{2,1,0:T(8,128)(2,1)S(1)} %get-tuple-element.152.refs_16_.x_all, bf16[4,1152,256]{2,1,0:T(8,128)(2,1)S(1)} %collective-permute-done.19.x_far, ...), custom_call_target="tpu_custom_call" | custom-call | flops 641728512 | bytes 10485760 | tf_op jit(solution)/shard_map/pallas_call | solution.py:45
  95.2 1.9 %collective-permute-done.23.refs_1_ = bf16[272,256]{1,0:T(8,128)(2,1)S(1)} collective-permute-done((bf16[272,256]{1,0:T(8,128)(2,1)S(1)}, bf16[272,256]{1,0:T(8,128)(2,1)S(1)}, u32[]{:S(2)}, u32[]{:S(2)}) %collective-permute-start.23) | collective-permute-done | bytes 139296 | tf_op jit(solution)/shard_map/ppermute | solution.py:580
  97.1 3.1 %collective-permute-done.21 = bf16[2,4,32,2176]{3,2,1,0:T(8,128)(2,1)S(1)} collective-permute-done((bf16[2,4,32,2176]{3,2,1,0:T(8,128)(2,1)S(1)}, bf16[2,4,32,2176]{3,2,1,0:T(8,128)(2,1)S(1)}, u32[]{:S(2)}, u32[]{:S(2)}) %collective-permute-start.21) | collective-permute-done | bytes 1114144 | tf_op jit(solution)/shard_map/ppermute | solution.py:578
  102.0 3.8 %shard_map.208 = (bf16[4,64,1152]{2,1,0:T(8,128)(2,1)S(1)}, bf16[4,64,1152]{2,1,0:T(8,128)(2,1)S(1)}, bf16[2,4,64,1152]{3,2,1,0:T(8,128)(2,1)S(1)}) custom-call(s32[4]{0:T(128)S(1)} %pad_add_fusion.idx, bf16[4,1152,256]{2,1,0:T(8,128)(2,1)S(1)} %get-tuple-element.152.refs_16_.x_all, bf16[4,1152,256]{2,1,0:T(8,128)(2,1)S(1)} %collective-permute-done.19.x_far, ...), custom_call_target="tpu_custom_call" | custom-call | flops 1283457024 | bytes 10485760 | tf_op jit(solution)/shard_map/pallas_call | solution.py:45
  105.7 4.4 %collective-permute-done.27.refs_2_ = bf16[272,256]{1,0:T(8,128)(2,1)S(1)} collective-permute-done((bf16[272,256]{1,0:T(8,128)(2,1)S(1)}, bf16[272,256]{1,0:T(8,128)(2,1)S(1)}, u32[]{:S(2)}, u32[]{:S(2)}) %collective-permute-start.27) | collective-permute-done | bytes 139296 | tf_op jit(solution)/shard_map/ppermute | solution.py:580
  110.6 4.2 %collective-permute-done.24 = bf16[4,32,2176]{2,1,0:T(8,128)(2,1)S(1)} collective-permute-done((bf16[4,32,2176]{2,1,0:T(8,128)(2,1)S(1)}, bf16[4,32,2176]{2,1,0:T(8,128)(2,1)S(1)}, u32[]{:S(2)}, u32[]{:S(2)}) %collective-permute-start.24) | collective-permute-done | bytes 557088 | tf_op jit(solution)/shard_map/ppermute | solution.py:578
  114.9 2.3 %collective-permute-start.30 = (bf16[2,4,64,1152]{3,2,1,0:T(8,128)(2,1)S(1)}, bf16[2,4,64,1152]{3,2,1,0:T(8,128)(2,1)S(1)}, u32[]{:S(2)}, u32[]{:S(2)}) collective-permute-start(bf16[2,4,64,1152]{3,2,1,0:T(8,128)(2,1)S(1)} %get-tuple-element.182), channel_id=1, source_target_pairs={{0,8},{4,20},{8,0},{12,28},{16,24},{20,4},{24,16},{28,12},{1,9},{5... | collective-permute-start | bytes 3538952 | tf_op jit(solution)/shard_map/ppermute | solution.py:578
  117.7 1.4 collective-permute-start.33
  119.0 1.6 shard_map.209
  121.8 6.7 %collective-permute-done.32 = bf16[32,2176]{1,0:T(8,128)(2,1)S(1)} collective-permute-done((bf16[32,2176]{1,0:T(8,128)(2,1)S(1)}, bf16[32,2176]{1,0:T(8,128)(2,1)S(1)}, u32[]{:S(2)}, u32[]{:S(2)}) %collective-permute-start.32) | collective-permute-done | bytes 139296 | tf_op jit(solution)/shard_map/ppermute | solution.py:580
  128.5 2.3 %collective-permute-done.33 = bf16[32,2176]{1,0:T(8,128)(2,1)S(1)} collective-permute-done((bf16[32,2176]{1,0:T(8,128)(2,1)S(1)}, bf16[32,2176]{1,0:T(8,128)(2,1)S(1)}, u32[]{:S(2)}, u32[]{:S(2)}) %collective-permute-start.33) | collective-permute-done | bytes 139296 | tf_op jit(solution)/shard_map/ppermute | solution.py:580
  130.8 3.2 %collective-permute-done.30 = bf16[2,4,64,1152]{3,2,1,0:T(8,128)(2,1)S(1)} collective-permute-done((bf16[2,4,64,1152]{3,2,1,0:T(8,128)(2,1)S(1)}, bf16[2,4,64,1152]{3,2,1,0:T(8,128)(2,1)S(1)}, u32[]{:S(2)}, u32[]{:S(2)}) %collective-permute-start.30) | collective-permute-done | bytes 1179680 | tf_op jit(solution)/shard_map/ppermute | solution.py:578
  134.9 1.5 collective-permute-start.35
  136.9 1.4 collective-permute-start.38
  138.2 1.9 %collective-permute-done.36 = bf16[32,1152]{1,0:T(8,128)(2,1)S(1)} collective-permute-done((bf16[32,1152]{1,0:T(8,128)(2,1)S(1)}, bf16[32,1152]{1,0:T(8,128)(2,1)S(1)}, u32[]{:S(2)}, u32[]{:S(2)}) %collective-permute-start.36) | collective-permute-done | bytes 73760 | tf_op jit(solution)/shard_map/ppermute | solution.py:580
  140.9 3.8 %collective-permute-done.38 = bf16[32,1152]{1,0:T(8,128)(2,1)S(1)} collective-permute-done((bf16[32,1152]{1,0:T(8,128)(2,1)S(1)}, bf16[32,1152]{1,0:T(8,128)(2,1)S(1)}, u32[]{:S(2)}, u32[]{:S(2)}) %collective-permute-start.38) | collective-permute-done | bytes 73760 | tf_op jit(solution)/shard_map/ppermute | solution.py:580
  145.1 1.6 collective-permute-start.42
  148.9 3.2 %collective-permute-done.40.refs_1_ = bf16[32,1152]{1,0:T(8,128)(2,1)S(1)} collective-permute-done((bf16[32,1152]{1,0:T(8,128)(2,1)S(1)}, bf16[32,1152]{1,0:T(8,128)(2,1)S(1)}, u32[]{:S(2)}, u32[]{:S(2)}) %collective-permute-start.40) | collective-permute-done | bytes 73760 | tf_op jit(solution)/shard_map/ppermute | solution.py:578
  152.1 5.2 %collective-permute-done.42 = bf16[64,1152]{1,0:T(8,128)(2,1)S(1)} collective-permute-done((bf16[64,1152]{1,0:T(8,128)(2,1)S(1)}, bf16[64,1152]{1,0:T(8,128)(2,1)S(1)}, u32[]{:S(2)}, u32[]{:S(2)}) %collective-permute-start.42) | collective-permute-done | bytes 147488 | tf_op jit(solution)/shard_map/ppermute | solution.py:580
  157.3 3.2 %collective-permute-done.43 = bf16[64,1152]{1,0:T(8,128)(2,1)S(1)} collective-permute-done((bf16[64,1152]{1,0:T(8,128)(2,1)S(1)}, bf16[64,1152]{1,0:T(8,128)(2,1)S(1)}, u32[]{:S(2)}, u32[]{:S(2)}) %collective-permute-start.43) | collective-permute-done | bytes 147488 | tf_op jit(solution)/shard_map/ppermute | solution.py:580
  162.7 2.8 %collective-permute-done.45.refs_2_ = bf16[2,32,1152]{2,1,0:T(8,128)(2,1)S(1)} collective-permute-done((bf16[2,32,1152]{2,1,0:T(8,128)(2,1)S(1)}, bf16[2,32,1152]{2,1,0:T(8,128)(2,1)S(1)}, u32[]{:S(2)}, u32[]{:S(2)}) %collective-permute-start.45) | collective-permute-done | bytes 147488 | tf_op jit(solution)/shard_map/ppermute | solution.py:578
  165.5 1.8 collective-permute-done.44.refs_1_
  167.7 1.6 collective-permute-start.47
  169.3 2.5 %shard_map.210 = (f32[1040,256]{1,0:T(8,128)}, f32[256,1024]{1,0:T(8,128)}, f32[3,256]{1,0:T(4,128)S(1)}, f32[1,1]{1,0:T(1,128)}) custom-call(s32[4]{0:T(128)S(1)} %pad_add_fusion.idx, bf16[32,2176]{1,0:T(8,128)(2,1)S(1)} %fusion.12.refs_0_, bf16[32,2176]{1,0:T(8,128)(2,1)S(1)} %collective-permute-done.35.refs_1_, ...), custom_call_target="tpu_custom_call" | custom-call | bytes 4194304 | tf_op jit(solution)/shard_map/pallas_call | solution.py:45
  171.8 1.8 %shard_map.211 = (f32[3,260,1040]{2,1,0:T(8,128)}, f32[1,260]{1,0:T(1,128)S(1)}) custom-call(s32[4]{0:T(128)S(1)} %pad_add_fusion.idx, bf16[32,1152]{1,0:T(8,128)(2,1)S(1)} %fusion.14.refs_0_, bf16[32,1152]{1,0:T(8,128)(2,1)S(1)} %collective-permute-done.40.refs_1_, bf16[2,32,1152]{2,1,0:T(8,128)(2,1)S(1)} %collective-permute-done.45.refs_2_, ...), custom_call_target="tpu_custom_call" | custom-call | bytes 4194304 | tf_op jit(solution)/shard_map/pallas_call | solution.py:45
  176.5 2.7 %shard_map.212 = (f32[3,260,1040]{2,1,0:T(8,128)}, f32[3,260]{1,0:T(4,128)}) custom-call(s32[4]{0:T(128)S(1)} %pad_add_fusion.idx, bf16[64,1152]{1,0:T(8,128)(2,1)S(1)} %fusion.9.refs_0_, bf16[64,1152]{1,0:T(8,128)(2,1)S(1)} %collective-permute-done.44.refs_1_, ...), custom_call_target="tpu_custom_call", output_to_operand_aliasing={{0}: (5, {})} | custom-call | bytes 4194304 | tf_op jit(solution)/shard_map/pallas_call | solution.py:45
  (115 shorter events, 35.4 us)
Async XLA Ops:
  1.7 15.7 %collective-permute-start = (bf16[96,1040]{1,0:T(8,128)(2,1)S(1)}, bf16[96,1040]{1,0:T(8,128)(2,1)S(1)}, u32[]{:S(2)}, u32[]{:S(2)}) collective-permute-start(bf16[96,1040]{1,0:T(8,128)(2,1)S(1)} %bitcast.113), channel_id=1, source_target_pairs={{0,1},{1,2},{2,3},{3,0},{4,5},{5,6},{6,7},{7,4},{8,9},{9,10},{10,1... | collective-permute-start | bytes 599048 | tf_op jit(solution)/shard_map/ppermute | solution.py:580
  3.0 18.3 %collective-permute-start.1 = (bf16[96,1040]{1,0:T(8,128)(2,1)S(1)}, bf16[96,1040]{1,0:T(8,128)(2,1)S(1)}, u32[]{:S(2)}, u32[]{:S(2)}) collective-permute-start(bf16[96,1040]{1,0:T(8,128)(2,1)S(1)} %bitcast.114), channel_id=1, source_target_pairs={{0,2},{1,3},{2,0},{3,1},{4,6},{5,7},{6,4},{7,5},{8,10},{9,11},{10,... | collective-permute-start | bytes 599048 | tf_op jit(solution)/shard_map/ppermute | solution.py:580
  4.1 20.1 %collective-permute-start.2 = (bf16[96,1040]{1,0:T(8,128)(2,1)S(1)}, bf16[96,1040]{1,0:T(8,128)(2,1)S(1)}, u32[]{:S(2)}, u32[]{:S(2)}) collective-permute-start(bf16[96,1040]{1,0:T(8,128)(2,1)S(1)} %bitcast.115), channel_id=1, source_target_pairs={{0,3},{1,0},{2,1},{3,2},{4,7},{5,4},{6,5},{7,6},{8,11},{9,8},{10,9... | collective-permute-start | bytes 599048 | tf_op jit(solution)/shard_map/ppermute | solution.py:580
  24.3 17.1 %collective-permute-start.3 = (bf16[3,96,1040]{2,1,0:T(8,128)(2,1)S(1)}, bf16[3,96,1040]{2,1,0:T(8,128)(2,1)S(1)}, u32[]{:S(2)}, u32[]{:S(2)}) collective-permute-start(bf16[3,96,1040]{2,1,0:T(8,128)(2,1)S(1)} %pad_maximum_fusion.1), channel_id=1, source_target_pairs={{0,8},{4,20},{8,0},{12,28},{16,24},{20,4},{24,16},{28,12},{1,9},{5... | collective-permute-start | bytes 1797128 | tf_op jit(solution)/shard_map/ppermute | solution.py:578
  25.6 16.4 %collective-permute-start.4 = (bf16[3,96,1040]{2,1,0:T(8,128)(2,1)S(1)}, bf16[3,96,1040]{2,1,0:T(8,128)(2,1)S(1)}, u32[]{:S(2)}, u32[]{:S(2)}) collective-permute-start(bf16[3,96,1040]{2,1,0:T(8,128)(2,1)S(1)} %pad_maximum_fusion.1), channel_id=1, source_target_pairs={{0,16},{4,12},{8,24},{12,4},{16,0},{20,28},{24,8},{28,20},{1,17},{... | collective-permute-start | bytes 1797128 | tf_op jit(solution)/shard_map/ppermute | solution.py:578
  26.8 4.3 %collective-permute-start.5 = (bf16[64,1152]{1,0:T(8,128)(2,1)S(1)}, bf16[64,1152]{1,0:T(8,128)(2,1)S(1)}, u32[]{:S(2)}, u32[]{:S(2)}) collective-permute-start(bf16[64,1152]{1,0:T(8,128)(2,1)S(1)} %get-tuple-element.126), channel_id=1, source_target_pairs={{0,1},{1,2},{2,3},{3,0},{4,5},{5,6},{6,7},{7,4},{8,9},{9,10},{10,1... | collective-permute-start | bytes 442376 | tf_op jit(solution)/shard_map/ppermute | solution.py:580
  26.8 11.7 %collective-permute-start.6 = (bf16[64,1152]{1,0:T(8,128)(2,1)S(1)}, bf16[64,1152]{1,0:T(8,128)(2,1)S(1)}, u32[]{:S(2)}, u32[]{:S(2)}) collective-permute-start(bf16[64,1152]{1,0:T(8,128)(2,1)S(1)} %get-tuple-element.126), channel_id=1, source_target_pairs={{0,2},{1,3},{2,0},{3,1},{4,6},{5,7},{6,4},{7,5},{8,10},{9,11},{10,... | collective-permute-start | bytes 442376 | tf_op jit(solution)/shard_map/ppermute | solution.py:580
  27.1 14.3 %collective-permute-start.7 = (bf16[64,1152]{1,0:T(8,128)(2,1)S(1)}, bf16[64,1152]{1,0:T(8,128)(2,1)S(1)}, u32[]{:S(2)}, u32[]{:S(2)}) collective-permute-start(bf16[64,1152]{1,0:T(8,128)(2,1)S(1)} %get-tuple-element.126), channel_id=1, source_target_pairs={{0,3},{1,0},{2,1},{3,2},{4,7},{5,4},{6,5},{7,6},{8,11},{9,8},{10,9... | collective-permute-start | bytes 442376 | tf_op jit(solution)/shard_map/ppermute | solution.py:580
  42.1 19.4 %collective-permute-start.8 = (bf16[3,160,1152]{2,1,0:T(8,128)(2,1)S(1)}, bf16[3,160,1152]{2,1,0:T(8,128)(2,1)S(1)}, u32[]{:S(2)}, u32[]{:S(2)}) collective-permute-start(bf16[3,160,1152]{2,1,0:T(8,128)(2,1)S(1)} %fusion.5), channel_id=1, source_target_pairs={{0,16},{4,12},{8,24},{12,4},{16,0},{20,28},{24,8},{28,20},{1,17},{... | collective-permute-start | bytes 3317768 | tf_op jit(solution)/shard_map/ppermute | solution.py:578
  43.4 16.6 %collective-permute-start.9 = (bf16[3,64,1152]{2,1,0:T(8,128)(2,1)S(1)}, bf16[3,64,1152]{2,1,0:T(8,128)(2,1)S(1)}, u32[]{:S(2)}, u32[]{:S(2)}) collective-permute-start(bf16[3,64,1152]{2,1,0:T(8,128)(2,1)S(1)} %maximum_add_fusion.refs_8_), channel_id=1, source_target_pairs={{0,8},{4,20},{8,0},{12,28},{16,24},{20,4},{24,16},{28,12},{1,9},{5... | collective-permute-start | bytes 1327112 | tf_op jit(solution)/shard_map/ppermute | solution.py:578
  43.5 4.6 %collective-permute-start.10 = (bf16[343,256]{1,0:T(8,128)(2,1)S(1)}, bf16[343,256]{1,0:T(8,128)(2,1)S(1)}, u32[]{:S(2)}, u32[]{:S(2)}) collective-permute-start(bf16[343,256]{1,0:T(8,128)(2,1)S(1)} %get-tuple-element.135), channel_id=1, source_target_pairs={{0,1},{1,2},{2,3},{3,0},{4,5},{5,6},{6,7},{7,4},{8,9},{9,10},{10,1... | collective-permute-start | bytes 526856 | tf_op jit(solution)/shard_map/ppermute | solution.py:580
  43.5 13.6 %collective-permute-start.11 = (bf16[343,256]{1,0:T(8,128)(2,1)S(1)}, bf16[343,256]{1,0:T(8,128)(2,1)S(1)}, u32[]{:S(2)}, u32[]{:S(2)}) collective-permute-start(bf16[343,256]{1,0:T(8,128)(2,1)S(1)} %get-tuple-element.137), channel_id=1, source_target_pairs={{0,2},{1,3},{2,0},{3,1},{4,6},{5,7},{6,4},{7,5},{8,10},{9,11},{10,... | collective-permute-start | bytes 526856 | tf_op jit(solution)/shard_map/ppermute | solution.py:580
  43.5 16.4 %collective-permute-start.12 = (bf16[343,256]{1,0:T(8,128)(2,1)S(1)}, bf16[343,256]{1,0:T(8,128)(2,1)S(1)}, u32[]{:S(2)}, u32[]{:S(2)}) collective-permute-start(bf16[343,256]{1,0:T(8,128)(2,1)S(1)} %get-tuple-element.139), channel_id=1, source_target_pairs={{0,3},{1,0},{2,1},{3,2},{4,7},{5,4},{6,5},{7,6},{8,11},{9,8},{10,9... | collective-permute-start | bytes 526856 | tf_op jit(solution)/shard_map/ppermute | solution.py:580
  61.5 7.7 %collective-permute-start.16 = (bf16[3,3,96,1040]{3,2,1,0:T(8,128)(2,1)S(1)}, bf16[3,3,96,1040]{3,2,1,0:T(8,128)(2,1)S(1)}, u32[]{:S(2)}, u32[]{:S(2)}) collective-permute-start(bf16[3,3,96,1040]{3,2,1,0:T(8,128)(2,1)S(1)} %pad_maximum_fusion.refs_5_.refs_6_), channel_id=1, source_target_pairs={{0,4},{4,0},{8,12},{12,8},{16,20},{20,16},{24,28},{28,24},{1,5},{5... | collective-permute-start | bytes 5391368 | tf_op jit(solution)/shard_map/ppermute | solution.py:578
  62.7 6.5 %collective-permute-start.13 = (bf16[3,160,1152]{2,1,0:T(8,128)(2,1)S(1)}, bf16[3,160,1152]{2,1,0:T(8,128)(2,1)S(1)}, u32[]{:S(2)}, u32[]{:S(2)}) collective-permute-start(bf16[3,160,1152]{2,1,0:T(8,128)(2,1)S(1)} %collective-permute-done.8.refs_6_.refs_10_.refs_7_), channel_id=1, source_target_pairs={{0,4},{4,0},{8,12},{12,8},{16,20},{20,16},{24,28},{28,24},{1,5},{5... | collective-permute-start | bytes 3317768 | tf_op jit(solution)/shard_map/ppermute | solution.py:578
  62.7 5.8 %collective-permute-start.14 = (bf16[3,64,1152]{2,1,0:T(8,128)(2,1)S(1)}, bf16[3,64,1152]{2,1,0:T(8,128)(2,1)S(1)}, u32[]{:S(2)}, u32[]{:S(2)}) collective-permute-start(bf16[3,64,1152]{2,1,0:T(8,128)(2,1)S(1)} %maximum_add_fusion.refs_8_), channel_id=1, source_target_pairs={{0,4},{4,0},{8,12},{12,8},{16,20},{20,16},{24,28},{28,24},{1,5},{5... | collective-permute-start | bytes 1327112 | tf_op jit(solution)/shard_map/ppermute | solution.py:578
  63.2 6.0 %collective-permute-start.15 = (bf16[3,64,1152]{2,1,0:T(8,128)(2,1)S(1)}, bf16[3,64,1152]{2,1,0:T(8,128)(2,1)S(1)}, u32[]{:S(2)}, u32[]{:S(2)}) collective-permute-start(bf16[3,64,1152]{2,1,0:T(8,128)(2,1)S(1)} %collective-permute-done.9.refs_9_), channel_id=1, source_target_pairs={{0,4},{4,0},{8,12},{12,8},{16,20},{20,16},{24,28},{28,24},{1,5},{5... | collective-permute-start | bytes 1327112 | tf_op jit(solution)/shard_map/ppermute | solution.py:578
  63.2 9.9 %collective-permute-start.17 = (bf16[3,64,1152]{2,1,0:T(8,128)(2,1)S(1)}, bf16[3,64,1152]{2,1,0:T(8,128)(2,1)S(1)}, u32[]{:S(2)}, u32[]{:S(2)}) collective-permute-start(bf16[3,64,1152]{2,1,0:T(8,128)(2,1)S(1)} %collective-permute-done.9.refs_9_), channel_id=1, source_target_pairs={{0,16},{4,12},{8,24},{12,4},{16,0},{20,28},{24,8},{28,20},{1,17},{... | collective-permute-start | bytes 1327112 | tf_op jit(solution)/shard_map/ppermute | solution.py:578
  75.0 7.5 %collective-permute-start.19 = (bf16[4,1152,256]{2,1,0:T(8,128)(2,1)S(1)}, bf16[4,1152,256]{2,1,0:T(8,128)(2,1)S(1)}, u32[]{:S(2)}, u32[]{:S(2)}) collective-permute-start(bf16[4,1152,256]{2,1,0:T(8,128)(2,1)S(1)} %get-tuple-element.152.refs_16_.x_all), channel_id=1, source_target_pairs={{0,4},{4,0},{8,12},{12,8},{16,20},{20,16},{24,28},{28,24},{1,5},{5... | collective-permute-start | bytes 7077896 | tf_op jit(solution)/shard_map/ppermute | solution.py:578
  79.7 2.7 %collective-permute-start.20 = (bf16[2048,256]{1,0:T(8,128)(2,1)S(1)}, bf16[2048,256]{1,0:T(8,128)(2,1)S(1)}, u32[]{:S(2)}, u32[]{:S(2)}) collective-permute-start(bf16[2048,256]{1,0:T(8,128)(2,1)S(1)} %get-tuple-element.157), channel_id=1, source_target_pairs={{0,4},{4,0},{8,12},{12,8},{16,20},{20,16},{24,28},{28,24},{1,5},{5... | collective-permute-start | bytes 3145736 | tf_op jit(solution)/shard_map/ppermute | solution.py:578
  85.4 14.7 %collective-permute-start.21 = (bf16[2,4,32,2176]{3,2,1,0:T(8,128)(2,1)S(1)}, bf16[2,4,32,2176]{3,2,1,0:T(8,128)(2,1)S(1)}, u32[]{:S(2)}, u32[]{:S(2)}) collective-permute-start(bf16[2,4,32,2176]{3,2,1,0:T(8,128)(2,1)S(1)} %get-tuple-element.160), channel_id=1, source_target_pairs={{0,8},{4,20},{8,0},{12,28},{16,24},{20,4},{24,16},{28,12},{1,9},{5... | collective-permute-start | bytes 3342344 | tf_op jit(solution)/shard_map/ppermute | solution.py:578
  91.8 5.2 %collective-permute-start.23 = (bf16[272,256]{1,0:T(8,128)(2,1)S(1)}, bf16[272,256]{1,0:T(8,128)(2,1)S(1)}, u32[]{:S(2)}, u32[]{:S(2)}) collective-permute-start(bf16[272,256]{1,0:T(8,128)(2,1)S(1)} %get-tuple-element.168), channel_id=1, source_target_pairs={{0,1},{1,2},{2,3},{3,0},{4,5},{5,6},{6,7},{7,4},{8,9},{9,10},{10,1... | collective-permute-start | bytes 417800 | tf_op jit(solution)/shard_map/ppermute | solution.py:580
  91.8 10.1 %collective-permute-start.26 = (bf16[2,528,256]{2,1,0:T(8,128)(2,1)S(1)}, bf16[2,528,256]{2,1,0:T(8,128)(2,1)S(1)}, u32[]{:S(2)}, u32[]{:S(2)}) collective-permute-start(bf16[2,528,256]{2,1,0:T(8,128)(2,1)S(1)} %get-tuple-element.173), channel_id=1, source_target_pairs={{0,4},{4,0},{8,12},{12,8},{16,20},{20,16},{24,28},{28,24},{1,5},{5... | collective-permute-start | bytes 1622024 | tf_op jit(solution)/shard_map/ppermute | solution.py:578
  100.1 14.6 %collective-permute-start.25 = (bf16[2,4,32,1152]{3,2,1,0:T(8,128)(2,1)S(1)}, bf16[2,4,32,1152]{3,2,1,0:T(8,128)(2,1)S(1)}, u32[]{:S(2)}, u32[]{:S(2)}) collective-permute-start(bf16[2,4,32,1152]{3,2,1,0:T(8,128)(2,1)S(1)} %get-tuple-element.171), channel_id=1, source_target_pairs={{0,8},{4,20},{8,0},{12,28},{16,24},{20,4},{24,16},{28,12},{1,9},{5... | collective-permute-start | bytes 1769480 | tf_op jit(solution)/shard_map/ppermute | solution.py:578
  100.8 14.0 %collective-permute-start.24 = (bf16[4,32,2176]{2,1,0:T(8,128)(2,1)S(1)}, bf16[4,32,2176]{2,1,0:T(8,128)(2,1)S(1)}, u32[]{:S(2)}, u32[]{:S(2)}) collective-permute-start(bf16[4,32,2176]{2,1,0:T(8,128)(2,1)S(1)} %fusion.3), channel_id=1, source_target_pairs={{0,16},{4,12},{8,24},{12,4},{16,0},{20,28},{24,8},{28,20},{1,17},{... | collective-permute-start | bytes 1671176 | tf_op jit(solution)/shard_map/ppermute | solution.py:578
  101.1 9.0 %collective-permute-start.27 = (bf16[272,256]{1,0:T(8,128)(2,1)S(1)}, bf16[272,256]{1,0:T(8,128)(2,1)S(1)}, u32[]{:S(2)}, u32[]{:S(2)}) collective-permute-start(bf16[272,256]{1,0:T(8,128)(2,1)S(1)} %get-tuple-element.177), channel_id=1, source_target_pairs={{0,2},{1,3},{2,0},{3,1},{4,6},{5,7},{6,4},{7,5},{8,10},{9,11},{10,... | collective-permute-start | bytes 417800 | tf_op jit(solution)/shard_map/ppermute | solution.py:580
  102.0 8.6 %collective-permute-start.28 = (bf16[272,256]{1,0:T(8,128)(2,1)S(1)}, bf16[272,256]{1,0:T(8,128)(2,1)S(1)}, u32[]{:S(2)}, u32[]{:S(2)}) collective-permute-start(bf16[272,256]{1,0:T(8,128)(2,1)S(1)} %get-tuple-element.178), channel_id=1, source_target_pairs={{0,3},{1,0},{2,1},{3,2},{4,7},{5,4},{6,5},{7,6},{8,11},{9,8},{10,9... | collective-permute-start | bytes 417800 | tf_op jit(solution)/shard_map/ppermute | solution.py:580
  114.8 16.0 %collective-permute-start.29 = (bf16[4,32,1152]{2,1,0:T(8,128)(2,1)S(1)}, bf16[4,32,1152]{2,1,0:T(8,128)(2,1)S(1)}, u32[]{:S(2)}, u32[]{:S(2)}) collective-permute-start(bf16[4,32,1152]{2,1,0:T(8,128)(2,1)S(1)} %fusion.7), channel_id=1, source_target_pairs={{0,16},{4,12},{8,24},{12,4},{16,0},{20,28},{24,8},{28,20},{1,17},{... | collective-permute-start | bytes 884744 | tf_op jit(solution)/shard_map/ppermute | solution.py:578
  114.9 19.1 %collective-permute-start.30 = (bf16[2,4,64,1152]{3,2,1,0:T(8,128)(2,1)S(1)}, bf16[2,4,64,1152]{3,2,1,0:T(8,128)(2,1)S(1)}, u32[]{:S(2)}, u32[]{:S(2)}) collective-permute-start(bf16[2,4,64,1152]{3,2,1,0:T(8,128)(2,1)S(1)} %get-tuple-element.182), channel_id=1, source_target_pairs={{0,8},{4,20},{8,0},{12,28},{16,24},{20,4},{24,16},{28,12},{1,9},{5... | collective-permute-start | bytes 3538952 | tf_op jit(solution)/shard_map/ppermute | solution.py:578
  117.5 4.3 %collective-permute-start.31 = (bf16[32,2176]{1,0:T(8,128)(2,1)S(1)}, bf16[32,2176]{1,0:T(8,128)(2,1)S(1)}, u32[]{:S(2)}, u32[]{:S(2)}) collective-permute-start(bf16[32,2176]{1,0:T(8,128)(2,1)S(1)} %get-tuple-element.237), channel_id=1, source_target_pairs={{0,1},{1,2},{2,3},{3,0},{4,5},{5,6},{6,7},{7,4},{8,9},{9,10},{10,1... | collective-permute-start | bytes 417800 | tf_op jit(solution)/shard_map/ppermute | solution.py:580
  117.6 10.9 %collective-permute-start.32 = (bf16[32,2176]{1,0:T(8,128)(2,1)S(1)}, bf16[32,2176]{1,0:T(8,128)(2,1)S(1)}, u32[]{:S(2)}, u32[]{:S(2)}) collective-permute-start(bf16[32,2176]{1,0:T(8,128)(2,1)S(1)} %get-tuple-element.236), channel_id=1, source_target_pairs={{0,2},{1,3},{2,0},{3,1},{4,6},{5,7},{6,4},{7,5},{8,10},{9,11},{10,... | collective-permute-start | bytes 417800 | tf_op jit(solution)/shard_map/ppermute | solution.py:580
  117.7 13.1 %collective-permute-start.33 = (bf16[32,2176]{1,0:T(8,128)(2,1)S(1)}, bf16[32,2176]{1,0:T(8,128)(2,1)S(1)}, u32[]{:S(2)}, u32[]{:S(2)}) collective-permute-start(bf16[32,2176]{1,0:T(8,128)(2,1)S(1)} %get-tuple-element.235), channel_id=1, source_target_pairs={{0,3},{1,0},{2,1},{3,2},{4,7},{5,4},{6,5},{7,6},{8,11},{9,8},{10,9... | collective-permute-start | bytes 417800 | tf_op jit(solution)/shard_map/ppermute | solution.py:580
  134.2 10.6 %collective-permute-start.34 = (bf16[4,64,1152]{2,1,0:T(8,128)(2,1)S(1)}, bf16[4,64,1152]{2,1,0:T(8,128)(2,1)S(1)}, u32[]{:S(2)}, u32[]{:S(2)}) collective-permute-start(bf16[4,64,1152]{2,1,0:T(8,128)(2,1)S(1)} %fusion.2), channel_id=1, source_target_pairs={{0,16},{4,12},{8,24},{12,4},{16,0},{20,28},{24,8},{28,20},{1,17},{... | collective-permute-start | bytes 1769480 | tf_op jit(solution)/shard_map/ppermute | solution.py:578
  134.9 9.7 %collective-permute-start.35 = (bf16[32,2176]{1,0:T(8,128)(2,1)S(1)}, bf16[32,2176]{1,0:T(8,128)(2,1)S(1)}, u32[]{:S(2)}, u32[]{:S(2)}) collective-permute-start(bf16[32,2176]{1,0:T(8,128)(2,1)S(1)} %fusion.12.refs_0_), channel_id=1, source_target_pairs={{0,8},{4,20},{8,0},{12,28},{16,24},{20,4},{24,16},{28,12},{1,9},{5... | collective-permute-start | bytes 417800 | tf_op jit(solution)/shard_map/ppermute | solution.py:578
  136.6 3.6 %collective-permute-start.36 = (bf16[32,1152]{1,0:T(8,128)(2,1)S(1)}, bf16[32,1152]{1,0:T(8,128)(2,1)S(1)}, u32[]{:S(2)}, u32[]{:S(2)}) collective-permute-start(bf16[32,1152]{1,0:T(8,128)(2,1)S(1)} %get-tuple-element.240), channel_id=1, source_target_pairs={{0,1},{1,2},{2,3},{3,0},{4,5},{5,6},{6,7},{7,4},{8,9},{9,10},{10,1... | collective-permute-start | bytes 221192 | tf_op jit(solution)/shard_map/ppermute | solution.py:580
  136.7 4.2 %collective-permute-start.37 = (bf16[32,1152]{1,0:T(8,128)(2,1)S(1)}, bf16[32,1152]{1,0:T(8,128)(2,1)S(1)}, u32[]{:S(2)}, u32[]{:S(2)}) collective-permute-start(bf16[32,1152]{1,0:T(8,128)(2,1)S(1)} %get-tuple-element.239), channel_id=1, source_target_pairs={{0,2},{1,3},{2,0},{3,1},{4,6},{5,7},{6,4},{7,5},{8,10},{9,11},{10,... | collective-permute-start | bytes 221192 | tf_op jit(solution)/shard_map/ppermute | solution.py:580
  136.9 7.8 %collective-permute-start.38 = (bf16[32,1152]{1,0:T(8,128)(2,1)S(1)}, bf16[32,1152]{1,0:T(8,128)(2,1)S(1)}, u32[]{:S(2)}, u32[]{:S(2)}) collective-permute-start(bf16[32,1152]{1,0:T(8,128)(2,1)S(1)} %get-tuple-element.238), channel_id=1, source_target_pairs={{0,3},{1,0},{2,1},{3,2},{4,7},{5,4},{6,5},{7,6},{8,11},{9,8},{10,9... | collective-permute-start | bytes 221192 | tf_op jit(solution)/shard_map/ppermute | solution.py:580
  145.0 7.1 %collective-permute-start.41 = (bf16[64,1152]{1,0:T(8,128)(2,1)S(1)}, bf16[64,1152]{1,0:T(8,128)(2,1)S(1)}, u32[]{:S(2)}, u32[]{:S(2)}) collective-permute-start(bf16[64,1152]{1,0:T(8,128)(2,1)S(1)} %get-tuple-element.234), channel_id=1, source_target_pairs={{0,1},{1,2},{2,3},{3,0},{4,5},{5,6},{6,7},{7,4},{8,9},{9,10},{10,1... | collective-permute-start | bytes 442376 | tf_op jit(solution)/shard_map/ppermute | solution.py:580
  145.1 12.2 %collective-permute-start.42 = (bf16[64,1152]{1,0:T(8,128)(2,1)S(1)}, bf16[64,1152]{1,0:T(8,128)(2,1)S(1)}, u32[]{:S(2)}, u32[]{:S(2)}) collective-permute-start(bf16[64,1152]{1,0:T(8,128)(2,1)S(1)} %get-tuple-element.233), channel_id=1, source_target_pairs={{0,2},{1,3},{2,0},{3,1},{4,6},{5,7},{6,4},{7,5},{8,10},{9,11},{10,... | collective-permute-start | bytes 442376 | tf_op jit(solution)/shard_map/ppermute | solution.py:580
  146.7 13.8 %collective-permute-start.43 = (bf16[64,1152]{1,0:T(8,128)(2,1)S(1)}, bf16[64,1152]{1,0:T(8,128)(2,1)S(1)}, u32[]{:S(2)}, u32[]{:S(2)}) collective-permute-start(bf16[64,1152]{1,0:T(8,128)(2,1)S(1)} %get-tuple-element.232), channel_id=1, source_target_pairs={{0,3},{1,0},{2,1},{3,2},{4,7},{5,4},{6,5},{7,6},{8,11},{9,8},{10,9... | collective-permute-start | bytes 442376 | tf_op jit(solution)/shard_map/ppermute | solution.py:580
  147.3 13.2 %collective-permute-start.39 = (bf16[2,32,2176]{2,1,0:T(8,128)(2,1)S(1)}, bf16[2,32,2176]{2,1,0:T(8,128)(2,1)S(1)}, u32[]{:S(2)}, u32[]{:S(2)}) collective-permute-start(bf16[2,32,2176]{2,1,0:T(8,128)(2,1)S(1)} %pad_maximum_fusion.6), channel_id=1, source_target_pairs={{0,16},{4,12},{8,24},{12,4},{16,0},{20,28},{24,8},{28,20},{1,17},{... | collective-permute-start | bytes 835592 | tf_op jit(solution)/shard_map/ppermute | solution.py:578
  148.6 3.6 %collective-permute-start.40 = (bf16[32,1152]{1,0:T(8,128)(2,1)S(1)}, bf16[32,1152]{1,0:T(8,128)(2,1)S(1)}, u32[]{:S(2)}, u32[]{:S(2)}) collective-permute-start(bf16[32,1152]{1,0:T(8,128)(2,1)S(1)} %fusion.14.refs_0_), channel_id=1, source_target_pairs={{0,8},{4,20},{8,0},{12,28},{16,24},{20,4},{24,16},{28,12},{1,9},{5... | collective-permute-start | bytes 221192 | tf_op jit(solution)/shard_map/ppermute | solution.py:578
  160.5 6.7 %collective-permute-start.46 = (bf16[4,32,2176]{2,1,0:T(8,128)(2,1)S(1)}, bf16[4,32,2176]{2,1,0:T(8,128)(2,1)S(1)}, u32[]{:S(2)}, u32[]{:S(2)}) collective-permute-start(bf16[4,32,2176]{2,1,0:T(8,128)(2,1)S(1)} %pad_maximum_fusion.3), channel_id=1, source_target_pairs={{0,4},{4,0},{8,12},{12,8},{16,20},{20,16},{24,28},{28,24},{1,5},{5... | collective-permute-start | bytes 1671176 | tf_op jit(solution)/shard_map/ppermute | solution.py:578
  161.1 4.4 %collective-permute-start.45 = (bf16[2,32,1152]{2,1,0:T(8,128)(2,1)S(1)}, bf16[2,32,1152]{2,1,0:T(8,128)(2,1)S(1)}, u32[]{:S(2)}, u32[]{:S(2)}) collective-permute-start(bf16[2,32,1152]{2,1,0:T(8,128)(2,1)S(1)} %pad_maximum_fusion.7), channel_id=1, source_target_pairs={{0,16},{4,12},{8,24},{12,4},{16,0},{20,28},{24,8},{28,20},{1,17},{... | collective-permute-start | bytes 442376 | tf_op jit(solution)/shard_map/ppermute | solution.py:578
  162.4 4.8 %collective-permute-start.44 = (bf16[64,1152]{1,0:T(8,128)(2,1)S(1)}, bf16[64,1152]{1,0:T(8,128)(2,1)S(1)}, u32[]{:S(2)}, u32[]{:S(2)}) collective-permute-start(bf16[64,1152]{1,0:T(8,128)(2,1)S(1)} %fusion.9.refs_0_), channel_id=1, source_target_pairs={{0,8},{4,20},{8,0},{12,28},{16,24},{20,4},{24,16},{28,12},{1,9},{5... | collective-permute-start | bytes 442376 | tf_op jit(solution)/shard_map/ppermute | solution.py:578
  167.3 4.5 %collective-permute-start.48 = (bf16[4,32,1152]{2,1,0:T(8,128)(2,1)S(1)}, bf16[4,32,1152]{2,1,0:T(8,128)(2,1)S(1)}, u32[]{:S(2)}, u32[]{:S(2)}) collective-permute-start(bf16[4,32,1152]{2,1,0:T(8,128)(2,1)S(1)} %pad_maximum_fusion.5), channel_id=1, source_target_pairs={{0,4},{4,0},{8,12},{12,8},{16,20},{20,16},{24,28},{28,24},{1,5},{5... | collective-permute-start | bytes 884744 | tf_op jit(solution)/shard_map/ppermute | solution.py:578
  167.7 6.0 %collective-permute-start.47 = (bf16[2,64,1152]{2,1,0:T(8,128)(2,1)S(1)}, bf16[2,64,1152]{2,1,0:T(8,128)(2,1)S(1)}, u32[]{:S(2)}, u32[]{:S(2)}) collective-permute-start(bf16[2,64,1152]{2,1,0:T(8,128)(2,1)S(1)} %pad_maximum_fusion.4), channel_id=1, source_target_pairs={{0,16},{4,12},{8,24},{12,4},{16,0},{20,28},{24,8},{28,20},{1,17},{... | collective-permute-start | bytes 884744 | tf_op jit(solution)/shard_map/ppermute | solution.py:578
  173.8 2.7 %collective-permute-start.49 = (bf16[4,64,1152]{2,1,0:T(8,128)(2,1)S(1)}, bf16[4,64,1152]{2,1,0:T(8,128)(2,1)S(1)}, u32[]{:S(2)}, u32[]{:S(2)}) collective-permute-start(bf16[4,64,1152]{2,1,0:T(8,128)(2,1)S(1)} %pad_maximum_fusion.2), channel_id=1, source_target_pairs={{0,4},{4,0},{8,12},{12,8},{16,20},{20,16},{24,28},{28,24},{1,5},{5... | collective-permute-start | bytes 1769480 | tf_op jit(solution)/shard_map/ppermute | solution.py:578
  (13 other events, 125.1 us)

commit v4 on v3

--- a/solution.py
+++ b/solution.py
@@ -15,7 +15,7 @@
 SHARE = 32
 HALF = MAIN // 2
 LANES = 128
-REST = 32
+APART = 64
 LOSS = 24
 COUNT = 16
 VMEM = pl.BlockSpec(memory_space=pltpu.VMEM)
@@ -129,9 +129,8 @@
 
     own1[:, 0:depth] = weight1[...].T
     own1[:, depth:] = jnp.zeros((size, full - depth), BF16)
-    out[0:SHARE, :] = own1[rows_at(own_row, SHARE), :]
-    out[SHARE:, 0 : weight2.shape[1]] = weight2[rows_at(own_row, SHARE), :]
-    out[SHARE:, weight2.shape[1] :] = jnp.zeros((SHARE, full - weight2.shape[1]), BF16)
+    out[:, 0:full] = own1[rows_at(own_row, SHARE), :]
+    out[:, full:] = weight2[rows_at(own_row, SHARE), :]
 
     first = 16 * len(rest)
     for turn in range(blocks):
@@ -163,12 +162,16 @@
 
 
 def place_cross(idx, weight, own, slices, blocks, layer, pad):
+    layers, depth = weight.shape[0], weight.shape[2]
+    low = depth // LANES * LANES
     weight[layer, rows_at(idx[0] * pad, MAIN), :] = own[layer, 0:MAIN, :]
-    at = SHARE * layer
+    tail = layers * low + (depth - low) * layer
     for turn in range(1, blocks):
         base = block_of(idx, turn, blocks) * pad
         for offset, piece in zip(places(idx), slices):
-            weight[layer, rows_at(base + offset, SHARE), :] = piece[turn - 1, at : at + SHARE, 0 : weight.shape[2]]
+            rows = rows_at(base + offset, SHARE)
+            weight[layer, rows, 0:low] = piece[turn - 1, :, low * layer : low * (layer + 1)]
+            weight[layer, rows, low:] = piece[turn - 1, :, tail : tail + depth - low]
 
 
 def place_rest(idx, weight, pieces, lines, tail, layers, left, pad):
@@ -244,9 +247,7 @@
         base = block_of(idx, turn, blocks) * size
         for offset, piece in zip(places(idx), slices):
             rows = rows_at(base + offset, SHARE)
-            start = piece.shape[1] - 2 * SHARE
-            tower[rows, 0:full] = piece[turn - 1, start : start + SHARE, :]
-            tower[rows, full:] = piece[turn - 1, start + SHARE :, 0:hidden]
+            tower[rows, :] = piece[turn - 1, :, piece.shape[2] - tower.shape[1] :]
     parts = [slice(size * block, size * (block + 1)) for block in range(blocks)]
     columns = []
     for block in range(blocks):
@@ -266,8 +267,8 @@
     half = BUCKETS // 2
     tally = jnp.zeros((half, LANES), F32)
     for piece in slices:
-        start = piece.shape[1] - 2 * SHARE
-        tally += piece[0 : half // SHARE, start : start + SHARE, low:].astype(F32).reshape(half, LANES)
+        at = piece.shape[2] - tower.shape[1] + low
+        tally += piece[0 : half // SHARE, :, at : at + LANES].astype(F32).reshape(half, LANES)
     count = jnp.concatenate([tally, pltpu.roll(tally, LANES - 2 * (fields + 1), 1)], axis=0)
     high = count[:, COUNT : COUNT + fields + 1]
     count = 256.0 * high + count[:, COUNT + fields + 1 : COUNT + 2 * (fields + 1)]
@@ -404,11 +405,12 @@
 
 
 def cross_grads(idx, x_all, x_far, dz, rest, dz_far, near_out, far_out, send_out, *refs, blocks, base, pad, depth):
-    x_cat, dz_in, far_in, rest_in, lhs, few, near, away, send, sems = refs
+    x_cat, dz_in, far_in, rest_in, lhs, few, extra, tiles, near, away, send, sems = refs
     part = dz.shape[2]
     low = depth // LANES * LANES
     groups = -(-depth // MAIN)
     count = dz_far.shape[0]
+    left = rest_in.shape[1] // blocks
     copies = Copies(sems)
     first = []
     for layer in reversed(range(count)):
@@ -424,18 +426,27 @@
     few[...] = jnp.zeros_like(few)
     order = [(where, slot) for where in range(4) for slot in range(blocks)]
     shares = relative(idx)
+    lane = lane_of((HALF, LANES))
+    bias = depth - low
+    span = left * groups
     for layer, started in zip(reversed(range(count)), first):
         wait(*started)
-        extra = jnp.zeros((HALF, LANES), F32)
+        value = jnp.zeros((HALF, LANES), F32)
+        near_rest = rest_in[layer].astype(F32)
+        far_rest = far_in[layer, HALF * blocks :, :].astype(F32)
         for group in range(groups):
-            lines = slice(REST + 16 * group, REST + 16 * (group + 1))
-            few[group, lines, 0:part] = rest_in[layer]
-            few[group, lines, part:] = far_in[layer, HALF * blocks :, :]
+            for block in range(blocks):
+                lines = slice(span * block + left * group, span * block + left * (group + 1))
+                few[group, lines, 0:part] = near_rest[left * block : left * (block + 1), :]
+                few[group, lines, part:] = far_rest[left * block : left * (block + 1), :]
             if MAIN * (group + 1) <= depth:
                 rows = rows_at(MAIN * group + idx[1] * HALF, HALF)
             else:
                 rows = slice(MAIN * group, MAIN * group + HALF)
-            extra += dot(x_cat[layer, rows, :], few[group], NT)
+            value += dot(x_cat[layer, rows, :], few[group].astype(BF16), NT)
+        inside = (lane > bias) & (lane <= bias + span)
+        for block in range(blocks):
+            extra[block] = jnp.where(inside, pltpu.roll(value, (bias + 1 - span * block) % LANES, 1), 0.0)
         for at, (where, slot) in enumerate(order):
             block = block_ahead(idx, slot, blocks)
             rows = rows_at(pad * block + idx[1] * HALF + SHARE * shares[where], SHARE)
@@ -444,16 +455,19 @@
             lhs[here, 0:part] = dz_in[layer, rows, :]
             lhs[here, part:] = far_in[layer, lines, :]
         grad = dot(lhs[...], x_cat[layer], NT)
-        lines = slice(SHARE * layer, SHARE * (layer + 1))
-        wide = [extra[SHARE * q : SHARE * (q + 1), :] for q in range(4)]
         for at, (where, slot) in enumerate(order):
             target = (near, away, send.at[0], send.at[1])[where].at[slot]
             here = slice(SHARE * at, SHARE * (at + 1))
-            target[lines, 0:low] = grad[here, 0:low].astype(BF16)
-            more = wide[0]
-            for q in range(1, 4):
-                more = jnp.where(shares[where] == q, wide[q], more)
-            target[lines, low:] = (grad[here, low:] + more).astype(BF16)
+            target[:, low * layer : low * (layer + 1)] = grad[here, 0:low].astype(BF16)
+            tile = grad[here, low:] + extra[block_ahead(idx, slot, blocks), rows_at(SHARE * shares[where], SHARE), :]
+            if layer < count - 1:
+                tile = tiles[here, :] + (pltpu.roll(tile, APART * layer, 1) if layer else tile)
+            elif layer:
+                tile = pltpu.roll(tile, APART * layer, 1)
+            if layer:
+                tiles[here, :] = tile
+            else:
+                target[:, low * count :] = tile.astype(BF16)
     wait(copies.start(send, send_out), copies.start(near, near_out), copies.start(away, far_out))
 
 
@@ -517,18 +531,18 @@
     last = []
     if more:
         bias_out[count:, :] = before[1][...]
+    for offset, piece in zip(places(idx), slices):
+        lines[rows_at(offset, SHARE), :] = piece[:, low * count :].astype(F32)
+    turned = lines[...].T
     for layer in range(count):
-        rows = slice(SHARE * layer, SHARE * (layer + 1))
         for offset, piece in zip(places(idx), slices):
-            held[layer, rows_at(offset, SHARE), :] = piece[rows, 0:depth].astype(F32)
-            lines[rows_at(offset, SHARE), :] = piece[rows, low:].astype(F32)
-        turned = lines[...].T
-        bias_out[layer : layer + 1, 0:MAIN] = turned[depth - low : depth - low + 1, :]
+            rows = rows_at(offset, SHARE)
+            held[layer, rows, 0:low] = piece[:, low * layer : low * (layer + 1)].astype(F32)
+        held[layer, 0:MAIN, low:] = lines[:, APART * layer : APART * layer + depth - low]
+        bias = APART * layer + depth - low
+        bias_out[layer : layer + 1, 0:MAIN] = turned[bias : bias + 1, :]
         for group in range(-(-depth // MAIN)):
-            rest = jnp.zeros((left, MAIN), F32)
-            for block in range(blocks):
-                at = REST + 16 * group + left * block
-                rest = jnp.where(idx[0] == block, turned[at : at + left, :], rest)
+            rest = turned[bias + 1 + left * group : bias + 1 + left * (group + 1), :]
             stop = min(depth, MAIN * (group + 1)) - MAIN * group
             held[layer, MAIN:width, MAIN * group : MAIN * group + stop] = rest[:, 0:stop]
         last.append(copies.start(held.at[layer], out.at[base + layer]))
@@ -582,7 +596,9 @@
 
     own_row = core * HALF + plane * SHARE
     cross_send = lax.dynamic_slice(cross_weight, (0, own_row, 0), (layers, SHARE, depth))
-    cross_send = cross_send.reshape(layers * SHARE, depth)
+    low = depth // LANES * LANES
+    fill = jnp.zeros((SHARE, LANES - layers * (depth - low)), BF16)
+    cross_send = jnp.concatenate([rows[:, :low] for rows in cross_send] + [rows[:, low:] for rows in cross_send] + [fill], axis=1)
     cross_turned = turns([cross_send] * (blocks - 1))
     vectors = jnp.stack([tower1_bias, head_weight, tower2_bias])
     wide = full + hidden
@@ -591,7 +607,7 @@
         functools.partial(pack_rest, blocks=blocks),
         tuple(
             [
-                shape((2 * SHARE, full), BF16),
+                shape((SHARE, wide), BF16),
                 shape((size, full), BF16),
                 shape(((blocks - 1) * SHARE, LANES), BF16),
             ]
@@ -614,7 +630,7 @@
     )
     for perm in others:
         tally = tally + hop(tally, perm)
-    tally = jnp.pad(tally.reshape(blocks - 1, SHARE, LANES), ((0, 0), (0, SHARE), (full - LANES, 0)))
+    tally = jnp.pad(tally.reshape(blocks - 1, SHARE, LANES), ((0, 0), (0, 0), (full - LANES, hidden)))
 
     join = lambda *values: lax.optimization_barrier(values)
     cross_mine = jnp.stack(cross_turned)
@@ -625,7 +641,7 @@
 
     pieces = [chunks[0]] + turns([after(chunk, tower_turned[0]) for chunk in chunks[1:]])
     tower_mine = jnp.stack(tower_turned) + tally
-    both = jnp.concatenate([jnp.pad(cross_one, ((0, 0), (0, 0), (0, full - depth))), tower_mine], axis=1)
+    both = jnp.concatenate([cross_one, tower_mine], axis=2)
     tower_one, both = hop(tower_mine, first), hop(both, second)
     cross_near = jnp.stack([cross_mine, cross_one, cross_two])
     both, tower_one, cross_near, *pieces = join(both, tower_one, cross_near, *pieces)
@@ -761,14 +777,16 @@
     def cross_parts_of(base, count, far, start):
         return grads(
             functools.partial(cross_grads, blocks=blocks, base=base, pad=pad, depth=depth),
-            (blocks, count * SHARE, full),
+            (blocks, SHARE, count * low + LANES),
             [
                 vmem((count, full, 2 * part), BF16),
                 vmem((count, flat, part), BF16),
                 vmem((count, HALF * blocks + 16, part), BF16),
                 vmem((count, 16, part), BF16),
                 vmem((HALF * blocks, 2 * part), BF16),
-                vmem((-(-depth // MAIN), LANES, 2 * part), BF16),
+                vmem((-(-depth // MAIN), LANES, 2 * part), F32),
+                vmem((blocks, HALF, LANES), F32),
+                vmem((HALF * blocks, LANES), F32),
             ],
             [start, x_all, x_far, dz, dz_rest, far],
             5 * count + 3,

time: 180 us -> 175 us (0.972)
  local copies, waits for them, and re-layouts: 11.1 us -> 5.03 us
  starting transfers between devices: 33.9 us -> 36.5 us
    unnamed x22 -> x26, local copies, waits for them, and re-layouts: 6.92 us -> 2.58 us
    ppermute x21, starting transfers between devices: 13.2 us -> 16.4 us  [per_device(): lax.ppermute(value, 'mp', turn_by(r + 1))]
    ppermute x29, waiting for transfers between devices: 31.3 us -> 28.5 us  [per_device(): hop = lambda value, perm: lax.ppermute(value, 'dp', perm)]
    another operation x3, local copies, waits for them, and re-layouts: 1.98 us -> 0.01 us  [per_device(): vectors = jnp.stack([tower1_bias, head_weight, tower2_bias])]
  transfers between devices with their start and end apart: 50 -> 50, of which waited for: 35 -> 33; matrix products, arithmetic and copies ran while one was open for 2% -> 1% of each run, Pallas kernels for 16% -> 16%
where the time goes in v4:
time: 175 us
  waiting for transfers between devices  96.1 us (55%)
  starting transfers between devices  36.5 us (21%)
  Pallas kernels  34.3 us (20%)
  local copies, waits for them, and re-layouts  5.03 us (3%)
  other arithmetic  1.81 us (1%)
    ppermute x21, waiting for transfers between devices, per_device(): lax.ppermute(value, 'mp', turn_by(r + 1))  67.5 us
    pallas_call x11, Pallas kernels, call(): pl.pallas_call(kernel, out_shape=outs, in_specs=[SMEM] + specs, out_specs...  34.3 us
    ppermute x29, waiting for transfers between devices, per_device(): hop = lambda value, perm: lax.ppermute(value, 'dp', perm)  28.5 us
    ppermute x29, starting transfers between devices, per_device(): hop = lambda value, perm: lax.ppermute(value, 'dp', perm)  20.2 us
    ppermute x21, starting transfers between devices, per_device(): lax.ppermute(value, 'mp', turn_by(r + 1))  16.4 us
  transfers between devices with their start and end apart: 50, of which 33 were waited for; matrix products, arithmetic and copies ran while one was open for 1% of the time, Pallas kernels for 16%

profile of v4, /device:TPU:9, one launch (start us, length us, event | category | flops | bytes accessed | tf_op | source)
XLA Modules:
  0.0 175.0 jit_solution(2678690448104860850)
XLA Ops:
  2.1 1.3 collective-permute-start
  4.5 1.4 collective-permute-start.2
  6.1 1.5 copy-done
  8.6 2.9 %shard_map.202 = (bf16[32,2176]{1,0:T(8,128)(2,1)S(1)}, bf16[256,1152]{1,0:T(8,128)(2,1)S(1)}, bf16[96,128]{1,0:T(8,128)(2,1)S(1)}, bf16[343,256]{1,0:T(8,128)(2...) custom-call(s32[4]{0:T(128)S(1)} %pad_add_fusion.idx, ...), custom_call_target="tpu_custom_call" | custom-call | bytes 2097152 | tf_op jit(solution)/shard_map/pallas_call | solution.py:45
  11.5 8.8 %collective-permute-done.1 = bf16[32,3200]{1,0:T(8,128)(2,1)S(1)} collective-permute-done((bf16[32,3200]{1,0:T(8,128)(2,1)S(1)}, bf16[32,3200]{1,0:T(8,128)(2,1)S(1)}, u32[]{:S(2)}, u32[]{:S(2)}) %collective-permute-start.1) | collective-permute-done | bytes 204832 | tf_op jit(solution)/shard_map/ppermute | solution.py:594
  20.3 2.8 %collective-permute-done.2 = bf16[32,3200]{1,0:T(8,128)(2,1)S(1)} collective-permute-done((bf16[32,3200]{1,0:T(8,128)(2,1)S(1)}, bf16[32,3200]{1,0:T(8,128)(2,1)S(1)}, u32[]{:S(2)}, u32[]{:S(2)}) %collective-permute-start.2) | collective-permute-done | bytes 204832 | tf_op jit(solution)/shard_map/ppermute | solution.py:594
  23.3 1.3 collective-permute-start.3
  26.0 1.5 collective-permute-start.7
  27.5 2.5 %collective-permute-done.5 = bf16[32,2176]{1,0:T(8,128)(2,1)S(1)} collective-permute-done((bf16[32,2176]{1,0:T(8,128)(2,1)S(1)}, bf16[32,2176]{1,0:T(8,128)(2,1)S(1)}, u32[]{:S(2)}, u32[]{:S(2)}) %collective-permute-start.5) | collective-permute-done | bytes 139296 | tf_op jit(solution)/shard_map/ppermute | solution.py:594
  30.0 6.8 %collective-permute-done.6 = bf16[32,2176]{1,0:T(8,128)(2,1)S(1)} collective-permute-done((bf16[32,2176]{1,0:T(8,128)(2,1)S(1)}, bf16[32,2176]{1,0:T(8,128)(2,1)S(1)}, u32[]{:S(2)}, u32[]{:S(2)}) %collective-permute-start.6) | collective-permute-done | bytes 139296 | tf_op jit(solution)/shard_map/ppermute | solution.py:594
  36.8 2.9 %collective-permute-done.7 = bf16[32,2176]{1,0:T(8,128)(2,1)S(1)} collective-permute-done((bf16[32,2176]{1,0:T(8,128)(2,1)S(1)}, bf16[32,2176]{1,0:T(8,128)(2,1)S(1)}, u32[]{:S(2)}, u32[]{:S(2)}) %collective-permute-start.7) | collective-permute-done | bytes 139296 | tf_op jit(solution)/shard_map/ppermute | solution.py:594
  40.0 1.2 collective-permute-start.8
  41.4 1.5 collective-permute-start.12
  43.1 2.9 %collective-permute-done.10.refs_1_.refs_3_.refs_2_ = bf16[343,256]{1,0:T(8,128)(2,1)S(1)} collective-permute-done((bf16[343,256]{1,0:T(8,128)(2,1)S(1)}, bf16[343,256]{1,0:T(8,128)(2,1)S(1)}, u32[]{:S(2)}, u32[]{:S(2)}) %collective-permute-start.10) | collective-permute-done | bytes 175648 | tf_op jit(solution)/shard_map/ppermute | solution.py:594
  45.9 9.0 %collective-permute-done.11.refs_2_.refs_4_.refs_3_ = bf16[343,256]{1,0:T(8,128)(2,1)S(1)} collective-permute-done((bf16[343,256]{1,0:T(8,128)(2,1)S(1)}, bf16[343,256]{1,0:T(8,128)(2,1)S(1)}, u32[]{:S(2)}, u32[]{:S(2)}) %collective-permute-start.11) | collective-permute-done | bytes 175648 | tf_op jit(solution)/shard_map/ppermute | solution.py:594
  54.9 2.9 %collective-permute-done.12.refs_3_.refs_5_.refs_4_ = bf16[343,256]{1,0:T(8,128)(2,1)S(1)} collective-permute-done((bf16[343,256]{1,0:T(8,128)(2,1)S(1)}, bf16[343,256]{1,0:T(8,128)(2,1)S(1)}, u32[]{:S(2)}, u32[]{:S(2)}) %collective-permute-start.12) | collective-permute-done | bytes 175648 | tf_op jit(solution)/shard_map/ppermute | solution.py:594
  58.3 1.3 collective-permute-start.16
  60.7 4.4 %collective-permute-done.14.refs_12_ = bf16[3,32,2176]{2,1,0:T(8,128)(2,1)S(1)} collective-permute-done((bf16[3,32,2176]{2,1,0:T(8,128)(2,1)S(1)}, bf16[3,32,2176]{2,1,0:T(8,128)(2,1)S(1)}, u32[]{:S(2)}, u32[]{:S(2)}) %collective-permute-start.14) | collective-permute-done | bytes 417824 | tf_op jit(solution)/shard_map/ppermute | solution.py:592
  65.7 3.9 %shard_map.203 = (f32[3,1088,256]{2,1,0:T(8,128)S(1)}, bf16[4,1152,256]{2,1,0:T(8,128)(2,1)S(1)}) custom-call(s32[4]{0:T(128)S(1)} %pad_add_fusion.idx, bf16[343,256]{1,0:T(8,128)(2,1)S(1)} %get-tuple-element.140.refs_0_.refs_2_.refs_1_, bf16[343,256]{1,0:T(8,128)(2,1)S(1)} %collective-permute-done.10.refs_1_.refs_3_.refs_2_, ...), custom_call_target="tpu_custom_call" | custom-call | flops 1925185536 | bytes 20971520 | tf_op jit(solution)/shard_map/pallas_call | solution.py:45
  70.0 1.4 collective-permute-done.18.refs_15_
  71.8 4.4 %shard_map.204 = (bf16[3,1024,256]{2,1,0:T(8,128)(2,1)S(1)}, bf16[2048,256]{1,0:T(8,128)(2,1)S(1)}, f32[1024,128]{1,0:T(8,128)S(1)}, f32[1040,256]{1,0:T(8,128)S...) custom-call(s32[4]{0:T(128)S(1)} %pad_add_fusion.idx, s32[1,1024]{1,0:T(1,128)S(1)} %bitcast.114, ...), custom_call_target="tpu_custom_call" | custom-call | flops 2415919104 | bytes 10485760 | tf_op jit(solution)/shard_map/pallas_call | solution.py:45
  76.4 2.5 %collective-permute-done.20.far = bf16[2048,256]{1,0:T(8,128)(2,1)S(1)} collective-permute-done((bf16[2048,256]{1,0:T(8,128)(2,1)S(1)}, bf16[2048,256]{1,0:T(8,128)(2,1)S(1)}, u32[]{:S(2)}, u32[]{:S(2)}) %collective-permute-start.20) | collective-permute-done | bytes 1048608 | tf_op jit(solution)/shard_map/ppermute | solution.py:592
  78.9 3.0 %shard_map.205 = (bf16[4,32,2176]{2,1,0:T(8,128)(2,1)S(1)}, bf16[4,32,2176]{2,1,0:T(8,128)(2,1)S(1)}, bf16[2,4,32,2176]{3,2,1,0:T(8,128)(2,1)S(1)}) custom-call(s32[4]{0:T(128)S(1)} %pad_add_fusion.idx, bf16[4,1152,256]{2,1,0:T(8,128)(2,1)S(1)} %get-tuple-element.152.refs_16_.x_all, bf16[4,1152,256]{2,1,0:T(8,128)(2,1)S(1)} %collective-permute-done.19.x_far, ...), custom_call_target="tpu_custom_call" | custom-call | flops 1207959552 | bytes 10485760 | tf_op jit(solution)/shard_map/pallas_call | solution.py:45
  82.4 5.5 %shard_map.206 = (bf16[272,256]{1,0:T(8,128)(2,1)S(1)}, bf16[272,256]{1,0:T(8,128)(2,1)S(1)}, bf16[272,256]{1,0:T(8,128)(2,1)S(1)}, bf16[272,256]{1,0:T(8,128)(2...) custom-call(s32[4]{0:T(128)S(1)} %pad_add_fusion.idx, ...), custom_call_target="tpu_custom_call" | custom-call | flops 1925185536 | bytes 20971520 | tf_op jit(solution)/shard_map/pallas_call | solution.py:45
  89.8 2.3 %shard_map.207 = (bf16[4,32,1152]{2,1,0:T(8,128)(2,1)S(1)}, bf16[4,32,1152]{2,1,0:T(8,128)(2,1)S(1)}, bf16[2,4,32,1152]{3,2,1,0:T(8,128)(2,1)S(1)}) custom-call(s32[4]{0:T(128)S(1)} %pad_add_fusion.idx, bf16[4,1152,256]{2,1,0:T(8,128)(2,1)S(1)} %get-tuple-element.152.refs_16_.x_all, bf16[4,1152,256]{2,1,0:T(8,128)(2,1)S(1)} %collective-permute-done.19.x_far, ...), custom_call_target="tpu_custom_call" | custom-call | flops 641728512 | bytes 10485760 | tf_op jit(solution)/shard_map/pallas_call | solution.py:45
  92.0 1.8 %collective-permute-done.23.refs_1_ = bf16[272,256]{1,0:T(8,128)(2,1)S(1)} collective-permute-done((bf16[272,256]{1,0:T(8,128)(2,1)S(1)}, bf16[272,256]{1,0:T(8,128)(2,1)S(1)}, u32[]{:S(2)}, u32[]{:S(2)}) %collective-permute-start.23) | collective-permute-done | bytes 139296 | tf_op jit(solution)/shard_map/ppermute | solution.py:594
  93.8 2.8 %collective-permute-done.21 = bf16[2,4,32,2176]{3,2,1,0:T(8,128)(2,1)S(1)} collective-permute-done((bf16[2,4,32,2176]{3,2,1,0:T(8,128)(2,1)S(1)}, bf16[2,4,32,2176]{3,2,1,0:T(8,128)(2,1)S(1)}, u32[]{:S(2)}, u32[]{:S(2)}) %collective-permute-start.21) | collective-permute-done | bytes 1114144 | tf_op jit(solution)/shard_map/ppermute | solution.py:592
  97.5 1.9 %collective-permute-start.27 = (bf16[272,256]{1,0:T(8,128)(2,1)S(1)}, bf16[272,256]{1,0:T(8,128)(2,1)S(1)}, u32[]{:S(2)}, u32[]{:S(2)}) collective-permute-start(bf16[272,256]{1,0:T(8,128)(2,1)S(1)} %get-tuple-element.177), channel_id=1, source_target_pairs={{0,2},{1,3},{2,0},{3,1},{4,6},{5,7},{6,4},{7,5},{8,10},{9,11},{10,... | collective-permute-start | bytes 417800 | tf_op jit(solution)/shard_map/ppermute | solution.py:594
  99.4 3.8 %shard_map.208 = (bf16[4,32,2176]{2,1,0:T(8,128)(2,1)S(1)}, bf16[4,32,2176]{2,1,0:T(8,128)(2,1)S(1)}, bf16[2,4,32,2176]{3,2,1,0:T(8,128)(2,1)S(1)}) custom-call(s32[4]{0:T(128)S(1)} %pad_add_fusion.idx, bf16[4,1152,256]{2,1,0:T(8,128)(2,1)S(1)} %get-tuple-element.152.refs_16_.x_all, bf16[4,1152,256]{2,1,0:T(8,128)(2,1)S(1)} %collective-permute-done.19.x_far, ...), custom_call_target="tpu_custom_call" | custom-call | flops 1283457024 | bytes 10485760 | tf_op jit(solution)/shard_map/pallas_call | solution.py:45
  103.2 3.8 %collective-permute-done.27.refs_2_ = bf16[272,256]{1,0:T(8,128)(2,1)S(1)} collective-permute-done((bf16[272,256]{1,0:T(8,128)(2,1)S(1)}, bf16[272,256]{1,0:T(8,128)(2,1)S(1)}, u32[]{:S(2)}, u32[]{:S(2)}) %collective-permute-start.27) | collective-permute-done | bytes 139296 | tf_op jit(solution)/shard_map/ppermute | solution.py:594
  107.2 3.9 %collective-permute-done.24 = bf16[4,32,2176]{2,1,0:T(8,128)(2,1)S(1)} collective-permute-done((bf16[4,32,2176]{2,1,0:T(8,128)(2,1)S(1)}, bf16[4,32,2176]{2,1,0:T(8,128)(2,1)S(1)}, u32[]{:S(2)}, u32[]{:S(2)}) %collective-permute-start.24) | collective-permute-done | bytes 557088 | tf_op jit(solution)/shard_map/ppermute | solution.py:592
  111.2 2.5 %collective-permute-start.30 = (bf16[2,4,32,2176]{3,2,1,0:T(8,128)(2,1)S(1)}, bf16[2,4,32,2176]{3,2,1,0:T(8,128)(2,1)S(1)}, u32[]{:S(2)}, u32[]{:S(2)}) collective-permute-start(bf16[2,4,32,2176]{3,2,1,0:T(8,128)(2,1)S(1)} %get-tuple-element.182), channel_id=1, source_target_pairs={{0,8},{4,20},{8,0},{12,28},{16,24},{20,4},{24,16},{28,12},{1,9},{5... | collective-permute-start | bytes 3342344 | tf_op jit(solution)/shard_map/ppermute | solution.py:592
  114.6 1.4 collective-permute-start.33
  116.0 1.6 shard_map.209
  118.2 6.7 %collective-permute-done.32 = bf16[32,2176]{1,0:T(8,128)(2,1)S(1)} collective-permute-done((bf16[32,2176]{1,0:T(8,128)(2,1)S(1)}, bf16[32,2176]{1,0:T(8,128)(2,1)S(1)}, u32[]{:S(2)}, u32[]{:S(2)}) %collective-permute-start.32) | collective-permute-done | bytes 139296 | tf_op jit(solution)/shard_map/ppermute | solution.py:594
  124.9 2.8 %collective-permute-done.33 = bf16[32,2176]{1,0:T(8,128)(2,1)S(1)} collective-permute-done((bf16[32,2176]{1,0:T(8,128)(2,1)S(1)}, bf16[32,2176]{1,0:T(8,128)(2,1)S(1)}, u32[]{:S(2)}, u32[]{:S(2)}) %collective-permute-start.33) | collective-permute-done | bytes 139296 | tf_op jit(solution)/shard_map/ppermute | solution.py:594
  127.7 2.0 %collective-permute-done.30 = bf16[2,4,32,2176]{3,2,1,0:T(8,128)(2,1)S(1)} collective-permute-done((bf16[2,4,32,2176]{3,2,1,0:T(8,128)(2,1)S(1)}, bf16[2,4,32,2176]{3,2,1,0:T(8,128)(2,1)S(1)}, u32[]{:S(2)}, u32[]{:S(2)}) %collective-permute-start.30) | collective-permute-done | bytes 1114144 | tf_op jit(solution)/shard_map/ppermute | solution.py:592
  130.6 1.5 collective-permute-start.35
  133.5 1.4 collective-permute-start.38
  136.8 4.0 %collective-permute-done.38 = bf16[32,1152]{1,0:T(8,128)(2,1)S(1)} collective-permute-done((bf16[32,1152]{1,0:T(8,128)(2,1)S(1)}, bf16[32,1152]{1,0:T(8,128)(2,1)S(1)}, u32[]{:S(2)}, u32[]{:S(2)}) %collective-permute-start.38) | collective-permute-done | bytes 73760 | tf_op jit(solution)/shard_map/ppermute | solution.py:594
  141.1 1.7 collective-permute-start.42
  145.2 3.5 %collective-permute-done.40.refs_1_ = bf16[32,1152]{1,0:T(8,128)(2,1)S(1)} collective-permute-done((bf16[32,1152]{1,0:T(8,128)(2,1)S(1)}, bf16[32,1152]{1,0:T(8,128)(2,1)S(1)}, u32[]{:S(2)}, u32[]{:S(2)}) %collective-permute-start.40) | collective-permute-done | bytes 73760 | tf_op jit(solution)/shard_map/ppermute | solution.py:592
  148.7 4.1 %collective-permute-done.42 = bf16[32,2176]{1,0:T(8,128)(2,1)S(1)} collective-permute-done((bf16[32,2176]{1,0:T(8,128)(2,1)S(1)}, bf16[32,2176]{1,0:T(8,128)(2,1)S(1)}, u32[]{:S(2)}, u32[]{:S(2)}) %collective-permute-start.42) | collective-permute-done | bytes 139296 | tf_op jit(solution)/shard_map/ppermute | solution.py:594
  152.8 3.0 %collective-permute-done.43 = bf16[32,2176]{1,0:T(8,128)(2,1)S(1)} collective-permute-done((bf16[32,2176]{1,0:T(8,128)(2,1)S(1)}, bf16[32,2176]{1,0:T(8,128)(2,1)S(1)}, u32[]{:S(2)}, u32[]{:S(2)}) %collective-permute-start.43) | collective-permute-done | bytes 139296 | tf_op jit(solution)/shard_map/ppermute | solution.py:594
  158.6 4.2 %collective-permute-done.44.refs_1_ = bf16[32,2176]{1,0:T(8,128)(2,1)S(1)} collective-permute-done((bf16[32,2176]{1,0:T(8,128)(2,1)S(1)}, bf16[32,2176]{1,0:T(8,128)(2,1)S(1)}, u32[]{:S(2)}, u32[]{:S(2)}) %collective-permute-start.44) | collective-permute-done | bytes 139296 | tf_op jit(solution)/shard_map/ppermute | solution.py:592
  164.2 2.5 %shard_map.210 = (f32[1040,256]{1,0:T(8,128)}, f32[256,1024]{1,0:T(8,128)}, f32[3,256]{1,0:T(4,128)S(1)}, f32[1,1]{1,0:T(1,128)}) custom-call(s32[4]{0:T(128)S(1)} %pad_add_fusion.idx, bf16[32,2176]{1,0:T(8,128)(2,1)S(1)} %fusion.10.refs_0_, bf16[32,2176]{1,0:T(8,128)(2,1)S(1)} %collective-permute-done.35.refs_1_, ...), custom_call_target="tpu_custom_call" | custom-call | bytes 4194304 | tf_op jit(solution)/shard_map/pallas_call | solution.py:45
  166.7 1.8 %shard_map.211 = (f32[3,260,1040]{2,1,0:T(8,128)}, f32[1,260]{1,0:T(1,128)S(1)}) custom-call(s32[4]{0:T(128)S(1)} %pad_add_fusion.idx, bf16[32,1152]{1,0:T(8,128)(2,1)S(1)} %fusion.12.refs_0_, bf16[32,1152]{1,0:T(8,128)(2,1)S(1)} %collective-permute-done.40.refs_1_, bf16[2,32,1152]{2,1,0:T(8,128)(2,1)S(1)} %collective-permute-done.45.refs_2_, ...), custom_call_target="tpu_custom_call" | custom-call | bytes 4194304 | tf_op jit(solution)/shard_map/pallas_call | solution.py:45
  172.2 2.7 %shard_map.212 = (f32[3,260,1040]{2,1,0:T(8,128)}, f32[3,260]{1,0:T(4,128)}) custom-call(s32[4]{0:T(128)S(1)} %pad_add_fusion.idx, bf16[32,2176]{1,0:T(8,128)(2,1)S(1)} %fusion.7.refs_0_, bf16[32,2176]{1,0:T(8,128)(2,1)S(1)} %collective-permute-done.44.refs_1_, ...), custom_call_target="tpu_custom_call", output_to_operand_aliasing={{0}: (5, {})} | custom-call | bytes 4194304 | tf_op jit(solution)/shard_map/pallas_call | solution.py:45
  (127 shorter events, 28.7 us)
Async XLA Ops:
  2.1 9.4 %collective-permute-start = (bf16[32,3200]{1,0:T(8,128)(2,1)S(1)}, bf16[32,3200]{1,0:T(8,128)(2,1)S(1)}, u32[]{:S(2)}, u32[]{:S(2)}) collective-permute-start(bf16[32,3200]{1,0:T(8,128)(2,1)S(1)} %concatenate.15), channel_id=1, source_target_pairs={{0,1},{1,2},{2,3},{3,0},{4,5},{5,6},{6,7},{7,4},{8,9},{9,10},{10,1... | collective-permute-start | bytes 614408 | tf_op jit(solution)/shard_map/ppermute | solution.py:594
  3.4 16.9 %collective-permute-start.1 = (bf16[32,3200]{1,0:T(8,128)(2,1)S(1)}, bf16[32,3200]{1,0:T(8,128)(2,1)S(1)}, u32[]{:S(2)}, u32[]{:S(2)}) collective-permute-start(bf16[32,3200]{1,0:T(8,128)(2,1)S(1)} %concatenate.15), channel_id=1, source_target_pairs={{0,2},{1,3},{2,0},{3,1},{4,6},{5,7},{6,4},{7,5},{8,10},{9,11},{10,... | collective-permute-start | bytes 614408 | tf_op jit(solution)/shard_map/ppermute | solution.py:594
  4.5 18.7 %collective-permute-start.2 = (bf16[32,3200]{1,0:T(8,128)(2,1)S(1)}, bf16[32,3200]{1,0:T(8,128)(2,1)S(1)}, u32[]{:S(2)}, u32[]{:S(2)}) collective-permute-start(bf16[32,3200]{1,0:T(8,128)(2,1)S(1)} %concatenate.15), channel_id=1, source_target_pairs={{0,3},{1,0},{2,1},{3,2},{4,7},{5,4},{6,5},{7,6},{8,11},{9,8},{10,9... | collective-permute-start | bytes 614408 | tf_op jit(solution)/shard_map/ppermute | solution.py:594
  23.3 16.5 %collective-permute-start.3 = (bf16[3,32,3200]{2,1,0:T(8,128)(2,1)S(1)}, bf16[3,32,3200]{2,1,0:T(8,128)(2,1)S(1)}, u32[]{:S(2)}, u32[]{:S(2)}) collective-permute-start(bf16[3,32,3200]{2,1,0:T(8,128)(2,1)S(1)} %pad_maximum_fusion.2), channel_id=1, source_target_pairs={{0,8},{4,20},{8,0},{12,28},{16,24},{20,4},{24,16},{28,12},{1,9},{5... | collective-permute-start | bytes 1843208 | tf_op jit(solution)/shard_map/ppermute | solution.py:592
  24.5 15.3 %collective-permute-start.4 = (bf16[3,32,3200]{2,1,0:T(8,128)(2,1)S(1)}, bf16[3,32,3200]{2,1,0:T(8,128)(2,1)S(1)}, u32[]{:S(2)}, u32[]{:S(2)}) collective-permute-start(bf16[3,32,3200]{2,1,0:T(8,128)(2,1)S(1)} %pad_maximum_fusion.2), channel_id=1, source_target_pairs={{0,16},{4,12},{8,24},{12,4},{16,0},{20,28},{24,8},{28,20},{1,17},{... | collective-permute-start | bytes 1843208 | tf_op jit(solution)/shard_map/ppermute | solution.py:592
  25.8 4.2 %collective-permute-start.5 = (bf16[32,2176]{1,0:T(8,128)(2,1)S(1)}, bf16[32,2176]{1,0:T(8,128)(2,1)S(1)}, u32[]{:S(2)}, u32[]{:S(2)}) collective-permute-start(bf16[32,2176]{1,0:T(8,128)(2,1)S(1)} %get-tuple-element.126), channel_id=1, source_target_pairs={{0,1},{1,2},{2,3},{3,0},{4,5},{5,6},{6,7},{7,4},{8,9},{9,10},{10,1... | collective-permute-start | bytes 417800 | tf_op jit(solution)/shard_map/ppermute | solution.py:594
  25.8 11.0 %collective-permute-start.6 = (bf16[32,2176]{1,0:T(8,128)(2,1)S(1)}, bf16[32,2176]{1,0:T(8,128)(2,1)S(1)}, u32[]{:S(2)}, u32[]{:S(2)}) collective-permute-start(bf16[32,2176]{1,0:T(8,128)(2,1)S(1)} %get-tuple-element.126), channel_id=1, source_target_pairs={{0,2},{1,3},{2,0},{3,1},{4,6},{5,7},{6,4},{7,5},{8,10},{9,11},{10,... | collective-permute-start | bytes 417800 | tf_op jit(solution)/shard_map/ppermute | solution.py:594
  26.0 13.7 %collective-permute-start.7 = (bf16[32,2176]{1,0:T(8,128)(2,1)S(1)}, bf16[32,2176]{1,0:T(8,128)(2,1)S(1)}, u32[]{:S(2)}, u32[]{:S(2)}) collective-permute-start(bf16[32,2176]{1,0:T(8,128)(2,1)S(1)} %get-tuple-element.126), channel_id=1, source_target_pairs={{0,3},{1,0},{2,1},{3,2},{4,7},{5,4},{6,5},{7,6},{8,11},{9,8},{10,9... | collective-permute-start | bytes 417800 | tf_op jit(solution)/shard_map/ppermute | solution.py:594
  40.0 18.3 %collective-permute-start.8 = (bf16[3,32,5376]{2,1,0:T(8,128)(2,1)S(1)}, bf16[3,32,5376]{2,1,0:T(8,128)(2,1)S(1)}, u32[]{:S(2)}, u32[]{:S(2)}) collective-permute-start(bf16[3,32,5376]{2,1,0:T(8,128)(2,1)S(1)} %pad_maximum_fusion.1), channel_id=1, source_target_pairs={{0,16},{4,12},{8,24},{12,4},{16,0},{20,28},{24,8},{28,20},{1,17},{... | collective-permute-start | bytes 3096584 | tf_op jit(solution)/shard_map/ppermute | solution.py:592
  41.2 16.6 %collective-permute-start.9 = (bf16[3,32,2176]{2,1,0:T(8,128)(2,1)S(1)}, bf16[3,32,2176]{2,1,0:T(8,128)(2,1)S(1)}, u32[]{:S(2)}, u32[]{:S(2)}) collective-permute-start(bf16[3,32,2176]{2,1,0:T(8,128)(2,1)S(1)} %maximum_add_fusion.refs_8_), channel_id=1, source_target_pairs={{0,8},{4,20},{8,0},{12,28},{16,24},{20,4},{24,16},{28,12},{1,9},{5... | collective-permute-start | bytes 1253384 | tf_op jit(solution)/shard_map/ppermute | solution.py:592
  41.3 4.6 %collective-permute-start.10 = (bf16[343,256]{1,0:T(8,128)(2,1)S(1)}, bf16[343,256]{1,0:T(8,128)(2,1)S(1)}, u32[]{:S(2)}, u32[]{:S(2)}) collective-permute-start(bf16[343,256]{1,0:T(8,128)(2,1)S(1)} %get-tuple-element.135), channel_id=1, source_target_pairs={{0,1},{1,2},{2,3},{3,0},{4,5},{5,6},{6,7},{7,4},{8,9},{9,10},{10,1... | collective-permute-start | bytes 526856 | tf_op jit(solution)/shard_map/ppermute | solution.py:594
  41.3 13.6 %collective-permute-start.11 = (bf16[343,256]{1,0:T(8,128)(2,1)S(1)}, bf16[343,256]{1,0:T(8,128)(2,1)S(1)}, u32[]{:S(2)}, u32[]{:S(2)}) collective-permute-start(bf16[343,256]{1,0:T(8,128)(2,1)S(1)} %get-tuple-element.137), channel_id=1, source_target_pairs={{0,2},{1,3},{2,0},{3,1},{4,6},{5,7},{6,4},{7,5},{8,10},{9,11},{10,... | collective-permute-start | bytes 526856 | tf_op jit(solution)/shard_map/ppermute | solution.py:594
  41.4 16.5 %collective-permute-start.12 = (bf16[343,256]{1,0:T(8,128)(2,1)S(1)}, bf16[343,256]{1,0:T(8,128)(2,1)S(1)}, u32[]{:S(2)}, u32[]{:S(2)}) collective-permute-start(bf16[343,256]{1,0:T(8,128)(2,1)S(1)} %get-tuple-element.139), channel_id=1, source_target_pairs={{0,3},{1,0},{2,1},{3,2},{4,7},{5,4},{6,5},{7,6},{8,11},{9,8},{10,9... | collective-permute-start | bytes 526856 | tf_op jit(solution)/shard_map/ppermute | solution.py:594
  58.3 7.4 %collective-permute-start.16 = (bf16[3,3,32,3200]{3,2,1,0:T(8,128)(2,1)S(1)}, bf16[3,3,32,3200]{3,2,1,0:T(8,128)(2,1)S(1)}, u32[]{:S(2)}, u32[]{:S(2)}) collective-permute-start(bf16[3,3,32,3200]{3,2,1,0:T(8,128)(2,1)S(1)} %pad_maximum_fusion.refs_5_.refs_6_), channel_id=1, source_target_pairs={{0,4},{4,0},{8,12},{12,8},{16,20},{20,16},{24,28},{28,24},{1,5},{5... | collective-permute-start | bytes 5529608 | tf_op jit(solution)/shard_map/ppermute | solution.py:592
  59.6 6.1 %collective-permute-start.13 = (bf16[3,32,5376]{2,1,0:T(8,128)(2,1)S(1)}, bf16[3,32,5376]{2,1,0:T(8,128)(2,1)S(1)}, u32[]{:S(2)}, u32[]{:S(2)}) collective-permute-start(bf16[3,32,5376]{2,1,0:T(8,128)(2,1)S(1)} %collective-permute-done.8.refs_6_.refs_10_.refs_7_), channel_id=1, source_target_pairs={{0,4},{4,0},{8,12},{12,8},{16,20},{20,16},{24,28},{28,24},{1,5},{5... | collective-permute-start | bytes 3096584 | tf_op jit(solution)/shard_map/ppermute | solution.py:592
  59.6 5.5 %collective-permute-start.14 = (bf16[3,32,2176]{2,1,0:T(8,128)(2,1)S(1)}, bf16[3,32,2176]{2,1,0:T(8,128)(2,1)S(1)}, u32[]{:S(2)}, u32[]{:S(2)}) collective-permute-start(bf16[3,32,2176]{2,1,0:T(8,128)(2,1)S(1)} %maximum_add_fusion.refs_8_), channel_id=1, source_target_pairs={{0,4},{4,0},{8,12},{12,8},{16,20},{20,16},{24,28},{28,24},{1,5},{5... | collective-permute-start | bytes 1253384 | tf_op jit(solution)/shard_map/ppermute | solution.py:592
  60.1 5.6 %collective-permute-start.15 = (bf16[3,32,2176]{2,1,0:T(8,128)(2,1)S(1)}, bf16[3,32,2176]{2,1,0:T(8,128)(2,1)S(1)}, u32[]{:S(2)}, u32[]{:S(2)}) collective-permute-start(bf16[3,32,2176]{2,1,0:T(8,128)(2,1)S(1)} %collective-permute-done.9.refs_9_), channel_id=1, source_target_pairs={{0,4},{4,0},{8,12},{12,8},{16,20},{20,16},{24,28},{28,24},{1,5},{5... | collective-permute-start | bytes 1253384 | tf_op jit(solution)/shard_map/ppermute | solution.py:592
  60.1 9.5 %collective-permute-start.17 = (bf16[3,32,2176]{2,1,0:T(8,128)(2,1)S(1)}, bf16[3,32,2176]{2,1,0:T(8,128)(2,1)S(1)}, u32[]{:S(2)}, u32[]{:S(2)}) collective-permute-start(bf16[3,32,2176]{2,1,0:T(8,128)(2,1)S(1)} %collective-permute-done.9.refs_9_), channel_id=1, source_target_pairs={{0,16},{4,12},{8,24},{12,4},{16,0},{20,28},{24,8},{28,20},{1,17},{... | collective-permute-start | bytes 1253384 | tf_op jit(solution)/shard_map/ppermute | solution.py:592
  71.4 7.5 %collective-permute-start.19 = (bf16[4,1152,256]{2,1,0:T(8,128)(2,1)S(1)}, bf16[4,1152,256]{2,1,0:T(8,128)(2,1)S(1)}, u32[]{:S(2)}, u32[]{:S(2)}) collective-permute-start(bf16[4,1152,256]{2,1,0:T(8,128)(2,1)S(1)} %get-tuple-element.152.refs_16_.x_all), channel_id=1, source_target_pairs={{0,4},{4,0},{8,12},{12,8},{16,20},{20,16},{24,28},{28,24},{1,5},{5... | collective-permute-start | bytes 7077896 | tf_op jit(solution)/shard_map/ppermute | solution.py:592
  76.2 2.7 %collective-permute-start.20 = (bf16[2048,256]{1,0:T(8,128)(2,1)S(1)}, bf16[2048,256]{1,0:T(8,128)(2,1)S(1)}, u32[]{:S(2)}, u32[]{:S(2)}) collective-permute-start(bf16[2048,256]{1,0:T(8,128)(2,1)S(1)} %get-tuple-element.157), channel_id=1, source_target_pairs={{0,4},{4,0},{8,12},{12,8},{16,20},{20,16},{24,28},{28,24},{1,5},{5... | collective-permute-start | bytes 3145736 | tf_op jit(solution)/shard_map/ppermute | solution.py:592
  81.9 14.7 %collective-permute-start.21 = (bf16[2,4,32,2176]{3,2,1,0:T(8,128)(2,1)S(1)}, bf16[2,4,32,2176]{3,2,1,0:T(8,128)(2,1)S(1)}, u32[]{:S(2)}, u32[]{:S(2)}) collective-permute-start(bf16[2,4,32,2176]{3,2,1,0:T(8,128)(2,1)S(1)} %get-tuple-element.160), channel_id=1, source_target_pairs={{0,8},{4,20},{8,0},{12,28},{16,24},{20,4},{24,16},{28,12},{1,9},{5... | collective-permute-start | bytes 3342344 | tf_op jit(solution)/shard_map/ppermute | solution.py:592
  88.6 5.2 %collective-permute-start.23 = (bf16[272,256]{1,0:T(8,128)(2,1)S(1)}, bf16[272,256]{1,0:T(8,128)(2,1)S(1)}, u32[]{:S(2)}, u32[]{:S(2)}) collective-permute-start(bf16[272,256]{1,0:T(8,128)(2,1)S(1)} %get-tuple-element.168), channel_id=1, source_target_pairs={{0,1},{1,2},{2,3},{3,0},{4,5},{5,6},{6,7},{7,4},{8,9},{9,10},{10,1... | collective-permute-start | bytes 417800 | tf_op jit(solution)/shard_map/ppermute | solution.py:594
  88.6 10.8 %collective-permute-start.26 = (bf16[2,528,256]{2,1,0:T(8,128)(2,1)S(1)}, bf16[2,528,256]{2,1,0:T(8,128)(2,1)S(1)}, u32[]{:S(2)}, u32[]{:S(2)}) collective-permute-start(bf16[2,528,256]{2,1,0:T(8,128)(2,1)S(1)} %get-tuple-element.173), channel_id=1, source_target_pairs={{0,4},{4,0},{8,12},{12,8},{16,20},{20,16},{24,28},{28,24},{1,5},{5... | collective-permute-start | bytes 1622024 | tf_op jit(solution)/shard_map/ppermute | solution.py:592
  96.6 14.5 %collective-permute-start.25 = (bf16[2,4,32,1152]{3,2,1,0:T(8,128)(2,1)S(1)}, bf16[2,4,32,1152]{3,2,1,0:T(8,128)(2,1)S(1)}, u32[]{:S(2)}, u32[]{:S(2)}) collective-permute-start(bf16[2,4,32,1152]{3,2,1,0:T(8,128)(2,1)S(1)} %get-tuple-element.171), channel_id=1, source_target_pairs={{0,8},{4,20},{8,0},{12,28},{16,24},{20,4},{24,16},{28,12},{1,9},{5... | collective-permute-start | bytes 1769480 | tf_op jit(solution)/shard_map/ppermute | solution.py:592
  97.1 13.9 %collective-permute-start.24 = (bf16[4,32,2176]{2,1,0:T(8,128)(2,1)S(1)}, bf16[4,32,2176]{2,1,0:T(8,128)(2,1)S(1)}, u32[]{:S(2)}, u32[]{:S(2)}) collective-permute-start(bf16[4,32,2176]{2,1,0:T(8,128)(2,1)S(1)} %fusion.2), channel_id=1, source_target_pairs={{0,16},{4,12},{8,24},{12,4},{16,0},{20,28},{24,8},{28,20},{1,17},{... | collective-permute-start | bytes 1671176 | tf_op jit(solution)/shard_map/ppermute | solution.py:592
  97.5 9.4 %collective-permute-start.27 = (bf16[272,256]{1,0:T(8,128)(2,1)S(1)}, bf16[272,256]{1,0:T(8,128)(2,1)S(1)}, u32[]{:S(2)}, u32[]{:S(2)}) collective-permute-start(bf16[272,256]{1,0:T(8,128)(2,1)S(1)} %get-tuple-element.177), channel_id=1, source_target_pairs={{0,2},{1,3},{2,0},{3,1},{4,6},{5,7},{6,4},{7,5},{8,10},{9,11},{10,... | collective-permute-start | bytes 417800 | tf_op jit(solution)/shard_map/ppermute | solution.py:594
  99.4 7.8 %collective-permute-start.28 = (bf16[272,256]{1,0:T(8,128)(2,1)S(1)}, bf16[272,256]{1,0:T(8,128)(2,1)S(1)}, u32[]{:S(2)}, u32[]{:S(2)}) collective-permute-start(bf16[272,256]{1,0:T(8,128)(2,1)S(1)} %get-tuple-element.178), channel_id=1, source_target_pairs={{0,3},{1,0},{2,1},{3,2},{4,7},{5,4},{6,5},{7,6},{8,11},{9,8},{10,9... | collective-permute-start | bytes 417800 | tf_op jit(solution)/shard_map/ppermute | solution.py:594
  111.1 16.6 %collective-permute-start.29 = (bf16[4,32,1152]{2,1,0:T(8,128)(2,1)S(1)}, bf16[4,32,1152]{2,1,0:T(8,128)(2,1)S(1)}, u32[]{:S(2)}, u32[]{:S(2)}) collective-permute-start(bf16[4,32,1152]{2,1,0:T(8,128)(2,1)S(1)} %fusion.5), channel_id=1, source_target_pairs={{0,16},{4,12},{8,24},{12,4},{16,0},{20,28},{24,8},{28,20},{1,17},{... | collective-permute-start | bytes 884744 | tf_op jit(solution)/shard_map/ppermute | solution.py:592
  111.2 18.5 %collective-permute-start.30 = (bf16[2,4,32,2176]{3,2,1,0:T(8,128)(2,1)S(1)}, bf16[2,4,32,2176]{3,2,1,0:T(8,128)(2,1)S(1)}, u32[]{:S(2)}, u32[]{:S(2)}) collective-permute-start(bf16[2,4,32,2176]{3,2,1,0:T(8,128)(2,1)S(1)} %get-tuple-element.182), channel_id=1, source_target_pairs={{0,8},{4,20},{8,0},{12,28},{16,24},{20,4},{24,16},{28,12},{1,9},{5... | collective-permute-start | bytes 3342344 | tf_op jit(solution)/shard_map/ppermute | solution.py:592
  114.0 4.3 %collective-permute-start.31 = (bf16[32,2176]{1,0:T(8,128)(2,1)S(1)}, bf16[32,2176]{1,0:T(8,128)(2,1)S(1)}, u32[]{:S(2)}, u32[]{:S(2)}) collective-permute-start(bf16[32,2176]{1,0:T(8,128)(2,1)S(1)} %get-tuple-element.240), channel_id=1, source_target_pairs={{0,1},{1,2},{2,3},{3,0},{4,5},{5,6},{6,7},{7,4},{8,9},{9,10},{10,1... | collective-permute-start | bytes 417800 | tf_op jit(solution)/shard_map/ppermute | solution.py:594
  114.0 10.9 %collective-permute-start.32 = (bf16[32,2176]{1,0:T(8,128)(2,1)S(1)}, bf16[32,2176]{1,0:T(8,128)(2,1)S(1)}, u32[]{:S(2)}, u32[]{:S(2)}) collective-permute-start(bf16[32,2176]{1,0:T(8,128)(2,1)S(1)} %get-tuple-element.239), channel_id=1, source_target_pairs={{0,2},{1,3},{2,0},{3,1},{4,6},{5,7},{6,4},{7,5},{8,10},{9,11},{10,... | collective-permute-start | bytes 417800 | tf_op jit(solution)/shard_map/ppermute | solution.py:594
  114.6 13.1 %collective-permute-start.33 = (bf16[32,2176]{1,0:T(8,128)(2,1)S(1)}, bf16[32,2176]{1,0:T(8,128)(2,1)S(1)}, u32[]{:S(2)}, u32[]{:S(2)}) collective-permute-start(bf16[32,2176]{1,0:T(8,128)(2,1)S(1)} %get-tuple-element.238), channel_id=1, source_target_pairs={{0,3},{1,0},{2,1},{3,2},{4,7},{5,4},{6,5},{7,6},{8,11},{9,8},{10,9... | collective-permute-start | bytes 417800 | tf_op jit(solution)/shard_map/ppermute | solution.py:594
  129.9 10.9 %collective-permute-start.34 = (bf16[4,32,2176]{2,1,0:T(8,128)(2,1)S(1)}, bf16[4,32,2176]{2,1,0:T(8,128)(2,1)S(1)}, u32[]{:S(2)}, u32[]{:S(2)}) collective-permute-start(bf16[4,32,2176]{2,1,0:T(8,128)(2,1)S(1)} %fusion.1), channel_id=1, source_target_pairs={{0,16},{4,12},{8,24},{12,4},{16,0},{20,28},{24,8},{28,20},{1,17},{... | collective-permute-start | bytes 1671176 | tf_op jit(solution)/shard_map/ppermute | solution.py:592
  130.6 10.2 %collective-permute-start.35 = (bf16[32,2176]{1,0:T(8,128)(2,1)S(1)}, bf16[32,2176]{1,0:T(8,128)(2,1)S(1)}, u32[]{:S(2)}, u32[]{:S(2)}) collective-permute-start(bf16[32,2176]{1,0:T(8,128)(2,1)S(1)} %fusion.10.refs_0_), channel_id=1, source_target_pairs={{0,8},{4,20},{8,0},{12,28},{16,24},{20,4},{24,16},{28,12},{1,9},{5... | collective-permute-start | bytes 417800 | tf_op jit(solution)/shard_map/ppermute | solution.py:592
  132.3 3.6 %collective-permute-start.36 = (bf16[32,1152]{1,0:T(8,128)(2,1)S(1)}, bf16[32,1152]{1,0:T(8,128)(2,1)S(1)}, u32[]{:S(2)}, u32[]{:S(2)}) collective-permute-start(bf16[32,1152]{1,0:T(8,128)(2,1)S(1)} %get-tuple-element.243), channel_id=1, source_target_pairs={{0,1},{1,2},{2,3},{3,0},{4,5},{5,6},{6,7},{7,4},{8,9},{9,10},{10,1... | collective-permute-start | bytes 221192 | tf_op jit(solution)/shard_map/ppermute | solution.py:594
  132.4 4.5 %collective-permute-start.37 = (bf16[32,1152]{1,0:T(8,128)(2,1)S(1)}, bf16[32,1152]{1,0:T(8,128)(2,1)S(1)}, u32[]{:S(2)}, u32[]{:S(2)}) collective-permute-start(bf16[32,1152]{1,0:T(8,128)(2,1)S(1)} %get-tuple-element.242), channel_id=1, source_target_pairs={{0,2},{1,3},{2,0},{3,1},{4,6},{5,7},{6,4},{7,5},{8,10},{9,11},{10,... | collective-permute-start | bytes 221192 | tf_op jit(solution)/shard_map/ppermute | solution.py:594
  133.5 7.3 %collective-permute-start.38 = (bf16[32,1152]{1,0:T(8,128)(2,1)S(1)}, bf16[32,1152]{1,0:T(8,128)(2,1)S(1)}, u32[]{:S(2)}, u32[]{:S(2)}) collective-permute-start(bf16[32,1152]{1,0:T(8,128)(2,1)S(1)} %get-tuple-element.241), channel_id=1, source_target_pairs={{0,3},{1,0},{2,1},{3,2},{4,7},{5,4},{6,5},{7,6},{8,11},{9,8},{10,9... | collective-permute-start | bytes 221192 | tf_op jit(solution)/shard_map/ppermute | solution.py:594
  141.0 7.6 %collective-permute-start.41 = (bf16[32,2176]{1,0:T(8,128)(2,1)S(1)}, bf16[32,2176]{1,0:T(8,128)(2,1)S(1)}, u32[]{:S(2)}, u32[]{:S(2)}) collective-permute-start(bf16[32,2176]{1,0:T(8,128)(2,1)S(1)} %get-tuple-element.237), channel_id=1, source_target_pairs={{0,1},{1,2},{2,3},{3,0},{4,5},{5,6},{6,7},{7,4},{8,9},{9,10},{10,1... | collective-permute-start | bytes 417800 | tf_op jit(solution)/shard_map/ppermute | solution.py:594
  141.1 11.7 %collective-permute-start.42 = (bf16[32,2176]{1,0:T(8,128)(2,1)S(1)}, bf16[32,2176]{1,0:T(8,128)(2,1)S(1)}, u32[]{:S(2)}, u32[]{:S(2)}) collective-permute-start(bf16[32,2176]{1,0:T(8,128)(2,1)S(1)} %get-tuple-element.236), channel_id=1, source_target_pairs={{0,2},{1,3},{2,0},{3,1},{4,6},{5,7},{6,4},{7,5},{8,10},{9,11},{10,... | collective-permute-start | bytes 417800 | tf_op jit(solution)/shard_map/ppermute | solution.py:594
  142.8 13.1 %collective-permute-start.43 = (bf16[32,2176]{1,0:T(8,128)(2,1)S(1)}, bf16[32,2176]{1,0:T(8,128)(2,1)S(1)}, u32[]{:S(2)}, u32[]{:S(2)}) collective-permute-start(bf16[32,2176]{1,0:T(8,128)(2,1)S(1)} %get-tuple-element.235), channel_id=1, source_target_pairs={{0,3},{1,0},{2,1},{3,2},{4,7},{5,4},{6,5},{7,6},{8,11},{9,8},{10,9... | collective-permute-start | bytes 417800 | tf_op jit(solution)/shard_map/ppermute | solution.py:594
  143.9 12.0 %collective-permute-start.39 = (bf16[2,32,2176]{2,1,0:T(8,128)(2,1)S(1)}, bf16[2,32,2176]{2,1,0:T(8,128)(2,1)S(1)}, u32[]{:S(2)}, u32[]{:S(2)}) collective-permute-start(bf16[2,32,2176]{2,1,0:T(8,128)(2,1)S(1)} %pad_maximum_fusion.6), channel_id=1, source_target_pairs={{0,16},{4,12},{8,24},{12,4},{16,0},{20,28},{24,8},{28,20},{1,17},{... | collective-permute-start | bytes 835592 | tf_op jit(solution)/shard_map/ppermute | solution.py:592
  145.1 3.6 %collective-permute-start.40 = (bf16[32,1152]{1,0:T(8,128)(2,1)S(1)}, bf16[32,1152]{1,0:T(8,128)(2,1)S(1)}, u32[]{:S(2)}, u32[]{:S(2)}) collective-permute-start(bf16[32,1152]{1,0:T(8,128)(2,1)S(1)} %fusion.12.refs_0_), channel_id=1, source_target_pairs={{0,8},{4,20},{8,0},{12,28},{16,24},{20,4},{24,16},{28,12},{1,9},{5... | collective-permute-start | bytes 221192 | tf_op jit(solution)/shard_map/ppermute | solution.py:592
  155.9 6.9 %collective-permute-start.46 = (bf16[4,32,2176]{2,1,0:T(8,128)(2,1)S(1)}, bf16[4,32,2176]{2,1,0:T(8,128)(2,1)S(1)}, u32[]{:S(2)}, u32[]{:S(2)}) collective-permute-start(bf16[4,32,2176]{2,1,0:T(8,128)(2,1)S(1)} %pad_maximum_fusion.3), channel_id=1, source_target_pairs={{0,4},{4,0},{8,12},{12,8},{16,20},{20,16},{24,28},{28,24},{1,5},{5... | collective-permute-start | bytes 1671176 | tf_op jit(solution)/shard_map/ppermute | solution.py:592
  156.5 6.3 %collective-permute-start.45 = (bf16[2,32,1152]{2,1,0:T(8,128)(2,1)S(1)}, bf16[2,32,1152]{2,1,0:T(8,128)(2,1)S(1)}, u32[]{:S(2)}, u32[]{:S(2)}) collective-permute-start(bf16[2,32,1152]{2,1,0:T(8,128)(2,1)S(1)} %pad_maximum_fusion.8), channel_id=1, source_target_pairs={{0,16},{4,12},{8,24},{12,4},{16,0},{20,28},{24,8},{28,20},{1,17},{... | collective-permute-start | bytes 442376 | tf_op jit(solution)/shard_map/ppermute | solution.py:592
  157.5 5.4 %collective-permute-start.44 = (bf16[32,2176]{1,0:T(8,128)(2,1)S(1)}, bf16[32,2176]{1,0:T(8,128)(2,1)S(1)}, u32[]{:S(2)}, u32[]{:S(2)}) collective-permute-start(bf16[32,2176]{1,0:T(8,128)(2,1)S(1)} %fusion.7.refs_0_), channel_id=1, source_target_pairs={{0,8},{4,20},{8,0},{12,28},{16,24},{20,4},{24,16},{28,12},{1,9},{5... | collective-permute-start | bytes 417800 | tf_op jit(solution)/shard_map/ppermute | solution.py:592
  162.9 3.8 %collective-permute-start.48 = (bf16[4,32,1152]{2,1,0:T(8,128)(2,1)S(1)}, bf16[4,32,1152]{2,1,0:T(8,128)(2,1)S(1)}, u32[]{:S(2)}, u32[]{:S(2)}) collective-permute-start(bf16[4,32,1152]{2,1,0:T(8,128)(2,1)S(1)} %pad_maximum_fusion.5), channel_id=1, source_target_pairs={{0,4},{4,0},{8,12},{12,8},{16,20},{20,16},{24,28},{28,24},{1,5},{5... | collective-permute-start | bytes 884744 | tf_op jit(solution)/shard_map/ppermute | solution.py:592
  163.8 5.8 %collective-permute-start.47 = (bf16[2,32,2176]{2,1,0:T(8,128)(2,1)S(1)}, bf16[2,32,2176]{2,1,0:T(8,128)(2,1)S(1)}, u32[]{:S(2)}, u32[]{:S(2)}) collective-permute-start(bf16[2,32,2176]{2,1,0:T(8,128)(2,1)S(1)} %pad_maximum_fusion.7), channel_id=1, source_target_pairs={{0,16},{4,12},{8,24},{12,4},{16,0},{20,28},{24,8},{28,20},{1,17},{... | collective-permute-start | bytes 835592 | tf_op jit(solution)/shard_map/ppermute | solution.py:592
  169.6 2.5 %collective-permute-start.49 = (bf16[4,32,2176]{2,1,0:T(8,128)(2,1)S(1)}, bf16[4,32,2176]{2,1,0:T(8,128)(2,1)S(1)}, u32[]{:S(2)}, u32[]{:S(2)}) collective-permute-start(bf16[4,32,2176]{2,1,0:T(8,128)(2,1)S(1)} %pad_maximum_fusion.4), channel_id=1, source_target_pairs={{0,4},{4,0},{8,12},{12,8},{16,20},{20,16},{24,28},{28,24},{1,5},{5... | collective-permute-start | bytes 1671176 | tf_op jit(solution)/shard_map/ppermute | solution.py:592
  (15 other events, 129.3 us)

commit v5 on v4

--- a/solution.py
+++ b/solution.py
@@ -639,17 +639,19 @@
     tower_turned = turns([tower_send] * (blocks - 1))
     cross_one, cross_two, *tower_turned = join(cross_one, cross_two, *tower_turned)
 
-    pieces = [chunks[0]] + turns([after(chunk, tower_turned[0]) for chunk in chunks[1:]])
+    turn = lambda value, r: lax.ppermute(value, "mp", turn_by(r))
+    pieces = [chunks[0]] + [turn(after(chunks[r], tower_turned[0]), r) for r in range(1, blocks - 1)]
     tower_mine = jnp.stack(tower_turned) + tally
     both = jnp.concatenate([cross_one, tower_mine], axis=2)
     tower_one, both = hop(tower_mine, first), hop(both, second)
     cross_near = jnp.stack([cross_mine, cross_one, cross_two])
-    both, tower_one, cross_near, *pieces = join(both, tower_one, cross_near, *pieces)
+    cross_far = hop(cross_near, pair)
+    pieces.append(turn(after(chunks[-1], cross_far), blocks - 1))
+    both, tower_one, cross_far, *pieces = join(both, tower_one, cross_far, *pieces)
 
     tower_three = hop(tower_one, second)
     both_far, tower_far, tower_next = hop(both, pair), hop(tower_mine, pair), hop(tower_one, pair)
-    cross_far = hop(cross_near, pair)
-    both_far, tower_far, tower_next, cross_far = join(both_far, tower_far, tower_next, cross_far)
+    both_far, tower_far, tower_next = join(both_far, tower_far, tower_next)
     cross_slices = [cross_near, both, cross_far, both_far]
 
     z_all, x_all = call(
@@ -840,10 +842,13 @@
         mib=16,
         nbytes=2 << 20,
     )
-    last_second, cross_arrived, losses, *tower_turned = join(last_second, cross_arrived, losses, *tower_turned)
-
     last_held = near_sum(last_parts, last_arrived, last_second)
     last_turned = send_blocks(last_held)
+    cross_arrived, losses, last_turned[0], *tower_turned = join(
+        cross_arrived, losses, last_turned[0], *tower_turned
+    )
+
+    last_turned[1:] = [after(value, last_turned[0]) for value in last_turned[1:]]
     cross_second = far_send(cross_parts, cross_arrived)
     tower_mine = down(total_of(tower_held, tower_turned) + jnp.pad(losses, ((0, 0), (full - LANES, hidden))))
     tower_one = hop(tower_mine, first)

time: 175 us -> 174 us (level)
    ppermute x21 -> x18, waiting for transfers between devices: 67.5 us -> 51.3 us  [per_device(): lax.ppermute(value, 'mp', turn_by(r + 1))]
    ppermute x0 -> x3, waiting for transfers between devices: none -> 13.4 us  [per_device(): turn = lambda value, r: lax.ppermute(value, 'mp', turn_by(r))]
    ppermute x29, waiting for transfers between devices: 28.5 us -> 31.4 us  [per_device(): hop = lambda value, perm: lax.ppermute(value, 'dp', perm)]
    ppermute x21 -> x18, starting transfers between devices: 16.4 us -> 14.4 us  [per_device(): lax.ppermute(value, 'mp', turn_by(r + 1))]
  transfers between devices with their start and end apart: 50 -> 50, of which waited for: 33 -> 34; matrix products, arithmetic and copies ran while one was open for 1% -> 1% of each run, Pallas kernels for 16% -> 16%
where the time goes in v5:
time: 174 us
  waiting for transfers between devices  96.1 us (55%)
  starting transfers between devices  35.2 us (20%)
  Pallas kernels  34.3 us (20%)
  local copies, waits for them, and re-layouts  5.04 us (3%)
  other arithmetic  1.82 us (1%)
    ppermute x18, waiting for transfers between devices, per_device(): lax.ppermute(value, 'mp', turn_by(r + 1))  51.3 us
    pallas_call x11, Pallas kernels, call(): pl.pallas_call(kernel, out_shape=outs, in_specs=[SMEM] + specs, out_specs...  34.3 us
    ppermute x29, waiting for transfers between devices, per_device(): hop = lambda value, perm: lax.ppermute(value, 'dp', perm)  31.4 us
    ppermute x29, starting transfers between devices, per_device(): hop = lambda value, perm: lax.ppermute(value, 'dp', perm)  20.1 us
    ppermute x18, starting transfers between devices, per_device(): lax.ppermute(value, 'mp', turn_by(r + 1))  14.4 us
    ppermute x3, waiting for transfers between devices, per_device(): turn = lambda value, r: lax.ppermute(value, 'mp', turn_by(r))  13.4 us
  transfers between devices with their start and end apart: 50, of which 34 were waited for; matrix products, arithmetic and copies ran while one was open for 1% of the time, Pallas kernels for 16%

profile of v5, /device:TPU:9, one launch (start us, length us, event | category | flops | bytes accessed | tf_op | source)
XLA Modules:
  0.0 173.7 jit_solution(13103580678471936316)
XLA Ops:
  0.7 1.1 dynamic-slice_bitcast_fusion
  2.1 1.3 collective-permute-start
  4.5 1.4 collective-permute-start.2
  6.1 1.5 copy-done
  8.6 2.9 %shard_map.202 = (bf16[32,2176]{1,0:T(8,128)(2,1)S(1)}, bf16[256,1152]{1,0:T(8,128)(2,1)S(1)}, bf16[96,128]{1,0:T(8,128)(2,1)S(1)}, bf16[343,256]{1,0:T(8,128)(2...) custom-call(s32[4]{0:T(128)S(1)} %pad_add_fusion.idx, ...), custom_call_target="tpu_custom_call" | custom-call | bytes 2097152 | tf_op jit(solution)/shard_map/pallas_call | solution.py:45
  11.5 8.8 %collective-permute-done.1 = bf16[32,3200]{1,0:T(8,128)(2,1)S(1)} collective-permute-done((bf16[32,3200]{1,0:T(8,128)(2,1)S(1)}, bf16[32,3200]{1,0:T(8,128)(2,1)S(1)}, u32[]{:S(2)}, u32[]{:S(2)}) %collective-permute-start.1) | collective-permute-done | bytes 204832 | tf_op jit(solution)/shard_map/ppermute | solution.py:594
  20.3 2.8 %collective-permute-done.2 = bf16[32,3200]{1,0:T(8,128)(2,1)S(1)} collective-permute-done((bf16[32,3200]{1,0:T(8,128)(2,1)S(1)}, bf16[32,3200]{1,0:T(8,128)(2,1)S(1)}, u32[]{:S(2)}, u32[]{:S(2)}) %collective-permute-start.2) | collective-permute-done | bytes 204832 | tf_op jit(solution)/shard_map/ppermute | solution.py:594
  23.3 1.3 collective-permute-start.3
  24.5 1.2 collective-permute-start.4
  26.0 1.5 collective-permute-start.7
  27.5 2.5 %collective-permute-done.5 = bf16[32,2176]{1,0:T(8,128)(2,1)S(1)} collective-permute-done((bf16[32,2176]{1,0:T(8,128)(2,1)S(1)}, bf16[32,2176]{1,0:T(8,128)(2,1)S(1)}, u32[]{:S(2)}, u32[]{:S(2)}) %collective-permute-start.5) | collective-permute-done | bytes 139296 | tf_op jit(solution)/shard_map/ppermute | solution.py:594
  30.0 6.8 %collective-permute-done.6 = bf16[32,2176]{1,0:T(8,128)(2,1)S(1)} collective-permute-done((bf16[32,2176]{1,0:T(8,128)(2,1)S(1)}, bf16[32,2176]{1,0:T(8,128)(2,1)S(1)}, u32[]{:S(2)}, u32[]{:S(2)}) %collective-permute-start.6) | collective-permute-done | bytes 139296 | tf_op jit(solution)/shard_map/ppermute | solution.py:594
  36.8 2.9 %collective-permute-done.7 = bf16[32,2176]{1,0:T(8,128)(2,1)S(1)} collective-permute-done((bf16[32,2176]{1,0:T(8,128)(2,1)S(1)}, bf16[32,2176]{1,0:T(8,128)(2,1)S(1)}, u32[]{:S(2)}, u32[]{:S(2)}) %collective-permute-start.7) | collective-permute-done | bytes 139296 | tf_op jit(solution)/shard_map/ppermute | solution.py:594
  40.7 1.2 collective-permute-start.8
  44.5 3.7 %collective-permute-done.11.refs_1_.refs_3_.refs_2_ = bf16[343,256]{1,0:T(8,128)(2,1)S(1)} collective-permute-done((bf16[343,256]{1,0:T(8,128)(2,1)S(1)}, bf16[343,256]{1,0:T(8,128)(2,1)S(1)}, u32[]{:S(2)}, u32[]{:S(2)}) %collective-permute-start.11) | collective-permute-done | bytes 175648 | tf_op jit(solution)/shard_map/ppermute | solution.py:642
  48.2 9.4 %collective-permute-done.12.refs_2_.refs_4_.refs_3_ = bf16[343,256]{1,0:T(8,128)(2,1)S(1)} collective-permute-done((bf16[343,256]{1,0:T(8,128)(2,1)S(1)}, bf16[343,256]{1,0:T(8,128)(2,1)S(1)}, u32[]{:S(2)}, u32[]{:S(2)}) %collective-permute-start.12) | collective-permute-done | bytes 175648 | tf_op jit(solution)/shard_map/ppermute | solution.py:642
  57.7 1.4 collective-permute-done.8.refs_6_.refs_10_.refs_7_
  61.4 1.5 collective-permute-done.15.refs_12_
  63.5 3.9 %shard_map.203 = (f32[3,1088,256]{2,1,0:T(8,128)S(1)}, bf16[4,1152,256]{2,1,0:T(8,128)(2,1)S(1)}) custom-call(s32[4]{0:T(128)S(1)} %pad_add_fusion.idx, bf16[343,256]{1,0:T(8,128)(2,1)S(1)} %get-tuple-element.141.refs_0_.refs_2_.refs_1_, bf16[343,256]{1,0:T(8,128)(2,1)S(1)} %collective-permute-done.11.refs_1_.refs_3_.refs_2_, ...), custom_call_target="tpu_custom_call" | custom-call | flops 1925185536 | bytes 20971520 | tf_op jit(solution)/shard_map/pallas_call | solution.py:45
  68.6 1.4 collective-permute-done.18.refs_15_
  70.3 4.4 %shard_map.204 = (bf16[3,1024,256]{2,1,0:T(8,128)(2,1)S(1)}, bf16[2048,256]{1,0:T(8,128)(2,1)S(1)}, f32[1024,128]{1,0:T(8,128)S(1)}, f32[1040,256]{1,0:T(8,128)S...) custom-call(s32[4]{0:T(128)S(1)} %pad_add_fusion.idx, s32[1,1024]{1,0:T(1,128)S(1)} %bitcast.114, ...), custom_call_target="tpu_custom_call" | custom-call | flops 2415919104 | bytes 10485760 | tf_op jit(solution)/shard_map/pallas_call | solution.py:45
  74.9 2.5 %collective-permute-done.20.far = bf16[2048,256]{1,0:T(8,128)(2,1)S(1)} collective-permute-done((bf16[2048,256]{1,0:T(8,128)(2,1)S(1)}, bf16[2048,256]{1,0:T(8,128)(2,1)S(1)}, u32[]{:S(2)}, u32[]{:S(2)}) %collective-permute-start.20) | collective-permute-done | bytes 1048608 | tf_op jit(solution)/shard_map/ppermute | solution.py:592
  77.4 3.0 %shard_map.205 = (bf16[4,32,2176]{2,1,0:T(8,128)(2,1)S(1)}, bf16[4,32,2176]{2,1,0:T(8,128)(2,1)S(1)}, bf16[2,4,32,2176]{3,2,1,0:T(8,128)(2,1)S(1)}) custom-call(s32[4]{0:T(128)S(1)} %pad_add_fusion.idx, bf16[4,1152,256]{2,1,0:T(8,128)(2,1)S(1)} %get-tuple-element.152.refs_16_.x_all, bf16[4,1152,256]{2,1,0:T(8,128)(2,1)S(1)} %collective-permute-done.19.x_far, ...), custom_call_target="tpu_custom_call" | custom-call | flops 1207959552 | bytes 10485760 | tf_op jit(solution)/shard_map/pallas_call | solution.py:45
  81.5 5.5 %shard_map.206 = (bf16[272,256]{1,0:T(8,128)(2,1)S(1)}, bf16[272,256]{1,0:T(8,128)(2,1)S(1)}, bf16[272,256]{1,0:T(8,128)(2,1)S(1)}, bf16[272,256]{1,0:T(8,128)(2...) custom-call(s32[4]{0:T(128)S(1)} %pad_add_fusion.idx, ...), custom_call_target="tpu_custom_call" | custom-call | flops 1925185536 | bytes 20971520 | tf_op jit(solution)/shard_map/pallas_call | solution.py:45
  88.7 2.3 %shard_map.207 = (bf16[4,32,1152]{2,1,0:T(8,128)(2,1)S(1)}, bf16[4,32,1152]{2,1,0:T(8,128)(2,1)S(1)}, bf16[2,4,32,1152]{3,2,1,0:T(8,128)(2,1)S(1)}) custom-call(s32[4]{0:T(128)S(1)} %pad_add_fusion.idx, bf16[4,1152,256]{2,1,0:T(8,128)(2,1)S(1)} %get-tuple-element.152.refs_16_.x_all, bf16[4,1152,256]{2,1,0:T(8,128)(2,1)S(1)} %collective-permute-done.19.x_far, ...), custom_call_target="tpu_custom_call" | custom-call | flops 641728512 | bytes 10485760 | tf_op jit(solution)/shard_map/pallas_call | solution.py:45
  90.9 1.5 collective-permute-done.23.refs_1_
  92.4 2.7 %collective-permute-done.21 = bf16[2,4,32,2176]{3,2,1,0:T(8,128)(2,1)S(1)} collective-permute-done((bf16[2,4,32,2176]{3,2,1,0:T(8,128)(2,1)S(1)}, bf16[2,4,32,2176]{3,2,1,0:T(8,128)(2,1)S(1)}, u32[]{:S(2)}, u32[]{:S(2)}) %collective-permute-start.21) | collective-permute-done | bytes 1114144 | tf_op jit(solution)/shard_map/ppermute | solution.py:592
  98.3 3.8 %shard_map.208 = (bf16[4,32,2176]{2,1,0:T(8,128)(2,1)S(1)}, bf16[4,32,2176]{2,1,0:T(8,128)(2,1)S(1)}, bf16[2,4,32,2176]{3,2,1,0:T(8,128)(2,1)S(1)}) custom-call(s32[4]{0:T(128)S(1)} %pad_add_fusion.idx, bf16[4,1152,256]{2,1,0:T(8,128)(2,1)S(1)} %get-tuple-element.152.refs_16_.x_all, bf16[4,1152,256]{2,1,0:T(8,128)(2,1)S(1)} %collective-permute-done.19.x_far, ...), custom_call_target="tpu_custom_call" | custom-call | flops 1283457024 | bytes 10485760 | tf_op jit(solution)/shard_map/pallas_call | solution.py:45
  102.1 4.1 %collective-permute-done.27.refs_2_ = bf16[272,256]{1,0:T(8,128)(2,1)S(1)} collective-permute-done((bf16[272,256]{1,0:T(8,128)(2,1)S(1)}, bf16[272,256]{1,0:T(8,128)(2,1)S(1)}, u32[]{:S(2)}, u32[]{:S(2)}) %collective-permute-start.27) | collective-permute-done | bytes 139296 | tf_op jit(solution)/shard_map/ppermute | solution.py:594
  106.9 3.9 %collective-permute-done.24 = bf16[4,32,2176]{2,1,0:T(8,128)(2,1)S(1)} collective-permute-done((bf16[4,32,2176]{2,1,0:T(8,128)(2,1)S(1)}, bf16[4,32,2176]{2,1,0:T(8,128)(2,1)S(1)}, u32[]{:S(2)}, u32[]{:S(2)}) %collective-permute-start.24) | collective-permute-done | bytes 557088 | tf_op jit(solution)/shard_map/ppermute | solution.py:592
  112.1 1.8 %collective-permute-start.33 = (bf16[32,2176]{1,0:T(8,128)(2,1)S(1)}, bf16[32,2176]{1,0:T(8,128)(2,1)S(1)}, u32[]{:S(2)}, u32[]{:S(2)}) collective-permute-start(bf16[32,2176]{1,0:T(8,128)(2,1)S(1)} %get-tuple-element.241), channel_id=1, source_target_pairs={{0,2},{1,3},{2,0},{3,1},{4,6},{5,7},{6,4},{7,5},{8,10},{9,11},{10,... | collective-permute-start | bytes 417800 | tf_op jit(solution)/shard_map/ppermute | solution.py:594
  113.9 1.4 collective-permute-start.34
  115.2 2.5 %collective-permute-done.30 = bf16[4,32,1152]{2,1,0:T(8,128)(2,1)S(1)} collective-permute-done((bf16[4,32,1152]{2,1,0:T(8,128)(2,1)S(1)}, bf16[4,32,1152]{2,1,0:T(8,128)(2,1)S(1)}, u32[]{:S(2)}, u32[]{:S(2)}) %collective-permute-start.30) | collective-permute-done | bytes 294944 | tf_op jit(solution)/shard_map/ppermute | solution.py:592
  117.9 1.6 shard_map.209
  119.6 9.0 %collective-permute-done.34 = bf16[32,2176]{1,0:T(8,128)(2,1)S(1)} collective-permute-done((bf16[32,2176]{1,0:T(8,128)(2,1)S(1)}, bf16[32,2176]{1,0:T(8,128)(2,1)S(1)}, u32[]{:S(2)}, u32[]{:S(2)}) %collective-permute-start.34) | collective-permute-done | bytes 139296 | tf_op jit(solution)/shard_map/ppermute | solution.py:594
  130.5 2.0 %collective-permute-start.37 = (bf16[32,1152]{1,0:T(8,128)(2,1)S(1)}, bf16[32,1152]{1,0:T(8,128)(2,1)S(1)}, u32[]{:S(2)}, u32[]{:S(2)}) collective-permute-start(bf16[32,1152]{1,0:T(8,128)(2,1)S(1)} %get-tuple-element.244), channel_id=1, source_target_pairs={{0,2},{1,3},{2,0},{3,1},{4,6},{5,7},{6,4},{7,5},{8,10},{9,11},{10,... | collective-permute-start | bytes 221192 | tf_op jit(solution)/shard_map/ppermute | solution.py:594
  132.6 1.5 collective-permute-done.38
  134.0 2.2 %collective-permute-done.37 = bf16[32,1152]{1,0:T(8,128)(2,1)S(1)} collective-permute-done((bf16[32,1152]{1,0:T(8,128)(2,1)S(1)}, bf16[32,1152]{1,0:T(8,128)(2,1)S(1)}, u32[]{:S(2)}, u32[]{:S(2)}) %collective-permute-start.37) | collective-permute-done | bytes 73760 | tf_op jit(solution)/shard_map/ppermute | solution.py:594
  136.2 3.4 %collective-permute-done.35 = bf16[4,32,2176]{2,1,0:T(8,128)(2,1)S(1)} collective-permute-done((bf16[4,32,2176]{2,1,0:T(8,128)(2,1)S(1)}, bf16[4,32,2176]{2,1,0:T(8,128)(2,1)S(1)}, u32[]{:S(2)}, u32[]{:S(2)}) %collective-permute-start.35) | collective-permute-done | bytes 557088 | tf_op jit(solution)/shard_map/ppermute | solution.py:592
  140.0 2.2 %collective-permute-start.42 = (bf16[32,2176]{1,0:T(8,128)(2,1)S(1)}, bf16[32,2176]{1,0:T(8,128)(2,1)S(1)}, u32[]{:S(2)}, u32[]{:S(2)}) collective-permute-start(bf16[32,2176]{1,0:T(8,128)(2,1)S(1)} %get-tuple-element.238), channel_id=1, source_target_pairs={{0,2},{1,3},{2,0},{3,1},{4,6},{5,7},{6,4},{7,5},{8,10},{9,11},{10,... | collective-permute-start | bytes 417800 | tf_op jit(solution)/shard_map/ppermute | solution.py:594
  144.5 2.3 %collective-permute-done.40.refs_1_ = bf16[32,1152]{1,0:T(8,128)(2,1)S(1)} collective-permute-done((bf16[32,1152]{1,0:T(8,128)(2,1)S(1)}, bf16[32,1152]{1,0:T(8,128)(2,1)S(1)}, u32[]{:S(2)}, u32[]{:S(2)}) %collective-permute-start.40) | collective-permute-done | bytes 73760 | tf_op jit(solution)/shard_map/ppermute | solution.py:592
  146.8 4.8 %collective-permute-done.42 = bf16[32,2176]{1,0:T(8,128)(2,1)S(1)} collective-permute-done((bf16[32,2176]{1,0:T(8,128)(2,1)S(1)}, bf16[32,2176]{1,0:T(8,128)(2,1)S(1)}, u32[]{:S(2)}, u32[]{:S(2)}) %collective-permute-start.42) | collective-permute-done | bytes 139296 | tf_op jit(solution)/shard_map/ppermute | solution.py:594
  151.7 3.6 %collective-permute-done.43 = bf16[32,2176]{1,0:T(8,128)(2,1)S(1)} collective-permute-done((bf16[32,2176]{1,0:T(8,128)(2,1)S(1)}, bf16[32,2176]{1,0:T(8,128)(2,1)S(1)}, u32[]{:S(2)}, u32[]{:S(2)}) %collective-permute-start.43) | collective-permute-done | bytes 139296 | tf_op jit(solution)/shard_map/ppermute | solution.py:594
  157.2 4.3 %collective-permute-done.44.refs_1_ = bf16[32,2176]{1,0:T(8,128)(2,1)S(1)} collective-permute-done((bf16[32,2176]{1,0:T(8,128)(2,1)S(1)}, bf16[32,2176]{1,0:T(8,128)(2,1)S(1)}, u32[]{:S(2)}, u32[]{:S(2)}) %collective-permute-start.44) | collective-permute-done | bytes 139296 | tf_op jit(solution)/shard_map/ppermute | solution.py:592
  162.8 2.5 %shard_map.210 = (f32[1040,256]{1,0:T(8,128)}, f32[256,1024]{1,0:T(8,128)}, f32[3,256]{1,0:T(4,128)S(1)}, f32[1,1]{1,0:T(1,128)}) custom-call(s32[4]{0:T(128)S(1)} %pad_add_fusion.idx, bf16[32,2176]{1,0:T(8,128)(2,1)S(1)} %fusion.10.refs_0_, bf16[32,2176]{1,0:T(8,128)(2,1)S(1)} %collective-permute-done.36.refs_1_, ...), custom_call_target="tpu_custom_call" | custom-call | bytes 4194304 | tf_op jit(solution)/shard_map/pallas_call | solution.py:45
  165.3 1.8 %shard_map.211 = (f32[3,260,1040]{2,1,0:T(8,128)}, f32[1,260]{1,0:T(1,128)S(1)}) custom-call(s32[4]{0:T(128)S(1)} %pad_add_fusion.idx, bf16[32,1152]{1,0:T(8,128)(2,1)S(1)} %fusion.12.refs_0_, bf16[32,1152]{1,0:T(8,128)(2,1)S(1)} %collective-permute-done.40.refs_1_, bf16[2,32,1152]{2,1,0:T(8,128)(2,1)S(1)} %collective-permute-done.45.refs_2_, ...), custom_call_target="tpu_custom_call" | custom-call | bytes 4194304 | tf_op jit(solution)/shard_map/pallas_call | solution.py:45
  167.1 1.2 collective-permute-done.47.refs_2_
  170.9 2.7 %shard_map.212 = (f32[3,260,1040]{2,1,0:T(8,128)}, f32[3,260]{1,0:T(4,128)}) custom-call(s32[4]{0:T(128)S(1)} %pad_add_fusion.idx, bf16[32,2176]{1,0:T(8,128)(2,1)S(1)} %fusion.7.refs_0_, bf16[32,2176]{1,0:T(8,128)(2,1)S(1)} %collective-permute-done.44.refs_1_, ...), custom_call_target="tpu_custom_call", output_to_operand_aliasing={{0}: (5, {})} | custom-call | bytes 4194304 | tf_op jit(solution)/shard_map/pallas_call | solution.py:45
  (127 shorter events, 29.4 us)
Async XLA Ops:
  2.1 9.4 %collective-permute-start = (bf16[32,3200]{1,0:T(8,128)(2,1)S(1)}, bf16[32,3200]{1,0:T(8,128)(2,1)S(1)}, u32[]{:S(2)}, u32[]{:S(2)}) collective-permute-start(bf16[32,3200]{1,0:T(8,128)(2,1)S(1)} %concatenate.15), channel_id=1, source_target_pairs={{0,1},{1,2},{2,3},{3,0},{4,5},{5,6},{6,7},{7,4},{8,9},{9,10},{10,1... | collective-permute-start | bytes 614408 | tf_op jit(solution)/shard_map/ppermute | solution.py:594
  3.4 16.9 %collective-permute-start.1 = (bf16[32,3200]{1,0:T(8,128)(2,1)S(1)}, bf16[32,3200]{1,0:T(8,128)(2,1)S(1)}, u32[]{:S(2)}, u32[]{:S(2)}) collective-permute-start(bf16[32,3200]{1,0:T(8,128)(2,1)S(1)} %concatenate.15), channel_id=1, source_target_pairs={{0,2},{1,3},{2,0},{3,1},{4,6},{5,7},{6,4},{7,5},{8,10},{9,11},{10,... | collective-permute-start | bytes 614408 | tf_op jit(solution)/shard_map/ppermute | solution.py:594
  4.5 18.7 %collective-permute-start.2 = (bf16[32,3200]{1,0:T(8,128)(2,1)S(1)}, bf16[32,3200]{1,0:T(8,128)(2,1)S(1)}, u32[]{:S(2)}, u32[]{:S(2)}) collective-permute-start(bf16[32,3200]{1,0:T(8,128)(2,1)S(1)} %concatenate.15), channel_id=1, source_target_pairs={{0,3},{1,0},{2,1},{3,2},{4,7},{5,4},{6,5},{7,6},{8,11},{9,8},{10,9... | collective-permute-start | bytes 614408 | tf_op jit(solution)/shard_map/ppermute | solution.py:594
  23.3 16.5 %collective-permute-start.3 = (bf16[3,32,3200]{2,1,0:T(8,128)(2,1)S(1)}, bf16[3,32,3200]{2,1,0:T(8,128)(2,1)S(1)}, u32[]{:S(2)}, u32[]{:S(2)}) collective-permute-start(bf16[3,32,3200]{2,1,0:T(8,128)(2,1)S(1)} %pad_maximum_fusion.2), channel_id=1, source_target_pairs={{0,8},{4,20},{8,0},{12,28},{16,24},{20,4},{24,16},{28,12},{1,9},{5... | collective-permute-start | bytes 1843208 | tf_op jit(solution)/shard_map/ppermute | solution.py:592
  24.5 15.3 %collective-permute-start.4 = (bf16[3,32,3200]{2,1,0:T(8,128)(2,1)S(1)}, bf16[3,32,3200]{2,1,0:T(8,128)(2,1)S(1)}, u32[]{:S(2)}, u32[]{:S(2)}) collective-permute-start(bf16[3,32,3200]{2,1,0:T(8,128)(2,1)S(1)} %pad_maximum_fusion.2), channel_id=1, source_target_pairs={{0,16},{4,12},{8,24},{12,4},{16,0},{20,28},{24,8},{28,20},{1,17},{... | collective-permute-start | bytes 1843208 | tf_op jit(solution)/shard_map/ppermute | solution.py:592
  25.8 4.2 %collective-permute-start.5 = (bf16[32,2176]{1,0:T(8,128)(2,1)S(1)}, bf16[32,2176]{1,0:T(8,128)(2,1)S(1)}, u32[]{:S(2)}, u32[]{:S(2)}) collective-permute-start(bf16[32,2176]{1,0:T(8,128)(2,1)S(1)} %get-tuple-element.127), channel_id=1, source_target_pairs={{0,1},{1,2},{2,3},{3,0},{4,5},{5,6},{6,7},{7,4},{8,9},{9,10},{10,1... | collective-permute-start | bytes 417800 | tf_op jit(solution)/shard_map/ppermute | solution.py:594
  25.8 11.0 %collective-permute-start.6 = (bf16[32,2176]{1,0:T(8,128)(2,1)S(1)}, bf16[32,2176]{1,0:T(8,128)(2,1)S(1)}, u32[]{:S(2)}, u32[]{:S(2)}) collective-permute-start(bf16[32,2176]{1,0:T(8,128)(2,1)S(1)} %get-tuple-element.127), channel_id=1, source_target_pairs={{0,2},{1,3},{2,0},{3,1},{4,6},{5,7},{6,4},{7,5},{8,10},{9,11},{10,... | collective-permute-start | bytes 417800 | tf_op jit(solution)/shard_map/ppermute | solution.py:594
  26.0 13.7 %collective-permute-start.7 = (bf16[32,2176]{1,0:T(8,128)(2,1)S(1)}, bf16[32,2176]{1,0:T(8,128)(2,1)S(1)}, u32[]{:S(2)}, u32[]{:S(2)}) collective-permute-start(bf16[32,2176]{1,0:T(8,128)(2,1)S(1)} %get-tuple-element.127), channel_id=1, source_target_pairs={{0,3},{1,0},{2,1},{3,2},{4,7},{5,4},{6,5},{7,6},{8,11},{9,8},{10,9... | collective-permute-start | bytes 417800 | tf_op jit(solution)/shard_map/ppermute | solution.py:594
  40.1 3.9 %collective-permute-start.10 = (bf16[3,3,32,3200]{3,2,1,0:T(8,128)(2,1)S(1)}, bf16[3,3,32,3200]{3,2,1,0:T(8,128)(2,1)S(1)}, u32[]{:S(2)}, u32[]{:S(2)}) collective-permute-start(bf16[3,3,32,3200]{3,2,1,0:T(8,128)(2,1)S(1)} %pad_maximum_fusion.refs_5_.refs_6_), channel_id=1, source_target_pairs={{0,4},{4,0},{8,12},{12,8},{16,20},{20,16},{24,28},{28,24},{1,5},{5... | collective-permute-start | bytes 5529608 | tf_op jit(solution)/shard_map/ppermute | solution.py:592
  40.7 18.3 %collective-permute-start.8 = (bf16[3,32,5376]{2,1,0:T(8,128)(2,1)S(1)}, bf16[3,32,5376]{2,1,0:T(8,128)(2,1)S(1)}, u32[]{:S(2)}, u32[]{:S(2)}) collective-permute-start(bf16[3,32,5376]{2,1,0:T(8,128)(2,1)S(1)} %pad_maximum_fusion.1), channel_id=1, source_target_pairs={{0,16},{4,12},{8,24},{12,4},{16,0},{20,28},{24,8},{28,20},{1,17},{... | collective-permute-start | bytes 3096584 | tf_op jit(solution)/shard_map/ppermute | solution.py:592
  42.0 15.7 %collective-permute-start.9 = (bf16[3,32,2176]{2,1,0:T(8,128)(2,1)S(1)}, bf16[3,32,2176]{2,1,0:T(8,128)(2,1)S(1)}, u32[]{:S(2)}, u32[]{:S(2)}) collective-permute-start(bf16[3,32,2176]{2,1,0:T(8,128)(2,1)S(1)} %maximum_add_fusion.refs_8_), channel_id=1, source_target_pairs={{0,8},{4,20},{8,0},{12,28},{16,24},{20,4},{24,16},{28,12},{1,9},{5... | collective-permute-start | bytes 1253384 | tf_op jit(solution)/shard_map/ppermute | solution.py:592
  42.8 5.4 %collective-permute-start.11 = (bf16[343,256]{1,0:T(8,128)(2,1)S(1)}, bf16[343,256]{1,0:T(8,128)(2,1)S(1)}, u32[]{:S(2)}, u32[]{:S(2)}) collective-permute-start(bf16[343,256]{1,0:T(8,128)(2,1)S(1)} %get-tuple-element.136), channel_id=1, source_target_pairs={{0,1},{1,2},{2,3},{3,0},{4,5},{5,6},{6,7},{7,4},{8,9},{9,10},{10,1... | collective-permute-start | bytes 526856 | tf_op jit(solution)/shard_map/ppermute | solution.py:642
  42.8 14.9 %collective-permute-start.12 = (bf16[343,256]{1,0:T(8,128)(2,1)S(1)}, bf16[343,256]{1,0:T(8,128)(2,1)S(1)}, u32[]{:S(2)}, u32[]{:S(2)}) collective-permute-start(bf16[343,256]{1,0:T(8,128)(2,1)S(1)} %get-tuple-element.138), channel_id=1, source_target_pairs={{0,2},{1,3},{2,0},{3,1},{4,6},{5,7},{6,4},{7,5},{8,10},{9,11},{10,... | collective-permute-start | bytes 526856 | tf_op jit(solution)/shard_map/ppermute | solution.py:642
  44.0 15.3 %collective-permute-start.13 = (bf16[343,256]{1,0:T(8,128)(2,1)S(1)}, bf16[343,256]{1,0:T(8,128)(2,1)S(1)}, u32[]{:S(2)}, u32[]{:S(2)}) collective-permute-start(bf16[343,256]{1,0:T(8,128)(2,1)S(1)} %get-tuple-element.140), channel_id=1, source_target_pairs={{0,3},{1,0},{2,1},{3,2},{4,7},{5,4},{6,5},{7,6},{8,11},{9,8},{10,9... | collective-permute-start | bytes 526856 | tf_op jit(solution)/shard_map/ppermute | solution.py:642
  59.3 4.2 %collective-permute-start.14 = (bf16[3,32,5376]{2,1,0:T(8,128)(2,1)S(1)}, bf16[3,32,5376]{2,1,0:T(8,128)(2,1)S(1)}, u32[]{:S(2)}, u32[]{:S(2)}) collective-permute-start(bf16[3,32,5376]{2,1,0:T(8,128)(2,1)S(1)} %collective-permute-done.8.refs_6_.refs_10_.refs_7_), channel_id=1, source_target_pairs={{0,4},{4,0},{8,12},{12,8},{16,20},{20,16},{24,28},{28,24},{1,5},{5... | collective-permute-start | bytes 3096584 | tf_op jit(solution)/shard_map/ppermute | solution.py:592
  60.0 2.9 %collective-permute-start.15 = (bf16[3,32,2176]{2,1,0:T(8,128)(2,1)S(1)}, bf16[3,32,2176]{2,1,0:T(8,128)(2,1)S(1)}, u32[]{:S(2)}, u32[]{:S(2)}) collective-permute-start(bf16[3,32,2176]{2,1,0:T(8,128)(2,1)S(1)} %maximum_add_fusion.refs_8_), channel_id=1, source_target_pairs={{0,4},{4,0},{8,12},{12,8},{16,20},{20,16},{24,28},{28,24},{1,5},{5... | collective-permute-start | bytes 1253384 | tf_op jit(solution)/shard_map/ppermute | solution.py:592
  60.0 3.5 %collective-permute-start.16 = (bf16[3,32,2176]{2,1,0:T(8,128)(2,1)S(1)}, bf16[3,32,2176]{2,1,0:T(8,128)(2,1)S(1)}, u32[]{:S(2)}, u32[]{:S(2)}) collective-permute-start(bf16[3,32,2176]{2,1,0:T(8,128)(2,1)S(1)} %collective-permute-done.9.refs_9_), channel_id=1, source_target_pairs={{0,4},{4,0},{8,12},{12,8},{16,20},{20,16},{24,28},{28,24},{1,5},{5... | collective-permute-start | bytes 1253384 | tf_op jit(solution)/shard_map/ppermute | solution.py:592
  60.5 7.2 %collective-permute-start.17 = (bf16[3,32,2176]{2,1,0:T(8,128)(2,1)S(1)}, bf16[3,32,2176]{2,1,0:T(8,128)(2,1)S(1)}, u32[]{:S(2)}, u32[]{:S(2)}) collective-permute-start(bf16[3,32,2176]{2,1,0:T(8,128)(2,1)S(1)} %collective-permute-done.9.refs_9_), channel_id=1, source_target_pairs={{0,16},{4,12},{8,24},{12,4},{16,0},{20,28},{24,8},{28,20},{1,17},{... | collective-permute-start | bytes 1253384 | tf_op jit(solution)/shard_map/ppermute | solution.py:592
  70.0 7.5 %collective-permute-start.19 = (bf16[4,1152,256]{2,1,0:T(8,128)(2,1)S(1)}, bf16[4,1152,256]{2,1,0:T(8,128)(2,1)S(1)}, u32[]{:S(2)}, u32[]{:S(2)}) collective-permute-start(bf16[4,1152,256]{2,1,0:T(8,128)(2,1)S(1)} %get-tuple-element.152.refs_16_.x_all), channel_id=1, source_target_pairs={{0,4},{4,0},{8,12},{12,8},{16,20},{20,16},{24,28},{28,24},{1,5},{5... | collective-permute-start | bytes 7077896 | tf_op jit(solution)/shard_map/ppermute | solution.py:592
  74.7 2.7 %collective-permute-start.20 = (bf16[2048,256]{1,0:T(8,128)(2,1)S(1)}, bf16[2048,256]{1,0:T(8,128)(2,1)S(1)}, u32[]{:S(2)}, u32[]{:S(2)}) collective-permute-start(bf16[2048,256]{1,0:T(8,128)(2,1)S(1)} %get-tuple-element.157), channel_id=1, source_target_pairs={{0,4},{4,0},{8,12},{12,8},{16,20},{20,16},{24,28},{28,24},{1,5},{5... | collective-permute-start | bytes 3145736 | tf_op jit(solution)/shard_map/ppermute | solution.py:592
  80.4 14.7 %collective-permute-start.21 = (bf16[2,4,32,2176]{3,2,1,0:T(8,128)(2,1)S(1)}, bf16[2,4,32,2176]{3,2,1,0:T(8,128)(2,1)S(1)}, u32[]{:S(2)}, u32[]{:S(2)}) collective-permute-start(bf16[2,4,32,2176]{3,2,1,0:T(8,128)(2,1)S(1)} %get-tuple-element.160), channel_id=1, source_target_pairs={{0,8},{4,20},{8,0},{12,28},{16,24},{20,4},{24,16},{28,12},{1,9},{5... | collective-permute-start | bytes 3342344 | tf_op jit(solution)/shard_map/ppermute | solution.py:592
  87.4 5.1 %collective-permute-start.23 = (bf16[272,256]{1,0:T(8,128)(2,1)S(1)}, bf16[272,256]{1,0:T(8,128)(2,1)S(1)}, u32[]{:S(2)}, u32[]{:S(2)}) collective-permute-start(bf16[272,256]{1,0:T(8,128)(2,1)S(1)} %get-tuple-element.168), channel_id=1, source_target_pairs={{0,1},{1,2},{2,3},{3,0},{4,5},{5,6},{6,7},{7,4},{8,9},{9,10},{10,1... | collective-permute-start | bytes 417800 | tf_op jit(solution)/shard_map/ppermute | solution.py:594
  87.4 10.9 %collective-permute-start.26 = (bf16[2,528,256]{2,1,0:T(8,128)(2,1)S(1)}, bf16[2,528,256]{2,1,0:T(8,128)(2,1)S(1)}, u32[]{:S(2)}, u32[]{:S(2)}) collective-permute-start(bf16[2,528,256]{2,1,0:T(8,128)(2,1)S(1)} %get-tuple-element.173), channel_id=1, source_target_pairs={{0,4},{4,0},{8,12},{12,8},{16,20},{20,16},{24,28},{28,24},{1,5},{5... | collective-permute-start | bytes 1622024 | tf_op jit(solution)/shard_map/ppermute | solution.py:592
  95.1 15.6 %collective-permute-start.25 = (bf16[2,4,32,1152]{3,2,1,0:T(8,128)(2,1)S(1)}, bf16[2,4,32,1152]{3,2,1,0:T(8,128)(2,1)S(1)}, u32[]{:S(2)}, u32[]{:S(2)}) collective-permute-start(bf16[2,4,32,1152]{3,2,1,0:T(8,128)(2,1)S(1)} %get-tuple-element.171), channel_id=1, source_target_pairs={{0,8},{4,20},{8,0},{12,28},{16,24},{20,4},{24,16},{28,12},{1,9},{5... | collective-permute-start | bytes 1769480 | tf_op jit(solution)/shard_map/ppermute | solution.py:592
  96.3 14.5 %collective-permute-start.24 = (bf16[4,32,2176]{2,1,0:T(8,128)(2,1)S(1)}, bf16[4,32,2176]{2,1,0:T(8,128)(2,1)S(1)}, u32[]{:S(2)}, u32[]{:S(2)}) collective-permute-start(bf16[4,32,2176]{2,1,0:T(8,128)(2,1)S(1)} %fusion.2), channel_id=1, source_target_pairs={{0,16},{4,12},{8,24},{12,4},{16,0},{20,28},{24,8},{28,20},{1,17},{... | collective-permute-start | bytes 1671176 | tf_op jit(solution)/shard_map/ppermute | solution.py:592
  97.2 8.9 %collective-permute-start.27 = (bf16[272,256]{1,0:T(8,128)(2,1)S(1)}, bf16[272,256]{1,0:T(8,128)(2,1)S(1)}, u32[]{:S(2)}, u32[]{:S(2)}) collective-permute-start(bf16[272,256]{1,0:T(8,128)(2,1)S(1)} %get-tuple-element.177), channel_id=1, source_target_pairs={{0,2},{1,3},{2,0},{3,1},{4,6},{5,7},{6,4},{7,5},{8,10},{9,11},{10,... | collective-permute-start | bytes 417800 | tf_op jit(solution)/shard_map/ppermute | solution.py:594
  98.3 8.6 %collective-permute-start.28 = (bf16[272,256]{1,0:T(8,128)(2,1)S(1)}, bf16[272,256]{1,0:T(8,128)(2,1)S(1)}, u32[]{:S(2)}, u32[]{:S(2)}) collective-permute-start(bf16[272,256]{1,0:T(8,128)(2,1)S(1)} %get-tuple-element.178), channel_id=1, source_target_pairs={{0,3},{1,0},{2,1},{3,2},{4,7},{5,4},{6,5},{7,6},{8,11},{9,8},{10,9... | collective-permute-start | bytes 417800 | tf_op jit(solution)/shard_map/ppermute | solution.py:594
  110.8 6.9 %collective-permute-start.30 = (bf16[4,32,1152]{2,1,0:T(8,128)(2,1)S(1)}, bf16[4,32,1152]{2,1,0:T(8,128)(2,1)S(1)}, u32[]{:S(2)}, u32[]{:S(2)}) collective-permute-start(bf16[4,32,1152]{2,1,0:T(8,128)(2,1)S(1)} %fusion.4), channel_id=1, source_target_pairs={{0,16},{4,12},{8,24},{12,4},{16,0},{20,28},{24,8},{28,20},{1,17},{... | collective-permute-start | bytes 884744 | tf_op jit(solution)/shard_map/ppermute | solution.py:592
  111.8 17.5 %collective-permute-start.29 = (bf16[2,4,32,2176]{3,2,1,0:T(8,128)(2,1)S(1)}, bf16[2,4,32,2176]{3,2,1,0:T(8,128)(2,1)S(1)}, u32[]{:S(2)}, u32[]{:S(2)}) collective-permute-start(bf16[2,4,32,2176]{3,2,1,0:T(8,128)(2,1)S(1)} %get-tuple-element.180), channel_id=1, source_target_pairs={{0,8},{4,20},{8,0},{12,28},{16,24},{20,4},{24,16},{28,12},{1,9},{5... | collective-permute-start | bytes 3342344 | tf_op jit(solution)/shard_map/ppermute | solution.py:592
  112.0 7.5 %collective-permute-start.32 = (bf16[32,2176]{1,0:T(8,128)(2,1)S(1)}, bf16[32,2176]{1,0:T(8,128)(2,1)S(1)}, u32[]{:S(2)}, u32[]{:S(2)}) collective-permute-start(bf16[32,2176]{1,0:T(8,128)(2,1)S(1)} %get-tuple-element.242), channel_id=1, source_target_pairs={{0,1},{1,2},{2,3},{3,0},{4,5},{5,6},{6,7},{7,4},{8,9},{9,10},{10,1... | collective-permute-start | bytes 417800 | tf_op jit(solution)/shard_map/ppermute | solution.py:594
  112.1 7.5 %collective-permute-start.33 = (bf16[32,2176]{1,0:T(8,128)(2,1)S(1)}, bf16[32,2176]{1,0:T(8,128)(2,1)S(1)}, u32[]{:S(2)}, u32[]{:S(2)}) collective-permute-start(bf16[32,2176]{1,0:T(8,128)(2,1)S(1)} %get-tuple-element.241), channel_id=1, source_target_pairs={{0,2},{1,3},{2,0},{3,1},{4,6},{5,7},{6,4},{7,5},{8,10},{9,11},{10,... | collective-permute-start | bytes 417800 | tf_op jit(solution)/shard_map/ppermute | solution.py:594
  113.9 14.7 %collective-permute-start.34 = (bf16[32,2176]{1,0:T(8,128)(2,1)S(1)}, bf16[32,2176]{1,0:T(8,128)(2,1)S(1)}, u32[]{:S(2)}, u32[]{:S(2)}) collective-permute-start(bf16[32,2176]{1,0:T(8,128)(2,1)S(1)} %get-tuple-element.240), channel_id=1, source_target_pairs={{0,3},{1,0},{2,1},{3,2},{4,7},{5,4},{6,5},{7,6},{8,11},{9,8},{10,9... | collective-permute-start | bytes 417800 | tf_op jit(solution)/shard_map/ppermute | solution.py:594
  117.9 10.7 %collective-permute-start.31 = (bf16[32,1152]{1,0:T(8,128)(2,1)S(1)}, bf16[32,1152]{1,0:T(8,128)(2,1)S(1)}, u32[]{:S(2)}, u32[]{:S(2)}) collective-permute-start(bf16[32,1152]{1,0:T(8,128)(2,1)S(1)} %get-tuple-element.245), channel_id=1, source_target_pairs={{0,1},{1,2},{2,3},{3,0},{4,5},{5,6},{6,7},{7,4},{8,9},{9,10},{10,1... | collective-permute-start | bytes 221192 | tf_op jit(solution)/shard_map/ppermute | solution.py:594
  129.4 10.2 %collective-permute-start.35 = (bf16[4,32,2176]{2,1,0:T(8,128)(2,1)S(1)}, bf16[4,32,2176]{2,1,0:T(8,128)(2,1)S(1)}, u32[]{:S(2)}, u32[]{:S(2)}) collective-permute-start(bf16[4,32,2176]{2,1,0:T(8,128)(2,1)S(1)} %fusion.1), channel_id=1, source_target_pairs={{0,16},{4,12},{8,24},{12,4},{16,0},{20,28},{24,8},{28,20},{1,17},{... | collective-permute-start | bytes 1671176 | tf_op jit(solution)/shard_map/ppermute | solution.py:592
  130.2 6.1 %collective-permute-start.36 = (bf16[32,2176]{1,0:T(8,128)(2,1)S(1)}, bf16[32,2176]{1,0:T(8,128)(2,1)S(1)}, u32[]{:S(2)}, u32[]{:S(2)}) collective-permute-start(bf16[32,2176]{1,0:T(8,128)(2,1)S(1)} %fusion.10.refs_0_), channel_id=1, source_target_pairs={{0,8},{4,20},{8,0},{12,28},{16,24},{20,4},{24,16},{28,12},{1,9},{5... | collective-permute-start | bytes 417800 | tf_op jit(solution)/shard_map/ppermute | solution.py:592
  130.5 3.5 %collective-permute-start.38 = (bf16[32,1152]{1,0:T(8,128)(2,1)S(1)}, bf16[32,1152]{1,0:T(8,128)(2,1)S(1)}, u32[]{:S(2)}, u32[]{:S(2)}) collective-permute-start(bf16[32,1152]{1,0:T(8,128)(2,1)S(1)} %get-tuple-element.243), channel_id=1, source_target_pairs={{0,3},{1,0},{2,1},{3,2},{4,7},{5,4},{6,5},{7,6},{8,11},{9,8},{10,9... | collective-permute-start | bytes 221192 | tf_op jit(solution)/shard_map/ppermute | solution.py:594
  130.5 5.7 %collective-permute-start.37 = (bf16[32,1152]{1,0:T(8,128)(2,1)S(1)}, bf16[32,1152]{1,0:T(8,128)(2,1)S(1)}, u32[]{:S(2)}, u32[]{:S(2)}) collective-permute-start(bf16[32,1152]{1,0:T(8,128)(2,1)S(1)} %get-tuple-element.244), channel_id=1, source_target_pairs={{0,2},{1,3},{2,0},{3,1},{4,6},{5,7},{6,4},{7,5},{8,10},{9,11},{10,... | collective-permute-start | bytes 221192 | tf_op jit(solution)/shard_map/ppermute | solution.py:594
  139.9 6.9 %collective-permute-start.41 = (bf16[32,2176]{1,0:T(8,128)(2,1)S(1)}, bf16[32,2176]{1,0:T(8,128)(2,1)S(1)}, u32[]{:S(2)}, u32[]{:S(2)}) collective-permute-start(bf16[32,2176]{1,0:T(8,128)(2,1)S(1)} %get-tuple-element.239), channel_id=1, source_target_pairs={{0,1},{1,2},{2,3},{3,0},{4,5},{5,6},{6,7},{7,4},{8,9},{9,10},{10,1... | collective-permute-start | bytes 417800 | tf_op jit(solution)/shard_map/ppermute | solution.py:594
  140.0 11.7 %collective-permute-start.42 = (bf16[32,2176]{1,0:T(8,128)(2,1)S(1)}, bf16[32,2176]{1,0:T(8,128)(2,1)S(1)}, u32[]{:S(2)}, u32[]{:S(2)}) collective-permute-start(bf16[32,2176]{1,0:T(8,128)(2,1)S(1)} %get-tuple-element.238), channel_id=1, source_target_pairs={{0,2},{1,3},{2,0},{3,1},{4,6},{5,7},{6,4},{7,5},{8,10},{9,11},{10,... | collective-permute-start | bytes 417800 | tf_op jit(solution)/shard_map/ppermute | solution.py:594
  142.2 13.1 %collective-permute-start.43 = (bf16[32,2176]{1,0:T(8,128)(2,1)S(1)}, bf16[32,2176]{1,0:T(8,128)(2,1)S(1)}, u32[]{:S(2)}, u32[]{:S(2)}) collective-permute-start(bf16[32,2176]{1,0:T(8,128)(2,1)S(1)} %get-tuple-element.237), channel_id=1, source_target_pairs={{0,3},{1,0},{2,1},{3,2},{4,7},{5,4},{6,5},{7,6},{8,11},{9,8},{10,9... | collective-permute-start | bytes 417800 | tf_op jit(solution)/shard_map/ppermute | solution.py:594
  142.3 13.0 %collective-permute-start.39 = (bf16[2,32,2176]{2,1,0:T(8,128)(2,1)S(1)}, bf16[2,32,2176]{2,1,0:T(8,128)(2,1)S(1)}, u32[]{:S(2)}, u32[]{:S(2)}) collective-permute-start(bf16[2,32,2176]{2,1,0:T(8,128)(2,1)S(1)} %pad_maximum_fusion.6), channel_id=1, source_target_pairs={{0,16},{4,12},{8,24},{12,4},{16,0},{20,28},{24,8},{28,20},{1,17},{... | collective-permute-start | bytes 835592 | tf_op jit(solution)/shard_map/ppermute | solution.py:592
  143.5 3.3 %collective-permute-start.40 = (bf16[32,1152]{1,0:T(8,128)(2,1)S(1)}, bf16[32,1152]{1,0:T(8,128)(2,1)S(1)}, u32[]{:S(2)}, u32[]{:S(2)}) collective-permute-start(bf16[32,1152]{1,0:T(8,128)(2,1)S(1)} %fusion.12.refs_0_), channel_id=1, source_target_pairs={{0,8},{4,20},{8,0},{12,28},{16,24},{20,4},{24,16},{28,12},{1,9},{5... | collective-permute-start | bytes 221192 | tf_op jit(solution)/shard_map/ppermute | solution.py:592
  155.4 6.2 %collective-permute-start.46 = (bf16[4,32,2176]{2,1,0:T(8,128)(2,1)S(1)}, bf16[4,32,2176]{2,1,0:T(8,128)(2,1)S(1)}, u32[]{:S(2)}, u32[]{:S(2)}) collective-permute-start(bf16[4,32,2176]{2,1,0:T(8,128)(2,1)S(1)} %pad_maximum_fusion.3), channel_id=1, source_target_pairs={{0,4},{4,0},{8,12},{12,8},{16,20},{20,16},{24,28},{28,24},{1,5},{5... | collective-permute-start | bytes 1671176 | tf_op jit(solution)/shard_map/ppermute | solution.py:592
  156.0 5.6 %collective-permute-start.45 = (bf16[2,32,1152]{2,1,0:T(8,128)(2,1)S(1)}, bf16[2,32,1152]{2,1,0:T(8,128)(2,1)S(1)}, u32[]{:S(2)}, u32[]{:S(2)}) collective-permute-start(bf16[2,32,1152]{2,1,0:T(8,128)(2,1)S(1)} %pad_maximum_fusion.8), channel_id=1, source_target_pairs={{0,16},{4,12},{8,24},{12,4},{16,0},{20,28},{24,8},{28,20},{1,17},{... | collective-permute-start | bytes 442376 | tf_op jit(solution)/shard_map/ppermute | solution.py:592
  156.1 5.4 %collective-permute-start.44 = (bf16[32,2176]{1,0:T(8,128)(2,1)S(1)}, bf16[32,2176]{1,0:T(8,128)(2,1)S(1)}, u32[]{:S(2)}, u32[]{:S(2)}) collective-permute-start(bf16[32,2176]{1,0:T(8,128)(2,1)S(1)} %fusion.7.refs_0_), channel_id=1, source_target_pairs={{0,8},{4,20},{8,0},{12,28},{16,24},{20,4},{24,16},{28,12},{1,9},{5... | collective-permute-start | bytes 417800 | tf_op jit(solution)/shard_map/ppermute | solution.py:592
  161.6 3.7 %collective-permute-start.48 = (bf16[4,32,1152]{2,1,0:T(8,128)(2,1)S(1)}, bf16[4,32,1152]{2,1,0:T(8,128)(2,1)S(1)}, u32[]{:S(2)}, u32[]{:S(2)}) collective-permute-start(bf16[4,32,1152]{2,1,0:T(8,128)(2,1)S(1)} %pad_maximum_fusion.5), channel_id=1, source_target_pairs={{0,4},{4,0},{8,12},{12,8},{16,20},{20,16},{24,28},{28,24},{1,5},{5... | collective-permute-start | bytes 884744 | tf_op jit(solution)/shard_map/ppermute | solution.py:592
  162.5 5.8 %collective-permute-start.47 = (bf16[2,32,2176]{2,1,0:T(8,128)(2,1)S(1)}, bf16[2,32,2176]{2,1,0:T(8,128)(2,1)S(1)}, u32[]{:S(2)}, u32[]{:S(2)}) collective-permute-start(bf16[2,32,2176]{2,1,0:T(8,128)(2,1)S(1)} %pad_maximum_fusion.7), channel_id=1, source_target_pairs={{0,16},{4,12},{8,24},{12,4},{16,0},{20,28},{24,8},{28,20},{1,17},{... | collective-permute-start | bytes 835592 | tf_op jit(solution)/shard_map/ppermute | solution.py:592
  168.3 2.5 %collective-permute-start.49 = (bf16[4,32,2176]{2,1,0:T(8,128)(2,1)S(1)}, bf16[4,32,2176]{2,1,0:T(8,128)(2,1)S(1)}, u32[]{:S(2)}, u32[]{:S(2)}) collective-permute-start(bf16[4,32,2176]{2,1,0:T(8,128)(2,1)S(1)} %pad_maximum_fusion.4), channel_id=1, source_target_pairs={{0,4},{4,0},{8,12},{12,8},{16,20},{20,16},{24,28},{28,24},{1,5},{5... | collective-permute-start | bytes 1671176 | tf_op jit(solution)/shard_map/ppermute | solution.py:592
  (15 other events, 131.2 us)

commit v6 on v5

--- a/solution.py
+++ b/solution.py
@@ -230,8 +230,8 @@
     pieces, refs = refs[:blocks], refs[blocks:]
     (own1, own2), refs = refs[:2], refs[2:]
     slices, refs = refs[:8], refs[8:]
-    x_all, acts, far, heads, flow, lines_out, day_out, field_out = refs[:8]
-    inputs, tower, slope1, act2, headed, vectors = refs[8:]
+    x_all, acts, far, heads, tower, lines_out, day_out, field_out = refs[:8]
+    inputs, slope1, act2, headed, vectors = refs[8:]
     hidden = tower.shape[0]
     full = x_all.shape[1]
     size = hidden // blocks
@@ -303,7 +303,6 @@
         far[at : at + HALF, :] = acts[2, rows, :]
     for rows in parts:
         heads[rows, :] = jnp.broadcast_to(jnp.sum(act2[rows, :] * dl, axis=1, keepdims=True), (size, LANES))
-    flow[...] = dot(tower[:, 0:depth], acts[2], TN)
 
 
 def cross_backward(idx, *refs, blocks, layers, width, pad, depth):
@@ -311,7 +310,7 @@
     pieces, refs = refs[:blocks], refs[blocks:]
     own, refs = refs[0], refs[1:]
     slices, refs = cross_eight(refs[:4]), refs[4:]
-    (dx3, z_all), refs = refs[:2], refs[2:]
+    (tower, acts, z_all), refs = refs[:3], refs[3:]
     eg_out, refs = refs[:blocks], refs[blocks:]
     dz_out, rest_out, dz_far_last, dz_far_out = refs[:4]
     weight, inputs, lines, tail, flow, padded, total, rest = refs[4:]
@@ -320,13 +319,13 @@
     at = 16 * -(-depth // pieces[0].shape[1])
     for turn, piece in enumerate(pieces):
         inputs[block_of(idx, turn, blocks)] = piece[at : at + width, :].astype(F32)
+    flow[...] = dot(tower[:, 0:depth], acts[2], TN)
     padded[...] = jnp.zeros_like(padded)
     rest[...] = jnp.zeros_like(rest)
     for layer in reversed(range(layers)):
-        source = dx3 if layer == layers - 1 else flow
         for block in range(blocks):
             rows = slice(pad * block, pad * (block + 1))
-            dx = source[width * block : width * (block + 1), :]
+            dx = flow[width * block : width * (block + 1), :]
             padded[block, 0:width, :] = dx
             dx = padded[block, 0:width, :]
             dz = dx * inputs[block]
@@ -342,7 +341,7 @@
             rows = rows_at(pad * block + (1 - idx[1]) * HALF, HALF)
             far[HALF * block : HALF * (block + 1), :] = dz_out[layer, rows, :]
         place_cross(idx, weight, own, slices, blocks, layer, pad)
-        flow[...] = source[...] + dot(weight[layer], dz_out[layer], TN)
+        flow[...] += dot(weight[layer], dz_out[layer], TN)
     extras = split3(extra_lines[0:1, :]) + split3(extra_lines[1:2, :])
     for block in range(blocks):
         total[block, 0:width, :] += flow[width * block : width * (block + 1), :]
@@ -353,8 +352,10 @@
         eg_out[turn][...] = total[block_ahead(idx, turn, blocks)].astype(BF16)
 
 
-def tower_grads(idx, x_all, x_far, acts, far, head, near_out, far_out, send_out, *refs, blocks, depth, layers):
-    x_cat, acts_in, far_in, heads, lhs, d_cat, near, away, send, sems = refs
+def tower_grads(idx, x_all, x_far, acts, far, head, *refs, blocks, depth, layers, wheres):
+    outs = refs[: 1 + (0 in wheres)]
+    x_cat, acts_in, far_in, heads, lhs, d_cat = refs[len(outs) : len(outs) + 6]
+    holds, sems = refs[len(outs) + 6 : -1], refs[-1]
     hidden = acts.shape[1]
     size = hidden // blocks
     part = acts.shape[2]
@@ -371,7 +372,7 @@
     wait(*first)
     lane = lane_of((SHARE, LANES))
     pick = (lax.broadcasted_iota(jnp.int32, (LANES, 2 * part), 0) == bias + 1).astype(BF16)
-    order = [(where, slot) for where in range(4) for slot in range(blocks)]
+    order = [(where, slot) for where in wheres for slot in range(blocks)]
     shares = relative(idx)
     d_cat[:, 0:part] = acts_in[1]
     d_cat[:, part:] = far_in[0:hidden, :]
@@ -396,12 +397,12 @@
     wide = dot(lhs[0], x_cat[...], NT)
     deep = dot(lhs[1], d_cat[...], NT)
     for at, (where, slot) in enumerate(order):
-        target = (near, away, send.at[0], send.at[1])[where].at[slot]
+        target = (holds[where] if 0 in wheres else holds[0].at[where - 2]).at[slot]
         here = slice(SHARE * at, SHARE * (at + 1))
         target[:, 0:low] = wide[here, 0:low].astype(BF16)
         target[:, low : low + LANES] = (wide[here, low:] + extra[here, :] + scale[at]).astype(BF16)
         target[:, low + LANES :] = deep[here, :].astype(BF16)
-    wait(copies.start(send, send_out), copies.start(near, near_out), copies.start(away, far_out))
+    wait(*[copies.start(hold, out) for hold, out in zip(holds, outs)])
 
 
 def cross_grads(idx, x_all, x_far, dz, rest, dz_far, near_out, far_out, send_out, *refs, blocks, base, pad, depth):
@@ -674,7 +675,7 @@
     tower_slices = [tower_mine, tower_one, both, tower_three, tower_far, tower_next, both_far, tower_last]
     x_far = hop(after(x_all, tower_last), pair)
     fields = feature_ids.shape[1]
-    acts, far, head_col, dx3, lines, day_line, field_counts = call(
+    acts, far, head_col, tower_all, lines, day_line, field_counts = call(
         functools.partial(
             tower_both, blocks=blocks, layers=layers, width=width, depth=depth, fields=fields, examples=examples
         ),
@@ -682,14 +683,13 @@
             shape((3, hidden, part), BF16),
             shape((2 * hidden, part), BF16),
             shape((hidden, LANES), F32),
-            shape((depth, part), F32),
+            shape((hidden, wide), BF16),
             shape((2, part), F32),
             shape((1, BUCKETS), jnp.int32),
             shape((fields, BUCKETS), jnp.int32),
         ),
         [
             vmem((blocks, 3, part), F32),
-            vmem((hidden, wide), BF16),
             vmem((hidden, part), F32),
             vmem((hidden, part), F32),
             vmem((hidden, part), F32),
@@ -725,21 +725,30 @@
             nbytes=10 << 20,
         )
 
-    tower_parts = grads(
-        functools.partial(tower_grads, blocks=blocks, depth=depth, layers=layers),
-        (blocks, SHARE, wide),
-        [
-            vmem((full, 2 * part), BF16),
-            vmem((3, hidden, part), BF16),
-            vmem((2 * hidden, part), BF16),
-            vmem((hidden, LANES), F32),
-            vmem((3, HALF * blocks, 2 * part), BF16),
-            vmem((hidden, 2 * part), BF16),
-        ],
-        [idx, x_all, x_far, acts, far, head_col],
-        8,
-        4 * hidden * full * part,
-    )
+    def tower_parts_of(wheres, outs, start):
+        return call(
+            functools.partial(tower_grads, blocks=blocks, depth=depth, layers=layers, wheres=wheres),
+            tuple(shape(s, BF16) for s in outs),
+            [
+                vmem((full, 2 * part), BF16),
+                vmem((3, hidden, part), BF16),
+                vmem((2 * hidden, part), BF16),
+                vmem((hidden, LANES), F32),
+                vmem((3, HALF * blocks // 2, 2 * part), BF16),
+                vmem((hidden, 2 * part), BF16),
+            ]
+            + [vmem(s, BF16) for s in outs],
+            [start, x_all, x_far, acts, far, head_col],
+            mib=20,
+            spec=HBM,
+            copies=7,
+            flops=2 * hidden * full * part,
+            nbytes=10 << 20,
+        )
+
+    keep = (blocks, SHARE, wide)
+    (tower_out,) = tower_parts_of((2, 3), [(2,) + keep], idx)
+    tower_parts = [*tower_parts_of((0, 1), [keep, keep], after(idx, tower_out)), tower_out]
     tower_arrived = hop(tower_parts[2], first)
     *input_grads, dz, dz_rest, last_far, dz_far = call(
         functools.partial(cross_backward, blocks=blocks, layers=layers, width=width, pad=pad, depth=depth),
@@ -766,10 +775,11 @@
             *pieces,
             cross_weight,
             *cross_slices,
-            dx3,
+            tower_all,
+            acts,
             z_all,
         ],
-        mib=34,
+        mib=22,
         flops=2 * layers * flat * full * part,
         nbytes=20 << 20,
     )
@@ -823,11 +833,11 @@
         return hop(jnp.concatenate([jnp.stack([mine, one]), two]), pair)
 
     grad_pieces = [input_grads[0]] + turns(input_grads[1:])
-    tower_arrived, last_send, grad_pieces[1] = join(tower_arrived, last_parts[2], grad_pieces[1])
+    grad_pieces[1], tower_arrived, last_send = join(grad_pieces[1], tower_arrived, last_parts[2])
     tower_second = far_send(tower_parts, tower_arrived)
     last_arrived = hop(last_send, first)
-    tower_second, last_arrived, cross_send, *grad_pieces = join(
-        tower_second, last_arrived, cross_parts[2], *grad_pieces
+    *grad_pieces, tower_second, last_arrived, cross_send = join(
+        *grad_pieces, tower_second, last_arrived, cross_parts[2]
     )
 
     tower_held = near_sum(tower_parts, tower_arrived, tower_second)

time: 174 us -> 173 us (level)
  waiting for transfers between devices: 96.1 us -> 93.6 us
    ppermute x29, waiting for transfers between devices: 31.4 us -> 29.4 us  [per_device(): hop = lambda value, perm: lax.ppermute(value, 'dp', perm)]
    pallas_call x11 -> x12, Pallas kernels: 34.3 us -> 35.9 us  [call(): pl.pallas_call(kernel, out_shape=outs, in_specs=[SMEM] + specs, out_specs...]
  transfers between devices with their start and end apart: 50 -> 50, of which waited for: 34 -> 33; matrix products, arithmetic and copies ran while one was open for 1% -> 1% of each run, Pallas kernels for 16% -> 18%
where the time goes in v6:
time: 173 us
  waiting for transfers between devices  93.6 us (54%)
  Pallas kernels  35.9 us (21%)
  starting transfers between devices  34.8 us (20%)
  local copies, waits for them, and re-layouts  5.04 us (3%)
  other arithmetic  1.9 us (1%)
    ppermute x18, waiting for transfers between devices, per_device(): lax.ppermute(value, 'mp', turn_by(r + 1))  50.8 us
    pallas_call x12, Pallas kernels, call(): pl.pallas_call(kernel, out_shape=outs, in_specs=[SMEM] + specs, out_specs...  35.9 us
    ppermute x29, waiting for transfers between devices, per_device(): hop = lambda value, perm: lax.ppermute(value, 'dp', perm)  29.4 us
    ppermute x29, starting transfers between devices, per_device(): hop = lambda value, perm: lax.ppermute(value, 'dp', perm)  20 us
    ppermute x18, starting transfers between devices, per_device(): lax.ppermute(value, 'mp', turn_by(r + 1))  14 us
    ppermute x3, waiting for transfers between devices, per_device(): turn = lambda value, r: lax.ppermute(value, 'mp', turn_by(r))  13.4 us
  transfers between devices with their start and end apart: 50, of which 33 were waited for; matrix products, arithmetic and copies ran while one was open for 1% of the time, Pallas kernels for 18%

profile of v6, /device:TPU:9, one launch (start us, length us, event | category | flops | bytes accessed | tf_op | source)
XLA Modules:
  0.0 172.6 jit_solution(1972553725902654338)
XLA Ops:
  0.7 1.1 dynamic-slice_bitcast_fusion
  2.1 1.3 collective-permute-start
  4.5 1.4 collective-permute-start.2
  6.1 1.5 copy-done
  8.6 2.9 %shard_map.202 = (bf16[32,2176]{1,0:T(8,128)(2,1)S(1)}, bf16[256,1152]{1,0:T(8,128)(2,1)S(1)}, bf16[96,128]{1,0:T(8,128)(2,1)S(1)}, bf16[343,256]{1,0:T(8,128)(2...) custom-call(s32[4]{0:T(128)S(1)} %pad_add_fusion.idx, ...), custom_call_target="tpu_custom_call" | custom-call | bytes 2097152 | tf_op jit(solution)/shard_map/pallas_call | solution.py:45
  11.5 8.8 %collective-permute-done.1 = bf16[32,3200]{1,0:T(8,128)(2,1)S(1)} collective-permute-done((bf16[32,3200]{1,0:T(8,128)(2,1)S(1)}, bf16[32,3200]{1,0:T(8,128)(2,1)S(1)}, u32[]{:S(2)}, u32[]{:S(2)}) %collective-permute-start.1) | collective-permute-done | bytes 204832 | tf_op jit(solution)/shard_map/ppermute | solution.py:595
  20.3 2.8 %collective-permute-done.2 = bf16[32,3200]{1,0:T(8,128)(2,1)S(1)} collective-permute-done((bf16[32,3200]{1,0:T(8,128)(2,1)S(1)}, bf16[32,3200]{1,0:T(8,128)(2,1)S(1)}, u32[]{:S(2)}, u32[]{:S(2)}) %collective-permute-start.2) | collective-permute-done | bytes 204832 | tf_op jit(solution)/shard_map/ppermute | solution.py:595
  23.3 1.3 collective-permute-start.3
  24.5 1.2 collective-permute-start.4
  26.0 1.5 collective-permute-start.7
  27.5 2.5 %collective-permute-done.5 = bf16[32,2176]{1,0:T(8,128)(2,1)S(1)} collective-permute-done((bf16[32,2176]{1,0:T(8,128)(2,1)S(1)}, bf16[32,2176]{1,0:T(8,128)(2,1)S(1)}, u32[]{:S(2)}, u32[]{:S(2)}) %collective-permute-start.5) | collective-permute-done | bytes 139296 | tf_op jit(solution)/shard_map/ppermute | solution.py:595
  30.0 6.8 %collective-permute-done.6 = bf16[32,2176]{1,0:T(8,128)(2,1)S(1)} collective-permute-done((bf16[32,2176]{1,0:T(8,128)(2,1)S(1)}, bf16[32,2176]{1,0:T(8,128)(2,1)S(1)}, u32[]{:S(2)}, u32[]{:S(2)}) %collective-permute-start.6) | collective-permute-done | bytes 139296 | tf_op jit(solution)/shard_map/ppermute | solution.py:595
  36.8 2.9 %collective-permute-done.7 = bf16[32,2176]{1,0:T(8,128)(2,1)S(1)} collective-permute-done((bf16[32,2176]{1,0:T(8,128)(2,1)S(1)}, bf16[32,2176]{1,0:T(8,128)(2,1)S(1)}, u32[]{:S(2)}, u32[]{:S(2)}) %collective-permute-start.7) | collective-permute-done | bytes 139296 | tf_op jit(solution)/shard_map/ppermute | solution.py:595
  40.7 1.2 collective-permute-start.8
  44.5 3.7 %collective-permute-done.11.refs_1_.refs_3_.refs_2_ = bf16[343,256]{1,0:T(8,128)(2,1)S(1)} collective-permute-done((bf16[343,256]{1,0:T(8,128)(2,1)S(1)}, bf16[343,256]{1,0:T(8,128)(2,1)S(1)}, u32[]{:S(2)}, u32[]{:S(2)}) %collective-permute-start.11) | collective-permute-done | bytes 175648 | tf_op jit(solution)/shard_map/ppermute | solution.py:643
  48.2 9.4 %collective-permute-done.12.refs_2_.refs_4_.refs_3_ = bf16[343,256]{1,0:T(8,128)(2,1)S(1)} collective-permute-done((bf16[343,256]{1,0:T(8,128)(2,1)S(1)}, bf16[343,256]{1,0:T(8,128)(2,1)S(1)}, u32[]{:S(2)}, u32[]{:S(2)}) %collective-permute-start.12) | collective-permute-done | bytes 175648 | tf_op jit(solution)/shard_map/ppermute | solution.py:643
  57.7 1.4 collective-permute-done.8.refs_6_.refs_10_.refs_7_
  61.4 1.5 collective-permute-done.15.refs_12_
  63.5 4.0 %shard_map.203 = (f32[3,1088,256]{2,1,0:T(8,128)S(1)}, bf16[4,1152,256]{2,1,0:T(8,128)(2,1)S(1)}) custom-call(s32[4]{0:T(128)S(1)} %pad_add_fusion.idx, bf16[343,256]{1,0:T(8,128)(2,1)S(1)} %get-tuple-element.140.refs_0_.refs_2_.refs_1_, bf16[343,256]{1,0:T(8,128)(2,1)S(1)} %collective-permute-done.11.refs_1_.refs_3_.refs_2_, ...), custom_call_target="tpu_custom_call" | custom-call | flops 1925185536 | bytes 20971520 | tf_op jit(solution)/shard_map/pallas_call | solution.py:45
  68.6 1.4 collective-permute-done.18.refs_15_
  70.3 3.8 %shard_map.204 = (bf16[3,1024,256]{2,1,0:T(8,128)(2,1)S(1)}, bf16[2048,256]{1,0:T(8,128)(2,1)S(1)}, f32[1024,128]{1,0:T(8,128)S(1)}, bf16[1024,2176]{1,0:T(8,128...) custom-call(s32[4]{0:T(128)S(1)} %pad_add_fusion.idx, s32[1,1024]{1,0:T(1,128)S(1)} %bitcast.114, ...), custom_call_target="tpu_custom_call" | custom-call | flops 2415919104 | bytes 10485760 | tf_op jit(solution)/shard_map/pallas_call | solution.py:45
  74.3 2.5 %collective-permute-done.20.far = bf16[2048,256]{1,0:T(8,128)(2,1)S(1)} collective-permute-done((bf16[2048,256]{1,0:T(8,128)(2,1)S(1)}, bf16[2048,256]{1,0:T(8,128)(2,1)S(1)}, u32[]{:S(2)}, u32[]{:S(2)}) %collective-permute-start.20) | collective-permute-done | bytes 1048608 | tf_op jit(solution)/shard_map/ppermute | solution.py:593
  76.9 2.1 %shard_map.205 = bf16[2,4,32,2176]{3,2,1,0:T(8,128)(2,1)S(1)} custom-call(s32[4]{0:T(128)S(1)} %pad_add_fusion.idx, bf16[4,1152,256]{2,1,0:T(8,128)(2,1)S(1)} %get-tuple-element.151.refs_16_.x_all, bf16[4,1152,256]{2,1,0:T(8,128)(2,1)S(1)} %collective-permute-done.19.x_far, bf16[3,1024,256]{2,1,0:T(8,128)(2,1)S(1)} %get-tuple-element.155.acts.refs_11_, ...), custom_call_target="tpu_custom_call" | custom-call | flops 603979776 | bytes 10485760 | tf_op jit(solution)/shard_map/pallas_call | solution.py:45
  80.1 6.6 %shard_map.207 = (bf16[272,256]{1,0:T(8,128)(2,1)S(1)}, bf16[272,256]{1,0:T(8,128)(2,1)S(1)}, bf16[272,256]{1,0:T(8,128)(2,1)S(1)}, bf16[272,256]{1,0:T(8,128)(2...) custom-call(s32[4]{0:T(128)S(1)} %pad_add_fusion.idx, ...), custom_call_target="tpu_custom_call" | custom-call | flops 1925185536 | bytes 20971520 | tf_op jit(solution)/shard_map/pallas_call | solution.py:45
  87.3 1.9 %shard_map.206 = (bf16[4,32,2176]{2,1,0:T(8,128)(2,1)S(1)}, bf16[4,32,2176]{2,1,0:T(8,128)(2,1)S(1)}) custom-call(s32[4]{0:T(128)S(1)} %pad_add_fusion.idx, bf16[4,1152,256]{2,1,0:T(8,128)(2,1)S(1)} %get-tuple-element.151.refs_16_.x_all, bf16[4,1152,256]{2,1,0:T(8,128)(2,1)S(1)} %collective-permute-done.19.x_far, ...), custom_call_target="tpu_custom_call" | custom-call | flops 603979776 | bytes 10485760 | tf_op jit(solution)/shard_map/pallas_call | solution.py:45
  89.2 2.3 %shard_map.208 = (bf16[4,32,1152]{2,1,0:T(8,128)(2,1)S(1)}, bf16[4,32,1152]{2,1,0:T(8,128)(2,1)S(1)}, bf16[2,4,32,1152]{3,2,1,0:T(8,128)(2,1)S(1)}) custom-call(s32[4]{0:T(128)S(1)} %pad_add_fusion.idx, bf16[4,1152,256]{2,1,0:T(8,128)(2,1)S(1)} %get-tuple-element.151.refs_16_.x_all, bf16[4,1152,256]{2,1,0:T(8,128)(2,1)S(1)} %collective-permute-done.19.x_far, ...), custom_call_target="tpu_custom_call" | custom-call | flops 641728512 | bytes 10485760 | tf_op jit(solution)/shard_map/pallas_call | solution.py:45
  92.1 1.6 collective-permute-done.22
  96.9 3.8 %shard_map.209 = (bf16[4,32,2176]{2,1,0:T(8,128)(2,1)S(1)}, bf16[4,32,2176]{2,1,0:T(8,128)(2,1)S(1)}, bf16[2,4,32,2176]{3,2,1,0:T(8,128)(2,1)S(1)}) custom-call(s32[4]{0:T(128)S(1)} %pad_add_fusion.idx, bf16[4,1152,256]{2,1,0:T(8,128)(2,1)S(1)} %get-tuple-element.151.refs_16_.x_all, bf16[4,1152,256]{2,1,0:T(8,128)(2,1)S(1)} %collective-permute-done.19.x_far, ...), custom_call_target="tpu_custom_call" | custom-call | flops 1283457024 | bytes 10485760 | tf_op jit(solution)/shard_map/pallas_call | solution.py:45
  100.7 4.9 %collective-permute-done.24.refs_2_ = bf16[272,256]{1,0:T(8,128)(2,1)S(1)} collective-permute-done((bf16[272,256]{1,0:T(8,128)(2,1)S(1)}, bf16[272,256]{1,0:T(8,128)(2,1)S(1)}, u32[]{:S(2)}, u32[]{:S(2)}) %collective-permute-start.24) | collective-permute-done | bytes 139296 | tf_op jit(solution)/shard_map/ppermute | solution.py:595
  105.6 3.7 %collective-permute-done.26 = bf16[4,32,2176]{2,1,0:T(8,128)(2,1)S(1)} collective-permute-done((bf16[4,32,2176]{2,1,0:T(8,128)(2,1)S(1)}, bf16[4,32,2176]{2,1,0:T(8,128)(2,1)S(1)}, u32[]{:S(2)}, u32[]{:S(2)}) %collective-permute-start.26) | collective-permute-done | bytes 557088 | tf_op jit(solution)/shard_map/ppermute | solution.py:593
  111.2 2.3 %collective-permute-start.33 = (bf16[32,2176]{1,0:T(8,128)(2,1)S(1)}, bf16[32,2176]{1,0:T(8,128)(2,1)S(1)}, u32[]{:S(2)}, u32[]{:S(2)}) collective-permute-start(bf16[32,2176]{1,0:T(8,128)(2,1)S(1)} %get-tuple-element.239), channel_id=1, source_target_pairs={{0,2},{1,3},{2,0},{3,1},{4,6},{5,7},{6,4},{7,5},{8,10},{9,11},{10,... | collective-permute-start | bytes 417800 | tf_op jit(solution)/shard_map/ppermute | solution.py:595
  113.8 2.5 %collective-permute-done.30 = bf16[4,32,1152]{2,1,0:T(8,128)(2,1)S(1)} collective-permute-done((bf16[4,32,1152]{2,1,0:T(8,128)(2,1)S(1)}, bf16[4,32,1152]{2,1,0:T(8,128)(2,1)S(1)}, u32[]{:S(2)}, u32[]{:S(2)}) %collective-permute-start.30) | collective-permute-done | bytes 294944 | tf_op jit(solution)/shard_map/ppermute | solution.py:593
  116.5 1.6 shard_map.210
  118.1 4.6 %collective-permute-done.33 = bf16[32,2176]{1,0:T(8,128)(2,1)S(1)} collective-permute-done((bf16[32,2176]{1,0:T(8,128)(2,1)S(1)}, bf16[32,2176]{1,0:T(8,128)(2,1)S(1)}, u32[]{:S(2)}, u32[]{:S(2)}) %collective-permute-start.33) | collective-permute-done | bytes 139296 | tf_op jit(solution)/shard_map/ppermute | solution.py:595
  122.8 4.9 %collective-permute-done.34 = bf16[32,2176]{1,0:T(8,128)(2,1)S(1)} collective-permute-done((bf16[32,2176]{1,0:T(8,128)(2,1)S(1)}, bf16[32,2176]{1,0:T(8,128)(2,1)S(1)}, u32[]{:S(2)}, u32[]{:S(2)}) %collective-permute-start.34) | collective-permute-done | bytes 139296 | tf_op jit(solution)/shard_map/ppermute | solution.py:595
  129.3 1.8 %collective-permute-start.37 = (bf16[32,1152]{1,0:T(8,128)(2,1)S(1)}, bf16[32,1152]{1,0:T(8,128)(2,1)S(1)}, u32[]{:S(2)}, u32[]{:S(2)}) collective-permute-start(bf16[32,1152]{1,0:T(8,128)(2,1)S(1)} %get-tuple-element.242), channel_id=1, source_target_pairs={{0,2},{1,3},{2,0},{3,1},{4,6},{5,7},{6,4},{7,5},{8,10},{9,11},{10,... | collective-permute-start | bytes 221192 | tf_op jit(solution)/shard_map/ppermute | solution.py:595
  131.2 1.6 collective-permute-done.38
  132.8 2.0 %collective-permute-done.37 = bf16[32,1152]{1,0:T(8,128)(2,1)S(1)} collective-permute-done((bf16[32,1152]{1,0:T(8,128)(2,1)S(1)}, bf16[32,1152]{1,0:T(8,128)(2,1)S(1)}, u32[]{:S(2)}, u32[]{:S(2)}) %collective-permute-start.37) | collective-permute-done | bytes 73760 | tf_op jit(solution)/shard_map/ppermute | solution.py:595
  134.8 3.7 %collective-permute-done.35 = bf16[4,32,2176]{2,1,0:T(8,128)(2,1)S(1)} collective-permute-done((bf16[4,32,2176]{2,1,0:T(8,128)(2,1)S(1)}, bf16[4,32,2176]{2,1,0:T(8,128)(2,1)S(1)}, u32[]{:S(2)}, u32[]{:S(2)}) %collective-permute-start.35) | collective-permute-done | bytes 557088 | tf_op jit(solution)/shard_map/ppermute | solution.py:593
  138.8 2.0 %collective-permute-start.42 = (bf16[32,2176]{1,0:T(8,128)(2,1)S(1)}, bf16[32,2176]{1,0:T(8,128)(2,1)S(1)}, u32[]{:S(2)}, u32[]{:S(2)}) collective-permute-start(bf16[32,2176]{1,0:T(8,128)(2,1)S(1)} %get-tuple-element.236), channel_id=1, source_target_pairs={{0,2},{1,3},{2,0},{3,1},{4,6},{5,7},{6,4},{7,5},{8,10},{9,11},{10,... | collective-permute-start | bytes 417800 | tf_op jit(solution)/shard_map/ppermute | solution.py:595
  141.0 1.1 collective-permute-start.39
  143.1 2.6 %collective-permute-done.40.refs_1_ = bf16[32,1152]{1,0:T(8,128)(2,1)S(1)} collective-permute-done((bf16[32,1152]{1,0:T(8,128)(2,1)S(1)}, bf16[32,1152]{1,0:T(8,128)(2,1)S(1)}, u32[]{:S(2)}, u32[]{:S(2)}) %collective-permute-start.40) | collective-permute-done | bytes 73760 | tf_op jit(solution)/shard_map/ppermute | solution.py:593
  145.7 4.3 %collective-permute-done.42 = bf16[32,2176]{1,0:T(8,128)(2,1)S(1)} collective-permute-done((bf16[32,2176]{1,0:T(8,128)(2,1)S(1)}, bf16[32,2176]{1,0:T(8,128)(2,1)S(1)}, u32[]{:S(2)}, u32[]{:S(2)}) %collective-permute-start.42) | collective-permute-done | bytes 139296 | tf_op jit(solution)/shard_map/ppermute | solution.py:595
  150.0 3.8 %collective-permute-done.43 = bf16[32,2176]{1,0:T(8,128)(2,1)S(1)} collective-permute-done((bf16[32,2176]{1,0:T(8,128)(2,1)S(1)}, bf16[32,2176]{1,0:T(8,128)(2,1)S(1)}, u32[]{:S(2)}, u32[]{:S(2)}) %collective-permute-start.43) | collective-permute-done | bytes 139296 | tf_op jit(solution)/shard_map/ppermute | solution.py:595
  156.0 4.7 %collective-permute-done.44.refs_1_ = bf16[32,2176]{1,0:T(8,128)(2,1)S(1)} collective-permute-done((bf16[32,2176]{1,0:T(8,128)(2,1)S(1)}, bf16[32,2176]{1,0:T(8,128)(2,1)S(1)}, u32[]{:S(2)}, u32[]{:S(2)}) %collective-permute-start.44) | collective-permute-done | bytes 139296 | tf_op jit(solution)/shard_map/ppermute | solution.py:593
  161.6 2.5 %shard_map.211 = (f32[1040,256]{1,0:T(8,128)}, f32[256,1024]{1,0:T(8,128)}, f32[3,256]{1,0:T(4,128)S(1)}, f32[1,1]{1,0:T(1,128)}) custom-call(s32[4]{0:T(128)S(1)} %pad_add_fusion.idx, bf16[32,2176]{1,0:T(8,128)(2,1)S(1)} %fusion.10.refs_0_, bf16[32,2176]{1,0:T(8,128)(2,1)S(1)} %collective-permute-done.36.refs_1_, ...), custom_call_target="tpu_custom_call" | custom-call | bytes 4194304 | tf_op jit(solution)/shard_map/pallas_call | solution.py:45
  164.2 1.8 %shard_map.212 = (f32[3,260,1040]{2,1,0:T(8,128)}, f32[1,260]{1,0:T(1,128)S(1)}) custom-call(s32[4]{0:T(128)S(1)} %pad_add_fusion.idx, bf16[32,1152]{1,0:T(8,128)(2,1)S(1)} %fusion.12.refs_0_, bf16[32,1152]{1,0:T(8,128)(2,1)S(1)} %collective-permute-done.40.refs_1_, bf16[2,32,1152]{2,1,0:T(8,128)(2,1)S(1)} %collective-permute-done.45.refs_2_, ...), custom_call_target="tpu_custom_call" | custom-call | bytes 4194304 | tf_op jit(solution)/shard_map/pallas_call | solution.py:45
  169.7 2.7 %shard_map.213 = (f32[3,260,1040]{2,1,0:T(8,128)}, f32[3,260]{1,0:T(4,128)}) custom-call(s32[4]{0:T(128)S(1)} %pad_add_fusion.idx, bf16[32,2176]{1,0:T(8,128)(2,1)S(1)} %fusion.7.refs_0_, bf16[32,2176]{1,0:T(8,128)(2,1)S(1)} %collective-permute-done.44.refs_1_, ...), custom_call_target="tpu_custom_call", output_to_operand_aliasing={{0}: (5, {})} | custom-call | bytes 4194304 | tf_op jit(solution)/shard_map/pallas_call | solution.py:45
  (128 shorter events, 28.8 us)
Async XLA Ops:
  2.1 9.4 %collective-permute-start = (bf16[32,3200]{1,0:T(8,128)(2,1)S(1)}, bf16[32,3200]{1,0:T(8,128)(2,1)S(1)}, u32[]{:S(2)}, u32[]{:S(2)}) collective-permute-start(bf16[32,3200]{1,0:T(8,128)(2,1)S(1)} %concatenate.15), channel_id=1, source_target_pairs={{0,1},{1,2},{2,3},{3,0},{4,5},{5,6},{6,7},{7,4},{8,9},{9,10},{10,1... | collective-permute-start | bytes 614408 | tf_op jit(solution)/shard_map/ppermute | solution.py:595
  3.4 16.9 %collective-permute-start.1 = (bf16[32,3200]{1,0:T(8,128)(2,1)S(1)}, bf16[32,3200]{1,0:T(8,128)(2,1)S(1)}, u32[]{:S(2)}, u32[]{:S(2)}) collective-permute-start(bf16[32,3200]{1,0:T(8,128)(2,1)S(1)} %concatenate.15), channel_id=1, source_target_pairs={{0,2},{1,3},{2,0},{3,1},{4,6},{5,7},{6,4},{7,5},{8,10},{9,11},{10,... | collective-permute-start | bytes 614408 | tf_op jit(solution)/shard_map/ppermute | solution.py:595
  4.5 18.7 %collective-permute-start.2 = (bf16[32,3200]{1,0:T(8,128)(2,1)S(1)}, bf16[32,3200]{1,0:T(8,128)(2,1)S(1)}, u32[]{:S(2)}, u32[]{:S(2)}) collective-permute-start(bf16[32,3200]{1,0:T(8,128)(2,1)S(1)} %concatenate.15), channel_id=1, source_target_pairs={{0,3},{1,0},{2,1},{3,2},{4,7},{5,4},{6,5},{7,6},{8,11},{9,8},{10,9... | collective-permute-start | bytes 614408 | tf_op jit(solution)/shard_map/ppermute | solution.py:595
  23.3 16.5 %collective-permute-start.3 = (bf16[3,32,3200]{2,1,0:T(8,128)(2,1)S(1)}, bf16[3,32,3200]{2,1,0:T(8,128)(2,1)S(1)}, u32[]{:S(2)}, u32[]{:S(2)}) collective-permute-start(bf16[3,32,3200]{2,1,0:T(8,128)(2,1)S(1)} %pad_maximum_fusion.2), channel_id=1, source_target_pairs={{0,8},{4,20},{8,0},{12,28},{16,24},{20,4},{24,16},{28,12},{1,9},{5... | collective-permute-start | bytes 1843208 | tf_op jit(solution)/shard_map/ppermute | solution.py:593
  24.5 15.3 %collective-permute-start.4 = (bf16[3,32,3200]{2,1,0:T(8,128)(2,1)S(1)}, bf16[3,32,3200]{2,1,0:T(8,128)(2,1)S(1)}, u32[]{:S(2)}, u32[]{:S(2)}) collective-permute-start(bf16[3,32,3200]{2,1,0:T(8,128)(2,1)S(1)} %pad_maximum_fusion.2), channel_id=1, source_target_pairs={{0,16},{4,12},{8,24},{12,4},{16,0},{20,28},{24,8},{28,20},{1,17},{... | collective-permute-start | bytes 1843208 | tf_op jit(solution)/shard_map/ppermute | solution.py:593
  25.8 4.2 %collective-permute-start.5 = (bf16[32,2176]{1,0:T(8,128)(2,1)S(1)}, bf16[32,2176]{1,0:T(8,128)(2,1)S(1)}, u32[]{:S(2)}, u32[]{:S(2)}) collective-permute-start(bf16[32,2176]{1,0:T(8,128)(2,1)S(1)} %get-tuple-element.126), channel_id=1, source_target_pairs={{0,1},{1,2},{2,3},{3,0},{4,5},{5,6},{6,7},{7,4},{8,9},{9,10},{10,1... | collective-permute-start | bytes 417800 | tf_op jit(solution)/shard_map/ppermute | solution.py:595
  25.8 11.0 %collective-permute-start.6 = (bf16[32,2176]{1,0:T(8,128)(2,1)S(1)}, bf16[32,2176]{1,0:T(8,128)(2,1)S(1)}, u32[]{:S(2)}, u32[]{:S(2)}) collective-permute-start(bf16[32,2176]{1,0:T(8,128)(2,1)S(1)} %get-tuple-element.126), channel_id=1, source_target_pairs={{0,2},{1,3},{2,0},{3,1},{4,6},{5,7},{6,4},{7,5},{8,10},{9,11},{10,... | collective-permute-start | bytes 417800 | tf_op jit(solution)/shard_map/ppermute | solution.py:595
  26.0 13.7 %collective-permute-start.7 = (bf16[32,2176]{1,0:T(8,128)(2,1)S(1)}, bf16[32,2176]{1,0:T(8,128)(2,1)S(1)}, u32[]{:S(2)}, u32[]{:S(2)}) collective-permute-start(bf16[32,2176]{1,0:T(8,128)(2,1)S(1)} %get-tuple-element.126), channel_id=1, source_target_pairs={{0,3},{1,0},{2,1},{3,2},{4,7},{5,4},{6,5},{7,6},{8,11},{9,8},{10,9... | collective-permute-start | bytes 417800 | tf_op jit(solution)/shard_map/ppermute | solution.py:595
  40.1 3.9 %collective-permute-start.10 = (bf16[3,3,32,3200]{3,2,1,0:T(8,128)(2,1)S(1)}, bf16[3,3,32,3200]{3,2,1,0:T(8,128)(2,1)S(1)}, u32[]{:S(2)}, u32[]{:S(2)}) collective-permute-start(bf16[3,3,32,3200]{3,2,1,0:T(8,128)(2,1)S(1)} %pad_maximum_fusion.refs_5_.refs_6_), channel_id=1, source_target_pairs={{0,4},{4,0},{8,12},{12,8},{16,20},{20,16},{24,28},{28,24},{1,5},{5... | collective-permute-start | bytes 5529608 | tf_op jit(solution)/shard_map/ppermute | solution.py:593
  40.7 18.3 %collective-permute-start.8 = (bf16[3,32,5376]{2,1,0:T(8,128)(2,1)S(1)}, bf16[3,32,5376]{2,1,0:T(8,128)(2,1)S(1)}, u32[]{:S(2)}, u32[]{:S(2)}) collective-permute-start(bf16[3,32,5376]{2,1,0:T(8,128)(2,1)S(1)} %pad_maximum_fusion.1), channel_id=1, source_target_pairs={{0,16},{4,12},{8,24},{12,4},{16,0},{20,28},{24,8},{28,20},{1,17},{... | collective-permute-start | bytes 3096584 | tf_op jit(solution)/shard_map/ppermute | solution.py:593
  42.0 15.7 %collective-permute-start.9 = (bf16[3,32,2176]{2,1,0:T(8,128)(2,1)S(1)}, bf16[3,32,2176]{2,1,0:T(8,128)(2,1)S(1)}, u32[]{:S(2)}, u32[]{:S(2)}) collective-permute-start(bf16[3,32,2176]{2,1,0:T(8,128)(2,1)S(1)} %maximum_add_fusion.refs_8_), channel_id=1, source_target_pairs={{0,8},{4,20},{8,0},{12,28},{16,24},{20,4},{24,16},{28,12},{1,9},{5... | collective-permute-start | bytes 1253384 | tf_op jit(solution)/shard_map/ppermute | solution.py:593
  42.8 5.4 %collective-permute-start.11 = (bf16[343,256]{1,0:T(8,128)(2,1)S(1)}, bf16[343,256]{1,0:T(8,128)(2,1)S(1)}, u32[]{:S(2)}, u32[]{:S(2)}) collective-permute-start(bf16[343,256]{1,0:T(8,128)(2,1)S(1)} %get-tuple-element.135), channel_id=1, source_target_pairs={{0,1},{1,2},{2,3},{3,0},{4,5},{5,6},{6,7},{7,4},{8,9},{9,10},{10,1... | collective-permute-start | bytes 526856 | tf_op jit(solution)/shard_map/ppermute | solution.py:643
  42.8 14.9 %collective-permute-start.12 = (bf16[343,256]{1,0:T(8,128)(2,1)S(1)}, bf16[343,256]{1,0:T(8,128)(2,1)S(1)}, u32[]{:S(2)}, u32[]{:S(2)}) collective-permute-start(bf16[343,256]{1,0:T(8,128)(2,1)S(1)} %get-tuple-element.137), channel_id=1, source_target_pairs={{0,2},{1,3},{2,0},{3,1},{4,6},{5,7},{6,4},{7,5},{8,10},{9,11},{10,... | collective-permute-start | bytes 526856 | tf_op jit(solution)/shard_map/ppermute | solution.py:643
  44.0 15.3 %collective-permute-start.13 = (bf16[343,256]{1,0:T(8,128)(2,1)S(1)}, bf16[343,256]{1,0:T(8,128)(2,1)S(1)}, u32[]{:S(2)}, u32[]{:S(2)}) collective-permute-start(bf16[343,256]{1,0:T(8,128)(2,1)S(1)} %get-tuple-element.139), channel_id=1, source_target_pairs={{0,3},{1,0},{2,1},{3,2},{4,7},{5,4},{6,5},{7,6},{8,11},{9,8},{10,9... | collective-permute-start | bytes 526856 | tf_op jit(solution)/shard_map/ppermute | solution.py:643
  59.3 4.2 %collective-permute-start.14 = (bf16[3,32,5376]{2,1,0:T(8,128)(2,1)S(1)}, bf16[3,32,5376]{2,1,0:T(8,128)(2,1)S(1)}, u32[]{:S(2)}, u32[]{:S(2)}) collective-permute-start(bf16[3,32,5376]{2,1,0:T(8,128)(2,1)S(1)} %collective-permute-done.8.refs_6_.refs_10_.refs_7_), channel_id=1, source_target_pairs={{0,4},{4,0},{8,12},{12,8},{16,20},{20,16},{24,28},{28,24},{1,5},{5... | collective-permute-start | bytes 3096584 | tf_op jit(solution)/shard_map/ppermute | solution.py:593
  60.0 2.9 %collective-permute-start.15 = (bf16[3,32,2176]{2,1,0:T(8,128)(2,1)S(1)}, bf16[3,32,2176]{2,1,0:T(8,128)(2,1)S(1)}, u32[]{:S(2)}, u32[]{:S(2)}) collective-permute-start(bf16[3,32,2176]{2,1,0:T(8,128)(2,1)S(1)} %maximum_add_fusion.refs_8_), channel_id=1, source_target_pairs={{0,4},{4,0},{8,12},{12,8},{16,20},{20,16},{24,28},{28,24},{1,5},{5... | collective-permute-start | bytes 1253384 | tf_op jit(solution)/shard_map/ppermute | solution.py:593
  60.0 3.5 %collective-permute-start.16 = (bf16[3,32,2176]{2,1,0:T(8,128)(2,1)S(1)}, bf16[3,32,2176]{2,1,0:T(8,128)(2,1)S(1)}, u32[]{:S(2)}, u32[]{:S(2)}) collective-permute-start(bf16[3,32,2176]{2,1,0:T(8,128)(2,1)S(1)} %collective-permute-done.9.refs_9_), channel_id=1, source_target_pairs={{0,4},{4,0},{8,12},{12,8},{16,20},{20,16},{24,28},{28,24},{1,5},{5... | collective-permute-start | bytes 1253384 | tf_op jit(solution)/shard_map/ppermute | solution.py:593
  60.5 7.2 %collective-permute-start.17 = (bf16[3,32,2176]{2,1,0:T(8,128)(2,1)S(1)}, bf16[3,32,2176]{2,1,0:T(8,128)(2,1)S(1)}, u32[]{:S(2)}, u32[]{:S(2)}) collective-permute-start(bf16[3,32,2176]{2,1,0:T(8,128)(2,1)S(1)} %collective-permute-done.9.refs_9_), channel_id=1, source_target_pairs={{0,16},{4,12},{8,24},{12,4},{16,0},{20,28},{24,8},{28,20},{1,17},{... | collective-permute-start | bytes 1253384 | tf_op jit(solution)/shard_map/ppermute | solution.py:593
  70.0 6.9 %collective-permute-start.19 = (bf16[4,1152,256]{2,1,0:T(8,128)(2,1)S(1)}, bf16[4,1152,256]{2,1,0:T(8,128)(2,1)S(1)}, u32[]{:S(2)}, u32[]{:S(2)}) collective-permute-start(bf16[4,1152,256]{2,1,0:T(8,128)(2,1)S(1)} %get-tuple-element.151.refs_16_.x_all), channel_id=1, source_target_pairs={{0,4},{4,0},{8,12},{12,8},{16,20},{20,16},{24,28},{28,24},{1,5},{5... | collective-permute-start | bytes 7077896 | tf_op jit(solution)/shard_map/ppermute | solution.py:593
  74.1 2.7 %collective-permute-start.20 = (bf16[2048,256]{1,0:T(8,128)(2,1)S(1)}, bf16[2048,256]{1,0:T(8,128)(2,1)S(1)}, u32[]{:S(2)}, u32[]{:S(2)}) collective-permute-start(bf16[2048,256]{1,0:T(8,128)(2,1)S(1)} %get-tuple-element.156), channel_id=1, source_target_pairs={{0,4},{4,0},{8,12},{12,8},{16,20},{20,16},{24,28},{28,24},{1,5},{5... | collective-permute-start | bytes 3145736 | tf_op jit(solution)/shard_map/ppermute | solution.py:593
  79.0 14.7 %collective-permute-start.22 = (bf16[2,4,32,2176]{3,2,1,0:T(8,128)(2,1)S(1)}, bf16[2,4,32,2176]{3,2,1,0:T(8,128)(2,1)S(1)}, u32[]{:S(2)}, u32[]{:S(2)}) collective-permute-start(bf16[2,4,32,2176]{3,2,1,0:T(8,128)(2,1)S(1)} %shard_map.205), channel_id=1, source_target_pairs={{0,8},{4,20},{8,0},{12,28},{16,24},{20,4},{24,16},{28,12},{1,9},{5... | collective-permute-start | bytes 3342344 | tf_op jit(solution)/shard_map/ppermute | solution.py:593
  87.1 5.0 %collective-permute-start.21 = (bf16[272,256]{1,0:T(8,128)(2,1)S(1)}, bf16[272,256]{1,0:T(8,128)(2,1)S(1)}, u32[]{:S(2)}, u32[]{:S(2)}) collective-permute-start(bf16[272,256]{1,0:T(8,128)(2,1)S(1)} %get-tuple-element.162), channel_id=1, source_target_pairs={{0,1},{1,2},{2,3},{3,0},{4,5},{5,6},{6,7},{7,4},{8,9},{9,10},{10,1... | collective-permute-start | bytes 417800 | tf_op jit(solution)/shard_map/ppermute | solution.py:595
  87.1 9.9 %collective-permute-start.28 = (bf16[2,528,256]{2,1,0:T(8,128)(2,1)S(1)}, bf16[2,528,256]{2,1,0:T(8,128)(2,1)S(1)}, u32[]{:S(2)}, u32[]{:S(2)}) collective-permute-start(bf16[2,528,256]{2,1,0:T(8,128)(2,1)S(1)} %get-tuple-element.175), channel_id=1, source_target_pairs={{0,4},{4,0},{8,12},{12,8},{16,20},{20,16},{24,28},{28,24},{1,5},{5... | collective-permute-start | bytes 1622024 | tf_op jit(solution)/shard_map/ppermute | solution.py:593
  93.7 15.7 %collective-permute-start.27 = (bf16[2,4,32,1152]{3,2,1,0:T(8,128)(2,1)S(1)}, bf16[2,4,32,1152]{3,2,1,0:T(8,128)(2,1)S(1)}, u32[]{:S(2)}, u32[]{:S(2)}) collective-permute-start(bf16[2,4,32,1152]{3,2,1,0:T(8,128)(2,1)S(1)} %get-tuple-element.173), channel_id=1, source_target_pairs={{0,8},{4,20},{8,0},{12,28},{16,24},{20,4},{24,16},{28,12},{1,9},{5... | collective-permute-start | bytes 1769480 | tf_op jit(solution)/shard_map/ppermute | solution.py:593
  94.9 14.5 %collective-permute-start.26 = (bf16[4,32,2176]{2,1,0:T(8,128)(2,1)S(1)}, bf16[4,32,2176]{2,1,0:T(8,128)(2,1)S(1)}, u32[]{:S(2)}, u32[]{:S(2)}) collective-permute-start(bf16[4,32,2176]{2,1,0:T(8,128)(2,1)S(1)} %fusion.2), channel_id=1, source_target_pairs={{0,16},{4,12},{8,24},{12,4},{16,0},{20,28},{24,8},{28,20},{1,17},{... | collective-permute-start | bytes 1671176 | tf_op jit(solution)/shard_map/ppermute | solution.py:593
  95.8 9.8 %collective-permute-start.24 = (bf16[272,256]{1,0:T(8,128)(2,1)S(1)}, bf16[272,256]{1,0:T(8,128)(2,1)S(1)}, u32[]{:S(2)}, u32[]{:S(2)}) collective-permute-start(bf16[272,256]{1,0:T(8,128)(2,1)S(1)} %get-tuple-element.170), channel_id=1, source_target_pairs={{0,2},{1,3},{2,0},{3,1},{4,6},{5,7},{6,4},{7,5},{8,10},{9,11},{10,... | collective-permute-start | bytes 417800 | tf_op jit(solution)/shard_map/ppermute | solution.py:595
  96.9 8.7 %collective-permute-start.25 = (bf16[272,256]{1,0:T(8,128)(2,1)S(1)}, bf16[272,256]{1,0:T(8,128)(2,1)S(1)}, u32[]{:S(2)}, u32[]{:S(2)}) collective-permute-start(bf16[272,256]{1,0:T(8,128)(2,1)S(1)} %get-tuple-element.171), channel_id=1, source_target_pairs={{0,3},{1,0},{2,1},{3,2},{4,7},{5,4},{6,5},{7,6},{8,11},{9,8},{10,9... | collective-permute-start | bytes 417800 | tf_op jit(solution)/shard_map/ppermute | solution.py:595
  109.4 6.9 %collective-permute-start.30 = (bf16[4,32,1152]{2,1,0:T(8,128)(2,1)S(1)}, bf16[4,32,1152]{2,1,0:T(8,128)(2,1)S(1)}, u32[]{:S(2)}, u32[]{:S(2)}) collective-permute-start(bf16[4,32,1152]{2,1,0:T(8,128)(2,1)S(1)} %fusion.4), channel_id=1, source_target_pairs={{0,16},{4,12},{8,24},{12,4},{16,0},{20,28},{24,8},{28,20},{1,17},{... | collective-permute-start | bytes 884744 | tf_op jit(solution)/shard_map/ppermute | solution.py:593
  110.3 17.7 %collective-permute-start.29 = (bf16[2,4,32,2176]{3,2,1,0:T(8,128)(2,1)S(1)}, bf16[2,4,32,2176]{3,2,1,0:T(8,128)(2,1)S(1)}, u32[]{:S(2)}, u32[]{:S(2)}) collective-permute-start(bf16[2,4,32,2176]{3,2,1,0:T(8,128)(2,1)S(1)} %get-tuple-element.178), channel_id=1, source_target_pairs={{0,8},{4,20},{8,0},{12,28},{16,24},{20,4},{24,16},{28,12},{1,9},{5... | collective-permute-start | bytes 3342344 | tf_op jit(solution)/shard_map/ppermute | solution.py:593
  110.6 7.6 %collective-permute-start.32 = (bf16[32,2176]{1,0:T(8,128)(2,1)S(1)}, bf16[32,2176]{1,0:T(8,128)(2,1)S(1)}, u32[]{:S(2)}, u32[]{:S(2)}) collective-permute-start(bf16[32,2176]{1,0:T(8,128)(2,1)S(1)} %get-tuple-element.240), channel_id=1, source_target_pairs={{0,1},{1,2},{2,3},{3,0},{4,5},{5,6},{6,7},{7,4},{8,9},{9,10},{10,1... | collective-permute-start | bytes 417800 | tf_op jit(solution)/shard_map/ppermute | solution.py:595
  111.2 11.6 %collective-permute-start.33 = (bf16[32,2176]{1,0:T(8,128)(2,1)S(1)}, bf16[32,2176]{1,0:T(8,128)(2,1)S(1)}, u32[]{:S(2)}, u32[]{:S(2)}) collective-permute-start(bf16[32,2176]{1,0:T(8,128)(2,1)S(1)} %get-tuple-element.239), channel_id=1, source_target_pairs={{0,2},{1,3},{2,0},{3,1},{4,6},{5,7},{6,4},{7,5},{8,10},{9,11},{10,... | collective-permute-start | bytes 417800 | tf_op jit(solution)/shard_map/ppermute | solution.py:595
  113.5 14.2 %collective-permute-start.34 = (bf16[32,2176]{1,0:T(8,128)(2,1)S(1)}, bf16[32,2176]{1,0:T(8,128)(2,1)S(1)}, u32[]{:S(2)}, u32[]{:S(2)}) collective-permute-start(bf16[32,2176]{1,0:T(8,128)(2,1)S(1)} %get-tuple-element.238), channel_id=1, source_target_pairs={{0,3},{1,0},{2,1},{3,2},{4,7},{5,4},{6,5},{7,6},{8,11},{9,8},{10,9... | collective-permute-start | bytes 417800 | tf_op jit(solution)/shard_map/ppermute | solution.py:595
  116.5 11.3 %collective-permute-start.31 = (bf16[32,1152]{1,0:T(8,128)(2,1)S(1)}, bf16[32,1152]{1,0:T(8,128)(2,1)S(1)}, u32[]{:S(2)}, u32[]{:S(2)}) collective-permute-start(bf16[32,1152]{1,0:T(8,128)(2,1)S(1)} %get-tuple-element.243), channel_id=1, source_target_pairs={{0,1},{1,2},{2,3},{3,0},{4,5},{5,6},{6,7},{7,4},{8,9},{9,10},{10,1... | collective-permute-start | bytes 221192 | tf_op jit(solution)/shard_map/ppermute | solution.py:595
  128.2 10.2 %collective-permute-start.35 = (bf16[4,32,2176]{2,1,0:T(8,128)(2,1)S(1)}, bf16[4,32,2176]{2,1,0:T(8,128)(2,1)S(1)}, u32[]{:S(2)}, u32[]{:S(2)}) collective-permute-start(bf16[4,32,2176]{2,1,0:T(8,128)(2,1)S(1)} %fusion.1), channel_id=1, source_target_pairs={{0,16},{4,12},{8,24},{12,4},{16,0},{20,28},{24,8},{28,20},{1,17},{... | collective-permute-start | bytes 1671176 | tf_op jit(solution)/shard_map/ppermute | solution.py:593
  128.8 6.0 %collective-permute-start.36 = (bf16[32,2176]{1,0:T(8,128)(2,1)S(1)}, bf16[32,2176]{1,0:T(8,128)(2,1)S(1)}, u32[]{:S(2)}, u32[]{:S(2)}) collective-permute-start(bf16[32,2176]{1,0:T(8,128)(2,1)S(1)} %fusion.10.refs_0_), channel_id=1, source_target_pairs={{0,8},{4,20},{8,0},{12,28},{16,24},{20,4},{24,16},{28,12},{1,9},{5... | collective-permute-start | bytes 417800 | tf_op jit(solution)/shard_map/ppermute | solution.py:593
  129.3 3.5 %collective-permute-start.38 = (bf16[32,1152]{1,0:T(8,128)(2,1)S(1)}, bf16[32,1152]{1,0:T(8,128)(2,1)S(1)}, u32[]{:S(2)}, u32[]{:S(2)}) collective-permute-start(bf16[32,1152]{1,0:T(8,128)(2,1)S(1)} %get-tuple-element.241), channel_id=1, source_target_pairs={{0,3},{1,0},{2,1},{3,2},{4,7},{5,4},{6,5},{7,6},{8,11},{9,8},{10,9... | collective-permute-start | bytes 221192 | tf_op jit(solution)/shard_map/ppermute | solution.py:595
  129.3 5.4 %collective-permute-start.37 = (bf16[32,1152]{1,0:T(8,128)(2,1)S(1)}, bf16[32,1152]{1,0:T(8,128)(2,1)S(1)}, u32[]{:S(2)}, u32[]{:S(2)}) collective-permute-start(bf16[32,1152]{1,0:T(8,128)(2,1)S(1)} %get-tuple-element.242), channel_id=1, source_target_pairs={{0,2},{1,3},{2,0},{3,1},{4,6},{5,7},{6,4},{7,5},{8,10},{9,11},{10,... | collective-permute-start | bytes 221192 | tf_op jit(solution)/shard_map/ppermute | solution.py:595
  138.7 7.0 %collective-permute-start.41 = (bf16[32,2176]{1,0:T(8,128)(2,1)S(1)}, bf16[32,2176]{1,0:T(8,128)(2,1)S(1)}, u32[]{:S(2)}, u32[]{:S(2)}) collective-permute-start(bf16[32,2176]{1,0:T(8,128)(2,1)S(1)} %get-tuple-element.237), channel_id=1, source_target_pairs={{0,1},{1,2},{2,3},{3,0},{4,5},{5,6},{6,7},{7,4},{8,9},{9,10},{10,1... | collective-permute-start | bytes 417800 | tf_op jit(solution)/shard_map/ppermute | solution.py:595
  138.8 11.2 %collective-permute-start.42 = (bf16[32,2176]{1,0:T(8,128)(2,1)S(1)}, bf16[32,2176]{1,0:T(8,128)(2,1)S(1)}, u32[]{:S(2)}, u32[]{:S(2)}) collective-permute-start(bf16[32,2176]{1,0:T(8,128)(2,1)S(1)} %get-tuple-element.236), channel_id=1, source_target_pairs={{0,2},{1,3},{2,0},{3,1},{4,6},{5,7},{6,4},{7,5},{8,10},{9,11},{10,... | collective-permute-start | bytes 417800 | tf_op jit(solution)/shard_map/ppermute | solution.py:595
  140.8 13.1 %collective-permute-start.43 = (bf16[32,2176]{1,0:T(8,128)(2,1)S(1)}, bf16[32,2176]{1,0:T(8,128)(2,1)S(1)}, u32[]{:S(2)}, u32[]{:S(2)}) collective-permute-start(bf16[32,2176]{1,0:T(8,128)(2,1)S(1)} %get-tuple-element.235), channel_id=1, source_target_pairs={{0,3},{1,0},{2,1},{3,2},{4,7},{5,4},{6,5},{7,6},{8,11},{9,8},{10,9... | collective-permute-start | bytes 417800 | tf_op jit(solution)/shard_map/ppermute | solution.py:595
  141.0 12.9 %collective-permute-start.39 = (bf16[2,32,2176]{2,1,0:T(8,128)(2,1)S(1)}, bf16[2,32,2176]{2,1,0:T(8,128)(2,1)S(1)}, u32[]{:S(2)}, u32[]{:S(2)}) collective-permute-start(bf16[2,32,2176]{2,1,0:T(8,128)(2,1)S(1)} %pad_maximum_fusion.6), channel_id=1, source_target_pairs={{0,16},{4,12},{8,24},{12,4},{16,0},{20,28},{24,8},{28,20},{1,17},{... | collective-permute-start | bytes 835592 | tf_op jit(solution)/shard_map/ppermute | solution.py:593
  142.1 3.6 %collective-permute-start.40 = (bf16[32,1152]{1,0:T(8,128)(2,1)S(1)}, bf16[32,1152]{1,0:T(8,128)(2,1)S(1)}, u32[]{:S(2)}, u32[]{:S(2)}) collective-permute-start(bf16[32,1152]{1,0:T(8,128)(2,1)S(1)} %fusion.12.refs_0_), channel_id=1, source_target_pairs={{0,8},{4,20},{8,0},{12,28},{16,24},{20,4},{24,16},{28,12},{1,9},{5... | collective-permute-start | bytes 221192 | tf_op jit(solution)/shard_map/ppermute | solution.py:593
  154.0 6.8 %collective-permute-start.46 = (bf16[4,32,2176]{2,1,0:T(8,128)(2,1)S(1)}, bf16[4,32,2176]{2,1,0:T(8,128)(2,1)S(1)}, u32[]{:S(2)}, u32[]{:S(2)}) collective-permute-start(bf16[4,32,2176]{2,1,0:T(8,128)(2,1)S(1)} %pad_maximum_fusion.3), channel_id=1, source_target_pairs={{0,4},{4,0},{8,12},{12,8},{16,20},{20,16},{24,28},{28,24},{1,5},{5... | collective-permute-start | bytes 1671176 | tf_op jit(solution)/shard_map/ppermute | solution.py:593
  154.5 6.2 %collective-permute-start.45 = (bf16[2,32,1152]{2,1,0:T(8,128)(2,1)S(1)}, bf16[2,32,1152]{2,1,0:T(8,128)(2,1)S(1)}, u32[]{:S(2)}, u32[]{:S(2)}) collective-permute-start(bf16[2,32,1152]{2,1,0:T(8,128)(2,1)S(1)} %pad_maximum_fusion.8), channel_id=1, source_target_pairs={{0,16},{4,12},{8,24},{12,4},{16,0},{20,28},{24,8},{28,20},{1,17},{... | collective-permute-start | bytes 442376 | tf_op jit(solution)/shard_map/ppermute | solution.py:593
  155.3 5.5 %collective-permute-start.44 = (bf16[32,2176]{1,0:T(8,128)(2,1)S(1)}, bf16[32,2176]{1,0:T(8,128)(2,1)S(1)}, u32[]{:S(2)}, u32[]{:S(2)}) collective-permute-start(bf16[32,2176]{1,0:T(8,128)(2,1)S(1)} %fusion.7.refs_0_), channel_id=1, source_target_pairs={{0,8},{4,20},{8,0},{12,28},{16,24},{20,4},{24,16},{28,12},{1,9},{5... | collective-permute-start | bytes 417800 | tf_op jit(solution)/shard_map/ppermute | solution.py:593
  160.8 3.4 %collective-permute-start.48 = (bf16[4,32,1152]{2,1,0:T(8,128)(2,1)S(1)}, bf16[4,32,1152]{2,1,0:T(8,128)(2,1)S(1)}, u32[]{:S(2)}, u32[]{:S(2)}) collective-permute-start(bf16[4,32,1152]{2,1,0:T(8,128)(2,1)S(1)} %pad_maximum_fusion.5), channel_id=1, source_target_pairs={{0,4},{4,0},{8,12},{12,8},{16,20},{20,16},{24,28},{28,24},{1,5},{5... | collective-permute-start | bytes 884744 | tf_op jit(solution)/shard_map/ppermute | solution.py:593
  161.3 5.8 %collective-permute-start.47 = (bf16[2,32,2176]{2,1,0:T(8,128)(2,1)S(1)}, bf16[2,32,2176]{2,1,0:T(8,128)(2,1)S(1)}, u32[]{:S(2)}, u32[]{:S(2)}) collective-permute-start(bf16[2,32,2176]{2,1,0:T(8,128)(2,1)S(1)} %pad_maximum_fusion.7), channel_id=1, source_target_pairs={{0,16},{4,12},{8,24},{12,4},{16,0},{20,28},{24,8},{28,20},{1,17},{... | collective-permute-start | bytes 835592 | tf_op jit(solution)/shard_map/ppermute | solution.py:593
  167.1 2.6 %collective-permute-start.49 = (bf16[4,32,2176]{2,1,0:T(8,128)(2,1)S(1)}, bf16[4,32,2176]{2,1,0:T(8,128)(2,1)S(1)}, u32[]{:S(2)}, u32[]{:S(2)}) collective-permute-start(bf16[4,32,2176]{2,1,0:T(8,128)(2,1)S(1)} %pad_maximum_fusion.4), channel_id=1, source_target_pairs={{0,4},{4,0},{8,12},{12,8},{16,20},{20,16},{24,28},{28,24},{1,5},{5... | collective-permute-start | bytes 1671176 | tf_op jit(solution)/shard_map/ppermute | solution.py:593
  (15 other events, 132.1 us)

commit v7 on v6

--- a/solution.py
+++ b/solution.py
@@ -748,8 +748,7 @@
 
     keep = (blocks, SHARE, wide)
     (tower_out,) = tower_parts_of((2, 3), [(2,) + keep], idx)
-    tower_parts = [*tower_parts_of((0, 1), [keep, keep], after(idx, tower_out)), tower_out]
-    tower_arrived = hop(tower_parts[2], first)
+    tower_arrived = hop(tower_out, first)
     *input_grads, dz, dz_rest, last_far, dz_far = call(
         functools.partial(cross_backward, blocks=blocks, layers=layers, width=width, pad=pad, depth=depth),
         tuple([shape((pad, part), BF16)] * blocks)
@@ -770,7 +769,7 @@
             vmem((16, part), F32),
         ],
         [
-            after(idx, tower_parts[2]),
+            after(idx, tower_out),
             lines,
             *pieces,
             cross_weight,
@@ -806,7 +805,9 @@
         )
 
     last_parts = cross_parts_of(layers - 1, 1, last_far, idx)
-    cross_parts = cross_parts_of(0, layers - 1, dz_far, after(idx, last_parts[2]))
+    tower_parts = [*tower_parts_of((0, 1), [keep, keep], after(idx, last_parts[2])), tower_out]
+    grad_pieces = [input_grads[0]] + turns(input_grads[1:])
+    cross_parts = cross_parts_of(0, layers - 1, dz_far, after(idx, last_parts[2], grad_pieces[1]))
 
     down = lambda value: value.astype(BF16)
     up = lambda value: value.astype(F32)
@@ -832,8 +833,7 @@
     def far_of(mine, one, two):
         return hop(jnp.concatenate([jnp.stack([mine, one]), two]), pair)
 
-    grad_pieces = [input_grads[0]] + turns(input_grads[1:])
-    grad_pieces[1], tower_arrived, last_send = join(grad_pieces[1], tower_arrived, last_parts[2])
+    tower_arrived, last_send = join(tower_arrived, last_parts[2])
     tower_second = far_send(tower_parts, tower_arrived)
     last_arrived = hop(last_send, first)
     *grad_pieces, tower_second, last_arrived, cross_send = join(

time: 173 us -> 173 us (level)
    ppermute x29, waiting for transfers between devices: 29.4 us -> 25.4 us  [per_device(): hop = lambda value, perm: lax.ppermute(value, 'dp', perm)]
    ppermute x29, starting transfers between devices: 20 us -> 23.5 us  [per_device(): hop = lambda value, perm: lax.ppermute(value, 'dp', perm)]
    ppermute x18, waiting for transfers between devices: 50.8 us -> 53.1 us  [per_device(): lax.ppermute(value, 'mp', turn_by(r + 1))]
    ppermute x18, starting transfers between devices: 14 us -> 12.2 us  [per_device(): lax.ppermute(value, 'mp', turn_by(r + 1))]
where the time goes in v7:
time: 173 us; the launch traced here: 172 us
  waiting for transfers between devices  91.9 us (53%)
  starting transfers between devices  36.5 us (21%)
  Pallas kernels  35.9 us (21%)
  local copies, waits for them, and re-layouts  5.04 us (3%)
  other arithmetic  1.88 us (1%)
    ppermute x18, waiting for transfers between devices, per_device(): lax.ppermute(value, 'mp', turn_by(r + 1))  53.1 us
    pallas_call x12, Pallas kernels, call(): pl.pallas_call(kernel, out_shape=outs, in_specs=[SMEM] + specs, out_specs...  35.9 us
    ppermute x29, waiting for transfers between devices, per_device(): hop = lambda value, perm: lax.ppermute(value, 'dp', perm)  25.4 us
    ppermute x29, starting transfers between devices, per_device(): hop = lambda value, perm: lax.ppermute(value, 'dp', perm)  23.5 us
    ppermute x3, waiting for transfers between devices, per_device(): turn = lambda value, r: lax.ppermute(value, 'mp', turn_by(r))  13.4 us
    ppermute x18, starting transfers between devices, per_device(): lax.ppermute(value, 'mp', turn_by(r + 1))  12.2 us
  transfers between devices with their start and end apart: 50, of which 33 were waited for; matrix products, arithmetic and copies ran while one was open for 1% of the time, Pallas kernels for 18%

profile of v7, /device:TPU:9, one launch (start us, length us, event | category | flops | bytes accessed | tf_op | source)
XLA Modules:
  0.0 172.5 jit_solution(18196712975665117415)
XLA Ops:
  0.7 1.1 dynamic-slice_bitcast_fusion
  2.1 1.3 collective-permute-start
  4.5 1.4 collective-permute-start.2
  6.1 1.5 copy-done
  8.6 2.9 %shard_map.202 = (bf16[32,2176]{1,0:T(8,128)(2,1)S(1)}, bf16[256,1152]{1,0:T(8,128)(2,1)S(1)}, bf16[96,128]{1,0:T(8,128)(2,1)S(1)}, bf16[343,256]{1,0:T(8,128)(2...) custom-call(s32[4]{0:T(128)S(1)} %pad_add_fusion.idx, ...), custom_call_target="tpu_custom_call" | custom-call | bytes 2097152 | tf_op jit(solution)/shard_map/pallas_call | solution.py:45
  11.5 8.8 %collective-permute-done.1 = bf16[32,3200]{1,0:T(8,128)(2,1)S(1)} collective-permute-done((bf16[32,3200]{1,0:T(8,128)(2,1)S(1)}, bf16[32,3200]{1,0:T(8,128)(2,1)S(1)}, u32[]{:S(2)}, u32[]{:S(2)}) %collective-permute-start.1) | collective-permute-done | bytes 204832 | tf_op jit(solution)/shard_map/ppermute | solution.py:595
  20.3 2.8 %collective-permute-done.2 = bf16[32,3200]{1,0:T(8,128)(2,1)S(1)} collective-permute-done((bf16[32,3200]{1,0:T(8,128)(2,1)S(1)}, bf16[32,3200]{1,0:T(8,128)(2,1)S(1)}, u32[]{:S(2)}, u32[]{:S(2)}) %collective-permute-start.2) | collective-permute-done | bytes 204832 | tf_op jit(solution)/shard_map/ppermute | solution.py:595
  23.3 1.3 collective-permute-start.3
  24.5 1.2 collective-permute-start.4
  26.0 1.5 collective-permute-start.7
  27.5 2.5 %collective-permute-done.5 = bf16[32,2176]{1,0:T(8,128)(2,1)S(1)} collective-permute-done((bf16[32,2176]{1,0:T(8,128)(2,1)S(1)}, bf16[32,2176]{1,0:T(8,128)(2,1)S(1)}, u32[]{:S(2)}, u32[]{:S(2)}) %collective-permute-start.5) | collective-permute-done | bytes 139296 | tf_op jit(solution)/shard_map/ppermute | solution.py:595
  30.0 6.8 %collective-permute-done.6 = bf16[32,2176]{1,0:T(8,128)(2,1)S(1)} collective-permute-done((bf16[32,2176]{1,0:T(8,128)(2,1)S(1)}, bf16[32,2176]{1,0:T(8,128)(2,1)S(1)}, u32[]{:S(2)}, u32[]{:S(2)}) %collective-permute-start.6) | collective-permute-done | bytes 139296 | tf_op jit(solution)/shard_map/ppermute | solution.py:595
  36.8 2.9 %collective-permute-done.7 = bf16[32,2176]{1,0:T(8,128)(2,1)S(1)} collective-permute-done((bf16[32,2176]{1,0:T(8,128)(2,1)S(1)}, bf16[32,2176]{1,0:T(8,128)(2,1)S(1)}, u32[]{:S(2)}, u32[]{:S(2)}) %collective-permute-start.7) | collective-permute-done | bytes 139296 | tf_op jit(solution)/shard_map/ppermute | solution.py:595
  40.7 1.2 collective-permute-start.8
  44.5 3.7 %collective-permute-done.11.refs_1_.refs_3_.refs_2_ = bf16[343,256]{1,0:T(8,128)(2,1)S(1)} collective-permute-done((bf16[343,256]{1,0:T(8,128)(2,1)S(1)}, bf16[343,256]{1,0:T(8,128)(2,1)S(1)}, u32[]{:S(2)}, u32[]{:S(2)}) %collective-permute-start.11) | collective-permute-done | bytes 175648 | tf_op jit(solution)/shard_map/ppermute | solution.py:643
  48.2 9.4 %collective-permute-done.12.refs_2_.refs_4_.refs_3_ = bf16[343,256]{1,0:T(8,128)(2,1)S(1)} collective-permute-done((bf16[343,256]{1,0:T(8,128)(2,1)S(1)}, bf16[343,256]{1,0:T(8,128)(2,1)S(1)}, u32[]{:S(2)}, u32[]{:S(2)}) %collective-permute-start.12) | collective-permute-done | bytes 175648 | tf_op jit(solution)/shard_map/ppermute | solution.py:643
  57.7 1.4 collective-permute-done.8.refs_6_.refs_10_.refs_7_
  61.4 1.5 collective-permute-done.15.refs_12_
  63.5 4.0 %shard_map.203 = (f32[3,1088,256]{2,1,0:T(8,128)S(1)}, bf16[4,1152,256]{2,1,0:T(8,128)(2,1)S(1)}) custom-call(s32[4]{0:T(128)S(1)} %pad_add_fusion.idx, bf16[343,256]{1,0:T(8,128)(2,1)S(1)} %get-tuple-element.140.refs_0_.refs_2_.refs_1_, bf16[343,256]{1,0:T(8,128)(2,1)S(1)} %collective-permute-done.11.refs_1_.refs_3_.refs_2_, ...), custom_call_target="tpu_custom_call" | custom-call | flops 1925185536 | bytes 20971520 | tf_op jit(solution)/shard_map/pallas_call | solution.py:45
  68.6 1.4 collective-permute-done.18.refs_15_
  70.3 3.8 %shard_map.204 = (bf16[3,1024,256]{2,1,0:T(8,128)(2,1)S(1)}, bf16[2048,256]{1,0:T(8,128)(2,1)S(1)}, f32[1024,128]{1,0:T(8,128)S(1)}, bf16[1024,2176]{1,0:T(8,128...) custom-call(s32[4]{0:T(128)S(1)} %pad_add_fusion.idx, s32[1,1024]{1,0:T(1,128)S(1)} %bitcast.114, ...), custom_call_target="tpu_custom_call" | custom-call | flops 2415919104 | bytes 10485760 | tf_op jit(solution)/shard_map/pallas_call | solution.py:45
  74.3 2.5 %collective-permute-done.20.far = bf16[2048,256]{1,0:T(8,128)(2,1)S(1)} collective-permute-done((bf16[2048,256]{1,0:T(8,128)(2,1)S(1)}, bf16[2048,256]{1,0:T(8,128)(2,1)S(1)}, u32[]{:S(2)}, u32[]{:S(2)}) %collective-permute-start.20) | collective-permute-done | bytes 1048608 | tf_op jit(solution)/shard_map/ppermute | solution.py:593
  76.9 2.1 %shard_map.205 = bf16[2,4,32,2176]{3,2,1,0:T(8,128)(2,1)S(1)} custom-call(s32[4]{0:T(128)S(1)} %pad_add_fusion.idx, bf16[4,1152,256]{2,1,0:T(8,128)(2,1)S(1)} %get-tuple-element.151.refs_16_.x_all, bf16[4,1152,256]{2,1,0:T(8,128)(2,1)S(1)} %collective-permute-done.19.x_far, bf16[3,1024,256]{2,1,0:T(8,128)(2,1)S(1)} %get-tuple-element.155.acts.refs_11_, ...), custom_call_target="tpu_custom_call" | custom-call | flops 603979776 | bytes 10485760 | tf_op jit(solution)/shard_map/pallas_call | solution.py:45
  80.1 6.6 %shard_map.206 = (bf16[272,256]{1,0:T(8,128)(2,1)S(1)}, bf16[272,256]{1,0:T(8,128)(2,1)S(1)}, bf16[272,256]{1,0:T(8,128)(2,1)S(1)}, bf16[272,256]{1,0:T(8,128)(2...) custom-call(s32[4]{0:T(128)S(1)} %pad_add_fusion.idx, ...), custom_call_target="tpu_custom_call" | custom-call | flops 1925185536 | bytes 20971520 | tf_op jit(solution)/shard_map/pallas_call | solution.py:45
  88.3 2.3 %shard_map.207 = (bf16[4,32,1152]{2,1,0:T(8,128)(2,1)S(1)}, bf16[4,32,1152]{2,1,0:T(8,128)(2,1)S(1)}, bf16[2,4,32,1152]{3,2,1,0:T(8,128)(2,1)S(1)}) custom-call(s32[4]{0:T(128)S(1)} %pad_add_fusion.idx, bf16[4,1152,256]{2,1,0:T(8,128)(2,1)S(1)} %get-tuple-element.151.refs_16_.x_all, bf16[4,1152,256]{2,1,0:T(8,128)(2,1)S(1)} %collective-permute-done.19.x_far, ...), custom_call_target="tpu_custom_call" | custom-call | flops 641728512 | bytes 10485760 | tf_op jit(solution)/shard_map/pallas_call | solution.py:45
  90.6 1.9 %shard_map.208 = (bf16[4,32,2176]{2,1,0:T(8,128)(2,1)S(1)}, bf16[4,32,2176]{2,1,0:T(8,128)(2,1)S(1)}) custom-call(s32[4]{0:T(128)S(1)} %pad_add_fusion.idx, bf16[4,1152,256]{2,1,0:T(8,128)(2,1)S(1)} %get-tuple-element.151.refs_16_.x_all, bf16[4,1152,256]{2,1,0:T(8,128)(2,1)S(1)} %collective-permute-done.19.x_far, ...), custom_call_target="tpu_custom_call" | custom-call | flops 603979776 | bytes 10485760 | tf_op jit(solution)/shard_map/pallas_call | solution.py:45
  92.5 1.2 collective-permute-done.22
  96.9 3.1 %collective-permute-done.23.refs_1_ = bf16[272,256]{1,0:T(8,128)(2,1)S(1)} collective-permute-done((bf16[272,256]{1,0:T(8,128)(2,1)S(1)}, bf16[272,256]{1,0:T(8,128)(2,1)S(1)}, u32[]{:S(2)}, u32[]{:S(2)}) %collective-permute-start.23) | collective-permute-done | bytes 139296 | tf_op jit(solution)/shard_map/ppermute | solution.py:595
  100.5 3.8 %shard_map.209 = (bf16[4,32,2176]{2,1,0:T(8,128)(2,1)S(1)}, bf16[4,32,2176]{2,1,0:T(8,128)(2,1)S(1)}, bf16[2,4,32,2176]{3,2,1,0:T(8,128)(2,1)S(1)}) custom-call(s32[4]{0:T(128)S(1)} %pad_add_fusion.idx, bf16[4,1152,256]{2,1,0:T(8,128)(2,1)S(1)} %get-tuple-element.151.refs_16_.x_all, bf16[4,1152,256]{2,1,0:T(8,128)(2,1)S(1)} %collective-permute-done.19.x_far, ...), custom_call_target="tpu_custom_call" | custom-call | flops 1283457024 | bytes 10485760 | tf_op jit(solution)/shard_map/pallas_call | solution.py:45
  104.3 4.3 %collective-permute-done.25.refs_3_ = bf16[272,256]{1,0:T(8,128)(2,1)S(1)} collective-permute-done((bf16[272,256]{1,0:T(8,128)(2,1)S(1)}, bf16[272,256]{1,0:T(8,128)(2,1)S(1)}, u32[]{:S(2)}, u32[]{:S(2)}) %collective-permute-start.25) | collective-permute-done | bytes 139296 | tf_op jit(solution)/shard_map/ppermute | solution.py:595
  110.3 1.7 %collective-permute-start.29 = (bf16[2,4,32,2176]{3,2,1,0:T(8,128)(2,1)S(1)}, bf16[2,4,32,2176]{3,2,1,0:T(8,128)(2,1)S(1)}, u32[]{:S(2)}, u32[]{:S(2)}) collective-permute-start(bf16[2,4,32,2176]{3,2,1,0:T(8,128)(2,1)S(1)} %get-tuple-element.178), channel_id=1, source_target_pairs={{0,8},{4,20},{8,0},{12,28},{16,24},{20,4},{24,16},{28,12},{1,9},{5... | collective-permute-start | bytes 3342344 | tf_op jit(solution)/shard_map/ppermute | solution.py:593
  112.7 1.2 collective-permute-start.34
  113.8 1.6 collective-permute-done.30
  115.6 1.6 shard_map.210
  118.0 10.0 %collective-permute-done.34 = bf16[32,2176]{1,0:T(8,128)(2,1)S(1)} collective-permute-done((bf16[32,2176]{1,0:T(8,128)(2,1)S(1)}, bf16[32,2176]{1,0:T(8,128)(2,1)S(1)}, u32[]{:S(2)}, u32[]{:S(2)}) %collective-permute-start.34) | collective-permute-done | bytes 139296 | tf_op jit(solution)/shard_map/ppermute | solution.py:595
  128.8 1.5 collective-permute-start.36
  131.2 2.5 %collective-permute-done.38 = bf16[32,1152]{1,0:T(8,128)(2,1)S(1)} collective-permute-done((bf16[32,1152]{1,0:T(8,128)(2,1)S(1)}, bf16[32,1152]{1,0:T(8,128)(2,1)S(1)}, u32[]{:S(2)}, u32[]{:S(2)}) %collective-permute-start.38) | collective-permute-done | bytes 73760 | tf_op jit(solution)/shard_map/ppermute | solution.py:595
  134.4 4.1 %collective-permute-done.35 = bf16[4,32,2176]{2,1,0:T(8,128)(2,1)S(1)} collective-permute-done((bf16[4,32,2176]{2,1,0:T(8,128)(2,1)S(1)}, bf16[4,32,2176]{2,1,0:T(8,128)(2,1)S(1)}, u32[]{:S(2)}, u32[]{:S(2)}) %collective-permute-start.35) | collective-permute-done | bytes 557088 | tf_op jit(solution)/shard_map/ppermute | solution.py:593
  138.9 2.0 %collective-permute-start.42 = (bf16[32,2176]{1,0:T(8,128)(2,1)S(1)}, bf16[32,2176]{1,0:T(8,128)(2,1)S(1)}, u32[]{:S(2)}, u32[]{:S(2)}) collective-permute-start(bf16[32,2176]{1,0:T(8,128)(2,1)S(1)} %get-tuple-element.236), channel_id=1, source_target_pairs={{0,2},{1,3},{2,0},{3,1},{4,6},{5,7},{6,4},{7,5},{8,10},{9,11},{10,... | collective-permute-start | bytes 417800 | tf_op jit(solution)/shard_map/ppermute | solution.py:595
  143.3 2.6 %collective-permute-done.40.refs_1_ = bf16[32,1152]{1,0:T(8,128)(2,1)S(1)} collective-permute-done((bf16[32,1152]{1,0:T(8,128)(2,1)S(1)}, bf16[32,1152]{1,0:T(8,128)(2,1)S(1)}, u32[]{:S(2)}, u32[]{:S(2)}) %collective-permute-start.40) | collective-permute-done | bytes 73760 | tf_op jit(solution)/shard_map/ppermute | solution.py:593
  145.9 4.2 %collective-permute-done.42 = bf16[32,2176]{1,0:T(8,128)(2,1)S(1)} collective-permute-done((bf16[32,2176]{1,0:T(8,128)(2,1)S(1)}, bf16[32,2176]{1,0:T(8,128)(2,1)S(1)}, u32[]{:S(2)}, u32[]{:S(2)}) %collective-permute-start.42) | collective-permute-done | bytes 139296 | tf_op jit(solution)/shard_map/ppermute | solution.py:595
  150.1 3.8 %collective-permute-done.43 = bf16[32,2176]{1,0:T(8,128)(2,1)S(1)} collective-permute-done((bf16[32,2176]{1,0:T(8,128)(2,1)S(1)}, bf16[32,2176]{1,0:T(8,128)(2,1)S(1)}, u32[]{:S(2)}, u32[]{:S(2)}) %collective-permute-start.43) | collective-permute-done | bytes 139296 | tf_op jit(solution)/shard_map/ppermute | solution.py:595
  154.6 1.1 collective-permute-start.45
  155.9 4.7 %collective-permute-done.44.refs_1_ = bf16[32,2176]{1,0:T(8,128)(2,1)S(1)} collective-permute-done((bf16[32,2176]{1,0:T(8,128)(2,1)S(1)}, bf16[32,2176]{1,0:T(8,128)(2,1)S(1)}, u32[]{:S(2)}, u32[]{:S(2)}) %collective-permute-start.44) | collective-permute-done | bytes 139296 | tf_op jit(solution)/shard_map/ppermute | solution.py:593
  161.0 1.6 collective-permute-start.47
  162.5 2.5 %shard_map.211 = (f32[1040,256]{1,0:T(8,128)}, f32[256,1024]{1,0:T(8,128)}, f32[3,256]{1,0:T(4,128)S(1)}, f32[1,1]{1,0:T(1,128)}) custom-call(s32[4]{0:T(128)S(1)} %pad_add_fusion.idx, bf16[32,2176]{1,0:T(8,128)(2,1)S(1)} %fusion.10.refs_0_, bf16[32,2176]{1,0:T(8,128)(2,1)S(1)} %collective-permute-done.36.refs_1_, ...), custom_call_target="tpu_custom_call" | custom-call | bytes 4194304 | tf_op jit(solution)/shard_map/pallas_call | solution.py:45
  165.1 1.8 %shard_map.212 = (f32[3,260,1040]{2,1,0:T(8,128)}, f32[1,260]{1,0:T(1,128)S(1)}) custom-call(s32[4]{0:T(128)S(1)} %pad_add_fusion.idx, bf16[32,1152]{1,0:T(8,128)(2,1)S(1)} %fusion.12.refs_0_, bf16[32,1152]{1,0:T(8,128)(2,1)S(1)} %collective-permute-done.40.refs_1_, bf16[2,32,1152]{2,1,0:T(8,128)(2,1)S(1)} %collective-permute-done.45.refs_2_, ...), custom_call_target="tpu_custom_call" | custom-call | bytes 4194304 | tf_op jit(solution)/shard_map/pallas_call | solution.py:45
  169.6 2.7 %shard_map.213 = (f32[3,260,1040]{2,1,0:T(8,128)}, f32[3,260]{1,0:T(4,128)}) custom-call(s32[4]{0:T(128)S(1)} %pad_add_fusion.idx, bf16[32,2176]{1,0:T(8,128)(2,1)S(1)} %fusion.7.refs_0_, bf16[32,2176]{1,0:T(8,128)(2,1)S(1)} %collective-permute-done.44.refs_1_, ...), custom_call_target="tpu_custom_call", output_to_operand_aliasing={{0}: (5, {})} | custom-call | bytes 4194304 | tf_op jit(solution)/shard_map/pallas_call | solution.py:45
  (128 shorter events, 29.8 us)
Async XLA Ops:
  2.1 9.4 %collective-permute-start = (bf16[32,3200]{1,0:T(8,128)(2,1)S(1)}, bf16[32,3200]{1,0:T(8,128)(2,1)S(1)}, u32[]{:S(2)}, u32[]{:S(2)}) collective-permute-start(bf16[32,3200]{1,0:T(8,128)(2,1)S(1)} %concatenate.15), channel_id=1, source_target_pairs={{0,1},{1,2},{2,3},{3,0},{4,5},{5,6},{6,7},{7,4},{8,9},{9,10},{10,1... | collective-permute-start | bytes 614408 | tf_op jit(solution)/shard_map/ppermute | solution.py:595
  3.4 16.9 %collective-permute-start.1 = (bf16[32,3200]{1,0:T(8,128)(2,1)S(1)}, bf16[32,3200]{1,0:T(8,128)(2,1)S(1)}, u32[]{:S(2)}, u32[]{:S(2)}) collective-permute-start(bf16[32,3200]{1,0:T(8,128)(2,1)S(1)} %concatenate.15), channel_id=1, source_target_pairs={{0,2},{1,3},{2,0},{3,1},{4,6},{5,7},{6,4},{7,5},{8,10},{9,11},{10,... | collective-permute-start | bytes 614408 | tf_op jit(solution)/shard_map/ppermute | solution.py:595
  4.5 18.7 %collective-permute-start.2 = (bf16[32,3200]{1,0:T(8,128)(2,1)S(1)}, bf16[32,3200]{1,0:T(8,128)(2,1)S(1)}, u32[]{:S(2)}, u32[]{:S(2)}) collective-permute-start(bf16[32,3200]{1,0:T(8,128)(2,1)S(1)} %concatenate.15), channel_id=1, source_target_pairs={{0,3},{1,0},{2,1},{3,2},{4,7},{5,4},{6,5},{7,6},{8,11},{9,8},{10,9... | collective-permute-start | bytes 614408 | tf_op jit(solution)/shard_map/ppermute | solution.py:595
  23.3 16.5 %collective-permute-start.3 = (bf16[3,32,3200]{2,1,0:T(8,128)(2,1)S(1)}, bf16[3,32,3200]{2,1,0:T(8,128)(2,1)S(1)}, u32[]{:S(2)}, u32[]{:S(2)}) collective-permute-start(bf16[3,32,3200]{2,1,0:T(8,128)(2,1)S(1)} %pad_maximum_fusion.2), channel_id=1, source_target_pairs={{0,8},{4,20},{8,0},{12,28},{16,24},{20,4},{24,16},{28,12},{1,9},{5... | collective-permute-start | bytes 1843208 | tf_op jit(solution)/shard_map/ppermute | solution.py:593
  24.5 15.3 %collective-permute-start.4 = (bf16[3,32,3200]{2,1,0:T(8,128)(2,1)S(1)}, bf16[3,32,3200]{2,1,0:T(8,128)(2,1)S(1)}, u32[]{:S(2)}, u32[]{:S(2)}) collective-permute-start(bf16[3,32,3200]{2,1,0:T(8,128)(2,1)S(1)} %pad_maximum_fusion.2), channel_id=1, source_target_pairs={{0,16},{4,12},{8,24},{12,4},{16,0},{20,28},{24,8},{28,20},{1,17},{... | collective-permute-start | bytes 1843208 | tf_op jit(solution)/shard_map/ppermute | solution.py:593
  25.8 4.2 %collective-permute-start.5 = (bf16[32,2176]{1,0:T(8,128)(2,1)S(1)}, bf16[32,2176]{1,0:T(8,128)(2,1)S(1)}, u32[]{:S(2)}, u32[]{:S(2)}) collective-permute-start(bf16[32,2176]{1,0:T(8,128)(2,1)S(1)} %get-tuple-element.126), channel_id=1, source_target_pairs={{0,1},{1,2},{2,3},{3,0},{4,5},{5,6},{6,7},{7,4},{8,9},{9,10},{10,1... | collective-permute-start | bytes 417800 | tf_op jit(solution)/shard_map/ppermute | solution.py:595
  25.8 11.0 %collective-permute-start.6 = (bf16[32,2176]{1,0:T(8,128)(2,1)S(1)}, bf16[32,2176]{1,0:T(8,128)(2,1)S(1)}, u32[]{:S(2)}, u32[]{:S(2)}) collective-permute-start(bf16[32,2176]{1,0:T(8,128)(2,1)S(1)} %get-tuple-element.126), channel_id=1, source_target_pairs={{0,2},{1,3},{2,0},{3,1},{4,6},{5,7},{6,4},{7,5},{8,10},{9,11},{10,... | collective-permute-start | bytes 417800 | tf_op jit(solution)/shard_map/ppermute | solution.py:595
  26.0 13.7 %collective-permute-start.7 = (bf16[32,2176]{1,0:T(8,128)(2,1)S(1)}, bf16[32,2176]{1,0:T(8,128)(2,1)S(1)}, u32[]{:S(2)}, u32[]{:S(2)}) collective-permute-start(bf16[32,2176]{1,0:T(8,128)(2,1)S(1)} %get-tuple-element.126), channel_id=1, source_target_pairs={{0,3},{1,0},{2,1},{3,2},{4,7},{5,4},{6,5},{7,6},{8,11},{9,8},{10,9... | collective-permute-start | bytes 417800 | tf_op jit(solution)/shard_map/ppermute | solution.py:595
  40.1 3.9 %collective-permute-start.10 = (bf16[3,3,32,3200]{3,2,1,0:T(8,128)(2,1)S(1)}, bf16[3,3,32,3200]{3,2,1,0:T(8,128)(2,1)S(1)}, u32[]{:S(2)}, u32[]{:S(2)}) collective-permute-start(bf16[3,3,32,3200]{3,2,1,0:T(8,128)(2,1)S(1)} %pad_maximum_fusion.refs_5_.refs_6_), channel_id=1, source_target_pairs={{0,4},{4,0},{8,12},{12,8},{16,20},{20,16},{24,28},{28,24},{1,5},{5... | collective-permute-start | bytes 5529608 | tf_op jit(solution)/shard_map/ppermute | solution.py:593
  40.7 18.3 %collective-permute-start.8 = (bf16[3,32,5376]{2,1,0:T(8,128)(2,1)S(1)}, bf16[3,32,5376]{2,1,0:T(8,128)(2,1)S(1)}, u32[]{:S(2)}, u32[]{:S(2)}) collective-permute-start(bf16[3,32,5376]{2,1,0:T(8,128)(2,1)S(1)} %pad_maximum_fusion.1), channel_id=1, source_target_pairs={{0,16},{4,12},{8,24},{12,4},{16,0},{20,28},{24,8},{28,20},{1,17},{... | collective-permute-start | bytes 3096584 | tf_op jit(solution)/shard_map/ppermute | solution.py:593
  42.0 15.7 %collective-permute-start.9 = (bf16[3,32,2176]{2,1,0:T(8,128)(2,1)S(1)}, bf16[3,32,2176]{2,1,0:T(8,128)(2,1)S(1)}, u32[]{:S(2)}, u32[]{:S(2)}) collective-permute-start(bf16[3,32,2176]{2,1,0:T(8,128)(2,1)S(1)} %maximum_add_fusion.refs_8_), channel_id=1, source_target_pairs={{0,8},{4,20},{8,0},{12,28},{16,24},{20,4},{24,16},{28,12},{1,9},{5... | collective-permute-start | bytes 1253384 | tf_op jit(solution)/shard_map/ppermute | solution.py:593
  42.8 5.4 %collective-permute-start.11 = (bf16[343,256]{1,0:T(8,128)(2,1)S(1)}, bf16[343,256]{1,0:T(8,128)(2,1)S(1)}, u32[]{:S(2)}, u32[]{:S(2)}) collective-permute-start(bf16[343,256]{1,0:T(8,128)(2,1)S(1)} %get-tuple-element.135), channel_id=1, source_target_pairs={{0,1},{1,2},{2,3},{3,0},{4,5},{5,6},{6,7},{7,4},{8,9},{9,10},{10,1... | collective-permute-start | bytes 526856 | tf_op jit(solution)/shard_map/ppermute | solution.py:643
  42.8 14.9 %collective-permute-start.12 = (bf16[343,256]{1,0:T(8,128)(2,1)S(1)}, bf16[343,256]{1,0:T(8,128)(2,1)S(1)}, u32[]{:S(2)}, u32[]{:S(2)}) collective-permute-start(bf16[343,256]{1,0:T(8,128)(2,1)S(1)} %get-tuple-element.137), channel_id=1, source_target_pairs={{0,2},{1,3},{2,0},{3,1},{4,6},{5,7},{6,4},{7,5},{8,10},{9,11},{10,... | collective-permute-start | bytes 526856 | tf_op jit(solution)/shard_map/ppermute | solution.py:643
  44.0 15.3 %collective-permute-start.13 = (bf16[343,256]{1,0:T(8,128)(2,1)S(1)}, bf16[343,256]{1,0:T(8,128)(2,1)S(1)}, u32[]{:S(2)}, u32[]{:S(2)}) collective-permute-start(bf16[343,256]{1,0:T(8,128)(2,1)S(1)} %get-tuple-element.139), channel_id=1, source_target_pairs={{0,3},{1,0},{2,1},{3,2},{4,7},{5,4},{6,5},{7,6},{8,11},{9,8},{10,9... | collective-permute-start | bytes 526856 | tf_op jit(solution)/shard_map/ppermute | solution.py:643
  59.3 4.2 %collective-permute-start.14 = (bf16[3,32,5376]{2,1,0:T(8,128)(2,1)S(1)}, bf16[3,32,5376]{2,1,0:T(8,128)(2,1)S(1)}, u32[]{:S(2)}, u32[]{:S(2)}) collective-permute-start(bf16[3,32,5376]{2,1,0:T(8,128)(2,1)S(1)} %collective-permute-done.8.refs_6_.refs_10_.refs_7_), channel_id=1, source_target_pairs={{0,4},{4,0},{8,12},{12,8},{16,20},{20,16},{24,28},{28,24},{1,5},{5... | collective-permute-start | bytes 3096584 | tf_op jit(solution)/shard_map/ppermute | solution.py:593
  60.0 2.9 %collective-permute-start.15 = (bf16[3,32,2176]{2,1,0:T(8,128)(2,1)S(1)}, bf16[3,32,2176]{2,1,0:T(8,128)(2,1)S(1)}, u32[]{:S(2)}, u32[]{:S(2)}) collective-permute-start(bf16[3,32,2176]{2,1,0:T(8,128)(2,1)S(1)} %maximum_add_fusion.refs_8_), channel_id=1, source_target_pairs={{0,4},{4,0},{8,12},{12,8},{16,20},{20,16},{24,28},{28,24},{1,5},{5... | collective-permute-start | bytes 1253384 | tf_op jit(solution)/shard_map/ppermute | solution.py:593
  60.0 3.5 %collective-permute-start.16 = (bf16[3,32,2176]{2,1,0:T(8,128)(2,1)S(1)}, bf16[3,32,2176]{2,1,0:T(8,128)(2,1)S(1)}, u32[]{:S(2)}, u32[]{:S(2)}) collective-permute-start(bf16[3,32,2176]{2,1,0:T(8,128)(2,1)S(1)} %collective-permute-done.9.refs_9_), channel_id=1, source_target_pairs={{0,4},{4,0},{8,12},{12,8},{16,20},{20,16},{24,28},{28,24},{1,5},{5... | collective-permute-start | bytes 1253384 | tf_op jit(solution)/shard_map/ppermute | solution.py:593
  60.5 7.2 %collective-permute-start.17 = (bf16[3,32,2176]{2,1,0:T(8,128)(2,1)S(1)}, bf16[3,32,2176]{2,1,0:T(8,128)(2,1)S(1)}, u32[]{:S(2)}, u32[]{:S(2)}) collective-permute-start(bf16[3,32,2176]{2,1,0:T(8,128)(2,1)S(1)} %collective-permute-done.9.refs_9_), channel_id=1, source_target_pairs={{0,16},{4,12},{8,24},{12,4},{16,0},{20,28},{24,8},{28,20},{1,17},{... | collective-permute-start | bytes 1253384 | tf_op jit(solution)/shard_map/ppermute | solution.py:593
  70.0 6.9 %collective-permute-start.19 = (bf16[4,1152,256]{2,1,0:T(8,128)(2,1)S(1)}, bf16[4,1152,256]{2,1,0:T(8,128)(2,1)S(1)}, u32[]{:S(2)}, u32[]{:S(2)}) collective-permute-start(bf16[4,1152,256]{2,1,0:T(8,128)(2,1)S(1)} %get-tuple-element.151.refs_16_.x_all), channel_id=1, source_target_pairs={{0,4},{4,0},{8,12},{12,8},{16,20},{20,16},{24,28},{28,24},{1,5},{5... | collective-permute-start | bytes 7077896 | tf_op jit(solution)/shard_map/ppermute | solution.py:593
  74.1 2.7 %collective-permute-start.20 = (bf16[2048,256]{1,0:T(8,128)(2,1)S(1)}, bf16[2048,256]{1,0:T(8,128)(2,1)S(1)}, u32[]{:S(2)}, u32[]{:S(2)}) collective-permute-start(bf16[2048,256]{1,0:T(8,128)(2,1)S(1)} %get-tuple-element.156), channel_id=1, source_target_pairs={{0,4},{4,0},{8,12},{12,8},{16,20},{20,16},{24,28},{28,24},{1,5},{5... | collective-permute-start | bytes 3145736 | tf_op jit(solution)/shard_map/ppermute | solution.py:593
  79.0 14.7 %collective-permute-start.22 = (bf16[2,4,32,2176]{3,2,1,0:T(8,128)(2,1)S(1)}, bf16[2,4,32,2176]{3,2,1,0:T(8,128)(2,1)S(1)}, u32[]{:S(2)}, u32[]{:S(2)}) collective-permute-start(bf16[2,4,32,2176]{3,2,1,0:T(8,128)(2,1)S(1)} %shard_map.205), channel_id=1, source_target_pairs={{0,8},{4,20},{8,0},{12,28},{16,24},{20,4},{24,16},{28,12},{1,9},{5... | collective-permute-start | bytes 3342344 | tf_op jit(solution)/shard_map/ppermute | solution.py:593
  87.1 13.5 %collective-permute-start.28 = (bf16[2,528,256]{2,1,0:T(8,128)(2,1)S(1)}, bf16[2,528,256]{2,1,0:T(8,128)(2,1)S(1)}, u32[]{:S(2)}, u32[]{:S(2)}) collective-permute-start(bf16[2,528,256]{2,1,0:T(8,128)(2,1)S(1)} %get-tuple-element.175), channel_id=1, source_target_pairs={{0,4},{4,0},{8,12},{12,8},{16,20},{20,16},{24,28},{28,24},{1,5},{5... | collective-permute-start | bytes 1622024 | tf_op jit(solution)/shard_map/ppermute | solution.py:593
  93.7 15.7 %collective-permute-start.27 = (bf16[2,4,32,1152]{3,2,1,0:T(8,128)(2,1)S(1)}, bf16[2,4,32,1152]{3,2,1,0:T(8,128)(2,1)S(1)}, u32[]{:S(2)}, u32[]{:S(2)}) collective-permute-start(bf16[2,4,32,1152]{3,2,1,0:T(8,128)(2,1)S(1)} %get-tuple-element.173), channel_id=1, source_target_pairs={{0,8},{4,20},{8,0},{12,28},{16,24},{20,4},{24,16},{28,12},{1,9},{5... | collective-permute-start | bytes 1769480 | tf_op jit(solution)/shard_map/ppermute | solution.py:593
  94.9 14.5 %collective-permute-start.26 = (bf16[4,32,2176]{2,1,0:T(8,128)(2,1)S(1)}, bf16[4,32,2176]{2,1,0:T(8,128)(2,1)S(1)}, u32[]{:S(2)}, u32[]{:S(2)}) collective-permute-start(bf16[4,32,2176]{2,1,0:T(8,128)(2,1)S(1)} %fusion.2), channel_id=1, source_target_pairs={{0,16},{4,12},{8,24},{12,4},{16,0},{20,28},{24,8},{28,20},{1,17},{... | collective-permute-start | bytes 1671176 | tf_op jit(solution)/shard_map/ppermute | solution.py:593
  95.8 4.2 %collective-permute-start.23 = (bf16[272,256]{1,0:T(8,128)(2,1)S(1)}, bf16[272,256]{1,0:T(8,128)(2,1)S(1)}, u32[]{:S(2)}, u32[]{:S(2)}) collective-permute-start(bf16[272,256]{1,0:T(8,128)(2,1)S(1)} %get-tuple-element.169), channel_id=1, source_target_pairs={{0,1},{1,2},{2,3},{3,0},{4,5},{5,6},{6,7},{7,4},{8,9},{9,10},{10,1... | collective-permute-start | bytes 417800 | tf_op jit(solution)/shard_map/ppermute | solution.py:595
  95.8 8.5 %collective-permute-start.24 = (bf16[272,256]{1,0:T(8,128)(2,1)S(1)}, bf16[272,256]{1,0:T(8,128)(2,1)S(1)}, u32[]{:S(2)}, u32[]{:S(2)}) collective-permute-start(bf16[272,256]{1,0:T(8,128)(2,1)S(1)} %get-tuple-element.170), channel_id=1, source_target_pairs={{0,2},{1,3},{2,0},{3,1},{4,6},{5,7},{6,4},{7,5},{8,10},{9,11},{10,... | collective-permute-start | bytes 417800 | tf_op jit(solution)/shard_map/ppermute | solution.py:595
  100.0 8.6 %collective-permute-start.25 = (bf16[272,256]{1,0:T(8,128)(2,1)S(1)}, bf16[272,256]{1,0:T(8,128)(2,1)S(1)}, u32[]{:S(2)}, u32[]{:S(2)}) collective-permute-start(bf16[272,256]{1,0:T(8,128)(2,1)S(1)} %get-tuple-element.171), channel_id=1, source_target_pairs={{0,3},{1,0},{2,1},{3,2},{4,7},{5,4},{6,5},{7,6},{8,11},{9,8},{10,9... | collective-permute-start | bytes 417800 | tf_op jit(solution)/shard_map/ppermute | solution.py:595
  109.4 6.0 %collective-permute-start.30 = (bf16[4,32,1152]{2,1,0:T(8,128)(2,1)S(1)}, bf16[4,32,1152]{2,1,0:T(8,128)(2,1)S(1)}, u32[]{:S(2)}, u32[]{:S(2)}) collective-permute-start(bf16[4,32,1152]{2,1,0:T(8,128)(2,1)S(1)} %fusion.4), channel_id=1, source_target_pairs={{0,16},{4,12},{8,24},{12,4},{16,0},{20,28},{24,8},{28,20},{1,17},{... | collective-permute-start | bytes 884744 | tf_op jit(solution)/shard_map/ppermute | solution.py:593
  110.3 17.8 %collective-permute-start.29 = (bf16[2,4,32,2176]{3,2,1,0:T(8,128)(2,1)S(1)}, bf16[2,4,32,2176]{3,2,1,0:T(8,128)(2,1)S(1)}, u32[]{:S(2)}, u32[]{:S(2)}) collective-permute-start(bf16[2,4,32,2176]{3,2,1,0:T(8,128)(2,1)S(1)} %get-tuple-element.178), channel_id=1, source_target_pairs={{0,8},{4,20},{8,0},{12,28},{16,24},{20,4},{24,16},{28,12},{1,9},{5... | collective-permute-start | bytes 3342344 | tf_op jit(solution)/shard_map/ppermute | solution.py:593
  112.3 4.9 %collective-permute-start.32 = (bf16[32,2176]{1,0:T(8,128)(2,1)S(1)}, bf16[32,2176]{1,0:T(8,128)(2,1)S(1)}, u32[]{:S(2)}, u32[]{:S(2)}) collective-permute-start(bf16[32,2176]{1,0:T(8,128)(2,1)S(1)} %get-tuple-element.240), channel_id=1, source_target_pairs={{0,1},{1,2},{2,3},{3,0},{4,5},{5,6},{6,7},{7,4},{8,9},{9,10},{10,1... | collective-permute-start | bytes 417800 | tf_op jit(solution)/shard_map/ppermute | solution.py:595
  112.4 5.6 %collective-permute-start.33 = (bf16[32,2176]{1,0:T(8,128)(2,1)S(1)}, bf16[32,2176]{1,0:T(8,128)(2,1)S(1)}, u32[]{:S(2)}, u32[]{:S(2)}) collective-permute-start(bf16[32,2176]{1,0:T(8,128)(2,1)S(1)} %get-tuple-element.239), channel_id=1, source_target_pairs={{0,2},{1,3},{2,0},{3,1},{4,6},{5,7},{6,4},{7,5},{8,10},{9,11},{10,... | collective-permute-start | bytes 417800 | tf_op jit(solution)/shard_map/ppermute | solution.py:595
  112.7 15.3 %collective-permute-start.34 = (bf16[32,2176]{1,0:T(8,128)(2,1)S(1)}, bf16[32,2176]{1,0:T(8,128)(2,1)S(1)}, u32[]{:S(2)}, u32[]{:S(2)}) collective-permute-start(bf16[32,2176]{1,0:T(8,128)(2,1)S(1)} %get-tuple-element.238), channel_id=1, source_target_pairs={{0,3},{1,0},{2,1},{3,2},{4,7},{5,4},{6,5},{7,6},{8,11},{9,8},{10,9... | collective-permute-start | bytes 417800 | tf_op jit(solution)/shard_map/ppermute | solution.py:595
  115.6 12.4 %collective-permute-start.31 = (bf16[32,1152]{1,0:T(8,128)(2,1)S(1)}, bf16[32,1152]{1,0:T(8,128)(2,1)S(1)}, u32[]{:S(2)}, u32[]{:S(2)}) collective-permute-start(bf16[32,1152]{1,0:T(8,128)(2,1)S(1)} %get-tuple-element.243), channel_id=1, source_target_pairs={{0,1},{1,2},{2,3},{3,0},{4,5},{5,6},{6,7},{7,4},{8,9},{9,10},{10,1... | collective-permute-start | bytes 221192 | tf_op jit(solution)/shard_map/ppermute | solution.py:595
  128.3 10.2 %collective-permute-start.35 = (bf16[4,32,2176]{2,1,0:T(8,128)(2,1)S(1)}, bf16[4,32,2176]{2,1,0:T(8,128)(2,1)S(1)}, u32[]{:S(2)}, u32[]{:S(2)}) collective-permute-start(bf16[4,32,2176]{2,1,0:T(8,128)(2,1)S(1)} %fusion.1), channel_id=1, source_target_pairs={{0,16},{4,12},{8,24},{12,4},{16,0},{20,28},{24,8},{28,20},{1,17},{... | collective-permute-start | bytes 1671176 | tf_op jit(solution)/shard_map/ppermute | solution.py:593
  128.8 5.6 %collective-permute-start.36 = (bf16[32,2176]{1,0:T(8,128)(2,1)S(1)}, bf16[32,2176]{1,0:T(8,128)(2,1)S(1)}, u32[]{:S(2)}, u32[]{:S(2)}) collective-permute-start(bf16[32,2176]{1,0:T(8,128)(2,1)S(1)} %fusion.10.refs_0_), channel_id=1, source_target_pairs={{0,8},{4,20},{8,0},{12,28},{16,24},{20,4},{24,16},{28,12},{1,9},{5... | collective-permute-start | bytes 417800 | tf_op jit(solution)/shard_map/ppermute | solution.py:593
  130.2 3.5 %collective-permute-start.38 = (bf16[32,1152]{1,0:T(8,128)(2,1)S(1)}, bf16[32,1152]{1,0:T(8,128)(2,1)S(1)}, u32[]{:S(2)}, u32[]{:S(2)}) collective-permute-start(bf16[32,1152]{1,0:T(8,128)(2,1)S(1)} %get-tuple-element.241), channel_id=1, source_target_pairs={{0,3},{1,0},{2,1},{3,2},{4,7},{5,4},{6,5},{7,6},{8,11},{9,8},{10,9... | collective-permute-start | bytes 221192 | tf_op jit(solution)/shard_map/ppermute | solution.py:595
  130.2 4.1 %collective-permute-start.37 = (bf16[32,1152]{1,0:T(8,128)(2,1)S(1)}, bf16[32,1152]{1,0:T(8,128)(2,1)S(1)}, u32[]{:S(2)}, u32[]{:S(2)}) collective-permute-start(bf16[32,1152]{1,0:T(8,128)(2,1)S(1)} %get-tuple-element.242), channel_id=1, source_target_pairs={{0,2},{1,3},{2,0},{3,1},{4,6},{5,7},{6,4},{7,5},{8,10},{9,11},{10,... | collective-permute-start | bytes 221192 | tf_op jit(solution)/shard_map/ppermute | solution.py:595
  138.8 7.1 %collective-permute-start.41 = (bf16[32,2176]{1,0:T(8,128)(2,1)S(1)}, bf16[32,2176]{1,0:T(8,128)(2,1)S(1)}, u32[]{:S(2)}, u32[]{:S(2)}) collective-permute-start(bf16[32,2176]{1,0:T(8,128)(2,1)S(1)} %get-tuple-element.237), channel_id=1, source_target_pairs={{0,1},{1,2},{2,3},{3,0},{4,5},{5,6},{6,7},{7,4},{8,9},{9,10},{10,1... | collective-permute-start | bytes 417800 | tf_op jit(solution)/shard_map/ppermute | solution.py:595
  138.9 11.3 %collective-permute-start.42 = (bf16[32,2176]{1,0:T(8,128)(2,1)S(1)}, bf16[32,2176]{1,0:T(8,128)(2,1)S(1)}, u32[]{:S(2)}, u32[]{:S(2)}) collective-permute-start(bf16[32,2176]{1,0:T(8,128)(2,1)S(1)} %get-tuple-element.236), channel_id=1, source_target_pairs={{0,2},{1,3},{2,0},{3,1},{4,6},{5,7},{6,4},{7,5},{8,10},{9,11},{10,... | collective-permute-start | bytes 417800 | tf_op jit(solution)/shard_map/ppermute | solution.py:595
  140.8 13.1 %collective-permute-start.43 = (bf16[32,2176]{1,0:T(8,128)(2,1)S(1)}, bf16[32,2176]{1,0:T(8,128)(2,1)S(1)}, u32[]{:S(2)}, u32[]{:S(2)}) collective-permute-start(bf16[32,2176]{1,0:T(8,128)(2,1)S(1)} %get-tuple-element.235), channel_id=1, source_target_pairs={{0,3},{1,0},{2,1},{3,2},{4,7},{5,4},{6,5},{7,6},{8,11},{9,8},{10,9... | collective-permute-start | bytes 417800 | tf_op jit(solution)/shard_map/ppermute | solution.py:595
  141.2 12.7 %collective-permute-start.39 = (bf16[2,32,2176]{2,1,0:T(8,128)(2,1)S(1)}, bf16[2,32,2176]{2,1,0:T(8,128)(2,1)S(1)}, u32[]{:S(2)}, u32[]{:S(2)}) collective-permute-start(bf16[2,32,2176]{2,1,0:T(8,128)(2,1)S(1)} %pad_maximum_fusion.6), channel_id=1, source_target_pairs={{0,16},{4,12},{8,24},{12,4},{16,0},{20,28},{24,8},{28,20},{1,17},{... | collective-permute-start | bytes 835592 | tf_op jit(solution)/shard_map/ppermute | solution.py:593
  142.4 3.6 %collective-permute-start.40 = (bf16[32,1152]{1,0:T(8,128)(2,1)S(1)}, bf16[32,1152]{1,0:T(8,128)(2,1)S(1)}, u32[]{:S(2)}, u32[]{:S(2)}) collective-permute-start(bf16[32,1152]{1,0:T(8,128)(2,1)S(1)} %fusion.12.refs_0_), channel_id=1, source_target_pairs={{0,8},{4,20},{8,0},{12,28},{16,24},{20,4},{24,16},{28,12},{1,9},{5... | collective-permute-start | bytes 221192 | tf_op jit(solution)/shard_map/ppermute | solution.py:593
  154.0 6.6 %collective-permute-start.46 = (bf16[4,32,2176]{2,1,0:T(8,128)(2,1)S(1)}, bf16[4,32,2176]{2,1,0:T(8,128)(2,1)S(1)}, u32[]{:S(2)}, u32[]{:S(2)}) collective-permute-start(bf16[4,32,2176]{2,1,0:T(8,128)(2,1)S(1)} %pad_maximum_fusion.3), channel_id=1, source_target_pairs={{0,4},{4,0},{8,12},{12,8},{16,20},{20,16},{24,28},{28,24},{1,5},{5... | collective-permute-start | bytes 1671176 | tf_op jit(solution)/shard_map/ppermute | solution.py:593
  154.6 6.0 %collective-permute-start.45 = (bf16[2,32,1152]{2,1,0:T(8,128)(2,1)S(1)}, bf16[2,32,1152]{2,1,0:T(8,128)(2,1)S(1)}, u32[]{:S(2)}, u32[]{:S(2)}) collective-permute-start(bf16[2,32,1152]{2,1,0:T(8,128)(2,1)S(1)} %pad_maximum_fusion.8), channel_id=1, source_target_pairs={{0,16},{4,12},{8,24},{12,4},{16,0},{20,28},{24,8},{28,20},{1,17},{... | collective-permute-start | bytes 442376 | tf_op jit(solution)/shard_map/ppermute | solution.py:593
  155.8 4.8 %collective-permute-start.44 = (bf16[32,2176]{1,0:T(8,128)(2,1)S(1)}, bf16[32,2176]{1,0:T(8,128)(2,1)S(1)}, u32[]{:S(2)}, u32[]{:S(2)}) collective-permute-start(bf16[32,2176]{1,0:T(8,128)(2,1)S(1)} %fusion.7.refs_0_), channel_id=1, source_target_pairs={{0,8},{4,20},{8,0},{12,28},{16,24},{20,4},{24,16},{28,12},{1,9},{5... | collective-permute-start | bytes 417800 | tf_op jit(solution)/shard_map/ppermute | solution.py:593
  160.6 4.4 %collective-permute-start.48 = (bf16[4,32,1152]{2,1,0:T(8,128)(2,1)S(1)}, bf16[4,32,1152]{2,1,0:T(8,128)(2,1)S(1)}, u32[]{:S(2)}, u32[]{:S(2)}) collective-permute-start(bf16[4,32,1152]{2,1,0:T(8,128)(2,1)S(1)} %pad_maximum_fusion.5), channel_id=1, source_target_pairs={{0,4},{4,0},{8,12},{12,8},{16,20},{20,16},{24,28},{28,24},{1,5},{5... | collective-permute-start | bytes 884744 | tf_op jit(solution)/shard_map/ppermute | solution.py:593
  161.0 5.9 %collective-permute-start.47 = (bf16[2,32,2176]{2,1,0:T(8,128)(2,1)S(1)}, bf16[2,32,2176]{2,1,0:T(8,128)(2,1)S(1)}, u32[]{:S(2)}, u32[]{:S(2)}) collective-permute-start(bf16[2,32,2176]{2,1,0:T(8,128)(2,1)S(1)} %pad_maximum_fusion.7), channel_id=1, source_target_pairs={{0,16},{4,12},{8,24},{12,4},{16,0},{20,28},{24,8},{28,20},{1,17},{... | collective-permute-start | bytes 835592 | tf_op jit(solution)/shard_map/ppermute | solution.py:593
  166.9 2.7 %collective-permute-start.49 = (bf16[4,32,2176]{2,1,0:T(8,128)(2,1)S(1)}, bf16[4,32,2176]{2,1,0:T(8,128)(2,1)S(1)}, u32[]{:S(2)}, u32[]{:S(2)}) collective-permute-start(bf16[4,32,2176]{2,1,0:T(8,128)(2,1)S(1)} %pad_maximum_fusion.4), channel_id=1, source_target_pairs={{0,4},{4,0},{8,12},{12,8},{16,20},{20,16},{24,28},{28,24},{1,5},{5... | collective-permute-start | bytes 1671176 | tf_op jit(solution)/shard_map/ppermute | solution.py:593
  (15 other events, 131.2 us)
